TPU v7x, 32 devices: a whole 2x2x4 slice. The times are simulated.
32 devices in a mesh: seq: 4 (over x, core), head: 4 (over z), rep: 2 (over y).
Axes of the slice: x: 2, y: 2, z: 4, core: 2. Of those that a mesh axis runs over, the one named last changes fastest.
Arguments:
- token_ids: int32 [2048], P(('rep', 'seq')), parts along dimension 0, may hold values from 0 to 15
- embedding: float32 [16, 256], replicated, may hold values from -6 to 6
- complement: int32 [256], replicated, may hold values from 0 to 255, each once
- prenorm_first: float32 [256], replicated, may hold values from 0.1 to 1.9
- inproj_first: float32 [256, 2, 512], P(None, None, 'head'), may hold values from -0.375 to 0.375
- statemap_first: float32 [256, 2, 128], replicated, may hold values from -0.375 to 0.375
- stepmap_first: float32 [256, 8], P(None, 'head'), may hold values from -0.375 to 0.375
- stepbias_first: float32 [8], P('head'), may hold values from -1 to 1
- rates_first: float32 [8], P('head'), may hold values from 0.000185546875 to 0.11, as said below
- skipgain_first: float32 [8], P('head'), may hold values from 0.5 to 1.5
- outnorm_first: float32 [512], P('head'), may hold values from 0.1 to 1.9
- outproj_first: float32 [512, 256], P('head'), may hold values from -0.25 to 0.25
- prenorm_second: float32 [256], replicated, may hold values from 0.1 to 1.9
- inproj_second: float32 [256, 2, 512], P(None, None, 'head'), may hold values from -0.375 to 0.375
- statemap_second: float32 [256, 2, 128], replicated, may hold values from -0.375 to 0.375
- stepmap_second: float32 [256, 8], P(None, 'head'), may hold values from -0.375 to 0.375
- stepbias_second: float32 [8], P('head'), may hold values from -1 to 1
- rates_second: float32 [8], P('head'), may hold values from 0.000185546875 to 0.11, as said below
- skipgain_second: float32 [8], P('head'), may hold values from 0.5 to 1.5
- outnorm_second: float32 [512], P('head'), may hold values from 0.1 to 1.9
- outproj_second: float32 [512, 256], P('head'), may hold values from -0.25 to 0.25
Outputs:
- strand_out: float32 [2048, 256], P(('rep', 'seq', 'head')), parts along dimension 0
There are 2 independent parts, one for each index of `rep`. A program takes and returns all parts, laid end to end along the dimension named above; an argument that names none is the same for every part. Nothing has to cross between parts.
Inputs may be any that keep to these rules, and one draw needn't show every extreme that they name: `complement`: each channel index appears once. `rates_first`: positive rates. `rates_second`: positive rates.
All inputs are finite; a program needn't handle non-finite values.
Results may differ from a plain program's by a relative error of at most 0.00018.
Values sent between devices are 32-bit elements; how exact they have to be, the bound alone decides.
No kernel may reach another device: no remote copies, remote signals or barrier semaphores. Data moves between devices by JAX's collectives and lax.ppermute only.
A program may use at most 64 MiB of HBM per device.

v0:
```python
import jax
import jax.numpy as jnp
from jax import lax
from jax.sharding import PartitionSpec as P

BLOCK = 256


highest = lax.Precision.HIGHEST
epsilon = 1e-05


def entering_2(value, axis, join, neutral, backward):
    count, mine = (lax.axis_size(axis), lax.axis_index(axis))
    pieces = jax.tree.map(lambda part: lax.all_gather(part, axis), value)
    if backward:
        pieces = jax.tree.map(lambda part: part[::-1], pieces)
        mine = count - 1 - mine
    running = jax.tree.map(
        lambda part, zero: jnp.full_like(part, 0) + jnp.asarray(zero, part.dtype), value, neutral
    )

    def step(position, running):
        longer = join(running, jax.tree.map(lambda part: part[position], pieces))
        return jax.tree.map(lambda new, old: jnp.where(position < mine, new, old), longer, running)

    return lax.fori_loop(0, count - 1, step, running)


def partner(value, axis, apart):
    mask = 2**apart
    pairs = [(source, source ^ mask) for source in range(lax.axis_size(axis))]
    return lax.ppermute(value, axis, pairs)


def matmul(left, right):
    return jnp.dot(left, right, precision=highest, preferred_element_type=jnp.float32)


def rms_scale(values, gain_vec):
    return (
        values * lax.rsqrt(jnp.mean(values * values, axis=-1, keepdims=True) + epsilon) * gain_vec
    )


def running(values, axis_number, reverse):
    if reverse:
        return jnp.flip(jnp.cumsum(jnp.flip(values, axis_number), axis_number), axis_number)
    return jnp.cumsum(values, axis_number)


def project(layer_in, prenorm, inproj, statemap, stepmap, stepbias, rates):
    normed = rms_scale(layer_in, prenorm)
    length = layer_in.shape[0]
    inner_width = inproj.shape[2]
    head_count = stepmap.shape[1]
    both_parts = matmul(normed, inproj.reshape(inproj.shape[0], 2 * inner_width))
    gate_vals = both_parts[:, :inner_width]
    x_heads = both_parts[:, inner_width:].reshape(length, head_count, inner_width // head_count)
    state_width = statemap.shape[2]
    write_read = matmul(normed, statemap.reshape(statemap.shape[0], 2 * state_width))
    write_vecs = write_read[:, :state_width]
    read_vecs = write_read[:, state_width:]
    step_sizes = jax.nn.softplus(matmul(normed, stepmap) + stepbias)
    log_decay = -rates * step_sizes
    return (gate_vals, x_heads, write_vecs, read_vecs, step_sizes, log_decay)


def gated_norm(outputs, gate_vals, outnorm):
    length, head_count, head_dim = outputs.shape
    gated_vals = outputs * jax.nn.silu(gate_vals).reshape(outputs.shape)
    normed = gated_vals * lax.rsqrt(
        jnp.mean(gated_vals * gated_vals, axis=-1, keepdims=True) + epsilon
    )
    return normed.reshape(length, head_count * head_dim) * outnorm


def pair_products(write_vecs, read_vecs):
    blocks = write_vecs.shape[0] // BLOCK
    return jnp.einsum(
        "kqn,ksn->kqs",
        read_vecs.reshape(blocks, BLOCK, -1),
        write_vecs.reshape(blocks, BLOCK, -1),
        precision=highest,
    )


def combine(earlier, latter):
    return (earlier[0] * latter[0], latter[0][:, None, None] * earlier[1] + latter[1])


def state_space(x_heads, step_sizes, log_decay, write_vecs, read_vecs, products, skipgain, reverse):
    length, head_count, head_dim = x_heads.shape
    blocks = length // BLOCK
    x_blocks = x_heads.reshape(blocks, BLOCK, head_count, head_dim)
    step_blocks = step_sizes.reshape(blocks, BLOCK, head_count).transpose(0, 2, 1)
    log_blocks = log_decay.reshape(blocks, BLOCK, head_count).transpose(0, 2, 1)
    write_blocks = write_vecs.reshape(blocks, BLOCK, -1)
    read_blocks = read_vecs.reshape(blocks, BLOCK, -1)
    cumulative = running(log_blocks, 2, reverse)
    differ = cumulative[:, :, :, None] - cumulative[:, :, None, :]
    positions = jnp.arange(BLOCK)
    if reverse:
        allowed = positions[None, :] >= positions[:, None]
        end_log = cumulative[:, :, 0]
    else:
        allowed = positions[None, :] <= positions[:, None]
        end_log = cumulative[:, :, -1]
    weights = (
        jnp.where(allowed, jnp.exp(jnp.where(allowed, differ, 0.0)), 0.0)
        * products[:, None]
        * step_blocks[:, :, None, :]
    )
    intra = jnp.einsum("khqs,kshp->kqhp", weights, x_blocks, precision=highest)
    scaled = (
        x_blocks
        * (jnp.exp(end_log[:, :, None] - cumulative) * step_blocks).transpose(0, 2, 1)[
            :, :, :, None
        ]
    )
    states = jnp.einsum("kshp,ksn->khpn", scaled, write_blocks, precision=highest)

    def block_step(carry_state, item_pair):
        decay_now, state_now = item_pair
        return (decay_now[:, None, None] * carry_state + state_now, carry_state)

    local_end, entering = lax.scan(
        block_step,
        jnp.zeros(states.shape[1:], jnp.float32),
        (jnp.exp(end_log), states),
        reverse=reverse,
    )
    prior_log = running(end_log, 0, reverse) - end_log
    decay_total = jnp.exp(jnp.sum(end_log, axis=0))
    identity = (jnp.ones_like(decay_total), jnp.zeros_like(local_end))
    if reverse:
        carried = entering_2((decay_total, local_end), "seq", combine, identity, True)[1]
    else:
        carried = entering_2((decay_total, local_end), "seq", combine, identity, False)[1]
    entering = entering + jnp.exp(prior_log)[:, :, None, None] * carried[None]
    inter = (
        jnp.einsum("kqn,khpn->kqhp", read_blocks, entering, precision=highest)
        * jnp.exp(cumulative).transpose(0, 2, 1)[:, :, :, None]
    )
    outputs = intra + inter + skipgain[None, None, :, None] * x_blocks
    return outputs.reshape(length, head_count, head_dim)


def per_device(
    token_ids,
    embedding,
    complement,
    prenorm_first,
    inproj_first,
    statemap_first,
    stepmap_first,
    stepbias_first,
    rates_first,
    skipgain_first,
    outnorm_first,
    outproj_first,
    prenorm_second,
    inproj_second,
    statemap_second,
    stepmap_second,
    stepbias_second,
    rates_second,
    skipgain_second,
    outnorm_second,
    outproj_second,
):
    onehot = (
        token_ids[:, None] == jnp.arange(embedding.shape[0], dtype=jnp.int32)[None, :]
    ).astype(jnp.float32)
    embedded = matmul(onehot, embedding)
    gate_vals, x_heads, write_vecs, read_vecs, step_sizes, log_decay = project(
        embedded,
        prenorm_first,
        inproj_first,
        statemap_first,
        stepmap_first,
        stepbias_first,
        rates_first,
    )
    products = pair_products(write_vecs, read_vecs)
    forward_out = state_space(
        x_heads, step_sizes, log_decay, write_vecs, read_vecs, products, skipgain_first, False
    )
    backward_out = state_space(
        x_heads, step_sizes, log_decay, write_vecs, read_vecs, products, skipgain_first, True
    )
    mixed = gated_norm(forward_out, gate_vals, outnorm_first) + gated_norm(
        backward_out, gate_vals, outnorm_first
    )
    partial_sum = matmul(mixed, outproj_first)
    bit_count = lax.axis_size("seq").bit_length() - 1
    share = lax.psum_scatter(partial_sum, "head", scatter_dimension=0, tiled=True)
    share_rows = share.shape[0]
    moved = (
        lax.dynamic_slice_in_dim(embedded, lax.axis_index("head") * share_rows, share_rows, 0)
        + share
    )
    for bit_index in range(bit_count):
        moved = partner(moved, "seq", bit_index)
    moved = lax.all_gather(moved, "head", axis=0, tiled=True)
    flipped = moved[::-1]
    mirrored = jnp.take(flipped, complement, axis=1)
    gate_two, x_two, write_two, read_two, step_two, log_two = project(
        mirrored,
        prenorm_second,
        inproj_second,
        statemap_second,
        stepmap_second,
        stepbias_second,
        rates_second,
    )
    products_two = pair_products(write_two, read_two)
    forward_two = state_space(
        x_two, step_two, log_two, write_two, read_two, products_two, skipgain_second, False
    )
    partial_two = matmul(gated_norm(forward_two, gate_two, outnorm_second), outproj_second)
    share_two = lax.psum_scatter(partial_two, "head", scatter_dimension=0, tiled=True)
    rows_two = share_two.shape[0]
    return (
        lax.dynamic_slice_in_dim(mirrored, lax.axis_index("head") * rows_two, rows_two, 0)
        + share_two
    )


def solution(mesh):
    return jax.shard_map(
        per_device,
        mesh=mesh,
        in_specs=(
            P(("rep", "seq")),
            P(),
            P(),
            P(),
            P(None, None, "head"),
            P(),
            P(None, "head"),
            P("head"),
            P("head"),
            P("head"),
            P("head"),
            P("head", None),
            P(),
            P(None, None, "head"),
            P(),
            P(None, "head"),
            P("head"),
            P("head"),
            P("head"),
            P("head"),
            P("head", None),
        ),
        out_specs=P(("rep", "seq", "head"), None),
        check_vma=False,
    )
```

profile of v0, /device:TPU:0, one launch (start us, length us, event | category | flops | bytes accessed | tf_op | source)
XLA Modules:
  0.0 133.8 jit_solution(8137411760633491869)
XLA Ops:
  6.5 1.2 multiply_reduce_fusion.1
  7.7 0.6 copy-done.15
  8.4 0.7 copy-done.8
  9.1 0.4 compare_select_fusion.1
  9.6 0.6 reduce-window.20
  10.5 0.6 reduce-window.24
  12.6 0.7 fusion.39
  13.5 0.4 fusion.36
  13.9 0.4 fusion.95
  14.6 7.2 %all-gather.1 = f32[8,64,128]{2,1,0:T(8,128)S(1)} all-gather(f32[2,64,128]{2,1,0:T(8,128)S(1)} %convolution_add_fusion.2), channel_id=3, replica_groups=mesh['seq'=4,'head'=4,'rep'=2] {'seq'}, dimensions={0}, use_global_device_ids=true | all-gather | bytes 327680 | tf_op jit(solution)/shard_map/all_gather | solution.py:15
  21.9 5.0 %all-gather = f32[4,2,1]{1,2,0:T(1,128)S(1)} all-gather(f32[1,2,1]{1,2,0:T(1,128)S(1)} %copy.38), channel_id=2, replica_groups=mesh['seq'=4,'head'=4,'rep'=2] {'seq'}, dimensions={0}, use_global_device_ids=true | all-gather | bytes 40 | tf_op jit(solution)/shard_map/all_gather | solution.py:15
  27.5 5.8 %all-gather.3 = f32[8,64,128]{2,1,0:T(8,128)S(1)} all-gather(f32[2,64,128]{2,1,0:T(8,128)S(1)} %convolution_add_fusion.1), channel_id=5, replica_groups=mesh['seq'=4,'head'=4,'rep'=2] {'seq'}, dimensions={0}, use_global_device_ids=true | all-gather | bytes 327680 | tf_op jit(solution)/shard_map/all_gather | solution.py:15
  33.4 5.0 %all-gather.2 = f32[4,2,1]{1,2,0:T(1,128)S(1)} all-gather(f32[1,2,1]{1,2,0:T(1,128)S(1)} %copy.41), channel_id=4, replica_groups=mesh['seq'=4,'head'=4,'rep'=2] {'seq'}, dimensions={0}, use_global_device_ids=true | all-gather | bytes 40 | tf_op jit(solution)/shard_map/all_gather | solution.py:15
  38.7 0.3 while.28
  39.0 0.3 fusion.5
  39.4 0.3 fusion.4
  39.7 0.6 copy-done.16
  40.3 0.8 fusion.9
  41.1 0.8 fusion.70
  42.0 0.6 copy-done.12
  42.7 1.1 fusion.114
  43.9 0.7 copy-done.10
  44.6 20.3 %reduce-scatter.3.cloned.1.call-done = f32[64,256]{1,0:T(8,128)} async-done(((f32[256,256]{1,0:T(8,128)}), f32[64,256]{1,0:T(8,128)}) %reduce-scatter.3.cloned.1.call-update) | async-done | bytes 65552 | tf_op jit(solution)/shard_map/reduce_scatter | solution.py:197
  64.9 0.8 dynamic-slice_add_fusion
  65.9 0.6 copy-done.17
  66.6 0.6 collective-permute-done
  67.1 1.5 %collective-permute-start.1 = (f32[64,256]{1,0:T(8,128)S(1)}, f32[64,256]{1,0:T(8,128)S(1)}, u32[]{:S(2)}, u32[]{:S(2)}) collective-permute-start(f32[64,256]{1,0:T(8,128)S(1)} %collective-permute-done), channel_id=1, source_target_pairs={{0,16},{8,24},{16,0},{24,8},{1,17},{9,25},{17,1},{25,9},{2,18},{10... | collective-permute-start | bytes 196616 | tf_op jit(solution)/shard_map/ppermute | solution.py:33
  68.6 2.8 %collective-permute-done.1 = f32[64,256]{1,0:T(8,128)S(1)} collective-permute-done((f32[64,256]{1,0:T(8,128)S(1)}, f32[64,256]{1,0:T(8,128)S(1)}, u32[]{:S(2)}, u32[]{:S(2)}) %collective-permute-start.1) | collective-permute-done | bytes 65568 | tf_op jit(solution)/shard_map/ppermute | solution.py:33
  71.4 14.0 %all_gather.31 = f32[256,256]{1,0:T(8,128)S(1)} all-gather(f32[64,256]{1,0:T(8,128)S(1)} %collective-permute-done.1), channel_id=1, replica_groups=mesh['seq'=4,'head'=4,'rep'=2] {'head'}, dimensions={0}, use_global_device_ids=true | all-gather | bytes 327680 | tf_op jit(solution)/shard_map/all_gather | solution.py:205
  85.7 1.0 gather_fusion
  86.9 0.5 copy-done.7
  87.5 0.4 compare_select_fusion
  88.0 0.6 reduce-window.26
  89.4 0.4 fusion.30
  89.8 0.5 copy-done.4
  90.4 0.7 fusion.33
  91.1 0.4 fusion.89
  91.8 5.8 %all-gather.5 = f32[8,64,128]{2,1,0:T(8,128)S(1)} all-gather(f32[2,64,128]{2,1,0:T(8,128)S(1)} %convolution_add_fusion), channel_id=7, replica_groups=mesh['seq'=4,'head'=4,'rep'=2] {'seq'}, dimensions={0}, use_global_device_ids=true | all-gather | bytes 327680 | tf_op jit(solution)/shard_map/all_gather | solution.py:15
  97.6 5.0 %all-gather.4 = f32[4,2,1]{1,2,0:T(1,128)S(1)} all-gather(f32[1,2,1]{1,2,0:T(1,128)S(1)} %copy.46), channel_id=6, replica_groups=mesh['seq'=4,'head'=4,'rep'=2] {'seq'}, dimensions={0}, use_global_device_ids=true | all-gather | bytes 40 | tf_op jit(solution)/shard_map/all_gather | solution.py:15
  102.6 0.3 while.29
  102.9 0.3 fusion.3
  103.2 0.6 copy-done.18
  103.9 0.8 fusion.62
  104.7 0.6 copy-done.14
  105.5 0.8 copy-done.5
  106.3 1.1 fusion.115
  107.4 18.1 %reduce-scatter.5.cloned.1.call-done = f32[64,256]{1,0:T(8,128)} async-done(((f32[256,256]{1,0:T(8,128)}), f32[64,256]{1,0:T(8,128)}) %reduce-scatter.5.cloned.1.call-update) | async-done | bytes 65552 | tf_op jit(solution)/shard_map/reduce_scatter | solution.py:222
  125.5 1.5 %bitcast_add_fusion.3 = f32[64,256]{1,0:T(8,128)} fusion(f32[64,256]{1,0:T(8,128)} %reduce-scatter.5.cloned.1.call-done, f32[256,256]{0,1:T(8,128)S(1)} %get-tuple-element.469, s32[]{:T(128)S(6)} %select_n.120), kind=kLoop, calls=%fused_computation.140 | loop fusion | flops 16384 | bytes 196612 | tf_op jit(solution)/shard_map/add | solution.py:225
  (123 shorter events, 6.4 us)
Async XLA Ops:
  6.5 36.2 %copy-start = (f32[128,256]{1,0:T(8,128)S(1)}, f32[128,256]{1,0:T(8,128)}, u32[]{:S(2)}) copy-start(f32[128,256]{1,0:T(8,128)} %param.38) | copy-start | bytes 393220
  6.5 58.4 %reduce-scatter.3.cloned.1.call-start = ((), (), s32[]{:S(2)}) async-start(), calls=%async_computation.2 | async-start | bytes 327680 | tf_op jit(solution)/shard_map/reduce_scatter | solution.py:197
  7.7 0.7 copy-start.15
  8.4 0.7 copy-start.8
  8.4 0.7 copy-start.6
  8.4 0.7 copy-start.11
  9.1 3.5 %copy-start.1 = (f32[256,2,128]{2,1,0:T(2,128)S(1)}, f32[256,2,128]{2,1,0:T(2,128)}, u32[]{:S(2)}) copy-start(f32[256,2,128]{2,1,0:T(2,128)} %param.31) | copy-start | bytes 786436
  12.5 1.0 copy-start.2
  39.7 0.7 copy-start.16
  42.0 0.7 copy-start.12
  43.9 81.7 %reduce-scatter.5.cloned.1.call-start = ((), (), s32[]{:S(2)}) async-start(), calls=%async_computation.3 | async-start | bytes 327680 | tf_op jit(solution)/shard_map/reduce_scatter | solution.py:222
  43.9 0.7 copy-start.10
  65.8 1.3 collective-permute-start
  65.9 0.7 copy-start.17
  67.1 4.3 %collective-permute-start.1 = (f32[64,256]{1,0:T(8,128)S(1)}, f32[64,256]{1,0:T(8,128)S(1)}, u32[]{:S(2)}, u32[]{:S(2)}) collective-permute-start(f32[64,256]{1,0:T(8,128)S(1)} %collective-permute-done), channel_id=1, source_target_pairs={{0,16},{8,24},{16,0},{24,8},{1,17},{9,25},{17,1},{25,9},{2,18},{10... | collective-permute-start | bytes 196616 | tf_op jit(solution)/shard_map/ppermute | solution.py:33
  86.8 0.7 copy-start.7
  86.8 0.7 copy-start.9
  86.8 0.7 copy-start.13
  86.9 2.5 %copy-start.3 = (f32[256,2,128]{2,1,0:T(2,128)S(1)}, f32[256,2,128]{2,1,0:T(2,128)}, u32[]{:S(2)}) copy-start(f32[256,2,128]{2,1,0:T(2,128)} %param.41) | copy-start | bytes 786436
  89.4 1.0 copy-start.4
  103.2 0.7 copy-start.18
  104.7 0.7 copy-start.14
  105.4 0.9 copy-start.5
Sparse Core Ops, SparseCore 0:
  44.0 20.9 reduce-scatter.2
  107.5 17.9 reduce-scatter.4
where the time goes:
time: 134 us
  blocking collectives  47.9 us (36%)
  waiting for transfers between devices  41.8 us (31%)
  between operations  13.8 us (10%)
  local copies, waits for them, and re-layouts  11.2 us (8%)
  matrix products  11.2 us (8%)
  other arithmetic  6.18 us (5%)
  starting transfers between devices  1.59 us (1%)
    all_gather x6, blocking collectives, entering_2(): pieces = jax.tree.map(lambda part: lax.all_gather(part, axis), value)  33.9 us
    reduce_scatter x1, waiting for transfers between devices, per_device(): lax.psum_scatter(partial_sum, 'head', scatter_dimension=0, tiled=True)  20.3 us
    reduce_scatter x1, waiting for transfers between devices, per_device(): lax.psum_scatter(partial_two, 'head', scatter_dimension=0, tiled=True)  18.1 us
    all_gather x1, blocking collectives, per_device(): moved = lax.all_gather(moved, 'head', axis=0, tiled=True)  14 us
    unnamed x41, local copies, waits for them, and re-layouts  7.68 us
    dot_general x9, matrix products, matmul(): jnp.dot(left, right, precision=highest, preferred_element_type=jnp.float32)  6.33 us
    ppermute x2, waiting for transfers between devices, partner(): return lax.ppermute(value, axis, pairs)  3.34 us
  transfers between devices with their start and end apart: 4, of which 4 were waited for; matrix products, arithmetic and copies ran while one was open for 0% of the time, Pallas kernels for 0%

commit v1 on v0

v1 whole, which is shorter than its diff:
```python
import functools

import jax
import jax.numpy as jnp
from jax import lax
from jax.experimental import pallas as pl
from jax.experimental.pallas import tpu as pltpu
from jax.sharding import PartitionSpec as P

epsilon = 1e-05
f32 = jnp.float32
bf16 = jnp.bfloat16
LIMIT = 48 * 1024 * 1024

MM = (((1,), (0,)), ((), ()))
NT = (((1,), (1,)), ((), ()))
TN = (((0,), (0,)), ((), ()))


def iota(shape, axis):
    return lax.broadcasted_iota(jnp.int32, shape, axis)


def split2(value):
    high = value.astype(bf16)
    return high, (value - high.astype(f32)).astype(bf16)


def split3(value):
    high = value.astype(bf16)
    rest = value - high.astype(f32)
    middle = rest.astype(bf16)
    return high, middle, (rest - middle.astype(f32)).astype(bf16)


def dot(left, right, dims=MM):
    return lax.dot_general(left, right, dims, preferred_element_type=f32)


def dot_split(left, right, dims=MM):
    return (
        dot(left[0], right[1], dims) + dot(left[1], right[0], dims)
    ) + dot(left[0], right[0], dims)


def dot3(left, right, dims=MM):
    return dot_split(split2(left), split2(right), dims)


def dot_left_exact(left, right, dims=MM):
    high, middle, low = split3(right)
    return (dot(left, low, dims) + dot(left, middle, dims)) + dot(left, high, dims)


def dot_right_exact(left, right, dims=MM):
    high, middle, low = split3(left)
    return (dot(low, right, dims) + dot(middle, right, dims)) + dot(high, right, dims)


def softplus(value):
    return jnp.maximum(value, 0.0) + jnp.log1p(jnp.exp(-jnp.abs(value)))


def silu(value):
    return value / (1.0 + jnp.exp(-value))


def rms(value):
    return value * lax.rsqrt(jnp.mean(value * value, axis=-1, keepdims=True) + epsilon)


def tables_kernel(
    dims, tok, emb, prenorm, inproj, statemap, stepmap, bias, rates, skip, outnorm, packet, pairs
):
    V, D, hl, ch, nh, ns, T, N = dims
    H, LV = nh * hl, nh * hl * V
    normed = split2(rms(emb[...]) * prenorm[...])
    gate = dot_split(normed, split2(inproj[pl.ds(0, D, stride=2), :]))
    inner = dot_split(normed, split2(inproj[pl.ds(1, D, stride=2), :]))
    write = dot_split(normed, split2(statemap[pl.ds(0, D, stride=2), :]))
    read = dot_split(normed, split2(statemap[pl.ds(1, D, stride=2), :]))
    pairs[...] = dot3(read, jnp.concatenate([write] * H, axis=0), NT)
    steps = split2(stepmap[...])
    raw = dot_split(normed, steps, NT)
    raw_t = dot_split(steps, normed, NT)
    lane = iota((V, LV), 1)
    own = (lane % V) == iota((V, LV), 0)
    of_head = (lane // V) % hl
    decay = jnp.zeros((V, LV), f32)
    step = jnp.zeros((V, LV), f32)
    gain = jnp.zeros((V, LV), f32)
    log_t = jnp.zeros((H, V), f32)
    row_head = iota((H, V), 0) % hl
    for head in range(hl):
        column = softplus(raw[:, head : head + 1] + bias[head])
        here = of_head == head
        decay = jnp.where(here, jnp.exp(-rates[head] * column), decay)
        step = jnp.where(here & own, column, step)
        gain = jnp.where(here & own, skip[head], gain)
        line = softplus(raw_t[head : head + 1, :] + bias[head])
        log_t = jnp.where(row_head == head, -rates[head] * line, log_t)
    flip = (iota((T, T), 0) + iota((T, T), 1) == T - 1).astype(f32).astype(bf16)
    tokens = jnp.broadcast_to(tok[...].astype(f32), (8, T)).astype(bf16)
    packet[0:V, 0:ch] = gate
    packet[0:V, ch : 2 * ch] = inner
    start = 2 * ch
    packet[0:V, start : start + LV] = decay
    packet[0:V, start + LV : start + 2 * LV] = step
    packet[0:V, start + 2 * LV : start + 3 * LV] = gain
    packet[V : V + 8, 0:T] = dot(tokens, flip)
    packet[V + 8 : V + 8 + H, 0:V] = log_t
    packet[V + 8 : V + 8 + H, LV : LV + ch] = jnp.broadcast_to(outnorm[...], (H, ch))


def shift_rows(value, amount, fill):
    size = value.shape[0]
    rolled = pltpu.roll(value, amount % size, 0)
    row = iota(value.shape, 0)
    have = (row >= amount) if amount > 0 else (row < size + amount)
    return jnp.where(have, rolled, fill)


def scan_rows(decay, value, sign):
    size = value.shape[0]
    amount = 1
    while amount < size:
        value = value + decay * shift_rows(value, sign * amount, 0.0)
        if 2 * amount < size:
            decay = decay * shift_rows(decay, sign * amount, 1.0)
        amount *= 2
    return value


def first_kernel(dims, *refs):
    V, D, hl, ch, nh, ns, T, N = dims
    H, LV, P = nh * hl, nh * hl * V, ch // hl
    C = nh * ch
    count = max(ns, nh)
    refs = list(refs)

    def take(number):
        taken, refs[:] = refs[:number], refs[number:]
        return taken

    packets = take(count)
    projections = take(nh)
    emb, pairs, complement = take(3)
    prenorm2, inproj2, statemap2, stepmap2, bias2, rates2, skip2 = take(7)
    out_state, out_read, out_base, out_scale, out_gate, out_own = take(6)
    tokens, mirrored_ref = take(2)
    mine = lax.axis_index("seq")

    for k in range(ns):
        block = ns - 1 - lax.rem(mine - k + ns, ns)
        tokens[pl.ds(block, 1), :] = packets[k][V : V + 1, 0:T]

    lane = iota((V, LV), 1) // (V * hl)
    start = 2 * ch

    def table(place):
        low, high = start + place * LV, start + (place + 1) * LV
        result = packets[0][0:V, low:high]
        for k in range(1, nh):
            result = jnp.where(lane == k, packets[k][0:V, low:high], result)
        return result

    decay_table, step_table, gain_table = table(0), table(1), table(2)
    log_t = packets[0][V + 8 : V + 8 + H, 0:V]
    for k in range(1, nh):
        log_t = jnp.where(iota((H, V), 0) // hl == k, packets[k][V + 8 : V + 8 + H, 0:V], log_t)
    gates = jnp.concatenate([packets[k][0:V, 0:ch] for k in range(nh)], axis=1)
    inners = jnp.concatenate([packets[k][0:V, ch : 2 * ch] for k in range(nh)], axis=1)
    gains = jnp.concatenate(
        [packets[k][V + 8 : V + 9, LV : LV + ch] for k in range(nh)], axis=1
    )

    token_row = iota((LV, T), 0) % V
    log_split = jnp.concatenate(split3(log_t), axis=1)
    onehots, logs = [], []
    for block in range(ns):
        onehot = (tokens[block : block + 1, :] == token_row.astype(f32)).astype(f32).astype(bf16)
        onehots.append(onehot)
        logs.append(dot(log_split, onehot[0 : 3 * V, :]))
    logs = jnp.concatenate(logs, axis=0)
    first, second = iota((T, T), 0), iota((T, T), 1)
    later = (first > second).astype(f32).astype(bf16)
    sooner = (first < second).astype(f32).astype(bf16)
    logs3 = split3(logs)
    after = dot(logs3[2], later) + dot(logs3[1], later) + dot(logs3[0], later)
    before = dot(logs3[2], sooner) + dot(logs3[1], sooner) + dot(logs3[0], sooner)
    totals = jnp.sum(logs, axis=1, keepdims=True)
    total_rows = jnp.broadcast_to(totals, (ns * H, 128))
    row, column = iota((ns * H, ns * H), 0), iota((ns * H, ns * H), 1)
    row_block, column_block = row // H, column // H
    between = ((row_block < column_block) & (column_block < mine)) | (
        (row_block > column_block) & (column_block > mine)
    )
    between = (between & (row % H == column % H)).astype(f32).astype(bf16)
    gap = dot_left_exact(between, total_rows)[:, 0:1]
    block_of = iota((ns * H, T), 0) // H
    weight_up = jnp.where(block_of < mine, jnp.exp(after + gap), 0.0)
    weight_down = jnp.where(block_of > mine, jnp.exp(before + gap), 0.0)
    entering = jnp.zeros((2 * H, LV), f32)
    for block in range(ns):
        both = jnp.concatenate(
            [weight_up[block * H : (block + 1) * H], weight_down[block * H : (block + 1) * H]],
            axis=0,
        )
        high, low = split2(both)
        entering = entering + (dot(low, onehots[block], NT) + dot(high, onehots[block], NT))
    diagonal = iota((H, LV), 1) // V == iota((H, LV), 0)
    step_row = jnp.sum(step_table, axis=0, keepdims=True)
    enter_up = step_row * jnp.sum(
        jnp.where(diagonal, entering[0:H], 0.0), axis=0, keepdims=True
    )
    enter_down = step_row * jnp.sum(
        jnp.where(diagonal, entering[H : 2 * H], 0.0), axis=0, keepdims=True
    )

    silus = silu(gates)
    looked = jnp.concatenate(
        [decay_table, step_table, pairs[...], gain_table, silus, emb[...]], axis=1
    )
    looked = jnp.concatenate(split3(looked), axis=0)
    token = tokens[pl.ds(mine, 1), :]
    onehot = (token == (iota((3 * V, T), 0) % V).astype(f32)).astype(f32).astype(bf16)
    rows = dot(onehot, looked, TN)
    decay, step = rows[:, 0:LV], rows[:, LV : 2 * LV]
    pair, gain = rows[:, 2 * LV : 3 * LV], rows[:, 3 * LV : 4 * LV]
    silu_rows = rows[:, 4 * LV : 4 * LV + C]
    embedded = rows[:, 4 * LV + C :]

    position = iota((T, LV), 0)
    up = scan_rows(decay, jnp.where(position == 0, step + decay * enter_up, step), 1)
    down = scan_rows(decay, jnp.where(position == T - 1, step + decay * enter_down, step), -1)

    tiled = jnp.concatenate([inners] * H, axis=0)
    spread = jnp.where(iota((LV, C), 0) // V == iota((LV, C), 1) // P, tiled, 0.0)
    spread_high, spread_low = split2(spread)
    half = (iota((C, C), 0) // P == iota((C, C), 1) // P).astype(f32).astype(bf16)

    def gated(coefficients):
        high, low = split2(coefficients * pair + gain)
        value = dot(high, spread_low) + dot(low, spread_high) + dot(high, spread_high)
        value = value * silu_rows
        high, low = split2(value * value)
        square = dot(low, half) + dot(high, half)
        return value * lax.rsqrt(square * (1.0 / P) + epsilon)

    mixed = split2((gated(up) + gated(down)) * gains)
    hidden = embedded
    for k in range(nh):
        part = (mixed[0][:, k * ch : (k + 1) * ch], mixed[1][:, k * ch : (k + 1) * ch])
        hidden = hidden + dot_split(part, split2(projections[k][...]))
    choose = (complement[...] == iota((D, D), 0)).astype(f32).astype(bf16)
    mirrored = dot_right_exact(hidden, choose)
    mirrored_ref[...] = mirrored
    share = T // nh
    out_own[...] = mirrored_ref[pl.ds(pl.multiple_of(lax.axis_index("head") * share, 8), share), :]

    normed = split2(rms(mirrored) * prenorm2[...])
    gate = dot_split(normed, split2(inproj2[pl.ds(0, D, stride=2), :]))
    inner = dot_split(normed, split2(inproj2[pl.ds(1, D, stride=2), :]))
    write = split2(dot_split(normed, split2(statemap2[pl.ds(0, D, stride=2), :])))
    read = dot_split(normed, split2(statemap2[pl.ds(1, D, stride=2), :]))
    out_read[...] = read
    read = split2(read)
    steps = split2(stepmap2[...])
    raw = dot_split(normed, steps, NT)
    raw_t = dot_split(steps, normed, NT)
    of_head = iota((T, ch), 1) // P
    step = jnp.zeros((T, ch), f32)
    log = jnp.zeros((T, ch), f32)
    skip = jnp.zeros((T, ch), f32)
    logs = []
    for head in range(hl):
        column = softplus(raw[:, head : head + 1] + bias2[head])
        here = of_head == head
        step = jnp.where(here, column, step)
        log = jnp.where(here, -rates2[head] * column, log)
        skip = jnp.where(here, skip2[head], skip)
        logs.append(-rates2[head] * softplus(raw_t[head : head + 1, :] + bias2[head]))
    upto = (first >= second).astype(f32).astype(bf16)
    total = dot_left_exact(upto, log)
    logs = jnp.concatenate(logs, axis=0)
    total_t = dot_right_exact(logs, (first <= second).astype(f32).astype(bf16))
    end = total[T - 1 : T, :]
    stepped = inner * step
    state = dot3(stepped * jnp.exp(end - total), write[0].astype(f32) + write[1].astype(f32), TN)
    out_state[0:ch, :] = state
    for head in range(hl):
        out_state[ch + head : ch + head + 1, :] = jnp.broadcast_to(
            end[:, head * P : head * P + 1], (1, state.shape[1])
        )
    products = dot_split(read, write, NT)
    stepped = split2(stepped)
    base = []
    for head in range(hl):
        differ = total[:, head * P : head * P + 1] - total_t[head : head + 1, :]
        allowed = first >= second
        weights = jnp.where(allowed, jnp.exp(jnp.where(allowed, differ, 0.0)), 0.0) * products
        part = (
            stepped[0][:, head * P : (head + 1) * P],
            stepped[1][:, head * P : (head + 1) * P],
        )
        base.append(dot_split(split2(weights), part))
    out_base[...] = jnp.concatenate(base, axis=1) + skip * inner
    out_scale[...] = jnp.exp(total)
    out_gate[...] = silu(gate)


def second_kernel(dims, *refs):
    V, D, hl, ch, nh, ns, T, N = dims
    P = ch // hl
    refs = list(refs)

    def take(number):
        taken, refs[:] = refs[:number], refs[number:]
        return taken

    states = take(ns - 1)
    read, base, scale, gate, own, outnorm, outproj = take(7)
    outs = take(nh)
    (partial_ref,) = take(1)
    entering = states[0][0:ch, :]
    if ns > 2:
        head_of = iota((ch, N), 0) // P

        def rows(values):
            result = jnp.broadcast_to(values[0:1, :], (ch, N))
            for head in range(1, hl):
                result = jnp.where(head_of == head, values[head : head + 1, :], result)
            return result

        logs = states[0][ch : ch + 8, :]
        for k in range(1, ns - 1):
            entering = entering + rows(jnp.exp(logs)) * states[k][0:ch, :]
            logs = logs + states[k][ch : ch + 8, :]
    value = (base[...] + dot3(read[...], entering, NT) * scale[...]) * gate[...]
    half = (iota((ch, ch), 0) // P == iota((ch, ch), 1) // P).astype(f32).astype(bf16)
    high, low = split2(value * value)
    square = dot(low, half) + dot(high, half)
    value = value * lax.rsqrt(square * (1.0 / P) + epsilon) * outnorm[...]
    partial_ref[...] = dot3(value, outproj[...])
    share = T // nh
    mine = lax.axis_index("head")
    for k in range(nh):
        place = pl.multiple_of(lax.rem(mine + k, nh) * share, 8)
        part = partial_ref[pl.ds(place, share), :]
        outs[k][...] = part + own[...] if k == 0 else part


def per_device(
    token_ids,
    embedding,
    complement,
    prenorm_first,
    inproj_first,
    statemap_first,
    stepmap_first,
    stepbias_first,
    rates_first,
    skipgain_first,
    outnorm_first,
    outproj_first,
    prenorm_second,
    inproj_second,
    statemap_second,
    stepmap_second,
    stepbias_second,
    rates_second,
    skipgain_second,
    outnorm_second,
    outproj_second,
):
    nh, ns = lax.axis_size("head"), lax.axis_size("seq")
    V, D = embedding.shape
    ch = inproj_first.shape[2]
    hl = stepmap_first.shape[1]
    N = statemap_first.shape[2]
    T = token_ids.shape[0]
    H, LV = nh * hl, nh * hl * V
    dims = (V, D, hl, ch, nh, ns, T, N)
    vmem = pl.BlockSpec(memory_space=pltpu.VMEM)
    smem = pl.BlockSpec(memory_space=pltpu.SMEM)
    params = pltpu.CompilerParams(vmem_limit_bytes=LIMIT)

    def line(value):
        return value.reshape(1, -1)

    def flat(value):
        return value.reshape(-1, value.shape[-1])

    projections = [outproj_first]
    for k in range(1, nh):
        pairs = [(source, (source + k) % nh) for source in range(nh)]
        projections.append(lax.ppermute(outproj_first, "head", pairs))

    width = max(2 * ch + 3 * LV, T, LV + ch)
    packet, pair_table = pl.pallas_call(
        functools.partial(tables_kernel, dims),
        out_shape=(
            jax.ShapeDtypeStruct((V + 8 + H, width), f32),
            jax.ShapeDtypeStruct((V, LV), f32),
        ),
        in_specs=[vmem] * 6 + [smem] * 3 + [vmem],
        out_specs=(vmem, vmem),
        compiler_params=params,
        name="tables",
    )(
        line(token_ids),
        embedding,
        line(prenorm_first),
        flat(inproj_first),
        flat(statemap_first),
        stepmap_first.T,
        stepbias_first,
        rates_first,
        skipgain_first,
        line(outnorm_first),
    )
    packets = [packet]
    for k in range(1, max(ns, nh)):
        pairs = [
            (seq * nh + head, ((seq + k) % ns) * nh + (head + k) % nh)
            for seq in range(ns)
            for head in range(nh)
        ]
        packets.append(lax.ppermute(packet, ("seq", "head"), pairs))

    share = T // nh
    state, read, base, scale, gate, own = pl.pallas_call(
        functools.partial(first_kernel, dims),
        out_shape=(
            jax.ShapeDtypeStruct((ch + 8, N), f32),
            jax.ShapeDtypeStruct((T, N), f32),
            jax.ShapeDtypeStruct((T, ch), f32),
            jax.ShapeDtypeStruct((T, ch), f32),
            jax.ShapeDtypeStruct((T, ch), f32),
            jax.ShapeDtypeStruct((share, D), f32),
        ),
        in_specs=[vmem] * (len(packets) + nh + 7) + [smem] * 3,
        out_specs=(vmem,) * 6,
        scratch_shapes=[pltpu.VMEM((max(ns, 8), T), f32), pltpu.VMEM((T, D), f32)],
        compiler_params=params,
        name="first",
    )(
        *packets,
        *projections,
        embedding,
        pair_table,
        line(complement),
        line(prenorm_second),
        flat(inproj_second),
        flat(statemap_second),
        stepmap_second.T,
        stepbias_second,
        rates_second,
        skipgain_second,
    )
    states = []
    for k in range(1, ns):
        states.append(lax.ppermute(state, "seq", [(s, s + k) for s in range(ns - k)]))
    parts = pl.pallas_call(
        functools.partial(second_kernel, dims),
        out_shape=(jax.ShapeDtypeStruct((share, D), f32),) * nh,
        in_specs=[vmem] * (ns - 1 + 7),
        out_specs=(vmem,) * nh,
        scratch_shapes=[pltpu.VMEM((T, D), f32)],
        compiler_params=params,
        name="second",
    )(*states, read, base, scale, gate, own, line(outnorm_second), outproj_second)
    result = parts[0]
    for k in range(1, nh):
        pairs = [(source, (source + k) % nh) for source in range(nh)]
        result = result + lax.ppermute(parts[k], "head", pairs)
    return result


def solution(mesh):
    return jax.shard_map(
        per_device,
        mesh=mesh,
        in_specs=(
            P(("rep", "seq")),
            P(),
            P(),
            P(),
            P(None, None, "head"),
            P(),
            P(None, "head"),
            P("head"),
            P("head"),
            P("head"),
            P("head"),
            P("head", None),
            P(),
            P(None, None, "head"),
            P(),
            P(None, "head"),
            P("head"),
            P("head"),
            P("head"),
            P("head"),
            P("head", None),
        ),
        out_specs=P(("rep", "seq", "head"), None),
        check_vma=False,
    )
```

time: 134 us -> 55 us (0.41)
  blocking collectives: 47.9 us -> 0 us
  waiting for transfers between devices: 41.8 us -> 19.9 us
  starting transfers between devices: 1.59 us -> 20.5 us
  between operations: 13.8 us -> 0.18 us
  matrix products: 11.2 us -> 0 us
  Pallas kernels: 0 us -> 7.78 us
  local copies, waits for them, and re-layouts: 11.2 us -> 5.59 us
  other arithmetic: 6.18 us -> 0.65 us
    all_gather x7 -> x0, blocking collectives: 47.9 us -> none  [the longest x6 33.9 us: entering_2(): pieces = jax.tree.map(lambda part: lax.all_gather(part, axis), value)]
    reduce_scatter x2 -> x0, waiting for transfers between devices: 38.5 us -> none  [the longest x1 20.3 us: per_device(): lax.psum_scatter(partial_sum, 'head', scatter_dimension=0, tiled=True)]
    ppermute x2 -> x12, starting transfers between devices: 1.55 us -> 20.5 us  [the longest x3 6.52 us: per_device(): packets.append(lax.ppermute(packet, ('seq', 'head'), pairs))]
    ppermute x2 -> x12, waiting for transfers between devices: 3.34 us -> 19.9 us  [the longest x3 15.3 us: per_device(): packets.append(lax.ppermute(packet, ('seq', 'head'), pairs))]
    dot_general x20 -> x0, matrix products: 11.2 us -> none  [the longest x9 6.33 us: matmul(): jnp.dot(left, right, precision=highest, preferred_element_type=jnp.float32)]
    pallas_call x0 -> x3, Pallas kernels: none -> 7.78 us  [the longest x1 6.04 us: per_device(): pl.pallas_call(functools.partial(first_kernel, dims), out_shape=(jax.Shap...]
    another operation x9 -> x0, other arithmetic: 2.36 us -> none
    unnamed x41 -> x44, local copies, waits for them, and re-layouts: 7.68 us -> 5.59 us
  transfers between devices with their start and end apart: 4 -> 12, of which waited for: 4 -> 4; matrix products, arithmetic and copies ran while one was open for 0% -> 0% of each run, Pallas kernels for 0% -> 0%
where the time goes in v1:
time: 55 us; the launch traced here: 54.6 us
  starting transfers between devices  20.5 us (37%)
  waiting for transfers between devices  19.9 us (36%)
  Pallas kernels  7.78 us (14%)
  local copies, waits for them, and re-layouts  5.59 us (10%)
  other arithmetic  0.65 us (1%)
    ppermute x3, waiting for transfers between devices, per_device(): packets.append(lax.ppermute(packet, ('seq', 'head'), pairs))  15.3 us
    ppermute x3, starting transfers between devices, per_device(): packets.append(lax.ppermute(packet, ('seq', 'head'), pairs))  6.52 us
    pallas_call x1, Pallas kernels, per_device(): pl.pallas_call(functools.partial(first_kernel, dims), out_shape=(jax.Shap...  6.04 us
    unnamed x44, local copies, waits for them, and re-layouts  5.59 us
    ppermute x3, starting transfers between devices, per_device(): lax.ppermute(state, 'seq', [(s, s + k) for s in range(ns - k)])  5.1 us
    ppermute x3, starting transfers between devices, per_device(): result = result + lax.ppermute(parts[k], 'head', pairs)  5.04 us
    ppermute x3, starting transfers between devices, per_device(): projections.append(lax.ppermute(outproj_first, 'head', pairs))  3.83 us
    ppermute x3, waiting for transfers between devices, per_device(): result = result + lax.ppermute(parts[k], 'head', pairs)  3.69 us
  transfers between devices with their start and end apart: 12, of which 4 were waited for; matrix products, arithmetic and copies ran while one was open for 0% of the time, Pallas kernels for 0%

profile of v1, /device:TPU:0, one launch (start us, length us, event | category | flops | bytes accessed | tf_op | source)
XLA Modules:
  0.0 54.6 jit_solution(10177507686645842032)
XLA Ops:
  0.0 0.6 %copy-done.21 = f32[128]{0:T(128)S(1)} copy-done((f32[128]{0:T(128)S(1)}, f32[128]{0:T(128)}, u32[]{:S(2)}) %copy-start.21) | copy-done | bytes 536
  0.7 0.0 copy-done.11
  0.7 0.0 copy-done.20
  0.7 0.0 copy-done.8
  0.7 0.0 copy-done.10
  0.8 0.9 %copy-done = f32[256,2,128]{2,1,0:T(2,128)S(1)} copy-done((f32[256,2,128]{2,1,0:T(2,128)S(1)}, f32[256,2,128]{2,1,0:T(2,128)}, u32[]{:S(2)}) %copy-start) | copy-done | bytes 262168
  1.7 0.9 %copy-done.1 = f32[256,2,128]{2,1,0:T(2,128)S(1)} copy-done((f32[256,2,128]{2,1,0:T(2,128)S(1)}, f32[256,2,128]{2,1,0:T(2,128)}, u32[]{:S(2)}) %copy-start.1) | copy-done | bytes 262168
  2.7 0.7 %copy-done.6 = f32[16,256]{1,0:T(8,128)S(1)} copy-done((f32[16,256]{1,0:T(8,128)S(1)}, f32[16,256]{1,0:T(8,128)}, u32[]{:S(2)}) %copy-start.6) | copy-done | bytes 16408
  3.4 1.0 %tables.1 = (f32[32,640]{1,0:T(8,128)S(1)}, f32[16,128]{1,0:T(8,128)S(1)}) custom-call(s32[1,256]{1,0:T(1,128)S(1)} %bitcast.18, f32[16,256]{1,0:T(8,128)S(1)} %copy-done.6, f32[1,256]{1,0:T(1,128)S(1)} %bitcast.19, f32[512,128]{1,0:T(8,128)S(1)} %bitcast.12, f32[512,128]{1,0:T(8,128)S(1)} %bitcast.13, f32[2,256]{1,0:T(2,128)S(1)} %bitcast.16, ...), custom_call_target="tpu_custom_call" | custom-call | tf_op jit(solution)/shard_map/tables/pallas_call | solution.py:400
  4.4 5.4 %collective-permute-start.2 = (f32[32,640]{1,0:T(8,128)S(1)}, f32[32,640]{1,0:T(8,128)S(1)}, u32[]{:S(2)}, u32[]{:S(2)}) collective-permute-start(f32[32,640]{1,0:T(8,128)S(1)} %get-tuple-element.17.refs_0_), channel_id=1, source_target_pairs={{0,30},{2,24},{4,26},{6,28},{8,6},{10,0},{12,2},{14,4},{16,14},{18... | collective-permute-start | bytes 245768 | tf_op jit(solution)/shard_map/ppermute | solution.py:429
  9.9 0.0 collective-permute-start.4
  9.9 1.0 %collective-permute-start.3 = (f32[128,256]{1,0:T(8,128)}, f32[128,256]{1,0:T(8,128)S(1)}, u32[]{:S(2)}, u32[]{:S(2)}) collective-permute-start(f32[128,256]{1,0:T(8,128)} %refs_4_.1), channel_id=1, source_target_pairs={{0,2},{2,4},{4,6},{6,0},{1,3},{3,5},{5,7},{7,1},{8,10},{10,12},{12... | collective-permute-start | bytes 393224 | tf_op jit(solution)/shard_map/ppermute | solution.py:397
  10.9 2.8 %collective-permute-start.5 = (f32[128,256]{1,0:T(8,128)}, f32[128,256]{1,0:T(8,128)S(1)}, u32[]{:S(2)}, u32[]{:S(2)}) collective-permute-start(f32[128,256]{1,0:T(8,128)} %refs_4_.1), channel_id=1, source_target_pairs={{0,6},{2,0},{4,2},{6,4},{1,7},{3,1},{5,3},{7,5},{8,14},{10,8},{12,... | collective-permute-start | bytes 393224 | tf_op jit(solution)/shard_map/ppermute | solution.py:397
  13.7 1.1 %collective-permute-start.1 = (f32[32,640]{1,0:T(8,128)S(1)}, f32[32,640]{1,0:T(8,128)S(1)}, u32[]{:S(2)}, u32[]{:S(2)}) collective-permute-start(f32[32,640]{1,0:T(8,128)S(1)} %get-tuple-element.17.refs_0_), channel_id=1, source_target_pairs={{0,20},{2,22},{4,16},{6,18},{8,28},{10,30},{12,24},{14,26},{16,4},... | collective-permute-start | bytes 245768 | tf_op jit(solution)/shard_map/ppermute | solution.py:429
  14.8 0.0 collective-permute-done.2.refs_3_
  14.8 0.0 collective-permute-start
  14.8 15.3 %collective-permute-done.1.refs_2_ = f32[32,640]{1,0:T(8,128)S(1)} collective-permute-done((f32[32,640]{1,0:T(8,128)S(1)}, f32[32,640]{1,0:T(8,128)S(1)}, u32[]{:S(2)}, u32[]{:S(2)}) %collective-permute-start.1) | collective-permute-done | bytes 81952 | tf_op jit(solution)/shard_map/ppermute | solution.py:429
  30.1 0.0 collective-permute-done.refs_1_
  30.1 0.0 collective-permute-done.4.refs_6_
  30.1 0.0 collective-permute-done.3.refs_5_
  30.1 0.0 collective-permute-done.5.refs_7_
  30.2 0.0 copy-start.13
  30.2 0.0 copy-start.15
  30.2 0.0 copy-start.16
  30.2 0.0 copy-start.9
  30.2 0.0 copy-start.12
  30.2 0.0 copy-start.14
  30.3 0.6 %copy-done.13 = f32[256]{0:T(256)S(1)} copy-done((f32[256]{0:T(256)S(1)}, f32[256]{0:T(256)}, u32[]{:S(2)}) %copy-start.13) | copy-done | bytes 1048
  30.8 0.0 copy-done.16
  30.8 0.0 copy-done.9
  30.9 0.0 copy-done.12
  30.9 0.9 %copy-done.4 = f32[128,256]{1,0:T(8,128)S(1)} copy-done((f32[128,256]{1,0:T(8,128)S(1)}, f32[128,256]{1,0:T(8,128)}, u32[]{:S(2)}) %copy-start.4) | copy-done | bytes 131096
  31.8 6.0 %first.1 = (f32[136,128]{1,0:T(8,128)S(1)}, f32[256,128]{1,0:T(8,128)S(1)}, f32[256,128]{1,0:T(8,128)S(1)}, f32[256,128]{1,0:T(8,128)S(1)}, f32[256,128]{1,0:T(8,128)S(1)}, /*index=5*/f32[64,256]{1,0:T(8,128)S(1)}) custom-call(f32[32,640]{1,0:T(8,128)S(1)} %get-tuple-element.17.refs_0_, f32[32,640]{1,0:T(8,128)S(1)} %collective-permute-done.refs_1_, ...), custom_call_target="tpu_custom_call" | custom-call | tf_op jit(solution)/shard_map/first/pallas_call | solution.py:432
  37.9 1.8 %collective-permute-start.8 = (f32[136,128]{1,0:T(8,128)S(1)}, f32[136,128]{1,0:T(8,128)S(1)}, u32[]{:S(2)}, u32[]{:S(2)}) collective-permute-start(f32[136,128]{1,0:T(8,128)S(1)} %get-tuple-element.19), channel_id=1, source_target_pairs={{0,24},{1,25},{2,26},{3,27},{4,28},{5,29},{6,30},{7,31}} | collective-permute-start | bytes 208904 | tf_op jit(solution)/shard_map/ppermute | solution.py:463
  39.7 1.3 %collective-permute-start.7 = (f32[136,128]{1,0:T(8,128)S(1)}, f32[136,128]{1,0:T(8,128)S(1)}, u32[]{:S(2)}, u32[]{:S(2)}) collective-permute-start(f32[136,128]{1,0:T(8,128)S(1)} %get-tuple-element.19), channel_id=1, source_target_pairs={{0,16},{8,24},{1,17},{9,25},{2,18},{10,26},{3,19},{11,27},{4,20},{... | collective-permute-start | bytes 208904 | tf_op jit(solution)/shard_map/ppermute | solution.py:463
  41.0 2.0 %collective-permute-start.6 = (f32[136,128]{1,0:T(8,128)S(1)}, f32[136,128]{1,0:T(8,128)S(1)}, u32[]{:S(2)}, u32[]{:S(2)}) collective-permute-start(f32[136,128]{1,0:T(8,128)S(1)} %get-tuple-element.19), channel_id=1, source_target_pairs={{0,8},{8,16},{16,24},{1,9},{9,17},{17,25},{2,10},{10,18},{18,26},{... | collective-permute-start | bytes 208904 | tf_op jit(solution)/shard_map/ppermute | solution.py:463
  43.0 0.0 collective-permute-done.8.refs_2_
  43.0 0.0 collective-permute-done.7.refs_1_
  43.0 0.9 %collective-permute-done.6.refs_0_ = f32[136,128]{1,0:T(8,128)S(1)} collective-permute-done((f32[136,128]{1,0:T(8,128)S(1)}, f32[136,128]{1,0:T(8,128)S(1)}, u32[]{:S(2)}, u32[]{:S(2)}) %collective-permute-start.6) | collective-permute-done | bytes 69664 | tf_op jit(solution)/shard_map/ppermute | solution.py:463
  43.9 0.7 %copy-done.17 = f32[128]{0:T(128)S(1)} copy-done((f32[128]{0:T(128)S(1)}, f32[128]{0:T(128)}, u32[]{:S(2)}) %copy-start.17) | copy-done | bytes 536
  44.5 0.7 %second.1 = (f32[64,256]{1,0:T(8,128)S(1)}, f32[64,256]{1,0:T(8,128)S(1)}, f32[64,256]{1,0:T(8,128)S(1)}, f32[64,256]{1,0:T(8,128)S(1)}) custom-call(f32[136,128]{1,0:T(8,128)S(1)} %collective-permute-done.6.refs_0_, f32[136,128]{1,0:T(8,128)S(1)} %collective-permute-done.7.refs_1_, f32[136,128]{1,0:T(8,128)S(1)} %collective-permute-done.8.refs_2_, ...), custom_call_target="tpu_custom_call" | custom-call | tf_op jit(solution)/shard_map/second/pallas_call | solution.py:464
  45.2 0.1 collective-permute-start.9
  45.3 2.1 %collective-permute-start.10 = (f32[64,256]{1,0:T(8,128)S(1)}, f32[64,256]{1,0:T(8,128)S(1)}, u32[]{:S(2)}, u32[]{:S(2)}) collective-permute-start(f32[64,256]{1,0:T(8,128)S(1)} %get-tuple-element.27), channel_id=1, source_target_pairs={{0,4},{2,6},{4,0},{6,2},{1,5},{3,7},{5,1},{7,3},{8,12},{10,14},{12... | collective-permute-start | bytes 196616 | tf_op jit(solution)/shard_map/ppermute | solution.py:476
  47.4 2.8 %collective-permute-start.11 = (f32[64,256]{1,0:T(8,128)S(1)}, f32[64,256]{1,0:T(8,128)S(1)}, u32[]{:S(2)}, u32[]{:S(2)}) collective-permute-start(f32[64,256]{1,0:T(8,128)S(1)} %get-tuple-element.28), channel_id=1, source_target_pairs={{0,6},{2,0},{4,2},{6,4},{1,7},{3,1},{5,3},{7,5},{8,14},{10,8},{12,... | collective-permute-start | bytes 196616 | tf_op jit(solution)/shard_map/ppermute | solution.py:476
  50.3 1.8 %collective-permute-done.9 = f32[64,256]{1,0:T(8,128)S(1)} collective-permute-done((f32[64,256]{1,0:T(8,128)S(1)}, f32[64,256]{1,0:T(8,128)S(1)}, u32[]{:S(2)}, u32[]{:S(2)}) %collective-permute-start.9) | collective-permute-done | bytes 65568 | tf_op jit(solution)/shard_map/ppermute | solution.py:476
  52.1 1.9 %collective-permute-done.10 = f32[64,256]{1,0:T(8,128)S(1)} collective-permute-done((f32[64,256]{1,0:T(8,128)S(1)}, f32[64,256]{1,0:T(8,128)S(1)}, u32[]{:S(2)}, u32[]{:S(2)}) %collective-permute-start.10) | collective-permute-done | bytes 65568 | tf_op jit(solution)/shard_map/ppermute | solution.py:476
  54.0 0.0 collective-permute-done.11
  54.0 0.6 %add_add_fusion = f32[64,256]{1,0:T(8,128)} fusion(f32[64,256]{1,0:T(8,128)S(1)} %collective-permute-done.11, f32[64,256]{1,0:T(8,128)S(1)} %collective-permute-done.10, f32[64,256]{1,0:T(8,128)S(1)} %get-tuple-element.25, f32[64,256]{1,0:T(8,128)S(1)} %collective-permute-done.9), kind=kLoop, calls=%fused_computation | loop fusion | flops 49152 | bytes 327680 | tf_op jit(solution)/shard_map/add | solution.py:476
  (24 shorter events, 0.0 us)
Async XLA Ops:
  0.0 0.7 %copy-start.21 = (f32[128]{0:T(128)S(1)}, f32[128]{0:T(128)}, u32[]{:S(2)}) copy-start(f32[128]{0:T(128)} %param.31) | copy-start | bytes 1540
  0.0 0.7 %copy-start.11 = (f32[256]{0:T(256)S(1)}, f32[256]{0:T(256)}, u32[]{:S(2)}) copy-start(f32[256]{0:T(256)} %param.24) | copy-start | bytes 3076
  0.0 0.7 %copy-start.19 = (f32[2]{0:T(128)S(1)}, f32[2]{0:T(128)}, u32[]{:S(2)}) copy-start(f32[2]{0:T(128)} %rates.1) | copy-start | bytes 28
  0.0 0.7 %copy-start.20 = (f32[2]{0:T(128)S(1)}, f32[2]{0:T(128)}, u32[]{:S(2)}) copy-start(f32[2]{0:T(128)} %skip.1) | copy-start | bytes 28
  0.0 0.7 %copy-start.8 = (f32[256,2]{0,1:T(2,128)S(1)}, f32[256,2]{0,1:T(2,128)}, u32[]{:S(2)}) copy-start(f32[256,2]{0,1:T(2,128)} %param.27) | copy-start | bytes 6148
  0.0 0.7 %copy-start.10 = (s32[256]{0:T(256)S(1)}, s32[256]{0:T(256)}, u32[]{:S(2)}) copy-start(s32[256]{0:T(256)} %param.21) | copy-start | bytes 3076
  0.0 0.7 %copy-start.18 = (f32[2]{0:T(128)S(1)}, f32[2]{0:T(128)}, u32[]{:S(2)}) copy-start(f32[2]{0:T(128)} %bias.1) | copy-start | bytes 28
  0.8 1.0 %copy-start = (f32[256,2,128]{2,1,0:T(2,128)S(1)}, f32[256,2,128]{2,1,0:T(2,128)}, u32[]{:S(2)}) copy-start(f32[256,2,128]{2,1,0:T(2,128)} %param.25) | copy-start | bytes 786436
  1.7 0.9 %copy-start.1 = (f32[256,2,128]{2,1,0:T(2,128)S(1)}, f32[256,2,128]{2,1,0:T(2,128)}, u32[]{:S(2)}) copy-start(f32[256,2,128]{2,1,0:T(2,128)} %param.26) | copy-start | bytes 786436
  2.7 0.7 %copy-start.6 = (f32[16,256]{1,0:T(8,128)S(1)}, f32[16,256]{1,0:T(8,128)}, u32[]{:S(2)}) copy-start(f32[16,256]{1,0:T(8,128)} %refs_8_.1) | copy-start | bytes 49156
  3.4 26.9 %copy-start.2 = (f32[256,2,128]{2,1,0:T(2,128)S(1)}, f32[256,2,128]{2,1,0:T(2,128)}, u32[]{:S(2)}) copy-start(f32[256,2,128]{2,1,0:T(2,128)} %param.34) | copy-start | bytes 786436
  3.4 26.9 %copy-start.3 = (f32[256,2,128]{2,1,0:T(2,128)S(1)}, f32[256,2,128]{2,1,0:T(2,128)}, u32[]{:S(2)}) copy-start(f32[256,2,128]{2,1,0:T(2,128)} %param.35) | copy-start | bytes 786436
  3.4 26.9 %copy-start.7 = (f32[16,256]{1,0:T(8,128)S(1)}, f32[16,256]{1,0:T(8,128)}, u32[]{:S(2)}) copy-start(f32[16,256]{1,0:T(8,128)} %refs_8_.1) | copy-start | bytes 49156
  4.4 10.4 %collective-permute-start.2 = (f32[32,640]{1,0:T(8,128)S(1)}, f32[32,640]{1,0:T(8,128)S(1)}, u32[]{:S(2)}, u32[]{:S(2)}) collective-permute-start(f32[32,640]{1,0:T(8,128)S(1)} %get-tuple-element.17.refs_0_), channel_id=1, source_target_pairs={{0,30},{2,24},{4,26},{6,28},{8,6},{10,0},{12,2},{14,4},{16,14},{18... | collective-permute-start | bytes 245768 | tf_op jit(solution)/shard_map/ppermute | solution.py:429
  9.9 20.3 %collective-permute-start.4 = (f32[128,256]{1,0:T(8,128)}, f32[128,256]{1,0:T(8,128)S(1)}, u32[]{:S(2)}, u32[]{:S(2)}) collective-permute-start(f32[128,256]{1,0:T(8,128)} %refs_4_.1), channel_id=1, source_target_pairs={{0,4},{2,6},{4,0},{6,2},{1,5},{3,7},{5,1},{7,3},{8,12},{10,14},{12... | collective-permute-start | bytes 393224 | tf_op jit(solution)/shard_map/ppermute | solution.py:397
  9.9 20.3 %collective-permute-start.3 = (f32[128,256]{1,0:T(8,128)}, f32[128,256]{1,0:T(8,128)S(1)}, u32[]{:S(2)}, u32[]{:S(2)}) collective-permute-start(f32[128,256]{1,0:T(8,128)} %refs_4_.1), channel_id=1, source_target_pairs={{0,2},{2,4},{4,6},{6,0},{1,3},{3,5},{5,7},{7,1},{8,10},{10,12},{12... | collective-permute-start | bytes 393224 | tf_op jit(solution)/shard_map/ppermute | solution.py:397
  10.9 19.3 %collective-permute-start.5 = (f32[128,256]{1,0:T(8,128)}, f32[128,256]{1,0:T(8,128)S(1)}, u32[]{:S(2)}, u32[]{:S(2)}) collective-permute-start(f32[128,256]{1,0:T(8,128)} %refs_4_.1), channel_id=1, source_target_pairs={{0,6},{2,0},{4,2},{6,4},{1,7},{3,1},{5,3},{7,5},{8,14},{10,8},{12,... | collective-permute-start | bytes 393224 | tf_op jit(solution)/shard_map/ppermute | solution.py:397
  13.7 16.4 %collective-permute-start.1 = (f32[32,640]{1,0:T(8,128)S(1)}, f32[32,640]{1,0:T(8,128)S(1)}, u32[]{:S(2)}, u32[]{:S(2)}) collective-permute-start(f32[32,640]{1,0:T(8,128)S(1)} %get-tuple-element.17.refs_0_), channel_id=1, source_target_pairs={{0,20},{2,22},{4,16},{6,18},{8,28},{10,30},{12,24},{14,26},{16,4},... | collective-permute-start | bytes 245768 | tf_op jit(solution)/shard_map/ppermute | solution.py:429
  14.8 15.3 %collective-permute-start = (f32[32,640]{1,0:T(8,128)S(1)}, f32[32,640]{1,0:T(8,128)S(1)}, u32[]{:S(2)}, u32[]{:S(2)}) collective-permute-start(f32[32,640]{1,0:T(8,128)S(1)} %get-tuple-element.17.refs_0_), channel_id=1, source_target_pairs={{0,10},{2,12},{4,14},{6,8},{8,18},{10,20},{12,22},{14,16},{16,26},... | collective-permute-start | bytes 245768 | tf_op jit(solution)/shard_map/ppermute | solution.py:429
  30.2 0.7 %copy-start.13 = (f32[256]{0:T(256)S(1)}, f32[256]{0:T(256)}, u32[]{:S(2)}) copy-start(f32[256]{0:T(256)} %param.33) | copy-start | bytes 3076
  30.2 0.7 %copy-start.15 = (f32[2]{0:T(128)S(1)}, f32[2]{0:T(128)}, u32[]{:S(2)}) copy-start(f32[2]{0:T(128)} %refs_16_.1) | copy-start | bytes 28
  30.2 0.7 %copy-start.16 = (f32[2]{0:T(128)S(1)}, f32[2]{0:T(128)}, u32[]{:S(2)}) copy-start(f32[2]{0:T(128)} %refs_17_.1) | copy-start | bytes 28
  30.2 0.7 %copy-start.9 = (f32[256,2]{0,1:T(2,128)S(1)}, f32[256,2]{0,1:T(2,128)}, u32[]{:S(2)}) copy-start(f32[256,2]{0,1:T(2,128)} %param.36) | copy-start | bytes 6148
  30.2 0.7 %copy-start.12 = (s32[256]{0:T(256)S(1)}, s32[256]{0:T(256)}, u32[]{:S(2)}) copy-start(s32[256]{0:T(256)} %param.23) | copy-start | bytes 3076
  30.2 0.7 %copy-start.14 = (f32[2]{0:T(128)S(1)}, f32[2]{0:T(128)}, u32[]{:S(2)}) copy-start(f32[2]{0:T(128)} %refs_15_.1) | copy-start | bytes 28
  30.9 0.9 %copy-start.4 = (f32[128,256]{1,0:T(8,128)S(1)}, f32[128,256]{1,0:T(8,128)}, u32[]{:S(2)}) copy-start(f32[128,256]{1,0:T(8,128)} %refs_4_.1) | copy-start | bytes 393220
  31.8 12.1 %copy-start.5 = (f32[128,256]{1,0:T(8,128)S(1)}, f32[128,256]{1,0:T(8,128)}, u32[]{:S(2)}) copy-start(f32[128,256]{1,0:T(8,128)} %refs_9_.1) | copy-start | bytes 393220
  37.9 5.1 %collective-permute-start.8 = (f32[136,128]{1,0:T(8,128)S(1)}, f32[136,128]{1,0:T(8,128)S(1)}, u32[]{:S(2)}, u32[]{:S(2)}) collective-permute-start(f32[136,128]{1,0:T(8,128)S(1)} %get-tuple-element.19), channel_id=1, source_target_pairs={{0,24},{1,25},{2,26},{3,27},{4,28},{5,29},{6,30},{7,31}} | collective-permute-start | bytes 208904 | tf_op jit(solution)/shard_map/ppermute | solution.py:463
  39.7 3.3 %collective-permute-start.7 = (f32[136,128]{1,0:T(8,128)S(1)}, f32[136,128]{1,0:T(8,128)S(1)}, u32[]{:S(2)}, u32[]{:S(2)}) collective-permute-start(f32[136,128]{1,0:T(8,128)S(1)} %get-tuple-element.19), channel_id=1, source_target_pairs={{0,16},{8,24},{1,17},{9,25},{2,18},{10,26},{3,19},{11,27},{4,20},{... | collective-permute-start | bytes 208904 | tf_op jit(solution)/shard_map/ppermute | solution.py:463
  41.0 2.9 %collective-permute-start.6 = (f32[136,128]{1,0:T(8,128)S(1)}, f32[136,128]{1,0:T(8,128)S(1)}, u32[]{:S(2)}, u32[]{:S(2)}) collective-permute-start(f32[136,128]{1,0:T(8,128)S(1)} %get-tuple-element.19), channel_id=1, source_target_pairs={{0,8},{8,16},{16,24},{1,9},{9,17},{17,25},{2,10},{10,18},{18,26},{... | collective-permute-start | bytes 208904 | tf_op jit(solution)/shard_map/ppermute | solution.py:463
  43.9 0.7 %copy-start.17 = (f32[128]{0:T(128)S(1)}, f32[128]{0:T(128)}, u32[]{:S(2)}) copy-start(f32[128]{0:T(128)} %param.40) | copy-start | bytes 1540
  45.2 6.8 %collective-permute-start.9 = (f32[64,256]{1,0:T(8,128)S(1)}, f32[64,256]{1,0:T(8,128)S(1)}, u32[]{:S(2)}, u32[]{:S(2)}) collective-permute-start(f32[64,256]{1,0:T(8,128)S(1)} %get-tuple-element.26), channel_id=1, source_target_pairs={{0,2},{2,4},{4,6},{6,0},{1,3},{3,5},{5,7},{7,1},{8,10},{10,12},{12... | collective-permute-start | bytes 196616 | tf_op jit(solution)/shard_map/ppermute | solution.py:476
  45.3 8.6 %collective-permute-start.10 = (f32[64,256]{1,0:T(8,128)S(1)}, f32[64,256]{1,0:T(8,128)S(1)}, u32[]{:S(2)}, u32[]{:S(2)}) collective-permute-start(f32[64,256]{1,0:T(8,128)S(1)} %get-tuple-element.27), channel_id=1, source_target_pairs={{0,4},{2,6},{4,0},{6,2},{1,5},{3,7},{5,1},{7,3},{8,12},{10,14},{12... | collective-permute-start | bytes 196616 | tf_op jit(solution)/shard_map/ppermute | solution.py:476
  47.4 6.5 %collective-permute-start.11 = (f32[64,256]{1,0:T(8,128)S(1)}, f32[64,256]{1,0:T(8,128)S(1)}, u32[]{:S(2)}, u32[]{:S(2)}) collective-permute-start(f32[64,256]{1,0:T(8,128)S(1)} %get-tuple-element.28), channel_id=1, source_target_pairs={{0,6},{2,0},{4,2},{6,4},{1,7},{3,1},{5,3},{7,5},{8,14},{10,8},{12,... | collective-permute-start | bytes 196616 | tf_op jit(solution)/shard_map/ppermute | solution.py:476

commit v2 on v1

v2 whole, which is shorter than its diff:
```python
import functools

import jax
import jax.numpy as jnp
from jax import lax
from jax.experimental import pallas as pl
from jax.experimental.pallas import tpu as pltpu
from jax.sharding import PartitionSpec as P

epsilon = 1e-05
f32 = jnp.float32
bf16 = jnp.bfloat16
LIMIT = 48 * 1024 * 1024

MM = (((1,), (0,)), ((), ()))
NT = (((1,), (1,)), ((), ()))
TN = (((0,), (0,)), ((), ()))


def iota(shape, axis):
    return lax.broadcasted_iota(jnp.int32, shape, axis)


def split2(value):
    high = value.astype(bf16)
    return high, (value - high.astype(f32)).astype(bf16)


def split3(value):
    high = value.astype(bf16)
    rest = value - high.astype(f32)
    middle = rest.astype(bf16)
    return high, middle, (rest - middle.astype(f32)).astype(bf16)


def dot(left, right, dims=MM):
    return lax.dot_general(left, right, dims, preferred_element_type=f32)


def dot_split(left, right, dims=MM):
    return (
        dot(left[0], right[1], dims) + dot(left[1], right[0], dims)
    ) + dot(left[0], right[0], dims)


def dot3(left, right, dims=MM):
    return dot_split(split2(left), split2(right), dims)


def dot_left_exact(left, right, dims=MM):
    high, middle, low = split3(right)
    return (dot(left, low, dims) + dot(left, middle, dims)) + dot(left, high, dims)


def dot_right_exact(left, right, dims=MM):
    high, middle, low = split3(left)
    return (dot(low, right, dims) + dot(middle, right, dims)) + dot(high, right, dims)


def softplus(value):
    return jnp.maximum(value, 0.0) + jnp.log1p(jnp.exp(-jnp.abs(value)))


def silu(value):
    return value / (1.0 + jnp.exp(-value))


def rms(value):
    return value * lax.rsqrt(jnp.mean(value * value, axis=-1, keepdims=True) + epsilon)


def fetch(sources, places, semaphores):
    copies = []
    for number, (source, place) in enumerate(zip(sources, places)):
        copies.append(pltpu.make_async_copy(source, place, semaphores.at[number]))
        copies[-1].start()
    return copies


def tables_kernel(dims, *refs):
    V, D, hl, ch, nh, ns, T, N = dims
    H, LV = nh * hl, nh * hl * V
    refs = list(refs)

    def take(number):
        taken, refs[:] = refs[:number], refs[number:]
        return taken

    sources = take(17)
    outproj_source = take(1)[0]
    message, pairs, small, outproj = take(4)
    places = take(17)
    semaphores = take(1)[0]
    half = ch // 2
    base = V + 2 + 3 * hl
    core = lax.rem(lax.axis_index("seq"), 2)
    copies = fetch(
        sources + [outproj_source],
        places + [outproj],
        semaphores,
    )
    for copy in copies:
        copy.wait()
    message[base : base + half, 0:D] = outproj[pl.ds(pl.multiple_of(core * half, 8), half), :]
    (tok, emb, prenorm, inproj, statemap, stepmap, bias, rates, skip, outnorm) = places[:10]
    (complement, prenorm2, stepmap2, bias2, rates2, skip2, outnorm2) = places[10:]

    normed = split2(rms(emb[...]) * prenorm[...])
    gate = dot_split(normed, split2(inproj[pl.ds(0, D, stride=2), :]))
    inner = dot_split(normed, split2(inproj[pl.ds(1, D, stride=2), :]))
    message[0:V, 0:ch] = gate
    message[0:V, ch : 2 * ch] = inner
    flip = (iota((T, T), 0) + iota((T, T), 1) == T - 1).astype(f32).astype(bf16)
    tokens = jnp.broadcast_to(tok[...].astype(f32), (8, T)).astype(bf16)
    message[V : V + 1, 0:T] = dot(tokens, flip)[0:1]
    message[V + 1 : V + 2, 0:ch] = outnorm[...]
    raw_t = dot_split(split2(stepmap[...]), normed, NT)
    for head in range(hl):
        line = softplus(raw_t[head : head + 1, :] + bias[:, head : head + 1])
        row = V + 2 + head
        message[row : row + 1, 0:V] = line
        message[row + hl : row + hl + 1, 0:V] = -rates[:, head : head + 1] * line
        message[row + 2 * hl : row + 2 * hl + 1, 0:V] = jnp.broadcast_to(
            skip[:, head : head + 1], (1, V)
        )

    write = dot_split(normed, split2(statemap[pl.ds(0, D, stride=2), :]))
    read = dot_split(normed, split2(statemap[pl.ds(1, D, stride=2), :]))
    pairs[...] = dot3(read, jnp.concatenate([write] * H, axis=0), NT)
    small[0:1, 0:D] = complement[...].astype(f32)
    small[1:2, 0:D] = prenorm2[...]
    small[2:3, 0:ch] = outnorm2[...]
    small[8 : 8 + hl, 0:D] = stepmap2[...]
    for place, ref in ((3, bias2), (4, rates2), (5, skip2)):
        small[place : place + 1, 0:hl] = ref[...]


def shift_rows(value, amount, fill):
    size = value.shape[0]
    rolled = pltpu.roll(value, amount % size, 0)
    row = iota(value.shape, 0)
    have = (row >= amount) if amount > 0 else (row < size + amount)
    return jnp.where(have, rolled, fill)


def scan_rows(decay, value, sign):
    size = value.shape[0]
    amount = 1
    while amount < size:
        value = value + decay * shift_rows(value, sign * amount, 0.0)
        if 2 * amount < size:
            decay = decay * shift_rows(decay, sign * amount, 1.0)
        amount *= 2
    return value


def mix_kernel(dims, *refs):
    V, D, hl, ch, nh, ns, T, N = dims
    H, LV, P = nh * hl, nh * hl * V, ch // hl
    C = nh * ch
    refs = list(refs)

    def take(number):
        taken, refs[:] = refs[:number], refs[number:]
        return taken

    packets = take(max(ns, nh))
    emb, pairs = take(2)
    out_high, out_low, out_embedded = take(3)
    tokens = take(1)[0]
    mine = lax.axis_index("seq")

    for k in range(ns):
        block = ns - 1 - lax.rem(mine - k + ns, ns)
        tokens[pl.ds(block, 1), :] = packets[k][V : V + 1, 0:T]

    def rows_of(place):
        low = V + 2 + place * hl
        return jnp.concatenate([packets[k][low : low + hl, 0:V] for k in range(nh)], axis=0)

    step_t, log_t, skip_t = rows_of(0), rows_of(1), rows_of(2)
    spread_heads = (iota((H, LV), 1) // V == iota((H, LV), 0)).astype(f32).astype(bf16)

    def widen(value):
        high, middle, low = split3(value)
        return (dot(low, spread_heads, TN) + dot(middle, spread_heads, TN)) + dot(
            high, spread_heads, TN
        )

    own = iota((V, LV), 1) % V == iota((V, LV), 0)
    decay_table = jnp.exp(widen(log_t))
    step_table = jnp.where(own, widen(step_t), 0.0)
    gain_table = jnp.where(own, widen(skip_t), 0.0)
    gates = jnp.concatenate([packets[k][0:V, 0:ch] for k in range(nh)], axis=1)
    inners = jnp.concatenate([packets[k][0:V, ch : 2 * ch] for k in range(nh)], axis=1)
    gains = jnp.concatenate([packets[k][V + 1 : V + 2, 0:ch] for k in range(nh)], axis=1)

    token_row = (iota((LV, T), 0) % V).astype(f32)
    log_split = jnp.concatenate(split3(log_t), axis=1)
    onehots, logs = [], []
    for block in range(ns):
        onehot = (tokens[block : block + 1, :] == token_row).astype(f32).astype(bf16)
        onehots.append(onehot)
        logs.append(dot(log_split, onehot[0 : 3 * V, :]))
    logs = jnp.concatenate(logs, axis=0)
    first, second = iota((T, T), 0), iota((T, T), 1)
    later = (first > second).astype(f32).astype(bf16)
    sooner = (first < second).astype(f32).astype(bf16)
    logs3 = split3(logs)
    after = dot(logs3[2], later) + dot(logs3[1], later) + dot(logs3[0], later)
    before = dot(logs3[2], sooner) + dot(logs3[1], sooner) + dot(logs3[0], sooner)
    totals = jnp.sum(logs, axis=1, keepdims=True)
    total_rows = jnp.broadcast_to(totals, (ns * H, 128))
    row, column = iota((ns * H, ns * H), 0), iota((ns * H, ns * H), 1)
    row_block, column_block = row // H, column // H
    between = ((row_block < column_block) & (column_block < mine)) | (
        (row_block > column_block) & (column_block > mine)
    )
    between = (between & (row % H == column % H)).astype(f32).astype(bf16)
    gap = dot_left_exact(between, total_rows)[:, 0:1]
    block_of = iota((ns * H, T), 0) // H
    weight_up = jnp.where(block_of < mine, jnp.exp(after + gap), 0.0)
    weight_down = jnp.where(block_of > mine, jnp.exp(before + gap), 0.0)
    entering = jnp.zeros((2 * H, LV), f32)
    for block in range(ns):
        both = jnp.concatenate(
            [weight_up[block * H : (block + 1) * H], weight_down[block * H : (block + 1) * H]],
            axis=0,
        )
        high, low = split2(both)
        entering = entering + (dot(low, onehots[block], NT) + dot(high, onehots[block], NT))
    diagonal = iota((H, LV), 1) // V == iota((H, LV), 0)
    step_row = jnp.sum(step_table, axis=0, keepdims=True)
    enter_up = step_row * jnp.sum(
        jnp.where(diagonal, entering[0:H], 0.0), axis=0, keepdims=True
    )
    enter_down = step_row * jnp.sum(
        jnp.where(diagonal, entering[H : 2 * H], 0.0), axis=0, keepdims=True
    )

    looked = jnp.concatenate(
        [decay_table, step_table, pairs[...], gain_table, silu(gates), emb[...]], axis=1
    )
    looked = jnp.concatenate(split3(looked), axis=0)
    token = tokens[pl.ds(mine, 1), :]
    onehot = (token == (iota((3 * V, T), 0) % V).astype(f32)).astype(f32).astype(bf16)
    rows = dot(onehot, looked, TN)
    decay, step = rows[:, 0:LV], rows[:, LV : 2 * LV]
    pair, gain = rows[:, 2 * LV : 3 * LV], rows[:, 3 * LV : 4 * LV]
    silu_rows = rows[:, 4 * LV : 4 * LV + C]
    out_embedded[...] = rows[:, 4 * LV + C :]

    position = iota((T, LV), 0)
    up = scan_rows(decay, jnp.where(position == 0, step + decay * enter_up, step), 1)
    down = scan_rows(decay, jnp.where(position == T - 1, step + decay * enter_down, step), -1)

    tiled = jnp.concatenate([inners] * H, axis=0)
    spread = jnp.where(iota((LV, C), 0) // V == iota((LV, C), 1) // P, tiled, 0.0)
    spread_high, spread_low = split2(spread)
    group = (iota((C, C), 0) // P == iota((C, C), 1) // P).astype(f32).astype(bf16)

    def gated(coefficients):
        high, low = split2(coefficients * pair + gain)
        value = dot(high, spread_low) + dot(low, spread_high) + dot(high, spread_high)
        value = value * silu_rows
        high, low = split2(value * value)
        square = dot(low, group) + dot(high, group)
        return value * lax.rsqrt(square * (1.0 / P) + epsilon)

    out_high[...], out_low[...] = split2((gated(up) + gated(down)) * gains)


def project_kernel(dims, *refs):
    V, D, hl, ch, nh, ns, T, N = dims
    P = ch // hl
    refs = list(refs)

    def take(number):
        taken, refs[:] = refs[:number], refs[number:]
        return taken

    high, low, embedded, small, outproj = take(5)
    nears = take(nh - 1)
    others = take(nh - 1)
    sources = take(2)
    out_state, out_read, out_write, out_inner, out_stepped, out_gate = take(6)
    out_total, out_total_t, out_own = take(3)
    places = take(2)
    mirrored_ref, semaphores = take(2)
    copies = fetch(sources, places, semaphores)
    inproj2, statemap2 = places
    half = ch // 2
    base = V + 2 + 3 * hl
    mine = lax.axis_index("seq")

    hidden = embedded[...]
    for k in range(1, nh):
        near = nears[k - 1][base : base + half, 0:D]
        other = others[k - 1][base : base + half, 0:D]
        even = lax.rem(mine - k + ns * nh, 2) == 0
        weights = jnp.concatenate(
            [jnp.where(even, near, other), jnp.where(even, other, near)], axis=0
        )
        part = (high[:, k * ch : (k + 1) * ch], low[:, k * ch : (k + 1) * ch])
        hidden = hidden + dot_split(part, split2(weights))
    hidden = hidden + dot_split((high[:, 0:ch], low[:, 0:ch]), split2(outproj[...]))
    choose = (small[0:1, 0:D] == iota((D, D), 0).astype(f32)).astype(f32).astype(bf16)
    mirrored = dot_right_exact(hidden, choose)
    mirrored_ref[...] = mirrored
    share = T // nh
    out_own[...] = mirrored_ref[pl.ds(pl.multiple_of(lax.axis_index("head") * share, 8), share), :]

    normed = split2(rms(mirrored) * small[1:2, 0:D])
    copies[0].wait()
    gate = dot_split(normed, split2(inproj2[pl.ds(0, D, stride=2), :]))
    inner = dot_split(normed, split2(inproj2[pl.ds(1, D, stride=2), :]))
    copies[1].wait()
    write = dot_split(normed, split2(statemap2[pl.ds(0, D, stride=2), :]))
    out_read[...] = dot_split(normed, split2(statemap2[pl.ds(1, D, stride=2), :]))
    out_write[...] = write
    out_inner[...] = inner
    out_gate[...] = silu(gate)
    steps = split2(small[8 : 8 + hl, 0:D])
    raw = dot_split(normed, steps, NT)
    raw_t = dot_split(steps, normed, NT)
    of_head = iota((T, ch), 1) // P
    step = jnp.zeros((T, ch), f32)
    log = jnp.zeros((T, ch), f32)
    logs = []
    for head in range(hl):
        bias2, rates2 = small[3:4, head : head + 1], small[4:5, head : head + 1]
        column = softplus(raw[:, head : head + 1] + bias2)
        here = of_head == head
        step = jnp.where(here, column, step)
        log = jnp.where(here, -rates2 * column, log)
        logs.append(-rates2 * softplus(raw_t[head : head + 1, :] + bias2))
    first, second = iota((T, T), 0), iota((T, T), 1)
    total = dot_left_exact((first >= second).astype(f32).astype(bf16), log)
    logs = jnp.concatenate(logs, axis=0)
    out_total_t[0:hl, :] = dot_right_exact(logs, (first <= second).astype(f32).astype(bf16))
    out_total[...] = total
    end = total[T - 1 : T, :]
    stepped = inner * step
    out_stepped[...] = stepped
    state = dot3(stepped * jnp.exp(end - total), write, TN)
    out_state[0:ch, :] = state
    for head in range(hl):
        out_state[ch + head : ch + head + 1, :] = jnp.broadcast_to(
            end[:, head * P : head * P + 1], (1, N)
        )


def block_kernel(dims, read, write, inner, stepped, total, total_t, small, base):
    V, D, hl, ch, nh, ns, T, N = dims
    P = ch // hl
    products = dot3(read[...], write[...], NT)
    stepped_high, stepped_low = split2(stepped[...])
    allowed = iota((T, T), 0) >= iota((T, T), 1)
    parts = []
    for head in range(hl):
        low, high = head * P, (head + 1) * P
        differ = total[:, low : low + 1] - total_t[head : head + 1, :]
        weights = jnp.where(allowed, jnp.exp(jnp.where(allowed, differ, 0.0)), 0.0) * products
        part = dot_split(split2(weights), (stepped_high[:, low:high], stepped_low[:, low:high]))
        parts.append(part + small[5:6, head : head + 1] * inner[:, low:high])
    base[...] = jnp.concatenate(parts, axis=1)


def state_rows(dims, values):
    V, D, hl, ch, nh, ns, T, N = dims
    head_of = iota((ch, N), 0) // (ch // hl)
    result = jnp.broadcast_to(values[0:1, :], (ch, N))
    for head in range(1, hl):
        result = jnp.where(head_of == head, values[head : head + 1, :], result)
    return result


def join_kernel(dims, bit, total, prefix, came, out_total, out_prefix):
    V, D, hl, ch, nh, ns, T, N = dims
    later = lax.rem(lax.div(lax.axis_index("seq"), 2**bit), 2) == 1
    came_state, came_log = came[0:ch, :], came[ch : ch + hl, :]
    state, log = total[0:ch, :], total[ch : ch + hl, :]
    factor = jnp.exp(state_rows(dims, jnp.where(later, log, came_log)))
    out_total[0:ch, :] = jnp.where(
        later, factor * came_state + state, factor * state + came_state
    )
    out_total[ch : ch + hl, :] = log + came_log
    if prefix is None:
        out_prefix[0:ch, :] = jnp.where(later, came_state, 0.0)
        out_prefix[ch : ch + hl, :] = jnp.where(later, came_log, 0.0)
    else:
        joined = prefix_joined(dims, bit, prefix, came)
        out_prefix[0:ch, :] = joined
        out_prefix[ch : ch + hl, :] = prefix[ch : ch + hl, :] + jnp.where(later, came_log, 0.0)


def prefix_joined(dims, bit, prefix, came):
    V, D, hl, ch, nh, ns, T, N = dims
    later = lax.rem(lax.div(lax.axis_index("seq"), 2**bit), 2) == 1
    factor = jnp.exp(state_rows(dims, prefix[ch : ch + hl, :]))
    return prefix[0:ch, :] + jnp.where(later, factor * came[0:ch, :], 0.0)


def output_kernel(dims, bit, *refs):
    V, D, hl, ch, nh, ns, T, N = dims
    P = ch // hl
    refs = list(refs)

    def take(number):
        taken, refs[:] = refs[:number], refs[number:]
        return taken

    prefix, came, read, base, total, gate, own, small, outproj_source = take(9)
    outs = take(nh)
    partial_ref, outproj, semaphore = take(3)
    copy = pltpu.make_async_copy(outproj_source, outproj, semaphore.at[0])
    copy.start()
    entering = prefix_joined(dims, bit, prefix, came)
    value = (base[...] + dot3(read[...], entering, NT) * jnp.exp(total[...])) * gate[...]
    group = (iota((ch, ch), 0) // P == iota((ch, ch), 1) // P).astype(f32).astype(bf16)
    high, low = split2(value * value)
    square = dot(low, group) + dot(high, group)
    value = value * lax.rsqrt(square * (1.0 / P) + epsilon) * small[2:3, 0:ch]
    copy.wait()
    partial_ref[...] = dot3(value, outproj[...])
    share = T // nh
    mine = lax.axis_index("head")
    for k in range(nh):
        place = pl.multiple_of(lax.rem(mine + k, nh) * share, 8)
        part = partial_ref[pl.ds(place, share), :]
        outs[k][...] = part + own[...] if k == 0 else part


def per_device(
    token_ids,
    embedding,
    complement,
    prenorm_first,
    inproj_first,
    statemap_first,
    stepmap_first,
    stepbias_first,
    rates_first,
    skipgain_first,
    outnorm_first,
    outproj_first,
    prenorm_second,
    inproj_second,
    statemap_second,
    stepmap_second,
    stepbias_second,
    rates_second,
    skipgain_second,
    outnorm_second,
    outproj_second,
):
    nh, ns = lax.axis_size("head"), lax.axis_size("seq")
    V, D = embedding.shape
    ch = inproj_first.shape[2]
    hl = stepmap_first.shape[1]
    N = statemap_first.shape[2]
    T = token_ids.shape[0]
    LV = nh * hl * V
    dims = (V, D, hl, ch, nh, ns, T, N)
    vmem = pl.BlockSpec(memory_space=pltpu.VMEM)
    anywhere = pl.BlockSpec(memory_space=pl.ANY)
    params = pltpu.CompilerParams(vmem_limit_bytes=LIMIT)

    def shape(*sizes, dtype=f32):
        return jax.ShapeDtypeStruct(sizes, dtype)

    def room(value):
        return pltpu.VMEM(value.shape, value.dtype)

    def line(value):
        return value.reshape(1, -1)

    def flat(value):
        return value.reshape(-1, value.shape[-1])

    def cost(flops):
        return pl.CostEstimate(flops=flops, bytes_accessed=4 * T * D, transcendentals=T * D)

    head_rows = V + 2 + 3 * hl
    half = ch // 2
    width = max(2 * ch, T, D)
    fetched = [
        line(token_ids),
        embedding,
        line(prenorm_first),
        flat(inproj_first),
        flat(statemap_first),
        stepmap_first.T,
        line(stepbias_first),
        line(rates_first),
        line(skipgain_first),
        line(outnorm_first),
        line(complement),
        line(prenorm_second),
        stepmap_second.T,
        line(stepbias_second),
        line(rates_second),
        line(skipgain_second),
        line(outnorm_second),
    ]
    message, pair_table, small, own_projection = pl.pallas_call(
        functools.partial(tables_kernel, dims),
        out_shape=(
            shape(head_rows + half, width),
            shape(V, LV),
            shape(16, D),
            shape(ch, D),
        ),
        in_specs=[anywhere] * (len(fetched) + 1),
        out_specs=(vmem,) * 4,
        scratch_shapes=[room(value) for value in fetched]
        + [pltpu.SemaphoreType.DMA((len(fetched) + 1,))],
        name="tables",
    )(*fetched, outproj_first)

    messages = [message]
    for k in range(1, max(ns, nh)):
        pairs = [
            (seq * nh + head, ((seq + k) % ns) * nh + (head + k) % nh)
            for seq in range(ns)
            for head in range(nh)
        ]
        sent = message if k < nh else message[0 : V + 8]
        messages.append(lax.ppermute(sent, ("seq", "head"), pairs))
    swap = [(seq, seq ^ 1) for seq in range(ns)]
    others = [lax.ppermute(messages[k], "seq", swap) for k in range(1, nh)]

    mixed_high, mixed_low, embedded = pl.pallas_call(
        functools.partial(mix_kernel, dims),
        out_shape=(
            shape(T, nh * ch, dtype=bf16),
            shape(T, nh * ch, dtype=bf16),
            shape(T, D),
        ),
        in_specs=[vmem] * (len(messages) + 2),
        out_specs=(vmem,) * 3,
        scratch_shapes=[pltpu.VMEM((max(ns, 8), T), f32)],
        compiler_params=params,
        cost_estimate=cost(6 * T * D * D * 16),
        name="mix",
    )(*messages, embedding, pair_table)

    fetched = [flat(inproj_second), flat(statemap_second)]
    share = T // nh
    state, read, write, inner, stepped, gate, total, total_t, own = pl.pallas_call(
        functools.partial(project_kernel, dims),
        out_shape=(
            shape(ch + 8, N),
            shape(T, N),
            shape(T, N),
            shape(T, ch),
            shape(T, ch),
            shape(T, ch),
            shape(T, ch),
            shape(8, T),
            shape(share, D),
        ),
        in_specs=[vmem] * (5 + 2 * (nh - 1)) + [anywhere] * len(fetched),
        out_specs=(vmem,) * 9,
        scratch_shapes=[room(value) for value in fetched]
        + [pltpu.VMEM((T, D), f32), pltpu.SemaphoreType.DMA((len(fetched),))],
        compiler_params=params,
        name="project",
    )(mixed_high, mixed_low, embedded, small, own_projection, *messages[1:nh], *others, *fetched)

    base = pl.pallas_call(
        functools.partial(block_kernel, dims),
        out_shape=shape(T, ch),
        in_specs=[vmem] * 7,
        out_specs=vmem,
        compiler_params=params,
        cost_estimate=cost(6 * T * D * D * 8),
        name="block",
    )(read, write, inner, stepped, total, total_t, small)

    prefix = None
    bits = ns.bit_length() - 1
    for bit in range(bits):
        came = lax.ppermute(state, "seq", [(seq, seq ^ 2**bit) for seq in range(ns)])
        if bit == bits - 1:
            break
        given = [state] + ([] if prefix is None else [prefix]) + [came]

        def join(bit, known, *refs):
            if known:
                join_kernel(dims, bit, *refs)
            else:
                join_kernel(dims, bit, refs[0], None, *refs[1:])

        state, prefix = pl.pallas_call(
            functools.partial(join, bit, prefix is not None),
            out_shape=(shape(ch + 8, N),) * 2,
            in_specs=[vmem] * len(given),
            out_specs=(vmem,) * 2,
            compiler_params=params,
            name="join",
        )(*given)
    if prefix is None:
        prefix = jnp.zeros_like(state)

    parts = pl.pallas_call(
        functools.partial(output_kernel, dims, bits - 1),
        out_shape=(shape(share, D),) * nh,
        in_specs=[vmem] * 8 + [anywhere],
        out_specs=(vmem,) * nh,
        scratch_shapes=[
            pltpu.VMEM((T, D), f32),
            room(outproj_second),
            pltpu.SemaphoreType.DMA((1,)),
        ],
        compiler_params=params,
        name="output",
    )(prefix, came, read, base, total, gate, own, small, outproj_second)
    result = parts[0]
    for k in range(1, nh):
        pairs = [(source, (source + k) % nh) for source in range(nh)]
        result = result + lax.ppermute(parts[k], "head", pairs)
    return result


def solution(mesh):
    return jax.shard_map(
        per_device,
        mesh=mesh,
        in_specs=(
            P(("rep", "seq")),
            P(),
            P(),
            P(),
            P(None, None, "head"),
            P(),
            P(None, "head"),
            P("head"),
            P("head"),
            P("head"),
            P("head"),
            P("head", None),
            P(),
            P(None, None, "head"),
            P(),
            P(None, "head"),
            P("head"),
            P("head"),
            P("head"),
            P("head"),
            P("head", None),
        ),
        out_specs=P(("rep", "seq", "head"), None),
        check_vma=False,
    )
```

time: 55 us -> 41.1 us (0.75)
  starting transfers between devices: 20.5 us -> 11.7 us
  local copies, waits for them, and re-layouts: 5.59 us -> 1.61 us
  waiting for transfers between devices: 19.9 us -> 16.7 us
  Pallas kernels: 7.78 us -> 10.2 us
    ppermute x9 -> x8, starting transfers between devices: 15.4 us -> 7.69 us  [the longest x3 6.48 us: per_device(): messages.append(lax.ppermute(sent, ('seq', 'head'), pairs))]
    unnamed x44 -> x16, local copies, waits for them, and re-layouts: 5.59 us -> 1.61 us
    ppermute x9 -> x8, waiting for transfers between devices: 16.2 us -> 13.1 us  [the longest x3 8.89 us: per_device(): messages.append(lax.ppermute(sent, ('seq', 'head'), pairs))]
    pallas_call x3 -> x6, Pallas kernels: 7.78 us -> 10.2 us  [the longest x1 3.17 us: per_device(): pl.pallas_call(functools.partial(project_kernel, dims), out_shape=(shape(...]
    ppermute x3, starting transfers between devices: 5.04 us -> 3.97 us  [per_device(): result = result + lax.ppermute(parts[k], 'head', pairs)]
  transfers between devices with their start and end apart: 12 -> 11, of which waited for: 4 -> 6; matrix products, arithmetic and copies ran while one was open for 0% -> 0% of each run, Pallas kernels for 0% -> 9%
where the time goes in v2:
time: 41.1 us; the launch traced here: 40.9 us
  waiting for transfers between devices  16.7 us (41%)
  starting transfers between devices  11.7 us (28%)
  Pallas kernels  10.2 us (25%)
  local copies, waits for them, and re-layouts  1.61 us (4%)
  other arithmetic  0.65 us (2%)
    ppermute x3, waiting for transfers between devices, per_device(): messages.append(lax.ppermute(sent, ('seq', 'head'), pairs))  8.89 us
    ppermute x3, starting transfers between devices, per_device(): messages.append(lax.ppermute(sent, ('seq', 'head'), pairs))  6.48 us
    ppermute x2, waiting for transfers between devices, per_device(): lax.ppermute(state, 'seq', [(seq, seq ^ 2 ** bit) for seq in range(ns)])  4.17 us
    ppermute x3, starting transfers between devices, per_device(): result = result + lax.ppermute(parts[k], 'head', pairs)  3.97 us
    ppermute x3, waiting for transfers between devices, per_device(): result = result + lax.ppermute(parts[k], 'head', pairs)  3.62 us
    pallas_call x1, Pallas kernels, per_device(): pl.pallas_call(functools.partial(project_kernel, dims), out_shape=(shape(...  3.17 us
    pallas_call x1, Pallas kernels, per_device(): pl.pallas_call(functools.partial(mix_kernel, dims), out_shape=(shape(T, n...  2.73 us
    pallas_call x1, Pallas kernels, per_device(): pl.pallas_call(functools.partial(tables_kernel, dims), out_shape=(shape(h...  2.5 us
  transfers between devices with their start and end apart: 11, of which 6 were waited for; matrix products, arithmetic and copies ran while one was open for 0% of the time, Pallas kernels for 9%

profile of v2, /device:TPU:0, one launch (start us, length us, event | category | flops | bytes accessed | tf_op | source)
XLA Modules:
  0.0 40.9 jit_solution(10134456137696346392)
XLA Ops:
  0.0 0.0 copy-start.5
  0.0 2.5 %tables.1 = (f32[88,256]{1,0:T(8,128)}, f32[16,128]{1,0:T(8,128)}, f32[16,256]{1,0:T(8,128)}, f32[128,256]{1,0:T(8,128)}) custom-call(s32[1,256]{1,0:T(1,128)} %bitcast.24, f32[16,256]{1,0:T(8,128)} %refs_4_.1, f32[1,256]{1,0:T(1,128)} %bitcast.25, f32[512,128]{1,0:T(8,128)} %bitcast.20, f32[512,128]{1,0:T(8,128)} %bitcast.21, f32[2,256]{1,0:T(2,128)} %bitcast.22, ...), custom_call_target="tpu_custom_call" | custom-call | tf_op jit(solution)/shard_map/tables/pallas_call | solution.py:506
  2.5 5.5 %collective-permute-start.2 = (f32[88,256]{1,0:T(8,128)}, f32[88,256]{1,0:T(8,128)S(1)}, u32[]{:S(2)}, u32[]{:S(2)}) collective-permute-start(f32[88,256]{1,0:T(8,128)} %get-tuple-element.27.refs_0_), channel_id=1, source_target_pairs={{0,30},{2,24},{4,26},{6,28},{8,6},{10,0},{12,2},{14,4},{16,14},{18... | collective-permute-start | bytes 270344 | tf_op jit(solution)/shard_map/ppermute | solution.py:529
  8.0 0.0 collective-permute-start.1
  8.0 1.0 %collective-permute-start = (f32[88,256]{1,0:T(8,128)}, f32[88,256]{1,0:T(8,128)S(1)}, u32[]{:S(2)}, u32[]{:S(2)}) collective-permute-start(f32[88,256]{1,0:T(8,128)} %get-tuple-element.27.refs_0_), channel_id=1, source_target_pairs={{0,10},{2,12},{4,14},{6,8},{8,18},{10,20},{12,22},{14,16},{16,26},... | collective-permute-start | bytes 270344 | tf_op jit(solution)/shard_map/ppermute | solution.py:529
  9.0 2.3 %collective-permute-done.2.refs_3_.refs_7_ = f32[88,256]{1,0:T(8,128)S(1)} collective-permute-done((f32[88,256]{1,0:T(8,128)}, f32[88,256]{1,0:T(8,128)S(1)}, u32[]{:S(2)}, u32[]{:S(2)}) %collective-permute-start.2) | collective-permute-done | bytes 90144 | tf_op jit(solution)/shard_map/ppermute | solution.py:529
  11.3 0.0 collective-permute-start.5
  11.3 6.5 %collective-permute-done.1.refs_2_.refs_6_ = f32[88,256]{1,0:T(8,128)S(1)} collective-permute-done((f32[88,256]{1,0:T(8,128)}, f32[88,256]{1,0:T(8,128)S(1)}, u32[]{:S(2)}, u32[]{:S(2)}) %collective-permute-start.1) | collective-permute-done | bytes 90144 | tf_op jit(solution)/shard_map/ppermute | solution.py:529
  17.9 0.0 collective-permute-start.4
  17.9 0.0 collective-permute-done.refs_1_.refs_5_
  17.9 0.5 %collective-permute-start.3 = (f32[88,256]{1,0:T(8,128)S(1)}, f32[88,256]{1,0:T(8,128)S(1)}, u32[]{:S(2)}, u32[]{:S(2)}) collective-permute-start(f32[88,256]{1,0:T(8,128)S(1)} %collective-permute-done.refs_1_.refs_5_), channel_id=1, source_target_pairs={{0,8},{8,0},{16,24},{24,16},{1,9},{9,1},{17,25},{25,17},{2,10},{10... | collective-permute-start | bytes 270344 | tf_op jit(solution)/shard_map/ppermute | solution.py:531
  18.4 0.0 copy-done.5
  18.4 0.0 copy-start.6
  18.4 0.9 %copy-done.6 = f32[88,256]{1,0:T(8,128)S(1)} copy-done((f32[88,256]{1,0:T(8,128)S(1)}, f32[88,256]{1,0:T(8,128)}, u32[]{:S(2)}) %copy-start.6) | copy-done | bytes 90136
  19.3 0.0 copy-start.7
  19.3 0.7 %copy-done.7 = f32[16,128]{1,0:T(8,128)S(1)} copy-done((f32[16,128]{1,0:T(8,128)S(1)}, f32[16,128]{1,0:T(8,128)}, u32[]{:S(2)}) %copy-start.7) | copy-done | bytes 8216
  20.0 0.0 copy-start
  20.0 0.0 copy-start.1
  20.0 0.0 copy-start.3
  20.0 0.0 copy-start.4
  20.0 2.7 %mix.1 = (bf16[256,512]{1,0:T(8,128)(2,1)S(1)}, bf16[256,512]{1,0:T(8,128)(2,1)S(1)}, f32[256,256]{1,0:T(8,128)S(1)}) custom-call(f32[88,256]{1,0:T(8,128)S(1)} %copy-done.6, f32[88,256]{1,0:T(8,128)S(1)} %collective-permute-done.refs_1_.refs_5_, f32[88,256]{1,0:T(8,128)S(1)} %collective-permute-done.1.refs_2_.refs_6_, ...), custom_call_target="tpu_custom_call" | custom-call | flops 1610612736 | bytes 262144 | tf_op jit(solution)/shard_map/mix/pallas_call | solution.py:533
  22.7 0.0 collective-permute-done.5.refs_10_
  22.8 0.0 collective-permute-done.4.refs_9_
  22.8 0.0 collective-permute-done.3.refs_8_
  22.8 0.0 copy-done
  22.8 0.0 copy-done.1
  22.8 0.0 copy-done.3
  22.8 0.0 copy-done.4
  22.8 3.2 %project.1 = (f32[136,128]{1,0:T(8,128)S(1)}, f32[256,128]{1,0:T(8,128)S(1)}, f32[256,128]{1,0:T(8,128)S(1)}, f32[256,128]{1,0:T(8,128)S(1)}, f32[256,128]{1,0:T...) custom-call(bf16[256,512]{1,0:T(8,128)(2,1)S(1)} %get-tuple-element., ...), custom_call_target="tpu_custom_call" | custom-call | tf_op jit(solution)/shard_map/project/pallas_call | solution.py:550
  26.0 0.1 collective-permute-start.6
  26.1 1.2 %collective-permute-done.6.refs_1_ = f32[136,128]{1,0:T(8,128)S(1)} collective-permute-done((f32[136,128]{1,0:T(8,128)S(1)}, f32[136,128]{1,0:T(8,128)S(1)}, u32[]{:S(2)}, u32[]{:S(2)}) %collective-permute-start.6) | collective-permute-done | bytes 69664 | tf_op jit(solution)/shard_map/ppermute | solution.py:584
  27.4 0.6 %collective-permute-start.7 = (f32[136,128]{1,0:T(8,128)S(1)}, f32[136,128]{1,0:T(8,128)S(1)}, u32[]{:S(2)}, u32[]{:S(2)}) collective-permute-start(f32[136,128]{1,0:T(8,128)S(1)} %get-tuple-element.36), channel_id=1, source_target_pairs={{0,16},{8,24},{16,0},{24,8},{1,17},{9,25},{17,1},{25,9},{2,18},{10... | collective-permute-start | bytes 208904 | tf_op jit(solution)/shard_map/ppermute | solution.py:584
  28.0 0.0 copy-start.2
  28.0 0.8 %block.1.refs_3_ = f32[256,128]{1,0:T(8,128)S(1)} custom-call(f32[256,128]{1,0:T(8,128)S(1)} %get-tuple-element.37.read.refs_2_, f32[256,128]{1,0:T(8,128)S(1)} %get-tuple-element.38.write, f32[256,128]{1,0:T(8,128)S(1)} %get-tuple-element.39.inner, f32[256,128]{1,0:T(8,128)S(1)} %get-tuple-element.40.stepped, ...), custom_call_target="tpu_custom_call" | custom-call | flops 805306368 | bytes 262144 | tf_op jit(solution)/shard_map/block/pallas_call | solution.py:571
  28.8 2.9 %collective-permute-done.7.refs_1_ = f32[136,128]{1,0:T(8,128)S(1)} collective-permute-done((f32[136,128]{1,0:T(8,128)S(1)}, f32[136,128]{1,0:T(8,128)S(1)}, u32[]{:S(2)}, u32[]{:S(2)}) %collective-permute-start.7) | collective-permute-done | bytes 69664 | tf_op jit(solution)/shard_map/ppermute | solution.py:584
  31.7 0.0 copy-done.2
  31.7 0.9 %output.1 = (f32[64,256]{1,0:T(8,128)S(1)}, f32[64,256]{1,0:T(8,128)S(1)}, f32[64,256]{1,0:T(8,128)S(1)}, f32[64,256]{1,0:T(8,128)S(1)}) custom-call(f32[136,128]{1,0:T(8,128)S(1)} %get-tuple-element.35.refs_0_, f32[136,128]{1,0:T(8,128)S(1)} %collective-permute-done.7.refs_1_, f32[256,128]{1,0:T(8,128)S(1)} %get-tuple-element.37.read.refs_2_, ...), custom_call_target="tpu_custom_call" | custom-call | tf_op jit(solution)/shard_map/output/pallas_call | solution.py:606
  32.6 0.1 collective-permute-start.8
  32.7 2.1 %collective-permute-start.9 = (f32[64,256]{1,0:T(8,128)S(1)}, f32[64,256]{1,0:T(8,128)S(1)}, u32[]{:S(2)}, u32[]{:S(2)}) collective-permute-start(f32[64,256]{1,0:T(8,128)S(1)} %get-tuple-element.47), channel_id=1, source_target_pairs={{0,4},{2,6},{4,0},{6,2},{1,5},{3,7},{5,1},{7,3},{8,12},{10,14},{12... | collective-permute-start | bytes 196616 | tf_op jit(solution)/shard_map/ppermute | solution.py:622
  34.8 1.8 %collective-permute-start.10 = (f32[64,256]{1,0:T(8,128)S(1)}, f32[64,256]{1,0:T(8,128)S(1)}, u32[]{:S(2)}, u32[]{:S(2)}) collective-permute-start(f32[64,256]{1,0:T(8,128)S(1)} %get-tuple-element.48), channel_id=1, source_target_pairs={{0,6},{2,0},{4,2},{6,4},{1,7},{3,1},{5,3},{7,5},{8,14},{10,8},{12,... | collective-permute-start | bytes 196616 | tf_op jit(solution)/shard_map/ppermute | solution.py:622
  36.6 2.4 %collective-permute-done.8 = f32[64,256]{1,0:T(8,128)S(1)} collective-permute-done((f32[64,256]{1,0:T(8,128)S(1)}, f32[64,256]{1,0:T(8,128)S(1)}, u32[]{:S(2)}, u32[]{:S(2)}) %collective-permute-start.8) | collective-permute-done | bytes 65568 | tf_op jit(solution)/shard_map/ppermute | solution.py:622
  39.0 1.2 %collective-permute-done.9 = f32[64,256]{1,0:T(8,128)S(1)} collective-permute-done((f32[64,256]{1,0:T(8,128)S(1)}, f32[64,256]{1,0:T(8,128)S(1)}, u32[]{:S(2)}, u32[]{:S(2)}) %collective-permute-start.9) | collective-permute-done | bytes 65568 | tf_op jit(solution)/shard_map/ppermute | solution.py:622
  40.2 0.0 collective-permute-done.10
  40.2 0.6 %add_add_fusion = f32[64,256]{1,0:T(8,128)} fusion(f32[64,256]{1,0:T(8,128)S(1)} %collective-permute-done.10, f32[64,256]{1,0:T(8,128)S(1)} %collective-permute-done.9, f32[64,256]{1,0:T(8,128)S(1)} %get-tuple-element.45, f32[64,256]{1,0:T(8,128)S(1)} %collective-permute-done.8), kind=kLoop, calls=%fused_computation | loop fusion | flops 49152 | bytes 327680 | tf_op jit(solution)/shard_map/add | solution.py:622
  (1 shorter events, 0.0 us)
Async XLA Ops:
  0.0 18.4 %copy-start.5 = (f32[16,256]{1,0:T(8,128)S(1)}, f32[16,256]{1,0:T(8,128)}, u32[]{:S(2)}) copy-start(f32[16,256]{1,0:T(8,128)} %refs_4_.1) | copy-start | bytes 49156
  2.5 8.8 %collective-permute-start.2 = (f32[88,256]{1,0:T(8,128)}, f32[88,256]{1,0:T(8,128)S(1)}, u32[]{:S(2)}, u32[]{:S(2)}) collective-permute-start(f32[88,256]{1,0:T(8,128)} %get-tuple-element.27.refs_0_), channel_id=1, source_target_pairs={{0,30},{2,24},{4,26},{6,28},{8,6},{10,0},{12,2},{14,4},{16,14},{18... | collective-permute-start | bytes 270344 | tf_op jit(solution)/shard_map/ppermute | solution.py:529
  8.0 9.9 %collective-permute-start.1 = (f32[88,256]{1,0:T(8,128)}, f32[88,256]{1,0:T(8,128)S(1)}, u32[]{:S(2)}, u32[]{:S(2)}) collective-permute-start(f32[88,256]{1,0:T(8,128)} %get-tuple-element.27.refs_0_), channel_id=1, source_target_pairs={{0,20},{2,22},{4,16},{6,18},{8,28},{10,30},{12,24},{14,26},{16,4},... | collective-permute-start | bytes 270344 | tf_op jit(solution)/shard_map/ppermute | solution.py:529
  8.0 9.9 %collective-permute-start = (f32[88,256]{1,0:T(8,128)}, f32[88,256]{1,0:T(8,128)S(1)}, u32[]{:S(2)}, u32[]{:S(2)}) collective-permute-start(f32[88,256]{1,0:T(8,128)} %get-tuple-element.27.refs_0_), channel_id=1, source_target_pairs={{0,10},{2,12},{4,14},{6,8},{8,18},{10,20},{12,22},{14,16},{16,26},... | collective-permute-start | bytes 270344 | tf_op jit(solution)/shard_map/ppermute | solution.py:529
  11.3 11.4 %collective-permute-start.5 = (f32[88,256]{1,0:T(8,128)S(1)}, f32[88,256]{1,0:T(8,128)S(1)}, u32[]{:S(2)}, u32[]{:S(2)}) collective-permute-start(f32[88,256]{1,0:T(8,128)S(1)} %collective-permute-done.2.refs_3_.refs_7_), channel_id=1, source_target_pairs={{0,8},{8,0},{16,24},{24,16},{1,9},{9,1},{17,25},{25,17},{2,10},{10... | collective-permute-start | bytes 270344 | tf_op jit(solution)/shard_map/ppermute | solution.py:531
  17.9 4.9 %collective-permute-start.4 = (f32[88,256]{1,0:T(8,128)S(1)}, f32[88,256]{1,0:T(8,128)S(1)}, u32[]{:S(2)}, u32[]{:S(2)}) collective-permute-start(f32[88,256]{1,0:T(8,128)S(1)} %collective-permute-done.1.refs_2_.refs_6_), channel_id=1, source_target_pairs={{0,8},{8,0},{16,24},{24,16},{1,9},{9,1},{17,25},{25,17},{2,10},{10... | collective-permute-start | bytes 270344 | tf_op jit(solution)/shard_map/ppermute | solution.py:531
  17.9 4.9 %collective-permute-start.3 = (f32[88,256]{1,0:T(8,128)S(1)}, f32[88,256]{1,0:T(8,128)S(1)}, u32[]{:S(2)}, u32[]{:S(2)}) collective-permute-start(f32[88,256]{1,0:T(8,128)S(1)} %collective-permute-done.refs_1_.refs_5_), channel_id=1, source_target_pairs={{0,8},{8,0},{16,24},{24,16},{1,9},{9,1},{17,25},{25,17},{2,10},{10... | collective-permute-start | bytes 270344 | tf_op jit(solution)/shard_map/ppermute | solution.py:531
  18.4 0.9 %copy-start.6 = (f32[88,256]{1,0:T(8,128)S(1)}, f32[88,256]{1,0:T(8,128)}, u32[]{:S(2)}) copy-start(f32[88,256]{1,0:T(8,128)} %get-tuple-element.27.refs_0_) | copy-start | bytes 270340
  19.3 0.7 %copy-start.7 = (f32[16,128]{1,0:T(8,128)S(1)}, f32[16,128]{1,0:T(8,128)}, u32[]{:S(2)}) copy-start(f32[16,128]{1,0:T(8,128)} %get-tuple-element.28.refs_5_) | copy-start | bytes 24580
  20.0 2.8 %copy-start = (f32[256,2,128]{2,1,0:T(2,128)S(1)}, f32[256,2,128]{2,1,0:T(2,128)}, u32[]{:S(2)}) copy-start(f32[256,2,128]{2,1,0:T(2,128)} %param.34) | copy-start | bytes 786436
  20.0 2.8 %copy-start.1 = (f32[256,2,128]{2,1,0:T(2,128)S(1)}, f32[256,2,128]{2,1,0:T(2,128)}, u32[]{:S(2)}) copy-start(f32[256,2,128]{2,1,0:T(2,128)} %param.35) | copy-start | bytes 786436
  20.0 2.8 %copy-start.3 = (f32[128,256]{1,0:T(8,128)S(1)}, f32[128,256]{1,0:T(8,128)}, u32[]{:S(2)}) copy-start(f32[128,256]{1,0:T(8,128)} %get-tuple-element.33.refs_4_) | copy-start | bytes 393220
  20.0 2.8 %copy-start.4 = (f32[16,256]{1,0:T(8,128)S(1)}, f32[16,256]{1,0:T(8,128)}, u32[]{:S(2)}) copy-start(f32[16,256]{1,0:T(8,128)} %get-tuple-element.32.refs_3_.small.refs_7_) | copy-start | bytes 49156
  26.0 1.3 %collective-permute-start.6 = (f32[136,128]{1,0:T(8,128)S(1)}, f32[136,128]{1,0:T(8,128)S(1)}, u32[]{:S(2)}, u32[]{:S(2)}) collective-permute-start(f32[136,128]{1,0:T(8,128)S(1)} %get-tuple-element.34.refs_0_), channel_id=1, source_target_pairs={{0,8},{8,0},{16,24},{24,16},{1,9},{9,1},{17,25},{25,17},{2,10},{10... | collective-permute-start | bytes 208904 | tf_op jit(solution)/shard_map/ppermute | solution.py:584
  27.4 4.4 %collective-permute-start.7 = (f32[136,128]{1,0:T(8,128)S(1)}, f32[136,128]{1,0:T(8,128)S(1)}, u32[]{:S(2)}, u32[]{:S(2)}) collective-permute-start(f32[136,128]{1,0:T(8,128)S(1)} %get-tuple-element.36), channel_id=1, source_target_pairs={{0,16},{8,24},{16,0},{24,8},{1,17},{9,25},{17,1},{25,9},{2,18},{10... | collective-permute-start | bytes 208904 | tf_op jit(solution)/shard_map/ppermute | solution.py:584
  28.0 3.8 %copy-start.2 = (f32[128,256]{1,0:T(8,128)S(1)}, f32[128,256]{1,0:T(8,128)}, u32[]{:S(2)}) copy-start(f32[128,256]{1,0:T(8,128)} %refs_8_.1) | copy-start | bytes 393220
  32.6 6.4 %collective-permute-start.8 = (f32[64,256]{1,0:T(8,128)S(1)}, f32[64,256]{1,0:T(8,128)S(1)}, u32[]{:S(2)}, u32[]{:S(2)}) collective-permute-start(f32[64,256]{1,0:T(8,128)S(1)} %get-tuple-element.46), channel_id=1, source_target_pairs={{0,2},{2,4},{4,6},{6,0},{1,3},{3,5},{5,7},{7,1},{8,10},{10,12},{12... | collective-permute-start | bytes 196616 | tf_op jit(solution)/shard_map/ppermute | solution.py:622
  32.7 7.5 %collective-permute-start.9 = (f32[64,256]{1,0:T(8,128)S(1)}, f32[64,256]{1,0:T(8,128)S(1)}, u32[]{:S(2)}, u32[]{:S(2)}) collective-permute-start(f32[64,256]{1,0:T(8,128)S(1)} %get-tuple-element.47), channel_id=1, source_target_pairs={{0,4},{2,6},{4,0},{6,2},{1,5},{3,7},{5,1},{7,3},{8,12},{10,14},{12... | collective-permute-start | bytes 196616 | tf_op jit(solution)/shard_map/ppermute | solution.py:622
  34.8 5.4 %collective-permute-start.10 = (f32[64,256]{1,0:T(8,128)S(1)}, f32[64,256]{1,0:T(8,128)S(1)}, u32[]{:S(2)}, u32[]{:S(2)}) collective-permute-start(f32[64,256]{1,0:T(8,128)S(1)} %get-tuple-element.48), channel_id=1, source_target_pairs={{0,6},{2,0},{4,2},{6,4},{1,7},{3,1},{5,3},{7,5},{8,14},{10,8},{12,... | collective-permute-start | bytes 196616 | tf_op jit(solution)/shard_map/ppermute | solution.py:622

commit v3 on v2

--- a/solution.py
+++ b/solution.py
@@ -11,6 +11,7 @@
 f32 = jnp.float32
 bf16 = jnp.bfloat16
 LIMIT = 48 * 1024 * 1024
+TABLES_LIMIT = 60 * 1000 * 1000
 
 MM = (((1,), (0,)), ((), ()))
 NT = (((1,), (1,)), ((), ()))
@@ -77,35 +78,39 @@
     return copies
 
 
+def fetch(sources, places, semaphores):
+    copies = []
+    for number, (source, place) in enumerate(zip(sources, places)):
+        copies.append(pltpu.make_async_copy(source, place, semaphores.at[number]))
+        copies[-1].start()
+    return copies
+
+
 def tables_kernel(dims, *refs):
     V, D, hl, ch, nh, ns, T, N = dims
-    H, LV = nh * hl, nh * hl * V
     refs = list(refs)
 
     def take(number):
         taken, refs[:] = refs[:number], refs[number:]
         return taken
 
-    sources = take(17)
-    outproj_source = take(1)[0]
-    message, pairs, small, outproj = take(4)
-    places = take(17)
+    sources = take(9)
+    outproj_source, message = take(2)
+    places = take(9)
     semaphores = take(1)[0]
     half = ch // 2
     base = V + 2 + 3 * hl
     core = lax.rem(lax.axis_index("seq"), 2)
     copies = fetch(
-        sources + [outproj_source],
-        places + [outproj],
+        sources + [outproj_source.at[pl.ds(pl.multiple_of(core * half, 8), half), :]],
+        places + [message.at[base : base + half, 0:D]],
         semaphores,
     )
-    for copy in copies:
+    for copy in copies[:9]:
         copy.wait()
-    message[base : base + half, 0:D] = outproj[pl.ds(pl.multiple_of(core * half, 8), half), :]
-    (tok, emb, prenorm, inproj, statemap, stepmap, bias, rates, skip, outnorm) = places[:10]
-    (complement, prenorm2, stepmap2, bias2, rates2, skip2, outnorm2) = places[10:]
-
+    (inproj, tok, emb, prenorm, stepmap, bias, rates, skip, outnorm) = places
     normed = split2(rms(emb[...]) * prenorm[...])
+    raw_t = dot_split(split2(stepmap[...]), normed, NT)
     gate = dot_split(normed, split2(inproj[pl.ds(0, D, stride=2), :]))
     inner = dot_split(normed, split2(inproj[pl.ds(1, D, stride=2), :]))
     message[0:V, 0:ch] = gate
@@ -114,7 +119,6 @@
     tokens = jnp.broadcast_to(tok[...].astype(f32), (8, T)).astype(bf16)
     message[V : V + 1, 0:T] = dot(tokens, flip)[0:1]
     message[V + 1 : V + 2, 0:ch] = outnorm[...]
-    raw_t = dot_split(split2(stepmap[...]), normed, NT)
     for head in range(hl):
         line = softplus(raw_t[head : head + 1, :] + bias[:, head : head + 1])
         row = V + 2 + head
@@ -123,20 +127,65 @@
         message[row + 2 * hl : row + 2 * hl + 1, 0:V] = jnp.broadcast_to(
             skip[:, head : head + 1], (1, V)
         )
-
+    copies[9].wait()
+
+
+def prepare_kernel(dims, *refs):
+    V, D, hl, ch, nh, ns, T, N = dims
+    H, P = nh * hl, ch // hl
+    refs = list(refs)
+
+    def take(number):
+        taken, refs[:] = refs[:number], refs[number:]
+        return taken
+
+    emb, prenorm, statemap, complement, outproj = take(5)
+    prenorm2, inproj2, statemap2, stepmap2, bias2, rates2, skip2, outnorm2, outproj2 = take(9)
+    pairs, small, choose_out, own_high, own_low = take(5)
+    state_high, state_low, rest_high, rest_low, out_high, out_low = take(6)
+    normed = split2(rms(emb[...]) * prenorm[...])
     write = dot_split(normed, split2(statemap[pl.ds(0, D, stride=2), :]))
     read = dot_split(normed, split2(statemap[pl.ds(1, D, stride=2), :]))
     pairs[...] = dot3(read, jnp.concatenate([write] * H, axis=0), NT)
-    small[0:1, 0:D] = complement[...].astype(f32)
-    small[1:2, 0:D] = prenorm2[...]
-    small[2:3, 0:ch] = outnorm2[...]
-    small[8 : 8 + hl, 0:D] = stepmap2[...]
-    for place, ref in ((3, bias2), (4, rates2), (5, skip2)):
-        small[place : place + 1, 0:hl] = ref[...]
+    own_high[...], own_low[...] = split2(outproj[...])
+    choose = (complement[...] == iota((D, D), 0)).astype(f32).astype(bf16)
+    choose_out[...] = choose
+    gain = jnp.transpose(jnp.broadcast_to(prenorm2[...], (128, D)))
+
+    def weights(values):
+        return split2(dot_left_exact(choose, values))
+
+    gain_wide = gain[:, 0:1]
+    inner = inproj2[pl.ds(1, D, stride=2), :] * gain_wide
+    step = jnp.transpose(
+        jnp.concatenate(
+            [jnp.broadcast_to(stepmap2[head : head + 1, :], (P, D)) for head in range(hl)], axis=0
+        )
+    )
+    write2 = statemap2[pl.ds(0, D, stride=2), :] * gain_wide
+    state_high[...], state_low[...] = weights(
+        jnp.concatenate([inner, step * gain_wide, write2], axis=1)
+    )
+    gate = inproj2[pl.ds(0, D, stride=2), :] * gain_wide
+    read2 = statemap2[pl.ds(1, D, stride=2), :] * gain_wide
+    rest_high[...], rest_low[...] = weights(jnp.concatenate([gate, read2], axis=1))
+    out_gain = jnp.transpose(jnp.broadcast_to(outnorm2[...], (128, ch)))
+    out_high[...], out_low[...] = split2(outproj2[...] * out_gain[:, 0:1])
+    lane_head = iota((1, ch), 1) // P
+    for place, ref in ((0, bias2), (1, rates2), (2, skip2)):
+        line = jnp.zeros((1, ch), f32)
+        for head in range(hl):
+            line = jnp.where(lane_head == head, ref[head], line)
+        small[place : place + 1, :] = line
 
 
 def shift_rows(value, amount, fill):
     size = value.shape[0]
+    if amount % 8 == 0:
+        empty = jnp.full((abs(amount),) + value.shape[1:], fill, value.dtype)
+        if amount > 0:
+            return jnp.concatenate([empty, value[: size - amount]], axis=0)
+        return jnp.concatenate([value[-amount:], empty], axis=0)
     rolled = pltpu.roll(value, amount % size, 0)
     row = iota(value.shape, 0)
     have = (row >= amount) if amount > 0 else (row < size + amount)
@@ -257,17 +306,23 @@
     tiled = jnp.concatenate([inners] * H, axis=0)
     spread = jnp.where(iota((LV, C), 0) // V == iota((LV, C), 1) // P, tiled, 0.0)
     spread_high, spread_low = split2(spread)
-    group = (iota((C, C), 0) // P == iota((C, C), 1) // P).astype(f32).astype(bf16)
-
-    def gated(coefficients):
-        high, low = split2(coefficients * pair + gain)
-        value = dot(high, spread_low) + dot(low, spread_high) + dot(high, spread_high)
-        value = value * silu_rows
-        high, low = split2(value * value)
-        square = dot(low, group) + dot(high, group)
-        return value * lax.rsqrt(square * (1.0 / P) + epsilon)
-
-    out_high[...], out_low[...] = split2((gated(up) + gated(down)) * gains)
+    both = jnp.concatenate([up * pair + gain, down * pair + gain], axis=0)
+    high, low = split2(both)
+    value = dot(high, spread_low) + dot(
+        jnp.concatenate([low, high], axis=1),
+        jnp.concatenate([spread_high, spread_high], axis=0),
+    )
+    value = value * jnp.concatenate([silu_rows, silu_rows], axis=0)
+    wide = max(ch, 256)
+    group = (iota((wide, wide), 0) // P == iota((wide, wide), 1) // P).astype(f32).astype(bf16)
+    high, low = split2(value * value)
+    for start in range(0, C, wide):
+        stop = start + wide
+        square = dot(low[:, start:stop], group) + dot(high[:, start:stop], group)
+        normed = value[:, start:stop] * lax.rsqrt(square * (1.0 / P) + epsilon)
+        out_high[:, start:stop], out_low[:, start:stop] = split2(
+            (normed[0:T] + normed[T : 2 * T]) * gains[:, start:stop]
+        )
 
 
 def project_kernel(dims, *refs):
@@ -279,91 +334,90 @@
         taken, refs[:] = refs[:number], refs[number:]
         return taken
 
-    high, low, embedded, small, outproj = take(5)
+    high, low, embedded, small, own_high, own_low, state_high, state_low = take(8)
     nears = take(nh - 1)
     others = take(nh - 1)
-    sources = take(2)
-    out_state, out_read, out_write, out_inner, out_stepped, out_gate = take(6)
-    out_total, out_total_t, out_own = take(3)
-    places = take(2)
-    mirrored_ref, semaphores = take(2)
-    copies = fetch(sources, places, semaphores)
-    inproj2, statemap2 = places
+    out_state, out_high, out_low, out_scale = take(4)
+    out_write, out_inner, out_stepped, out_total = take(4)
     half = ch // 2
     base = V + 2 + 3 * hl
     mine = lax.axis_index("seq")
 
-    hidden = embedded[...]
+    pieces = []
     for k in range(1, nh):
         near = nears[k - 1][base : base + half, 0:D]
         other = others[k - 1][base : base + half, 0:D]
         even = lax.rem(mine - k + ns * nh, 2) == 0
-        weights = jnp.concatenate(
-            [jnp.where(even, near, other), jnp.where(even, other, near)], axis=0
-        )
-        part = (high[:, k * ch : (k + 1) * ch], low[:, k * ch : (k + 1) * ch])
-        hidden = hidden + dot_split(part, split2(weights))
-    hidden = hidden + dot_split((high[:, 0:ch], low[:, 0:ch]), split2(outproj[...]))
-    choose = (small[0:1, 0:D] == iota((D, D), 0).astype(f32)).astype(f32).astype(bf16)
-    mirrored = dot_right_exact(hidden, choose)
-    mirrored_ref[...] = mirrored
-    share = T // nh
-    out_own[...] = mirrored_ref[pl.ds(pl.multiple_of(lax.axis_index("head") * share, 8), share), :]
-
-    normed = split2(rms(mirrored) * small[1:2, 0:D])
-    copies[0].wait()
-    gate = dot_split(normed, split2(inproj2[pl.ds(0, D, stride=2), :]))
-    inner = dot_split(normed, split2(inproj2[pl.ds(1, D, stride=2), :]))
-    copies[1].wait()
-    write = dot_split(normed, split2(statemap2[pl.ds(0, D, stride=2), :]))
-    out_read[...] = dot_split(normed, split2(statemap2[pl.ds(1, D, stride=2), :]))
-    out_write[...] = write
-    out_inner[...] = inner
-    out_gate[...] = silu(gate)
-    steps = split2(small[8 : 8 + hl, 0:D])
-    raw = dot_split(normed, steps, NT)
-    raw_t = dot_split(steps, normed, NT)
-    of_head = iota((T, ch), 1) // P
-    step = jnp.zeros((T, ch), f32)
-    log = jnp.zeros((T, ch), f32)
-    logs = []
-    for head in range(hl):
-        bias2, rates2 = small[3:4, head : head + 1], small[4:5, head : head + 1]
-        column = softplus(raw[:, head : head + 1] + bias2)
-        here = of_head == head
-        step = jnp.where(here, column, step)
-        log = jnp.where(here, -rates2 * column, log)
-        logs.append(-rates2 * softplus(raw_t[head : head + 1, :] + bias2))
-    first, second = iota((T, T), 0), iota((T, T), 1)
-    total = dot_left_exact((first >= second).astype(f32).astype(bf16), log)
-    logs = jnp.concatenate(logs, axis=0)
-    out_total_t[0:hl, :] = dot_right_exact(logs, (first <= second).astype(f32).astype(bf16))
-    out_total[...] = total
+        pieces.append(jnp.where(even, near, other))
+        pieces.append(jnp.where(even, other, near))
+    weights = split2(jnp.concatenate(pieces, axis=0))
+    weights = (
+        jnp.concatenate([own_high[...], weights[0]], axis=0),
+        jnp.concatenate([own_low[...], weights[1]], axis=0),
+    )
+    hidden = embedded[...] + dot_split((high[...], low[...]), weights)
+    split = split2(hidden)
+    out_high[...], out_low[...] = split
+    scale = lax.rsqrt(jnp.mean(hidden * hidden, axis=-1, keepdims=True) + epsilon)
+    out_scale[...] = jnp.broadcast_to(scale, (T, ch))
+
+    rows = dot_split(split, (state_high[...], state_low[...])) * scale
+    inner, write = rows[:, 0:ch], rows[:, 2 * ch :]
+    step = softplus(rows[:, ch : 2 * ch] + small[0:1, :])
+    stepped = inner * step
+    upto = (iota((T, T), 0) >= iota((T, T), 1)).astype(f32).astype(bf16)
+    total = dot_left_exact(upto, -small[1:2, :] * step)
     end = total[T - 1 : T, :]
-    stepped = inner * step
-    out_stepped[...] = stepped
     state = dot3(stepped * jnp.exp(end - total), write, TN)
     out_state[0:ch, :] = state
     for head in range(hl):
         out_state[ch + head : ch + head + 1, :] = jnp.broadcast_to(
             end[:, head * P : head * P + 1], (1, N)
         )
-
-
-def block_kernel(dims, read, write, inner, stepped, total, total_t, small, base):
+    out_write[...] = write
+    out_inner[...] = inner
+    out_stepped[...] = stepped
+    out_total[...] = total
+
+
+def block_kernel(dims, *refs):
     V, D, hl, ch, nh, ns, T, N = dims
     P = ch // hl
-    products = dot3(read[...], write[...], NT)
+    refs = list(refs)
+
+    def take(number):
+        taken, refs[:] = refs[:number], refs[number:]
+        return taken
+
+    high, low, scale, write, inner, stepped, total, small, choose = take(9)
+    rest_high, rest_low = take(2)
+    base, out_read, out_gate, own, hidden_ref = take(5)
+    rows = dot_split((high[...], low[...]), (rest_high[...], rest_low[...]))
+    out_gate[...] = silu(rows[:, 0:ch] * scale[...])
+    read = rows[:, ch:] * scale[...]
+    out_read[...] = read
+    products = dot3(read, write[...], NT)
     stepped_high, stepped_low = split2(stepped[...])
+    select = (iota((8, ch), 1) == iota((8, ch), 0) * P).astype(f32).astype(bf16)
+    total_high, total_middle, total_low = split3(total[...])
+    total_t = (dot(select, total_low, NT) + dot(select, total_middle, NT)) + dot(
+        select, total_high, NT
+    )
     allowed = iota((T, T), 0) >= iota((T, T), 1)
     parts = []
     for head in range(hl):
-        low, high = head * P, (head + 1) * P
-        differ = total[:, low : low + 1] - total_t[head : head + 1, :]
+        start, stop = head * P, (head + 1) * P
+        differ = total[:, start : start + 1] - total_t[head : head + 1, :]
         weights = jnp.where(allowed, jnp.exp(jnp.where(allowed, differ, 0.0)), 0.0) * products
-        part = dot_split(split2(weights), (stepped_high[:, low:high], stepped_low[:, low:high]))
-        parts.append(part + small[5:6, head : head + 1] * inner[:, low:high])
+        part = dot_split(
+            split2(weights), (stepped_high[:, start:stop], stepped_low[:, start:stop])
+        )
+        parts.append(part + small[2:3, start:stop] * inner[:, start:stop])
     base[...] = jnp.concatenate(parts, axis=1)
+    share = T // nh
+    hidden_ref[...] = high[...].astype(f32) + low[...].astype(f32)
+    place = pl.multiple_of(lax.axis_index("head") * share, 8)
+    own[...] = dot_right_exact(hidden_ref[pl.ds(place, share), :], choose[...])
 
 
 def state_rows(dims, values):
@@ -404,31 +458,18 @@
 def output_kernel(dims, bit, *refs):
     V, D, hl, ch, nh, ns, T, N = dims
     P = ch // hl
-    refs = list(refs)
-
-    def take(number):
-        taken, refs[:] = refs[:number], refs[number:]
-        return taken
-
-    prefix, came, read, base, total, gate, own, small, outproj_source = take(9)
-    outs = take(nh)
-    partial_ref, outproj, semaphore = take(3)
-    copy = pltpu.make_async_copy(outproj_source, outproj, semaphore.at[0])
-    copy.start()
+    prefix, came, read, base, total, gate, own, proj_high, proj_low, out = refs
     entering = prefix_joined(dims, bit, prefix, came)
     value = (base[...] + dot3(read[...], entering, NT) * jnp.exp(total[...])) * gate[...]
     group = (iota((ch, ch), 0) // P == iota((ch, ch), 1) // P).astype(f32).astype(bf16)
     high, low = split2(value * value)
     square = dot(low, group) + dot(high, group)
-    value = value * lax.rsqrt(square * (1.0 / P) + epsilon) * small[2:3, 0:ch]
-    copy.wait()
-    partial_ref[...] = dot3(value, outproj[...])
+    value = value * lax.rsqrt(square * (1.0 / P) + epsilon)
     share = T // nh
+    partial = dot_split(split2(value), (proj_high[...], proj_low[...]))
+    out[...] = partial.reshape(nh, share, D)
     mine = lax.axis_index("head")
-    for k in range(nh):
-        place = pl.multiple_of(lax.rem(mine + k, nh) * share, 8)
-        part = partial_ref[pl.ds(place, share), :]
-        outs[k][...] = part + own[...] if k == 0 else part
+    out[pl.ds(mine, 1)] = out[pl.ds(mine, 1)] + own[...].reshape(1, share, D)
 
 
 def per_device(
@@ -463,11 +504,15 @@
     LV = nh * hl * V
     dims = (V, D, hl, ch, nh, ns, T, N)
     vmem = pl.BlockSpec(memory_space=pltpu.VMEM)
+    smem = pl.BlockSpec(memory_space=pltpu.SMEM)
     anywhere = pl.BlockSpec(memory_space=pl.ANY)
     params = pltpu.CompilerParams(vmem_limit_bytes=LIMIT)
 
     def shape(*sizes, dtype=f32):
         return jax.ShapeDtypeStruct(sizes, dtype)
+
+    def halves(*sizes):
+        return [shape(*sizes, dtype=bf16)] * 2
 
     def room(value):
         return pltpu.VMEM(value.shape, value.dtype)
@@ -484,39 +529,74 @@
     head_rows = V + 2 + 3 * hl
     half = ch // 2
     width = max(2 * ch, T, D)
+    share = T // nh
     fetched = [
+        flat(inproj_first),
         line(token_ids),
         embedding,
         line(prenorm_first),
-        flat(inproj_first),
-        flat(statemap_first),
         stepmap_first.T,
         line(stepbias_first),
         line(rates_first),
         line(skipgain_first),
         line(outnorm_first),
-        line(complement),
-        line(prenorm_second),
-        stepmap_second.T,
-        line(stepbias_second),
-        line(rates_second),
-        line(skipgain_second),
-        line(outnorm_second),
     ]
-    message, pair_table, small, own_projection = pl.pallas_call(
+    message = pl.pallas_call(
         functools.partial(tables_kernel, dims),
-        out_shape=(
-            shape(head_rows + half, width),
-            shape(V, LV),
-            shape(16, D),
-            shape(ch, D),
-        ),
+        out_shape=shape(head_rows + half, width),
         in_specs=[anywhere] * (len(fetched) + 1),
-        out_specs=(vmem,) * 4,
+        out_specs=vmem,
         scratch_shapes=[room(value) for value in fetched]
         + [pltpu.SemaphoreType.DMA((len(fetched) + 1,))],
+        compiler_params=pltpu.CompilerParams(vmem_limit_bytes=TABLES_LIMIT),
         name="tables",
     )(*fetched, outproj_first)
+
+    prepared = [
+        embedding,
+        line(prenorm_first),
+        flat(statemap_first),
+        line(complement),
+        outproj_first,
+        line(prenorm_second),
+        flat(inproj_second),
+        flat(statemap_second),
+        stepmap_second.T,
+        stepbias_second,
+        rates_second,
+        skipgain_second,
+        line(outnorm_second),
+        outproj_second,
+    ]
+    (
+        pair_table,
+        small,
+        choose,
+        own_high,
+        own_low,
+        state_high,
+        state_low,
+        rest_high,
+        rest_low,
+        proj_high,
+        proj_low,
+    ) = pl.pallas_call(
+        functools.partial(prepare_kernel, dims),
+        out_shape=(
+            shape(V, LV),
+            shape(8, ch),
+            shape(D, D, dtype=bf16),
+            *halves(ch, D),
+            *halves(D, 2 * ch + N),
+            *halves(D, ch + N),
+            *halves(ch, D),
+        ),
+        in_specs=[vmem] * 9 + [smem] * 3 + [vmem] * 2,
+        out_specs=(vmem,) * 11,
+        compiler_params=params,
+        cost_estimate=cost(6 * T * D * D * 4),
+        name="prepare",
+    )(*prepared)
 
     messages = [message]
     for k in range(1, max(ns, nh)):
@@ -525,18 +605,14 @@
             for seq in range(ns)
             for head in range(nh)
         ]
-        sent = message if k < nh else message[0 : V + 8]
+        sent = message if k < nh else message[0:head_rows]
         messages.append(lax.ppermute(sent, ("seq", "head"), pairs))
     swap = [(seq, seq ^ 1) for seq in range(ns)]
     others = [lax.ppermute(messages[k], "seq", swap) for k in range(1, nh)]
 
     mixed_high, mixed_low, embedded = pl.pallas_call(
         functools.partial(mix_kernel, dims),
-        out_shape=(
-            shape(T, nh * ch, dtype=bf16),
-            shape(T, nh * ch, dtype=bf16),
-            shape(T, D),
-        ),
+        out_shape=(*halves(T, nh * ch), shape(T, D)),
         in_specs=[vmem] * (len(messages) + 2),
         out_specs=(vmem,) * 3,
         scratch_shapes=[pltpu.VMEM((max(ns, 8), T), f32)],
@@ -545,38 +621,56 @@
         name="mix",
     )(*messages, embedding, pair_table)
 
-    fetched = [flat(inproj_second), flat(statemap_second)]
-    share = T // nh
-    state, read, write, inner, stepped, gate, total, total_t, own = pl.pallas_call(
+    state, hidden_high, hidden_low, scale, write, inner, stepped, total = pl.pallas_call(
         functools.partial(project_kernel, dims),
         out_shape=(
             shape(ch + 8, N),
-            shape(T, N),
+            *halves(T, D),
+            shape(T, ch),
             shape(T, N),
             shape(T, ch),
             shape(T, ch),
             shape(T, ch),
-            shape(T, ch),
-            shape(8, T),
-            shape(share, D),
         ),
-        in_specs=[vmem] * (5 + 2 * (nh - 1)) + [anywhere] * len(fetched),
-        out_specs=(vmem,) * 9,
-        scratch_shapes=[room(value) for value in fetched]
-        + [pltpu.VMEM((T, D), f32), pltpu.SemaphoreType.DMA((len(fetched),))],
+        in_specs=[vmem] * (8 + 2 * (nh - 1)),
+        out_specs=(vmem,) * 8,
         compiler_params=params,
         name="project",
-    )(mixed_high, mixed_low, embedded, small, own_projection, *messages[1:nh], *others, *fetched)
-
-    base = pl.pallas_call(
+    )(
+        mixed_high,
+        mixed_low,
+        embedded,
+        small,
+        own_high,
+        own_low,
+        state_high,
+        state_low,
+        *messages[1:nh],
+        *others,
+    )
+
+    base, read, gate, own = pl.pallas_call(
         functools.partial(block_kernel, dims),
-        out_shape=shape(T, ch),
-        in_specs=[vmem] * 7,
-        out_specs=vmem,
+        out_shape=(shape(T, ch), shape(T, N), shape(T, ch), shape(share, D)),
+        in_specs=[vmem] * 11,
+        out_specs=(vmem,) * 4,
+        scratch_shapes=[pltpu.VMEM((T, D), f32)],
         compiler_params=params,
         cost_estimate=cost(6 * T * D * D * 8),
         name="block",
-    )(read, write, inner, stepped, total, total_t, small)
+    )(
+        hidden_high,
+        hidden_low,
+        scale,
+        write,
+        inner,
+        stepped,
+        total,
+        small,
+        choose,
+        rest_high,
+        rest_low,
+    )
 
     prefix = None
     bits = ns.bit_length() - 1
@@ -605,22 +699,14 @@
 
     parts = pl.pallas_call(
         functools.partial(output_kernel, dims, bits - 1),
-        out_shape=(shape(share, D),) * nh,
-        in_specs=[vmem] * 8 + [anywhere],
-        out_specs=(vmem,) * nh,
-        scratch_shapes=[
-            pltpu.VMEM((T, D), f32),
-            room(outproj_second),
-            pltpu.SemaphoreType.DMA((1,)),
-        ],
+        out_shape=shape(nh, share, D),
+        in_specs=[vmem] * 9,
+        out_specs=vmem,
         compiler_params=params,
         name="output",
-    )(prefix, came, read, base, total, gate, own, small, outproj_second)
-    result = parts[0]
-    for k in range(1, nh):
-        pairs = [(source, (source + k) % nh) for source in range(nh)]
-        result = result + lax.ppermute(parts[k], "head", pairs)
-    return result
+    )(prefix, came, read, base, total, gate, own, proj_high, proj_low)
+    parts = lax.all_to_all(parts, "head", 0, 0, tiled=True)
+    return jnp.sum(parts, axis=0)
 
 
 def solution(mesh):

time: 41.1 us -> 39.4 us (0.959)
  blocking collectives: 0 us -> 10.7 us
  waiting for transfers between devices: 16.7 us -> 6.75 us
  starting transfers between devices: 11.7 us -> 8.76 us
  local copies, waits for them, and re-layouts: 1.61 us -> 3.52 us
  Pallas kernels: 10.2 us -> 8.6 us
    all_to_all x0 -> x1, blocking collectives: none -> 10.7 us  [per_device(): parts = lax.all_to_all(parts, 'head', 0, 0, tiled=True)]
    ppermute x3, waiting for transfers between devices: 8.89 us -> 2.91 us  [per_device(): messages.append(lax.ppermute(sent, ('seq', 'head'), pairs))]
    ppermute x3 -> x0, starting transfers between devices: 3.97 us -> none  [per_device(): result = result + lax.ppermute(parts[k], 'head', pairs)]
    ppermute x3 -> x0, waiting for transfers between devices: 3.62 us -> none  [per_device(): result = result + lax.ppermute(parts[k], 'head', pairs)]
    unnamed x16 -> x30, local copies, waits for them, and re-layouts: 1.61 us -> 3.52 us
    pallas_call x1, Pallas kernels: 3.17 us -> 1.52 us  [per_device(): pl.pallas_call(functools.partial(project_kernel, dims), out_shape=(shape(...]
    ppermute x3, starting transfers between devices: 0.51 us -> 1.59 us  [per_device(): others = [lax.ppermute(messages[k], 'seq', swap) for k in range(1, nh)]]
    add x1 -> x0, other arithmetic: 0.65 us -> none  [per_device(): result = result + lax.ppermute(parts[k], 'head', pairs)]
  transfers between devices with their start and end apart: 11 -> 8, of which waited for: 6 -> 3; matrix products, arithmetic and copies ran while one was open for 0% -> 0% of each run, Pallas kernels for 9% -> 11%
where the time goes in v3:
time: 39.4 us; the launch traced here: 39.1 us
  blocking collectives  10.7 us (27%)
  starting transfers between devices  8.76 us (22%)
  Pallas kernels  8.6 us (22%)
  waiting for transfers between devices  6.75 us (17%)
  local copies, waits for them, and re-layouts  3.52 us (9%)
  other arithmetic  0.65 us (2%)
    all_to_all x1, blocking collectives, per_device(): parts = lax.all_to_all(parts, 'head', 0, 0, tiled=True)  10.7 us
    ppermute x3, starting transfers between devices, per_device(): messages.append(lax.ppermute(sent, ('seq', 'head'), pairs))  6.49 us
    ppermute x2, waiting for transfers between devices, per_device(): lax.ppermute(state, 'seq', [(seq, seq ^ 2 ** bit) for seq in range(ns)])  3.83 us
    unnamed x30, local copies, waits for them, and re-layouts  3.52 us
    ppermute x3, waiting for transfers between devices, per_device(): messages.append(lax.ppermute(sent, ('seq', 'head'), pairs))  2.91 us
    pallas_call x1, Pallas kernels, per_device(): pl.pallas_call(functools.partial(tables_kernel, dims), out_shape=shape(he...  2.04 us
    pallas_call x1, Pallas kernels, per_device(): pl.pallas_call(functools.partial(mix_kernel, dims), out_shape=(*halves(T,...  1.85 us
    ppermute x3, starting transfers between devices, per_device(): others = [lax.ppermute(messages[k], 'seq', swap) for k in range(1, nh)]  1.59 us
  transfers between devices with their start and end apart: 8, of which 3 were waited for; matrix products, arithmetic and copies ran while one was open for 0% of the time, Pallas kernels for 11%

profile of v3, /device:TPU:0, one launch (start us, length us, event | category | flops | bytes accessed | tf_op | source)
XLA Modules:
  0.0 39.1 jit_solution(9885229931466012404)
XLA Ops:
  0.0 0.0 copy-start.4
  0.0 0.0 copy-start
  0.0 0.0 copy-start.2
  0.0 2.0 %tables.1.refs_0_ = f32[88,256]{1,0:T(8,128)} custom-call(f32[512,128]{1,0:T(8,128)} %bitcast.24, s32[1,256]{1,0:T(1,128)} %bitcast.26, f32[16,256]{1,0:T(8,128)} %refs_4_.3, f32[1,256]{1,0:T(1,128)} %bitcast.15, f32[2,256]{1,0:T(2,128)} %bitcast.25, f32[1,2]{1,0:T(1,128)} %bitcast.27, f32[1,2]{1,0:T(1,128)} %bitcast.28, f32[1,2]{1,0:T(1,128)} %bitcast.29, ...), custom_call_target="tpu_custom_call" | custom-call | tf_op jit(solution)/shard_map/tables/pallas_call | solution.py:544
  2.1 5.5 %collective-permute-start.2 = (f32[88,256]{1,0:T(8,128)}, f32[88,256]{1,0:T(8,128)S(1)}, u32[]{:S(2)}, u32[]{:S(2)}) collective-permute-start(f32[88,256]{1,0:T(8,128)} %tables.1.refs_0_), channel_id=1, source_target_pairs={{0,30},{2,24},{4,26},{6,28},{8,6},{10,0},{12,2},{14,4},{16,14},{18... | collective-permute-start | bytes 270344 | tf_op jit(solution)/shard_map/ppermute | solution.py:609
  7.5 0.0 collective-permute-start.1
  7.5 1.0 %collective-permute-start = (f32[88,256]{1,0:T(8,128)}, f32[88,256]{1,0:T(8,128)S(1)}, u32[]{:S(2)}, u32[]{:S(2)}) collective-permute-start(f32[88,256]{1,0:T(8,128)} %tables.1.refs_0_), channel_id=1, source_target_pairs={{0,10},{2,12},{4,14},{6,8},{8,18},{10,20},{12,22},{14,16},{16,26},... | collective-permute-start | bytes 270344 | tf_op jit(solution)/shard_map/ppermute | solution.py:609
  8.5 0.0 copy-start.9
  8.5 0.0 copy-start.12
  8.6 0.0 copy-start.14
  8.6 0.0 copy-start.8
  8.6 0.0 copy-start.3
  8.6 0.0 copy-start.11
  8.6 0.0 copy-done.4
  8.6 0.0 copy-done
  8.6 0.0 copy-done.2
  8.6 0.6 %copy-done.9 = s32[256]{0:T(256)S(1)} copy-done((s32[256]{0:T(256)S(1)}, s32[256]{0:T(256)}, u32[]{:S(2)}) %copy-start.9) | copy-done | bytes 1048
  9.2 0.0 copy-done.10
  9.2 0.0 copy-done.12
  9.2 0.0 copy-done.13
  9.2 0.0 copy-done.14
  9.3 0.0 copy-done.8
  9.3 0.0 copy-done.3
  9.3 0.0 copy-done.11
  9.3 0.9 %copy-done.5 = f32[256,2,128]{2,1,0:T(2,128)S(1)} copy-done((f32[256,2,128]{2,1,0:T(2,128)S(1)}, f32[256,2,128]{2,1,0:T(2,128)}, u32[]{:S(2)}) %copy-start.5) | copy-done | bytes 262168
  10.3 0.9 %copy-done.6 = f32[256,2,128]{2,1,0:T(2,128)S(1)} copy-done((f32[256,2,128]{2,1,0:T(2,128)S(1)}, f32[256,2,128]{2,1,0:T(2,128)}, u32[]{:S(2)}) %copy-start.6) | copy-done | bytes 262168
  11.2 0.9 %copy-done.7 = f32[128,256]{1,0:T(8,128)S(1)} copy-done((f32[128,256]{1,0:T(8,128)S(1)}, f32[128,256]{1,0:T(8,128)}, u32[]{:S(2)}) %copy-start.7) | copy-done | bytes 131096
  12.1 1.3 %prepare.1 = (f32[16,128]{1,0:T(8,128)S(1)}, f32[8,128]{1,0:T(8,128)S(1)}, bf16[256,256]{1,0:T(8,128)(2,1)S(1)}, bf16[128,256]{1,0:T(8,128)(2,1)S(1)}, bf16[128,...) custom-call(f32[16,256]{1,0:T(8,128)S(1)} %copy-done.2, ...), custom_call_target="tpu_custom_call" | custom-call | flops 402653184 | bytes 262144 | tf_op jit(solution)/shard_map/prepare/pallas_call | solution.py:583
  13.4 0.0 collective-permute-done.2.refs_3_.refs_10_
  13.4 1.1 %collective-permute-start.5 = (f32[88,256]{1,0:T(8,128)S(1)}, f32[88,256]{1,0:T(8,128)S(1)}, u32[]{:S(2)}, u32[]{:S(2)}) collective-permute-start(f32[88,256]{1,0:T(8,128)S(1)} %collective-permute-done.2.refs_3_.refs_10_), channel_id=1, source_target_pairs={{0,8},{8,0},{16,24},{24,16},{1,9},{9,1},{17,25},{25,17},{2,10},{10... | collective-permute-start | bytes 270344 | tf_op jit(solution)/shard_map/ppermute | solution.py:611
  14.5 2.9 %collective-permute-done.1.refs_2_.refs_9_ = f32[88,256]{1,0:T(8,128)S(1)} collective-permute-done((f32[88,256]{1,0:T(8,128)}, f32[88,256]{1,0:T(8,128)S(1)}, u32[]{:S(2)}, u32[]{:S(2)}) %collective-permute-start.1) | collective-permute-done | bytes 90144 | tf_op jit(solution)/shard_map/ppermute | solution.py:609
  17.4 0.0 collective-permute-start.4
  17.4 0.0 collective-permute-done.refs_1_.refs_8_
  17.5 0.5 %collective-permute-start.3 = (f32[88,256]{1,0:T(8,128)S(1)}, f32[88,256]{1,0:T(8,128)S(1)}, u32[]{:S(2)}, u32[]{:S(2)}) collective-permute-start(f32[88,256]{1,0:T(8,128)S(1)} %collective-permute-done.refs_1_.refs_8_), channel_id=1, source_target_pairs={{0,8},{8,0},{16,24},{24,16},{1,9},{9,1},{17,25},{25,17},{2,10},{10... | collective-permute-start | bytes 270344 | tf_op jit(solution)/shard_map/ppermute | solution.py:611
  17.9 0.0 copy-done.1
  17.9 1.8 %mix.1 = (bf16[256,512]{1,0:T(8,128)(2,1)S(1)}, bf16[256,512]{1,0:T(8,128)(2,1)S(1)}, f32[256,256]{1,0:T(8,128)S(1)}) custom-call(f32[88,256]{1,0:T(8,128)S(1)} %copy-done.1, f32[88,256]{1,0:T(8,128)S(1)} %collective-permute-done.refs_1_.refs_8_, f32[88,256]{1,0:T(8,128)S(1)} %collective-permute-done.1.refs_2_.refs_9_, ...), custom_call_target="tpu_custom_call" | custom-call | flops 1610612736 | bytes 262144 | tf_op jit(solution)/shard_map/mix/pallas_call | solution.py:613
  19.8 0.0 collective-permute-done.5.refs_13_
  19.8 0.0 collective-permute-done.4.refs_12_
  19.8 0.0 collective-permute-done.3.refs_11_
  19.8 1.5 %project.1 = (f32[136,128]{1,0:T(8,128)S(1)}, bf16[256,256]{1,0:T(8,128)(2,1)S(1)}, bf16[256,256]{1,0:T(8,128)(2,1)S(1)}, f32[256,128]{1,0:T(8,128)S(1)}, f32[25...) custom-call(bf16[256,512]{1,0:T(8,128)(2,1)S(1)} %get-tuple-element.34.refs_0_, ...), custom_call_target="tpu_custom_call" | custom-call | tf_op jit(solution)/shard_map/project/pallas_call | solution.py:624
  21.4 0.1 collective-permute-start.6
  21.4 1.2 %collective-permute-done.6.refs_1_ = f32[136,128]{1,0:T(8,128)S(1)} collective-permute-done((f32[136,128]{1,0:T(8,128)S(1)}, f32[136,128]{1,0:T(8,128)S(1)}, u32[]{:S(2)}, u32[]{:S(2)}) %collective-permute-start.6) | collective-permute-done | bytes 69664 | tf_op jit(solution)/shard_map/ppermute | solution.py:678
  22.7 0.6 %collective-permute-start.7 = (f32[136,128]{1,0:T(8,128)S(1)}, f32[136,128]{1,0:T(8,128)S(1)}, u32[]{:S(2)}, u32[]{:S(2)}) collective-permute-start(f32[136,128]{1,0:T(8,128)S(1)} %get-tuple-element.44), channel_id=1, source_target_pairs={{0,16},{8,24},{16,0},{24,8},{1,17},{9,25},{17,1},{25,9},{2,18},{10... | collective-permute-start | bytes 208904 | tf_op jit(solution)/shard_map/ppermute | solution.py:678
  23.3 1.2 %block.1 = (f32[256,128]{1,0:T(8,128)S(1)}, f32[256,128]{1,0:T(8,128)S(1)}, f32[256,128]{1,0:T(8,128)S(1)}, f32[64,256]{1,0:T(8,128)S(1)}) custom-call(bf16[256,256]{1,0:T(8,128)(2,1)S(1)} %get-tuple-element.45.refs_0_, bf16[256,256]{1,0:T(8,128)(2,1)S(1)} %get-tuple-element.46.refs_1_, f32[256,128]{1,0:T(8,128)S(1)} %get-tuple-element.47.refs_2_, ...), custom_call_target="tpu_custom_call" | custom-call | flops 805306368 | bytes 262144 | tf_op jit(solution)/shard_map/block/pallas_call | solution.py:652
  24.5 2.6 %collective-permute-done.7.refs_1_ = f32[136,128]{1,0:T(8,128)S(1)} collective-permute-done((f32[136,128]{1,0:T(8,128)S(1)}, f32[136,128]{1,0:T(8,128)S(1)}, u32[]{:S(2)}, u32[]{:S(2)}) %collective-permute-start.7) | collective-permute-done | bytes 69664 | tf_op jit(solution)/shard_map/ppermute | solution.py:678
  27.1 0.7 %output.1 = f32[4,64,256]{2,1,0:T(8,128)S(1)} custom-call(f32[136,128]{1,0:T(8,128)S(1)} %get-tuple-element.43.refs_0_, f32[136,128]{1,0:T(8,128)S(1)} %collective-permute-done.7.refs_1_, f32[256,128]{1,0:T(8,128)S(1)} %get-tuple-element.55.refs_2_, f32[256,128]{1,0:T(8,128)S(1)} %get-tuple-element.56.refs_3_, ...), custom_call_target="tpu_custom_call" | custom-call | tf_op jit(solution)/shard_map/output/pallas_call | solution.py:700
  27.8 10.7 %all_to_all.5 = f32[4,64,256]{2,1,0:T(8,128)S(1)} all-to-all(f32[4,64,256]{2,1,0:T(8,128)S(1)} %output.1), channel_id=1, replica_groups=mesh['seq'=4,'head'=4,'rep'=2] {'head'}, dimensions={0} | all-to-all | bytes 524288 | tf_op jit(solution)/shard_map/all_to_all | solution.py:708
  38.5 0.6 %reduce_sum.9 = f32[64,256]{1,0:T(8,128)} reduce(f32[4,64,256]{2,1,0:T(8,128)S(1)} %all_to_all.5, f32[]{:T(128)} %constant.0.clone.1), dimensions={0}, to_apply=%region_0.0 | reduce | flops 49152 | bytes 327684 | tf_op jit(solution)/shard_map/reduce_sum | solution.py:709
  (7 shorter events, 0.0 us)
Async XLA Ops:
  0.0 8.6 %copy-start.4 = (f32[256,2,128]{2,1,0:T(2,128)S(1)}, f32[256,2,128]{2,1,0:T(2,128)}, u32[]{:S(2)}) copy-start(f32[256,2,128]{2,1,0:T(2,128)} %param.26) | copy-start | bytes 786436
  0.0 8.6 %copy-start = (f32[128,256]{1,0:T(8,128)S(1)}, f32[128,256]{1,0:T(8,128)}, u32[]{:S(2)}) copy-start(f32[128,256]{1,0:T(8,128)} %refs_4_.2) | copy-start | bytes 393220
  0.0 8.6 %copy-start.2 = (f32[16,256]{1,0:T(8,128)S(1)}, f32[16,256]{1,0:T(8,128)}, u32[]{:S(2)}) copy-start(f32[16,256]{1,0:T(8,128)} %refs_4_.3) | copy-start | bytes 49156
  2.1 11.4 %collective-permute-start.2 = (f32[88,256]{1,0:T(8,128)}, f32[88,256]{1,0:T(8,128)S(1)}, u32[]{:S(2)}, u32[]{:S(2)}) collective-permute-start(f32[88,256]{1,0:T(8,128)} %tables.1.refs_0_), channel_id=1, source_target_pairs={{0,30},{2,24},{4,26},{6,28},{8,6},{10,0},{12,2},{14,4},{16,14},{18... | collective-permute-start | bytes 270344 | tf_op jit(solution)/shard_map/ppermute | solution.py:609
  7.5 9.9 %collective-permute-start.1 = (f32[88,256]{1,0:T(8,128)}, f32[88,256]{1,0:T(8,128)S(1)}, u32[]{:S(2)}, u32[]{:S(2)}) collective-permute-start(f32[88,256]{1,0:T(8,128)} %tables.1.refs_0_), channel_id=1, source_target_pairs={{0,20},{2,22},{4,16},{6,18},{8,28},{10,30},{12,24},{14,26},{16,4},... | collective-permute-start | bytes 270344 | tf_op jit(solution)/shard_map/ppermute | solution.py:609
  7.5 9.9 %collective-permute-start = (f32[88,256]{1,0:T(8,128)}, f32[88,256]{1,0:T(8,128)S(1)}, u32[]{:S(2)}, u32[]{:S(2)}) collective-permute-start(f32[88,256]{1,0:T(8,128)} %tables.1.refs_0_), channel_id=1, source_target_pairs={{0,10},{2,12},{4,14},{6,8},{8,18},{10,20},{12,22},{14,16},{16,26},... | collective-permute-start | bytes 270344 | tf_op jit(solution)/shard_map/ppermute | solution.py:609
  8.5 0.7 %copy-start.9 = (s32[256]{0:T(256)S(1)}, s32[256]{0:T(256)}, u32[]{:S(2)}) copy-start(s32[256]{0:T(256)} %param.23) | copy-start | bytes 3076
  8.5 0.7 %copy-start.10 = (f32[256]{0:T(256)S(1)}, f32[256]{0:T(256)}, u32[]{:S(2)}) copy-start(f32[256]{0:T(256)} %param.33) | copy-start | bytes 3076
  8.5 0.7 %copy-start.12 = (f32[2]{0:T(128)S(1)}, f32[2]{0:T(128)}, u32[]{:S(2)}) copy-start(f32[2]{0:T(128)} %refs_10_.1) | copy-start | bytes 28
  8.5 0.7 %copy-start.13 = (f32[2]{0:T(128)S(1)}, f32[2]{0:T(128)}, u32[]{:S(2)}) copy-start(f32[2]{0:T(128)} %refs_11_.1) | copy-start | bytes 28
  8.6 0.7 %copy-start.14 = (f32[128]{0:T(128)S(1)}, f32[128]{0:T(128)}, u32[]{:S(2)}) copy-start(f32[128]{0:T(128)} %param.40) | copy-start | bytes 1540
  8.6 0.7 %copy-start.8 = (f32[256,2]{0,1:T(2,128)S(1)}, f32[256,2]{0,1:T(2,128)}, u32[]{:S(2)}) copy-start(f32[256,2]{0,1:T(2,128)} %param.36) | copy-start | bytes 6148
  8.6 0.7 %copy-start.3 = (f32[256]{0:T(256)S(1)}, f32[256]{0:T(256)}, u32[]{:S(2)}) copy-start(f32[256]{0:T(256)} %param.24) | copy-start | bytes 3076
  8.6 0.7 %copy-start.11 = (f32[2]{0:T(128)S(1)}, f32[2]{0:T(128)}, u32[]{:S(2)}) copy-start(f32[2]{0:T(128)} %refs_9_.3) | copy-start | bytes 28
  9.3 1.0 %copy-start.5 = (f32[256,2,128]{2,1,0:T(2,128)S(1)}, f32[256,2,128]{2,1,0:T(2,128)}, u32[]{:S(2)}) copy-start(f32[256,2,128]{2,1,0:T(2,128)} %param.34) | copy-start | bytes 786436
  10.3 0.9 %copy-start.6 = (f32[256,2,128]{2,1,0:T(2,128)S(1)}, f32[256,2,128]{2,1,0:T(2,128)}, u32[]{:S(2)}) copy-start(f32[256,2,128]{2,1,0:T(2,128)} %param.35) | copy-start | bytes 786436
  11.2 0.9 %copy-start.7 = (f32[128,256]{1,0:T(8,128)S(1)}, f32[128,256]{1,0:T(8,128)}, u32[]{:S(2)}) copy-start(f32[128,256]{1,0:T(8,128)} %refs_13_.1) | copy-start | bytes 393220
  12.1 5.8 %copy-start.1 = (f32[88,256]{1,0:T(8,128)S(1)}, f32[88,256]{1,0:T(8,128)}, u32[]{:S(2)}) copy-start(f32[88,256]{1,0:T(8,128)} %tables.1.refs_0_) | copy-start | bytes 270340
  13.4 6.4 %collective-permute-start.5 = (f32[88,256]{1,0:T(8,128)S(1)}, f32[88,256]{1,0:T(8,128)S(1)}, u32[]{:S(2)}, u32[]{:S(2)}) collective-permute-start(f32[88,256]{1,0:T(8,128)S(1)} %collective-permute-done.2.refs_3_.refs_10_), channel_id=1, source_target_pairs={{0,8},{8,0},{16,24},{24,16},{1,9},{9,1},{17,25},{25,17},{2,10},{10... | collective-permute-start | bytes 270344 | tf_op jit(solution)/shard_map/ppermute | solution.py:611
  17.4 2.4 %collective-permute-start.4 = (f32[88,256]{1,0:T(8,128)S(1)}, f32[88,256]{1,0:T(8,128)S(1)}, u32[]{:S(2)}, u32[]{:S(2)}) collective-permute-start(f32[88,256]{1,0:T(8,128)S(1)} %collective-permute-done.1.refs_2_.refs_9_), channel_id=1, source_target_pairs={{0,8},{8,0},{16,24},{24,16},{1,9},{9,1},{17,25},{25,17},{2,10},{10... | collective-permute-start | bytes 270344 | tf_op jit(solution)/shard_map/ppermute | solution.py:611
  17.5 2.4 %collective-permute-start.3 = (f32[88,256]{1,0:T(8,128)S(1)}, f32[88,256]{1,0:T(8,128)S(1)}, u32[]{:S(2)}, u32[]{:S(2)}) collective-permute-start(f32[88,256]{1,0:T(8,128)S(1)} %collective-permute-done.refs_1_.refs_8_), channel_id=1, source_target_pairs={{0,8},{8,0},{16,24},{24,16},{1,9},{9,1},{17,25},{25,17},{2,10},{10... | collective-permute-start | bytes 270344 | tf_op jit(solution)/shard_map/ppermute | solution.py:611
  21.4 1.3 %collective-permute-start.6 = (f32[136,128]{1,0:T(8,128)S(1)}, f32[136,128]{1,0:T(8,128)S(1)}, u32[]{:S(2)}, u32[]{:S(2)}) collective-permute-start(f32[136,128]{1,0:T(8,128)S(1)} %get-tuple-element.42.refs_0_), channel_id=1, source_target_pairs={{0,8},{8,0},{16,24},{24,16},{1,9},{9,1},{17,25},{25,17},{2,10},{10... | collective-permute-start | bytes 208904 | tf_op jit(solution)/shard_map/ppermute | solution.py:678
  22.7 4.4 %collective-permute-start.7 = (f32[136,128]{1,0:T(8,128)S(1)}, f32[136,128]{1,0:T(8,128)S(1)}, u32[]{:S(2)}, u32[]{:S(2)}) collective-permute-start(f32[136,128]{1,0:T(8,128)S(1)} %get-tuple-element.44), channel_id=1, source_target_pairs={{0,16},{8,24},{16,0},{24,8},{1,17},{9,25},{17,1},{25,9},{2,18},{10... | collective-permute-start | bytes 208904 | tf_op jit(solution)/shard_map/ppermute | solution.py:678

commit v4 on v3

--- a/solution.py
+++ b/solution.py
@@ -213,7 +213,7 @@
         taken, refs[:] = refs[:number], refs[number:]
         return taken
 
-    packets = take(max(ns, nh))
+    packets = take(max(ns, nh))[::-1]
     emb, pairs = take(2)
     out_high, out_low, out_embedded = take(3)
     tokens = take(1)[0]
@@ -335,8 +335,8 @@
         return taken
 
     high, low, embedded, small, own_high, own_low, state_high, state_low = take(8)
-    nears = take(nh - 1)
-    others = take(nh - 1)
+    nears = take(nh - 1)[::-1]
+    others = take(nh - 1)[::-1]
     out_state, out_high, out_low, out_scale = take(4)
     out_write, out_inner, out_stepped, out_total = take(4)
     half = ch // 2
@@ -458,7 +458,8 @@
 def output_kernel(dims, bit, *refs):
     V, D, hl, ch, nh, ns, T, N = dims
     P = ch // hl
-    prefix, came, read, base, total, gate, own, proj_high, proj_low, out = refs
+    prefix, came, read, base, total, gate, own, proj_high, proj_low = refs[:9]
+    outs, partial_ref = refs[9 : 9 + nh], refs[9 + nh]
     entering = prefix_joined(dims, bit, prefix, came)
     value = (base[...] + dot3(read[...], entering, NT) * jnp.exp(total[...])) * gate[...]
     group = (iota((ch, ch), 0) // P == iota((ch, ch), 1) // P).astype(f32).astype(bf16)
@@ -466,10 +467,12 @@
     square = dot(low, group) + dot(high, group)
     value = value * lax.rsqrt(square * (1.0 / P) + epsilon)
     share = T // nh
-    partial = dot_split(split2(value), (proj_high[...], proj_low[...]))
-    out[...] = partial.reshape(nh, share, D)
+    partial_ref[...] = dot_split(split2(value), (proj_high[...], proj_low[...]))
     mine = lax.axis_index("head")
-    out[pl.ds(mine, 1)] = out[pl.ds(mine, 1)] + own[...].reshape(1, share, D)
+    for k in range(nh):
+        place = pl.multiple_of(lax.rem(mine + k, nh) * share, 8)
+        part = partial_ref[pl.ds(place, share), :]
+        outs[k][...] = part + own[...] if k == 0 else part
 
 
 def per_device(
@@ -619,7 +622,7 @@
         compiler_params=params,
         cost_estimate=cost(6 * T * D * D * 16),
         name="mix",
-    )(*messages, embedding, pair_table)
+    )(*messages[::-1], embedding, pair_table)
 
     state, hidden_high, hidden_low, scale, write, inner, stepped, total = pl.pallas_call(
         functools.partial(project_kernel, dims),
@@ -645,8 +648,8 @@
         own_low,
         state_high,
         state_low,
-        *messages[1:nh],
-        *others,
+        *messages[1:nh][::-1],
+        *others[::-1],
     )
 
     base, read, gate, own = pl.pallas_call(
@@ -699,14 +702,18 @@
 
     parts = pl.pallas_call(
         functools.partial(output_kernel, dims, bits - 1),
-        out_shape=shape(nh, share, D),
+        out_shape=(shape(share, D),) * nh,
         in_specs=[vmem] * 9,
-        out_specs=vmem,
+        out_specs=(vmem,) * nh,
+        scratch_shapes=[pltpu.VMEM((T, D), f32)],
         compiler_params=params,
         name="output",
     )(prefix, came, read, base, total, gate, own, proj_high, proj_low)
-    parts = lax.all_to_all(parts, "head", 0, 0, tiled=True)
-    return jnp.sum(parts, axis=0)
+    result = parts[0]
+    for k in range(1, nh):
+        pairs = [(source, (source + k) % nh) for source in range(nh)]
+        result = result + lax.ppermute(parts[k], "head", pairs)
+    return result
 
 
 def solution(mesh):

time: 39.4 us -> 35.7 us (0.906)
  blocking collectives: 10.7 us -> 0 us
  starting transfers between devices: 8.76 us -> 14.2 us
  waiting for transfers between devices: 6.75 us -> 8.38 us
    all_to_all x1 -> x0, blocking collectives: 10.7 us -> none  [per_device(): parts = lax.all_to_all(parts, 'head', 0, 0, tiled=True)]
    ppermute x0 -> x3, waiting for transfers between devices: none -> 5 us  [per_device(): result = result + lax.ppermute(parts[k], 'head', pairs)]
    ppermute x0 -> x3, starting transfers between devices: none -> 3.89 us  [per_device(): result = result + lax.ppermute(parts[k], 'head', pairs)]
    ppermute x3, waiting for transfers between devices: 2.91 us -> 0.01 us  [per_device(): messages.append(lax.ppermute(sent, ('seq', 'head'), pairs))]
    ppermute x3, starting transfers between devices: 6.49 us -> 8.28 us  [per_device(): messages.append(lax.ppermute(sent, ('seq', 'head'), pairs))]
    ppermute x3, starting transfers between devices: 1.59 us -> 0.65 us  [per_device(): others = [lax.ppermute(messages[k], 'seq', swap) for k in range(1, nh)]]
    ppermute x2, starting transfers between devices: 0.69 us -> 1.35 us  [per_device(): lax.ppermute(state, 'seq', [(seq, seq ^ 2 ** bit) for seq in range(ns)])]
    add x0 -> x1, other arithmetic: none -> 0.65 us  [per_device(): result = result + lax.ppermute(parts[k], 'head', pairs)]
  transfers between devices with their start and end apart: 8 -> 11, of which waited for: 3 -> 5; matrix products, arithmetic and copies ran while one was open for 0% -> 0% of each run, Pallas kernels for 11% -> 12%
where the time goes in v4:
time: 35.7 us; the launch traced here: 35.5 us
  starting transfers between devices  14.2 us (40%)
  Pallas kernels  8.62 us (24%)
  waiting for transfers between devices  8.38 us (23%)
  local copies, waits for them, and re-layouts  3.52 us (10%)
  other arithmetic  0.65 us (2%)
    ppermute x3, starting transfers between devices, per_device(): messages.append(lax.ppermute(sent, ('seq', 'head'), pairs))  8.28 us
    ppermute x3, waiting for transfers between devices, per_device(): result = result + lax.ppermute(parts[k], 'head', pairs)  5 us
    ppermute x3, starting transfers between devices, per_device(): result = result + lax.ppermute(parts[k], 'head', pairs)  3.89 us
    unnamed x30, local copies, waits for them, and re-layouts  3.52 us
    ppermute x2, waiting for transfers between devices, per_device(): lax.ppermute(state, 'seq', [(seq, seq ^ 2 ** bit) for seq in range(ns)])  3.37 us
    pallas_call x1, Pallas kernels, per_device(): pl.pallas_call(functools.partial(tables_kernel, dims), out_shape=shape(he...  2.04 us
    pallas_call x1, Pallas kernels, per_device(): pl.pallas_call(functools.partial(mix_kernel, dims), out_shape=(*halves(T,...  1.85 us
    pallas_call x1, Pallas kernels, per_device(): pl.pallas_call(functools.partial(project_kernel, dims), out_shape=(shape(...  1.52 us
  transfers between devices with their start and end apart: 11, of which 5 were waited for; matrix products, arithmetic and copies ran while one was open for 0% of the time, Pallas kernels for 12%

profile of v4, /device:TPU:0, one launch (start us, length us, event | category | flops | bytes accessed | tf_op | source)
XLA Modules:
  0.0 35.5 jit_solution(9837054461322119849)
XLA Ops:
  0.0 2.0 %tables.1.refs_3_ = f32[88,256]{1,0:T(8,128)} custom-call(f32[512,128]{1,0:T(8,128)} %bitcast.24, s32[1,256]{1,0:T(1,128)} %bitcast.26, f32[16,256]{1,0:T(8,128)} %refs_4_.3, f32[1,256]{1,0:T(1,128)} %bitcast.15, f32[2,256]{1,0:T(2,128)} %bitcast.25, f32[1,2]{1,0:T(1,128)} %bitcast.27, f32[1,2]{1,0:T(1,128)} %bitcast.28, f32[1,2]{1,0:T(1,128)} %bitcast.29, ...), custom_call_target="tpu_custom_call" | custom-call | tf_op jit(solution)/shard_map/tables/pallas_call | solution.py:547
  2.1 2.5 %collective-permute-start.2 = (f32[88,256]{1,0:T(8,128)}, f32[88,256]{1,0:T(8,128)S(1)}, u32[]{:S(2)}, u32[]{:S(2)}) collective-permute-start(f32[88,256]{1,0:T(8,128)} %tables.1.refs_3_), channel_id=1, source_target_pairs={{0,10},{2,12},{4,14},{6,8},{8,18},{10,20},{12,22},{14,16},{16,26},... | collective-permute-start | bytes 270344 | tf_op jit(solution)/shard_map/ppermute | solution.py:612
  4.6 3.5 %collective-permute-start.1 = (f32[88,256]{1,0:T(8,128)}, f32[88,256]{1,0:T(8,128)S(1)}, u32[]{:S(2)}, u32[]{:S(2)}) collective-permute-start(f32[88,256]{1,0:T(8,128)} %tables.1.refs_3_), channel_id=1, source_target_pairs={{0,20},{2,22},{4,16},{6,18},{8,28},{10,30},{12,24},{14,26},{16,4},... | collective-permute-start | bytes 270344 | tf_op jit(solution)/shard_map/ppermute | solution.py:612
  8.1 2.2 %collective-permute-start = (f32[88,256]{1,0:T(8,128)}, f32[88,256]{1,0:T(8,128)S(1)}, u32[]{:S(2)}, u32[]{:S(2)}) collective-permute-start(f32[88,256]{1,0:T(8,128)} %tables.1.refs_3_), channel_id=1, source_target_pairs={{0,30},{2,24},{4,26},{6,28},{8,6},{10,0},{12,2},{14,4},{16,14},{18... | collective-permute-start | bytes 270344 | tf_op jit(solution)/shard_map/ppermute | solution.py:612
  10.4 0.0 copy-start.14
  10.4 0.0 copy-start.8
  10.4 0.0 copy-start.3
  10.4 0.0 copy-start.11
  10.4 0.0 copy-done.4
  10.4 0.0 copy-done
  10.4 0.0 copy-done.2
  10.4 0.6 %copy-done.9 = s32[256]{0:T(256)S(1)} copy-done((s32[256]{0:T(256)S(1)}, s32[256]{0:T(256)}, u32[]{:S(2)}) %copy-start.9) | copy-done | bytes 1048
  11.0 0.0 copy-done.10
  11.0 0.0 copy-done.12
  11.0 0.0 copy-done.13
  11.0 0.0 copy-done.14
  11.1 0.0 copy-done.8
  11.1 0.0 copy-done.3
  11.1 0.0 copy-done.11
  11.1 0.9 %copy-done.5 = f32[256,2,128]{2,1,0:T(2,128)S(1)} copy-done((f32[256,2,128]{2,1,0:T(2,128)S(1)}, f32[256,2,128]{2,1,0:T(2,128)}, u32[]{:S(2)}) %copy-start.5) | copy-done | bytes 262168
  12.1 0.9 %copy-done.6 = f32[256,2,128]{2,1,0:T(2,128)S(1)} copy-done((f32[256,2,128]{2,1,0:T(2,128)S(1)}, f32[256,2,128]{2,1,0:T(2,128)}, u32[]{:S(2)}) %copy-start.6) | copy-done | bytes 262168
  13.0 0.9 %copy-done.7 = f32[128,256]{1,0:T(8,128)S(1)} copy-done((f32[128,256]{1,0:T(8,128)S(1)}, f32[128,256]{1,0:T(8,128)}, u32[]{:S(2)}) %copy-start.7) | copy-done | bytes 131096
  13.9 1.3 %prepare.1 = (f32[16,128]{1,0:T(8,128)S(1)}, f32[8,128]{1,0:T(8,128)S(1)}, bf16[256,256]{1,0:T(8,128)(2,1)S(1)}, bf16[128,256]{1,0:T(8,128)(2,1)S(1)}, bf16[128,...) custom-call(f32[16,256]{1,0:T(8,128)S(1)} %copy-done.2, ...), custom_call_target="tpu_custom_call" | custom-call | flops 402653184 | bytes 262144 | tf_op jit(solution)/shard_map/prepare/pallas_call | solution.py:586
  15.2 0.0 collective-permute-done.2.refs_2_.refs_10_
  15.2 0.1 collective-permute-start.5
  15.3 0.0 collective-permute-done.1.refs_1_.refs_9_
  15.3 0.5 %collective-permute-start.4 = (f32[88,256]{1,0:T(8,128)S(1)}, f32[88,256]{1,0:T(8,128)S(1)}, u32[]{:S(2)}, u32[]{:S(2)}) collective-permute-start(f32[88,256]{1,0:T(8,128)S(1)} %collective-permute-done.1.refs_1_.refs_9_), channel_id=1, source_target_pairs={{0,8},{8,0},{16,24},{24,16},{1,9},{9,1},{17,25},{25,17},{2,10},{10... | collective-permute-start | bytes 270344 | tf_op jit(solution)/shard_map/ppermute | solution.py:614
  15.8 0.0 collective-permute-done.refs_0_.refs_8_
  15.8 0.1 collective-permute-start.3
  15.9 0.0 copy-done.1
  15.9 1.8 %mix.1 = (bf16[256,512]{1,0:T(8,128)(2,1)S(1)}, bf16[256,512]{1,0:T(8,128)(2,1)S(1)}, f32[256,256]{1,0:T(8,128)S(1)}) custom-call(f32[88,256]{1,0:T(8,128)S(1)} %collective-permute-done.refs_0_.refs_8_, f32[88,256]{1,0:T(8,128)S(1)} %collective-permute-done.1.refs_1_.refs_9_, f32[88,256]{1,0:T(8,128)S(1)} %collective-permute-done.2.refs_2_.refs_10_, ...), custom_call_target="tpu_custom_call" | custom-call | flops 1610612736 | bytes 262144 | tf_op jit(solution)/shard_map/mix/pallas_call | solution.py:616
  17.8 0.0 collective-permute-done.5.refs_13_
  17.8 0.0 collective-permute-done.4.refs_12_
  17.8 0.0 collective-permute-done.3.refs_11_
  17.8 1.5 %project.1 = (f32[136,128]{1,0:T(8,128)S(1)}, bf16[256,256]{1,0:T(8,128)(2,1)S(1)}, bf16[256,256]{1,0:T(8,128)(2,1)S(1)}, f32[256,128]{1,0:T(8,128)S(1)}, f32[25...) custom-call(bf16[256,512]{1,0:T(8,128)(2,1)S(1)} %get-tuple-element.38.refs_0_, ...), custom_call_target="tpu_custom_call" | custom-call | tf_op jit(solution)/shard_map/project/pallas_call | solution.py:627
  19.3 0.5 %collective-permute-start.6 = (f32[136,128]{1,0:T(8,128)S(1)}, f32[136,128]{1,0:T(8,128)S(1)}, u32[]{:S(2)}, u32[]{:S(2)}) collective-permute-start(f32[136,128]{1,0:T(8,128)S(1)} %get-tuple-element.46.refs_0_), channel_id=1, source_target_pairs={{0,8},{8,0},{16,24},{24,16},{1,9},{9,1},{17,25},{25,17},{2,10},{10... | collective-permute-start | bytes 208904 | tf_op jit(solution)/shard_map/ppermute | solution.py:681
  19.8 0.9 %collective-permute-done.6.refs_1_ = f32[136,128]{1,0:T(8,128)S(1)} collective-permute-done((f32[136,128]{1,0:T(8,128)S(1)}, f32[136,128]{1,0:T(8,128)S(1)}, u32[]{:S(2)}, u32[]{:S(2)}) %collective-permute-start.6) | collective-permute-done | bytes 69664 | tf_op jit(solution)/shard_map/ppermute | solution.py:681
  20.8 0.9 %collective-permute-start.7 = (f32[136,128]{1,0:T(8,128)S(1)}, f32[136,128]{1,0:T(8,128)S(1)}, u32[]{:S(2)}, u32[]{:S(2)}) collective-permute-start(f32[136,128]{1,0:T(8,128)S(1)} %get-tuple-element.48), channel_id=1, source_target_pairs={{0,16},{8,24},{16,0},{24,8},{1,17},{9,25},{17,1},{25,9},{2,18},{10... | collective-permute-start | bytes 208904 | tf_op jit(solution)/shard_map/ppermute | solution.py:681
  21.6 1.2 %block.1 = (f32[256,128]{1,0:T(8,128)S(1)}, f32[256,128]{1,0:T(8,128)S(1)}, f32[256,128]{1,0:T(8,128)S(1)}, f32[64,256]{1,0:T(8,128)S(1)}) custom-call(bf16[256,256]{1,0:T(8,128)(2,1)S(1)} %get-tuple-element.49.refs_0_, bf16[256,256]{1,0:T(8,128)(2,1)S(1)} %get-tuple-element.50.refs_1_, f32[256,128]{1,0:T(8,128)S(1)} %get-tuple-element.51.refs_2_, ...), custom_call_target="tpu_custom_call" | custom-call | flops 805306368 | bytes 262144 | tf_op jit(solution)/shard_map/block/pallas_call | solution.py:655
  22.8 2.5 %collective-permute-done.7.refs_1_ = f32[136,128]{1,0:T(8,128)S(1)} collective-permute-done((f32[136,128]{1,0:T(8,128)S(1)}, f32[136,128]{1,0:T(8,128)S(1)}, u32[]{:S(2)}, u32[]{:S(2)}) %collective-permute-start.7) | collective-permute-done | bytes 69664 | tf_op jit(solution)/shard_map/ppermute | solution.py:681
  25.3 0.7 %output.1 = (f32[64,256]{1,0:T(8,128)S(1)}, f32[64,256]{1,0:T(8,128)S(1)}, f32[64,256]{1,0:T(8,128)S(1)}, f32[64,256]{1,0:T(8,128)S(1)}) custom-call(f32[136,128]{1,0:T(8,128)S(1)} %get-tuple-element.47.refs_0_, f32[136,128]{1,0:T(8,128)S(1)} %collective-permute-done.7.refs_1_, f32[256,128]{1,0:T(8,128)S(1)} %get-tuple-element.59.refs_2_, ...), custom_call_target="tpu_custom_call" | custom-call | tf_op jit(solution)/shard_map/output/pallas_call | solution.py:703
  26.0 1.4 %collective-permute-start.8 = (f32[64,256]{1,0:T(8,128)S(1)}, f32[64,256]{1,0:T(8,128)S(1)}, u32[]{:S(2)}, u32[]{:S(2)}) collective-permute-start(f32[64,256]{1,0:T(8,128)S(1)} %get-tuple-element.66), channel_id=1, source_target_pairs={{0,2},{2,4},{4,6},{6,0},{1,3},{3,5},{5,7},{7,1},{8,10},{10,12},{12... | collective-permute-start | bytes 196616 | tf_op jit(solution)/shard_map/ppermute | solution.py:715
  27.4 2.4 %collective-permute-start.9 = (f32[64,256]{1,0:T(8,128)S(1)}, f32[64,256]{1,0:T(8,128)S(1)}, u32[]{:S(2)}, u32[]{:S(2)}) collective-permute-start(f32[64,256]{1,0:T(8,128)S(1)} %get-tuple-element.67), channel_id=1, source_target_pairs={{0,4},{2,6},{4,0},{6,2},{1,5},{3,7},{5,1},{7,3},{8,12},{10,14},{12... | collective-permute-start | bytes 196616 | tf_op jit(solution)/shard_map/ppermute | solution.py:715
  29.9 0.0 collective-permute-start.10
  29.9 3.0 %collective-permute-done.8 = f32[64,256]{1,0:T(8,128)S(1)} collective-permute-done((f32[64,256]{1,0:T(8,128)S(1)}, f32[64,256]{1,0:T(8,128)S(1)}, u32[]{:S(2)}, u32[]{:S(2)}) %collective-permute-start.8) | collective-permute-done | bytes 65568 | tf_op jit(solution)/shard_map/ppermute | solution.py:715
  32.8 1.7 %collective-permute-done.9 = f32[64,256]{1,0:T(8,128)S(1)} collective-permute-done((f32[64,256]{1,0:T(8,128)S(1)}, f32[64,256]{1,0:T(8,128)S(1)}, u32[]{:S(2)}, u32[]{:S(2)}) %collective-permute-start.9) | collective-permute-done | bytes 65568 | tf_op jit(solution)/shard_map/ppermute | solution.py:715
  34.5 0.4 collective-permute-done.10
  34.9 0.6 %add_add_fusion = f32[64,256]{1,0:T(8,128)} fusion(f32[64,256]{1,0:T(8,128)S(1)} %collective-permute-done.10, f32[64,256]{1,0:T(8,128)S(1)} %collective-permute-done.9, f32[64,256]{1,0:T(8,128)S(1)} %get-tuple-element.65, f32[64,256]{1,0:T(8,128)S(1)} %collective-permute-done.8), kind=kLoop, calls=%fused_computation | loop fusion | flops 49152 | bytes 327680 | tf_op jit(solution)/shard_map/add | solution.py:715
  (12 shorter events, 0.0 us)
Async XLA Ops:
  0.0 10.4 %copy-start.4 = (f32[256,2,128]{2,1,0:T(2,128)S(1)}, f32[256,2,128]{2,1,0:T(2,128)}, u32[]{:S(2)}) copy-start(f32[256,2,128]{2,1,0:T(2,128)} %param.26) | copy-start | bytes 786436
  0.0 10.4 %copy-start = (f32[128,256]{1,0:T(8,128)S(1)}, f32[128,256]{1,0:T(8,128)}, u32[]{:S(2)}) copy-start(f32[128,256]{1,0:T(8,128)} %refs_4_.2) | copy-start | bytes 393220
  0.0 10.4 %copy-start.2 = (f32[16,256]{1,0:T(8,128)S(1)}, f32[16,256]{1,0:T(8,128)}, u32[]{:S(2)}) copy-start(f32[16,256]{1,0:T(8,128)} %refs_4_.3) | copy-start | bytes 49156
  2.1 13.2 %collective-permute-start.2 = (f32[88,256]{1,0:T(8,128)}, f32[88,256]{1,0:T(8,128)S(1)}, u32[]{:S(2)}, u32[]{:S(2)}) collective-permute-start(f32[88,256]{1,0:T(8,128)} %tables.1.refs_3_), channel_id=1, source_target_pairs={{0,10},{2,12},{4,14},{6,8},{8,18},{10,20},{12,22},{14,16},{16,26},... | collective-permute-start | bytes 270344 | tf_op jit(solution)/shard_map/ppermute | solution.py:612
  4.6 10.8 %collective-permute-start.1 = (f32[88,256]{1,0:T(8,128)}, f32[88,256]{1,0:T(8,128)S(1)}, u32[]{:S(2)}, u32[]{:S(2)}) collective-permute-start(f32[88,256]{1,0:T(8,128)} %tables.1.refs_3_), channel_id=1, source_target_pairs={{0,20},{2,22},{4,16},{6,18},{8,28},{10,30},{12,24},{14,26},{16,4},... | collective-permute-start | bytes 270344 | tf_op jit(solution)/shard_map/ppermute | solution.py:612
  8.1 7.7 %collective-permute-start = (f32[88,256]{1,0:T(8,128)}, f32[88,256]{1,0:T(8,128)S(1)}, u32[]{:S(2)}, u32[]{:S(2)}) collective-permute-start(f32[88,256]{1,0:T(8,128)} %tables.1.refs_3_), channel_id=1, source_target_pairs={{0,30},{2,24},{4,26},{6,28},{8,6},{10,0},{12,2},{14,4},{16,14},{18... | collective-permute-start | bytes 270344 | tf_op jit(solution)/shard_map/ppermute | solution.py:612
  10.3 0.7 %copy-start.9 = (s32[256]{0:T(256)S(1)}, s32[256]{0:T(256)}, u32[]{:S(2)}) copy-start(s32[256]{0:T(256)} %param.23) | copy-start | bytes 3076
  10.3 0.7 %copy-start.10 = (f32[256]{0:T(256)S(1)}, f32[256]{0:T(256)}, u32[]{:S(2)}) copy-start(f32[256]{0:T(256)} %param.33) | copy-start | bytes 3076
  10.3 0.7 %copy-start.12 = (f32[2]{0:T(128)S(1)}, f32[2]{0:T(128)}, u32[]{:S(2)}) copy-start(f32[2]{0:T(128)} %refs_10_.1) | copy-start | bytes 28
  10.3 0.7 %copy-start.13 = (f32[2]{0:T(128)S(1)}, f32[2]{0:T(128)}, u32[]{:S(2)}) copy-start(f32[2]{0:T(128)} %refs_11_.1) | copy-start | bytes 28
  10.4 0.7 %copy-start.14 = (f32[128]{0:T(128)S(1)}, f32[128]{0:T(128)}, u32[]{:S(2)}) copy-start(f32[128]{0:T(128)} %param.40) | copy-start | bytes 1540
  10.4 0.7 %copy-start.8 = (f32[256,2]{0,1:T(2,128)S(1)}, f32[256,2]{0,1:T(2,128)}, u32[]{:S(2)}) copy-start(f32[256,2]{0,1:T(2,128)} %param.36) | copy-start | bytes 6148
  10.4 0.7 %copy-start.3 = (f32[256]{0:T(256)S(1)}, f32[256]{0:T(256)}, u32[]{:S(2)}) copy-start(f32[256]{0:T(256)} %param.24) | copy-start | bytes 3076
  10.4 0.7 %copy-start.11 = (f32[2]{0:T(128)S(1)}, f32[2]{0:T(128)}, u32[]{:S(2)}) copy-start(f32[2]{0:T(128)} %refs_9_.3) | copy-start | bytes 28
  11.1 1.0 %copy-start.5 = (f32[256,2,128]{2,1,0:T(2,128)S(1)}, f32[256,2,128]{2,1,0:T(2,128)}, u32[]{:S(2)}) copy-start(f32[256,2,128]{2,1,0:T(2,128)} %param.34) | copy-start | bytes 786436
  12.1 0.9 %copy-start.6 = (f32[256,2,128]{2,1,0:T(2,128)S(1)}, f32[256,2,128]{2,1,0:T(2,128)}, u32[]{:S(2)}) copy-start(f32[256,2,128]{2,1,0:T(2,128)} %param.35) | copy-start | bytes 786436
  13.0 0.9 %copy-start.7 = (f32[128,256]{1,0:T(8,128)S(1)}, f32[128,256]{1,0:T(8,128)}, u32[]{:S(2)}) copy-start(f32[128,256]{1,0:T(8,128)} %refs_13_.1) | copy-start | bytes 393220
  13.9 2.0 %copy-start.1 = (f32[88,256]{1,0:T(8,128)S(1)}, f32[88,256]{1,0:T(8,128)}, u32[]{:S(2)}) copy-start(f32[88,256]{1,0:T(8,128)} %tables.1.refs_3_) | copy-start | bytes 270340
  15.2 2.5 %collective-permute-start.5 = (f32[88,256]{1,0:T(8,128)S(1)}, f32[88,256]{1,0:T(8,128)S(1)}, u32[]{:S(2)}, u32[]{:S(2)}) collective-permute-start(f32[88,256]{1,0:T(8,128)S(1)} %collective-permute-done.2.refs_2_.refs_10_), channel_id=1, source_target_pairs={{0,8},{8,0},{16,24},{24,16},{1,9},{9,1},{17,25},{25,17},{2,10},{10... | collective-permute-start | bytes 270344 | tf_op jit(solution)/shard_map/ppermute | solution.py:614
  15.3 2.4 %collective-permute-start.4 = (f32[88,256]{1,0:T(8,128)S(1)}, f32[88,256]{1,0:T(8,128)S(1)}, u32[]{:S(2)}, u32[]{:S(2)}) collective-permute-start(f32[88,256]{1,0:T(8,128)S(1)} %collective-permute-done.1.refs_1_.refs_9_), channel_id=1, source_target_pairs={{0,8},{8,0},{16,24},{24,16},{1,9},{9,1},{17,25},{25,17},{2,10},{10... | collective-permute-start | bytes 270344 | tf_op jit(solution)/shard_map/ppermute | solution.py:614
  15.8 2.0 %collective-permute-start.3 = (f32[88,256]{1,0:T(8,128)S(1)}, f32[88,256]{1,0:T(8,128)S(1)}, u32[]{:S(2)}, u32[]{:S(2)}) collective-permute-start(f32[88,256]{1,0:T(8,128)S(1)} %collective-permute-done.refs_0_.refs_8_), channel_id=1, source_target_pairs={{0,8},{8,0},{16,24},{24,16},{1,9},{9,1},{17,25},{25,17},{2,10},{10... | collective-permute-start | bytes 270344 | tf_op jit(solution)/shard_map/ppermute | solution.py:614
  19.3 1.4 %collective-permute-start.6 = (f32[136,128]{1,0:T(8,128)S(1)}, f32[136,128]{1,0:T(8,128)S(1)}, u32[]{:S(2)}, u32[]{:S(2)}) collective-permute-start(f32[136,128]{1,0:T(8,128)S(1)} %get-tuple-element.46.refs_0_), channel_id=1, source_target_pairs={{0,8},{8,0},{16,24},{24,16},{1,9},{9,1},{17,25},{25,17},{2,10},{10... | collective-permute-start | bytes 208904 | tf_op jit(solution)/shard_map/ppermute | solution.py:681
  20.8 4.5 %collective-permute-start.7 = (f32[136,128]{1,0:T(8,128)S(1)}, f32[136,128]{1,0:T(8,128)S(1)}, u32[]{:S(2)}, u32[]{:S(2)}) collective-permute-start(f32[136,128]{1,0:T(8,128)S(1)} %get-tuple-element.48), channel_id=1, source_target_pairs={{0,16},{8,24},{16,0},{24,8},{1,17},{9,25},{17,1},{25,9},{2,18},{10... | collective-permute-start | bytes 208904 | tf_op jit(solution)/shard_map/ppermute | solution.py:681
  26.0 6.9 %collective-permute-start.8 = (f32[64,256]{1,0:T(8,128)S(1)}, f32[64,256]{1,0:T(8,128)S(1)}, u32[]{:S(2)}, u32[]{:S(2)}) collective-permute-start(f32[64,256]{1,0:T(8,128)S(1)} %get-tuple-element.66), channel_id=1, source_target_pairs={{0,2},{2,4},{4,6},{6,0},{1,3},{3,5},{5,7},{7,1},{8,10},{10,12},{12... | collective-permute-start | bytes 196616 | tf_op jit(solution)/shard_map/ppermute | solution.py:715
  27.4 7.1 %collective-permute-start.9 = (f32[64,256]{1,0:T(8,128)S(1)}, f32[64,256]{1,0:T(8,128)S(1)}, u32[]{:S(2)}, u32[]{:S(2)}) collective-permute-start(f32[64,256]{1,0:T(8,128)S(1)} %get-tuple-element.67), channel_id=1, source_target_pairs={{0,4},{2,6},{4,0},{6,2},{1,5},{3,7},{5,1},{7,3},{8,12},{10,14},{12... | collective-permute-start | bytes 196616 | tf_op jit(solution)/shard_map/ppermute | solution.py:715
  29.9 5.0 %collective-permute-start.10 = (f32[64,256]{1,0:T(8,128)S(1)}, f32[64,256]{1,0:T(8,128)S(1)}, u32[]{:S(2)}, u32[]{:S(2)}) collective-permute-start(f32[64,256]{1,0:T(8,128)S(1)} %get-tuple-element.68), channel_id=1, source_target_pairs={{0,6},{2,0},{4,2},{6,4},{1,7},{3,1},{5,3},{7,5},{8,14},{10,8},{12,... | collective-permute-start | bytes 196616 | tf_op jit(solution)/shard_map/ppermute | solution.py:715

commit v5 on v4

--- a/solution.py
+++ b/solution.py
@@ -97,7 +97,7 @@
     sources = take(9)
     outproj_source, message = take(2)
     places = take(9)
-    semaphores = take(1)[0]
+    top, semaphores = take(2)
     half = ch // 2
     base = V + 2 + 3 * hl
     core = lax.rem(lax.axis_index("seq"), 2)
@@ -106,6 +106,7 @@
         places + [message.at[base : base + half, 0:D]],
         semaphores,
     )
+    flip = (iota((T, T), 0) + iota((T, T), 1) == T - 1).astype(f32).astype(bf16)
     for copy in copies[:9]:
         copy.wait()
     (inproj, tok, emb, prenorm, stepmap, bias, rates, skip, outnorm) = places
@@ -113,40 +114,46 @@
     raw_t = dot_split(split2(stepmap[...]), normed, NT)
     gate = dot_split(normed, split2(inproj[pl.ds(0, D, stride=2), :]))
     inner = dot_split(normed, split2(inproj[pl.ds(1, D, stride=2), :]))
-    message[0:V, 0:ch] = gate
-    message[0:V, ch : 2 * ch] = inner
-    flip = (iota((T, T), 0) + iota((T, T), 1) == T - 1).astype(f32).astype(bf16)
+    top[0:V, 0:ch] = gate
+    top[0:V, ch : 2 * ch] = inner
     tokens = jnp.broadcast_to(tok[...].astype(f32), (8, T)).astype(bf16)
-    message[V : V + 1, 0:T] = dot(tokens, flip)[0:1]
-    message[V + 1 : V + 2, 0:ch] = outnorm[...]
+    top[V : V + 1, 0:T] = dot(tokens, flip)[0:1]
+    top[V + 1 : V + 2, 0:ch] = outnorm[...]
     for head in range(hl):
         line = softplus(raw_t[head : head + 1, :] + bias[:, head : head + 1])
         row = V + 2 + head
-        message[row : row + 1, 0:V] = line
-        message[row + hl : row + hl + 1, 0:V] = -rates[:, head : head + 1] * line
-        message[row + 2 * hl : row + 2 * hl + 1, 0:V] = jnp.broadcast_to(
+        top[row : row + 1, 0:V] = line
+        top[row + hl : row + hl + 1, 0:V] = -rates[:, head : head + 1] * line
+        top[row + 2 * hl : row + 2 * hl + 1, 0:V] = jnp.broadcast_to(
             skip[:, head : head + 1], (1, V)
         )
+    last = pltpu.make_async_copy(top, message.at[0:base, :], semaphores.at[10])
+    last.start()
     copies[9].wait()
+    last.wait()
 
 
 def prepare_kernel(dims, *refs):
     V, D, hl, ch, nh, ns, T, N = dims
-    H, P = nh * hl, ch // hl
+    P = ch // hl
     refs = list(refs)
 
     def take(number):
         taken, refs[:] = refs[:number], refs[number:]
         return taken
 
-    emb, prenorm, statemap, complement, outproj = take(5)
-    prenorm2, inproj2, statemap2, stepmap2, bias2, rates2, skip2, outnorm2, outproj2 = take(9)
-    pairs, small, choose_out, own_high, own_low = take(5)
+    sources = take(11)
+    small, choose_out, own_high, own_low = take(4)
     state_high, state_low, rest_high, rest_low, out_high, out_low = take(6)
-    normed = split2(rms(emb[...]) * prenorm[...])
-    write = dot_split(normed, split2(statemap[pl.ds(0, D, stride=2), :]))
-    read = dot_split(normed, split2(statemap[pl.ds(1, D, stride=2), :]))
-    pairs[...] = dot3(read, jnp.concatenate([write] * H, axis=0), NT)
+    places = take(11)
+    semaphores = take(1)[0]
+    copies = fetch(sources, places, semaphores)
+    for copy in copies:
+        copy.wait()
+    complement, outproj, prenorm2, inproj2, statemap2, stepmap2 = places[:6]
+    bias2, rates2, skip2, outnorm2, outproj2 = places[6:]
+    out_gain = jnp.transpose(jnp.broadcast_to(outnorm2[...], (128, ch)))
+    out_high[...], out_low[...] = split2(outproj2[...] * out_gain[:, 0:1])
     own_high[...], own_low[...] = split2(outproj[...])
     choose = (complement[...] == iota((D, D), 0)).astype(f32).astype(bf16)
     choose_out[...] = choose
@@ -169,14 +176,20 @@
     gate = inproj2[pl.ds(0, D, stride=2), :] * gain_wide
     read2 = statemap2[pl.ds(1, D, stride=2), :] * gain_wide
     rest_high[...], rest_low[...] = weights(jnp.concatenate([gate, read2], axis=1))
-    out_gain = jnp.transpose(jnp.broadcast_to(outnorm2[...], (128, ch)))
-    out_high[...], out_low[...] = split2(outproj2[...] * out_gain[:, 0:1])
     lane_head = iota((1, ch), 1) // P
     for place, ref in ((0, bias2), (1, rates2), (2, skip2)):
         line = jnp.zeros((1, ch), f32)
         for head in range(hl):
-            line = jnp.where(lane_head == head, ref[head], line)
+            line = jnp.where(lane_head == head, ref[:, head : head + 1], line)
         small[place : place + 1, :] = line
+
+
+def pairs_kernel(dims, emb, prenorm, statemap, small, pairs):
+    V, D, hl, ch, nh, ns, T, N = dims
+    normed = split2(rms(emb[...]) * prenorm[...])
+    write = dot_split(normed, split2(statemap[pl.ds(0, D, stride=2), :]))
+    read = dot_split(normed, split2(statemap[pl.ds(1, D, stride=2), :]))
+    pairs[...] = dot3(read, jnp.concatenate([write] * (nh * hl), axis=0), NT)
 
 
 def shift_rows(value, amount, fill):
@@ -526,8 +539,8 @@
     def flat(value):
         return value.reshape(-1, value.shape[-1])
 
-    def cost(flops):
-        return pl.CostEstimate(flops=flops, bytes_accessed=4 * T * D, transcendentals=T * D)
+    light = pl.CostEstimate(flops=1000, bytes_accessed=1000, transcendentals=0)
+    heavy = pl.CostEstimate(flops=960 * T * D * D, bytes_accessed=4 * T * D, transcendentals=T * D)
 
     head_rows = V + 2 + 3 * hl
     half = ch // 2
@@ -548,31 +561,27 @@
         functools.partial(tables_kernel, dims),
         out_shape=shape(head_rows + half, width),
         in_specs=[anywhere] * (len(fetched) + 1),
-        out_specs=vmem,
+        out_specs=anywhere,
         scratch_shapes=[room(value) for value in fetched]
-        + [pltpu.SemaphoreType.DMA((len(fetched) + 1,))],
+        + [pltpu.VMEM((head_rows, width), f32), pltpu.SemaphoreType.DMA((len(fetched) + 2,))],
         compiler_params=pltpu.CompilerParams(vmem_limit_bytes=TABLES_LIMIT),
         name="tables",
     )(*fetched, outproj_first)
 
     prepared = [
-        embedding,
-        line(prenorm_first),
-        flat(statemap_first),
         line(complement),
         outproj_first,
         line(prenorm_second),
         flat(inproj_second),
         flat(statemap_second),
         stepmap_second.T,
-        stepbias_second,
-        rates_second,
-        skipgain_second,
+        line(stepbias_second),
+        line(rates_second),
+        line(skipgain_second),
         line(outnorm_second),
         outproj_second,
     ]
     (
-        pair_table,
         small,
         choose,
         own_high,
@@ -586,7 +595,6 @@
     ) = pl.pallas_call(
         functools.partial(prepare_kernel, dims),
         out_shape=(
-            shape(V, LV),
             shape(8, ch),
             shape(D, D, dtype=bf16),
             *halves(ch, D),
@@ -594,12 +602,23 @@
             *halves(D, ch + N),
             *halves(ch, D),
         ),
-        in_specs=[vmem] * 9 + [smem] * 3 + [vmem] * 2,
-        out_specs=(vmem,) * 11,
-        compiler_params=params,
-        cost_estimate=cost(6 * T * D * D * 4),
+        in_specs=[anywhere] * len(prepared),
+        out_specs=(vmem,) * 10,
+        scratch_shapes=[room(value) for value in prepared]
+        + [pltpu.SemaphoreType.DMA((len(prepared),))],
+        compiler_params=pltpu.CompilerParams(vmem_limit_bytes=TABLES_LIMIT),
+        cost_estimate=heavy,
         name="prepare",
     )(*prepared)
+    pair_table = pl.pallas_call(
+        functools.partial(pairs_kernel, dims),
+        out_shape=shape(V, LV),
+        in_specs=[vmem] * 4,
+        out_specs=vmem,
+        compiler_params=params,
+        cost_estimate=light,
+        name="pairs",
+    )(embedding, line(prenorm_first), flat(statemap_first), small)
 
     messages = [message]
     for k in range(1, max(ns, nh)):
@@ -620,7 +639,7 @@
         out_specs=(vmem,) * 3,
         scratch_shapes=[pltpu.VMEM((max(ns, 8), T), f32)],
         compiler_params=params,
-        cost_estimate=cost(6 * T * D * D * 16),
+        cost_estimate=heavy,
         name="mix",
     )(*messages[::-1], embedding, pair_table)
 
@@ -659,7 +678,7 @@
         out_specs=(vmem,) * 4,
         scratch_shapes=[pltpu.VMEM((T, D), f32)],
         compiler_params=params,
-        cost_estimate=cost(6 * T * D * D * 8),
+        cost_estimate=heavy,
         name="block",
     )(
         hidden_high,

time: 35.7 us -> 37.4 us (1.048)
  Pallas kernels: 8.62 us -> 11.7 us
  local copies, waits for them, and re-layouts: 3.52 us -> 2.05 us
  starting transfers between devices: 14.2 us -> 14.7 us
  waiting for transfers between devices: 8.38 us -> 7.91 us
    pallas_call x1, Pallas kernels: 1.3 us -> 2.84 us  [per_device(): pl.pallas_call(functools.partial(prepare_kernel, dims), out_shape=(shape(...]
    unnamed x30, local copies, waits for them, and re-layouts: 3.52 us -> 2.05 us
    pallas_call x1, Pallas kernels: 2.04 us -> 3.2 us  [per_device(): pl.pallas_call(functools.partial(tables_kernel, dims), out_shape=shape(he...]
  transfers between devices with their start and end apart: 11 -> 11, of which waited for: 5 -> 5; matrix products, arithmetic and copies ran while one was open for 0% -> 0% of each run, Pallas kernels for 12% -> 17%
where the time goes in v5:
time: 37.4 us; the launch traced here: 37.1 us
  starting transfers between devices  14.7 us (39%)
  Pallas kernels  11.7 us (31%)
  waiting for transfers between devices  7.91 us (21%)
  local copies, waits for them, and re-layouts  2.05 us (5%)
  other arithmetic  0.65 us (2%)
    ppermute x3, starting transfers between devices, per_device(): messages.append(lax.ppermute(sent, ('seq', 'head'), pairs))  8.28 us
    ppermute x3, waiting for transfers between devices, per_device(): result = result + lax.ppermute(parts[k], 'head', pairs)  4.81 us
    ppermute x3, starting transfers between devices, per_device(): result = result + lax.ppermute(parts[k], 'head', pairs)  4.14 us
    pallas_call x1, Pallas kernels, per_device(): pl.pallas_call(functools.partial(tables_kernel, dims), out_shape=shape(he...  3.2 us
    ppermute x2, waiting for transfers between devices, per_device(): lax.ppermute(state, 'seq', [(seq, seq ^ 2 ** bit) for seq in range(ns)])  3.09 us
    pallas_call x1, Pallas kernels, per_device(): pl.pallas_call(functools.partial(prepare_kernel, dims), out_shape=(shape(...  2.84 us
    unnamed x30, local copies, waits for them, and re-layouts  2.05 us
    pallas_call x1, Pallas kernels, per_device(): pl.pallas_call(functools.partial(mix_kernel, dims), out_shape=(*halves(T,...  1.85 us
  transfers between devices with their start and end apart: 11, of which 5 were waited for; matrix products, arithmetic and copies ran while one was open for 0% of the time, Pallas kernels for 17%

profile of v5, /device:TPU:0, one launch (start us, length us, event | category | flops | bytes accessed | tf_op | source)
XLA Modules:
  0.0 37.1 jit_solution(5280672619475177299)
XLA Ops:
  0.0 3.2 %tables.1.refs_3_ = f32[88,256]{1,0:T(8,128)} custom-call(f32[512,128]{1,0:T(8,128)} %bitcast.21, s32[1,256]{1,0:T(1,128)} %bitcast.23, f32[16,256]{1,0:T(8,128)} %refs_4_.1, f32[1,256]{1,0:T(1,128)} %bitcast.19, f32[2,256]{1,0:T(2,128)} %bitcast.22, f32[1,2]{1,0:T(1,128)} %bitcast.24, f32[1,2]{1,0:T(1,128)} %bitcast.25, f32[1,2]{1,0:T(1,128)} %bitcast.26, ...), custom_call_target="tpu_custom_call" | custom-call | tf_op jit(solution)/shard_map/tables/pallas_call | solution.py:560
  3.2 2.5 %collective-permute-start.2 = (f32[88,256]{1,0:T(8,128)}, f32[88,256]{1,0:T(8,128)S(1)}, u32[]{:S(2)}, u32[]{:S(2)}) collective-permute-start(f32[88,256]{1,0:T(8,128)} %tables.1.refs_3_), channel_id=1, source_target_pairs={{0,10},{2,12},{4,14},{6,8},{8,18},{10,20},{12,22},{14,16},{16,26},... | collective-permute-start | bytes 270344 | tf_op jit(solution)/shard_map/ppermute | solution.py:631
  5.7 3.5 %collective-permute-start.1 = (f32[88,256]{1,0:T(8,128)}, f32[88,256]{1,0:T(8,128)S(1)}, u32[]{:S(2)}, u32[]{:S(2)}) collective-permute-start(f32[88,256]{1,0:T(8,128)} %tables.1.refs_3_), channel_id=1, source_target_pairs={{0,20},{2,22},{4,16},{6,18},{8,28},{10,30},{12,24},{14,26},{16,4},... | collective-permute-start | bytes 270344 | tf_op jit(solution)/shard_map/ppermute | solution.py:631
  9.2 2.2 %collective-permute-start = (f32[88,256]{1,0:T(8,128)}, f32[88,256]{1,0:T(8,128)S(1)}, u32[]{:S(2)}, u32[]{:S(2)}) collective-permute-start(f32[88,256]{1,0:T(8,128)} %tables.1.refs_3_), channel_id=1, source_target_pairs={{0,30},{2,24},{4,26},{6,28},{8,6},{10,0},{12,2},{14,4},{16,14},{18... | collective-permute-start | bytes 270344 | tf_op jit(solution)/shard_map/ppermute | solution.py:631
  11.5 2.8 %prepare.1 = (f32[8,128]{1,0:T(8,128)}, bf16[256,256]{1,0:T(8,128)(2,1)}, bf16[128,256]{1,0:T(8,128)(2,1)}, bf16[128,256]{1,0:T(8,128)(2,1)}, bf16[256,384]{1,0:...) custom-call(s32[1,256]{1,0:T(1,128)} %bitcast.31, ...), custom_call_target="tpu_custom_call" | custom-call | flops 16106127360 | bytes 262144 | tf_op jit(solution)/shard_map/prepare/pallas_call | solution.py:595
  14.3 0.0 copy-start.11
  14.4 0.0 copy-done
  14.4 0.0 copy-done.6
  14.4 0.7 %copy-done.11 = f32[256]{0:T(256)S(1)} copy-done((f32[256]{0:T(256)S(1)}, f32[256]{0:T(256)}, u32[]{:S(2)}) %copy-start.11) | copy-done | bytes 1048
  15.0 0.7 %copy-done.9 = f32[8,128]{1,0:T(8,128)S(1)} copy-done((f32[8,128]{1,0:T(8,128)S(1)}, f32[8,128]{1,0:T(8,128)}, u32[]{:S(2)}) %copy-start.9) | copy-done | bytes 4120
  15.7 0.4 pairs.1.refs_5_
  16.1 0.0 copy-start.4
  16.1 0.0 copy-start.5
  16.1 0.0 collective-permute-done.2.refs_2_.refs_10_
  16.1 0.1 collective-permute-start.5
  16.2 0.0 collective-permute-done.1.refs_1_.refs_9_
  16.2 0.5 %collective-permute-start.4 = (f32[88,256]{1,0:T(8,128)S(1)}, f32[88,256]{1,0:T(8,128)S(1)}, u32[]{:S(2)}, u32[]{:S(2)}) collective-permute-start(f32[88,256]{1,0:T(8,128)S(1)} %collective-permute-done.1.refs_1_.refs_9_), channel_id=1, source_target_pairs={{0,8},{8,0},{16,24},{24,16},{1,9},{9,1},{17,25},{25,17},{2,10},{10... | collective-permute-start | bytes 270344 | tf_op jit(solution)/shard_map/ppermute | solution.py:633
  16.7 0.0 collective-permute-done.refs_0_.refs_8_
  16.7 0.1 collective-permute-start.3
  16.8 0.0 copy-done.3
  16.8 1.9 %mix.1 = (bf16[256,512]{1,0:T(8,128)(2,1)S(1)}, bf16[256,512]{1,0:T(8,128)(2,1)S(1)}, f32[256,256]{1,0:T(8,128)S(1)}) custom-call(f32[88,256]{1,0:T(8,128)S(1)} %collective-permute-done.refs_0_.refs_8_, f32[88,256]{1,0:T(8,128)S(1)} %collective-permute-done.1.refs_1_.refs_9_, f32[88,256]{1,0:T(8,128)S(1)} %collective-permute-done.2.refs_2_.refs_10_, ...), custom_call_target="tpu_custom_call" | custom-call | flops 16106127360 | bytes 262144 | tf_op jit(solution)/shard_map/mix/pallas_call | solution.py:635
  18.7 0.0 collective-permute-done.5.refs_13_
  18.7 0.0 collective-permute-done.4.refs_12_
  18.7 0.0 collective-permute-done.3.refs_11_
  18.7 0.0 copy-start.10
  18.7 0.0 copy-done.1
  18.7 0.0 copy-done.2
  18.7 0.0 copy-done.4
  18.7 0.0 copy-done.5
  18.7 0.6 %copy-done.10 = f32[8,128]{1,0:T(8,128)S(1)} copy-done((f32[8,128]{1,0:T(8,128)S(1)}, f32[8,128]{1,0:T(8,128)}, u32[]{:S(2)}) %copy-start.10) | copy-done | bytes 4120
  19.4 1.5 %project.1 = (f32[136,128]{1,0:T(8,128)S(1)}, bf16[256,256]{1,0:T(8,128)(2,1)S(1)}, bf16[256,256]{1,0:T(8,128)(2,1)S(1)}, f32[256,128]{1,0:T(8,128)S(1)}, f32[25...) custom-call(bf16[256,512]{1,0:T(8,128)(2,1)S(1)} %get-tuple-element.37.refs_0_, ...), custom_call_target="tpu_custom_call" | custom-call | tf_op jit(solution)/shard_map/project/pallas_call | solution.py:646
  20.9 0.0 copy-start.12
  20.9 0.5 %collective-permute-start.6 = (f32[136,128]{1,0:T(8,128)S(1)}, f32[136,128]{1,0:T(8,128)S(1)}, u32[]{:S(2)}, u32[]{:S(2)}) collective-permute-start(f32[136,128]{1,0:T(8,128)S(1)} %get-tuple-element.44.refs_0_), channel_id=1, source_target_pairs={{0,8},{8,0},{16,24},{24,16},{1,9},{9,1},{17,25},{25,17},{2,10},{10... | collective-permute-start | bytes 208904 | tf_op jit(solution)/shard_map/ppermute | solution.py:700
  21.4 0.9 %collective-permute-done.6.refs_1_ = f32[136,128]{1,0:T(8,128)S(1)} collective-permute-done((f32[136,128]{1,0:T(8,128)S(1)}, f32[136,128]{1,0:T(8,128)S(1)}, u32[]{:S(2)}, u32[]{:S(2)}) %collective-permute-start.6) | collective-permute-done | bytes 69664 | tf_op jit(solution)/shard_map/ppermute | solution.py:700
  22.3 1.1 %collective-permute-start.7 = (f32[136,128]{1,0:T(8,128)S(1)}, f32[136,128]{1,0:T(8,128)S(1)}, u32[]{:S(2)}, u32[]{:S(2)}) collective-permute-start(f32[136,128]{1,0:T(8,128)S(1)} %get-tuple-element.46), channel_id=1, source_target_pairs={{0,16},{8,24},{16,0},{24,8},{1,17},{9,25},{17,1},{25,9},{2,18},{10... | collective-permute-start | bytes 208904 | tf_op jit(solution)/shard_map/ppermute | solution.py:700
  23.5 0.0 copy-done.13
  23.5 0.0 copy-done.14
  23.5 0.0 copy-done.12
  23.5 1.2 %block.1 = (f32[256,128]{1,0:T(8,128)S(1)}, f32[256,128]{1,0:T(8,128)S(1)}, f32[256,128]{1,0:T(8,128)S(1)}, f32[64,256]{1,0:T(8,128)S(1)}) custom-call(bf16[256,256]{1,0:T(8,128)(2,1)S(1)} %get-tuple-element.47.refs_0_, bf16[256,256]{1,0:T(8,128)(2,1)S(1)} %get-tuple-element.48.refs_1_, f32[256,128]{1,0:T(8,128)S(1)} %get-tuple-element.49.refs_2_, ...), custom_call_target="tpu_custom_call" | custom-call | flops 16106127360 | bytes 262144 | tf_op jit(solution)/shard_map/block/pallas_call | solution.py:674
  24.7 2.2 %collective-permute-done.7.refs_1_ = f32[136,128]{1,0:T(8,128)S(1)} collective-permute-done((f32[136,128]{1,0:T(8,128)S(1)}, f32[136,128]{1,0:T(8,128)S(1)}, u32[]{:S(2)}, u32[]{:S(2)}) %collective-permute-start.7) | collective-permute-done | bytes 69664 | tf_op jit(solution)/shard_map/ppermute | solution.py:700
  26.8 0.7 %output.1 = (f32[64,256]{1,0:T(8,128)S(1)}, f32[64,256]{1,0:T(8,128)S(1)}, f32[64,256]{1,0:T(8,128)S(1)}, f32[64,256]{1,0:T(8,128)S(1)}) custom-call(f32[136,128]{1,0:T(8,128)S(1)} %get-tuple-element.45.refs_0_, f32[136,128]{1,0:T(8,128)S(1)} %collective-permute-done.7.refs_1_, f32[256,128]{1,0:T(8,128)S(1)} %get-tuple-element.57.refs_2_, ...), custom_call_target="tpu_custom_call" | custom-call | tf_op jit(solution)/shard_map/output/pallas_call | solution.py:722
  27.5 1.7 %collective-permute-start.8 = (f32[64,256]{1,0:T(8,128)S(1)}, f32[64,256]{1,0:T(8,128)S(1)}, u32[]{:S(2)}, u32[]{:S(2)}) collective-permute-start(f32[64,256]{1,0:T(8,128)S(1)} %get-tuple-element.64), channel_id=1, source_target_pairs={{0,2},{2,4},{4,6},{6,0},{1,3},{3,5},{5,7},{7,1},{8,10},{10,12},{12... | collective-permute-start | bytes 196616 | tf_op jit(solution)/shard_map/ppermute | solution.py:734
  29.2 2.4 %collective-permute-start.9 = (f32[64,256]{1,0:T(8,128)S(1)}, f32[64,256]{1,0:T(8,128)S(1)}, u32[]{:S(2)}, u32[]{:S(2)}) collective-permute-start(f32[64,256]{1,0:T(8,128)S(1)} %get-tuple-element.65), channel_id=1, source_target_pairs={{0,4},{2,6},{4,0},{6,2},{1,5},{3,7},{5,1},{7,3},{8,12},{10,14},{12... | collective-permute-start | bytes 196616 | tf_op jit(solution)/shard_map/ppermute | solution.py:734
  31.7 0.0 collective-permute-start.10
  31.7 2.5 %collective-permute-done.8 = f32[64,256]{1,0:T(8,128)S(1)} collective-permute-done((f32[64,256]{1,0:T(8,128)S(1)}, f32[64,256]{1,0:T(8,128)S(1)}, u32[]{:S(2)}, u32[]{:S(2)}) %collective-permute-start.8) | collective-permute-done | bytes 65568 | tf_op jit(solution)/shard_map/ppermute | solution.py:734
  34.2 1.9 %collective-permute-done.9 = f32[64,256]{1,0:T(8,128)S(1)} collective-permute-done((f32[64,256]{1,0:T(8,128)S(1)}, f32[64,256]{1,0:T(8,128)S(1)}, u32[]{:S(2)}, u32[]{:S(2)}) %collective-permute-start.9) | collective-permute-done | bytes 65568 | tf_op jit(solution)/shard_map/ppermute | solution.py:734
  36.1 0.4 %collective-permute-done.10 = f32[64,256]{1,0:T(8,128)S(1)} collective-permute-done((f32[64,256]{1,0:T(8,128)S(1)}, f32[64,256]{1,0:T(8,128)S(1)}, u32[]{:S(2)}, u32[]{:S(2)}) %collective-permute-start.10) | collective-permute-done | bytes 65568 | tf_op jit(solution)/shard_map/ppermute | solution.py:734
  36.5 0.6 %add_add_fusion = f32[64,256]{1,0:T(8,128)} fusion(f32[64,256]{1,0:T(8,128)S(1)} %collective-permute-done.10, f32[64,256]{1,0:T(8,128)S(1)} %collective-permute-done.9, f32[64,256]{1,0:T(8,128)S(1)} %get-tuple-element.63, f32[64,256]{1,0:T(8,128)S(1)} %collective-permute-done.8), kind=kLoop, calls=%fused_computation | loop fusion | flops 49152 | bytes 327680 | tf_op jit(solution)/shard_map/add | solution.py:734
  (13 shorter events, 0.0 us)
Async XLA Ops:
  3.2 12.9 %collective-permute-start.2 = (f32[88,256]{1,0:T(8,128)}, f32[88,256]{1,0:T(8,128)S(1)}, u32[]{:S(2)}, u32[]{:S(2)}) collective-permute-start(f32[88,256]{1,0:T(8,128)} %tables.1.refs_3_), channel_id=1, source_target_pairs={{0,10},{2,12},{4,14},{6,8},{8,18},{10,20},{12,22},{14,16},{16,26},... | collective-permute-start | bytes 270344 | tf_op jit(solution)/shard_map/ppermute | solution.py:631
  5.7 10.5 %collective-permute-start.1 = (f32[88,256]{1,0:T(8,128)}, f32[88,256]{1,0:T(8,128)S(1)}, u32[]{:S(2)}, u32[]{:S(2)}) collective-permute-start(f32[88,256]{1,0:T(8,128)} %tables.1.refs_3_), channel_id=1, source_target_pairs={{0,20},{2,22},{4,16},{6,18},{8,28},{10,30},{12,24},{14,26},{16,4},... | collective-permute-start | bytes 270344 | tf_op jit(solution)/shard_map/ppermute | solution.py:631
  9.2 7.5 %collective-permute-start = (f32[88,256]{1,0:T(8,128)}, f32[88,256]{1,0:T(8,128)S(1)}, u32[]{:S(2)}, u32[]{:S(2)}) collective-permute-start(f32[88,256]{1,0:T(8,128)} %tables.1.refs_3_), channel_id=1, source_target_pairs={{0,30},{2,24},{4,26},{6,28},{8,6},{10,0},{12,2},{14,4},{16,14},{18... | collective-permute-start | bytes 270344 | tf_op jit(solution)/shard_map/ppermute | solution.py:631
  11.5 2.9 %copy-start = (f32[256,2,128]{2,1,0:T(2,128)S(1)}, f32[256,2,128]{2,1,0:T(2,128)}, u32[]{:S(2)}) copy-start(f32[256,2,128]{2,1,0:T(2,128)} %param.26) | copy-start | bytes 786436
  11.5 2.9 %copy-start.6 = (f32[16,256]{1,0:T(8,128)S(1)}, f32[16,256]{1,0:T(8,128)}, u32[]{:S(2)}) copy-start(f32[16,256]{1,0:T(8,128)} %refs_4_.1) | copy-start | bytes 49156
  14.3 0.7 %copy-start.11 = (f32[256]{0:T(256)S(1)}, f32[256]{0:T(256)}, u32[]{:S(2)}) copy-start(f32[256]{0:T(256)} %param.24) | copy-start | bytes 3076
  15.0 0.7 %copy-start.9 = (f32[8,128]{1,0:T(8,128)S(1)}, f32[8,128]{1,0:T(8,128)}, u32[]{:S(2)}) copy-start(f32[8,128]{1,0:T(8,128)} %get-tuple-element.36.small.refs_3_.refs_7_) | copy-start | bytes 12292
  15.7 1.1 %copy-start.3 = (f32[88,256]{1,0:T(8,128)S(1)}, f32[88,256]{1,0:T(8,128)}, u32[]{:S(2)}) copy-start(f32[88,256]{1,0:T(8,128)} %tables.1.refs_3_) | copy-start | bytes 270340
  16.1 2.7 %copy-start.1 = (bf16[256,384]{1,0:T(8,128)(2,1)S(1)}, bf16[256,384]{1,0:T(8,128)(2,1)}, u32[]{:S(2)}) copy-start(bf16[256,384]{1,0:T(8,128)(2,1)} %get-tuple-element.42.refs_6_) | copy-start | bytes 589828
  16.1 2.7 %copy-start.2 = (bf16[256,384]{1,0:T(8,128)(2,1)S(1)}, bf16[256,384]{1,0:T(8,128)(2,1)}, u32[]{:S(2)}) copy-start(bf16[256,384]{1,0:T(8,128)(2,1)} %get-tuple-element.43.refs_7_) | copy-start | bytes 589828
  16.1 2.7 %copy-start.4 = (bf16[128,256]{1,0:T(8,128)(2,1)S(1)}, bf16[128,256]{1,0:T(8,128)(2,1)}, u32[]{:S(2)}) copy-start(bf16[128,256]{1,0:T(8,128)(2,1)} %get-tuple-element.40.refs_4_) | copy-start | bytes 196612
  16.1 2.6 %copy-start.5 = (bf16[128,256]{1,0:T(8,128)(2,1)S(1)}, bf16[128,256]{1,0:T(8,128)(2,1)}, u32[]{:S(2)}) copy-start(bf16[128,256]{1,0:T(8,128)(2,1)} %get-tuple-element.41.refs_5_) | copy-start | bytes 196612
  16.1 2.5 %collective-permute-start.5 = (f32[88,256]{1,0:T(8,128)S(1)}, f32[88,256]{1,0:T(8,128)S(1)}, u32[]{:S(2)}, u32[]{:S(2)}) collective-permute-start(f32[88,256]{1,0:T(8,128)S(1)} %collective-permute-done.2.refs_2_.refs_10_), channel_id=1, source_target_pairs={{0,8},{8,0},{16,24},{24,16},{1,9},{9,1},{17,25},{25,17},{2,10},{10... | collective-permute-start | bytes 270344 | tf_op jit(solution)/shard_map/ppermute | solution.py:633
  16.2 2.5 %collective-permute-start.4 = (f32[88,256]{1,0:T(8,128)S(1)}, f32[88,256]{1,0:T(8,128)S(1)}, u32[]{:S(2)}, u32[]{:S(2)}) collective-permute-start(f32[88,256]{1,0:T(8,128)S(1)} %collective-permute-done.1.refs_1_.refs_9_), channel_id=1, source_target_pairs={{0,8},{8,0},{16,24},{24,16},{1,9},{9,1},{17,25},{25,17},{2,10},{10... | collective-permute-start | bytes 270344 | tf_op jit(solution)/shard_map/ppermute | solution.py:633
  16.7 2.0 %collective-permute-start.3 = (f32[88,256]{1,0:T(8,128)S(1)}, f32[88,256]{1,0:T(8,128)S(1)}, u32[]{:S(2)}, u32[]{:S(2)}) collective-permute-start(f32[88,256]{1,0:T(8,128)S(1)} %collective-permute-done.refs_0_.refs_8_), channel_id=1, source_target_pairs={{0,8},{8,0},{16,24},{24,16},{1,9},{9,1},{17,25},{25,17},{2,10},{10... | collective-permute-start | bytes 270344 | tf_op jit(solution)/shard_map/ppermute | solution.py:633
  18.7 0.7 %copy-start.10 = (f32[8,128]{1,0:T(8,128)S(1)}, f32[8,128]{1,0:T(8,128)}, u32[]{:S(2)}) copy-start(f32[8,128]{1,0:T(8,128)} %get-tuple-element.36.small.refs_3_.refs_7_) | copy-start | bytes 12292
  19.4 4.1 %copy-start.13 = (bf16[256,256]{1,0:T(8,128)(2,1)S(1)}, bf16[256,256]{1,0:T(8,128)(2,1)}, u32[]{:S(2)}) copy-start(bf16[256,256]{1,0:T(8,128)(2,1)} %get-tuple-element.55.refs_9_) | copy-start | bytes 393220
  19.4 4.1 %copy-start.14 = (bf16[256,256]{1,0:T(8,128)(2,1)S(1)}, bf16[256,256]{1,0:T(8,128)(2,1)}, u32[]{:S(2)}) copy-start(bf16[256,256]{1,0:T(8,128)(2,1)} %get-tuple-element.56.refs_10_) | copy-start | bytes 393220
  20.9 2.6 %copy-start.12 = (bf16[256,256]{1,0:T(8,128)(2,1)S(1)}, bf16[256,256]{1,0:T(8,128)(2,1)}, u32[]{:S(2)}) copy-start(bf16[256,256]{1,0:T(8,128)(2,1)} %get-tuple-element.54.refs_8_) | copy-start | bytes 393220
  20.9 1.4 %collective-permute-start.6 = (f32[136,128]{1,0:T(8,128)S(1)}, f32[136,128]{1,0:T(8,128)S(1)}, u32[]{:S(2)}, u32[]{:S(2)}) collective-permute-start(f32[136,128]{1,0:T(8,128)S(1)} %get-tuple-element.44.refs_0_), channel_id=1, source_target_pairs={{0,8},{8,0},{16,24},{24,16},{1,9},{9,1},{17,25},{25,17},{2,10},{10... | collective-permute-start | bytes 208904 | tf_op jit(solution)/shard_map/ppermute | solution.py:700
  22.3 4.5 %collective-permute-start.7 = (f32[136,128]{1,0:T(8,128)S(1)}, f32[136,128]{1,0:T(8,128)S(1)}, u32[]{:S(2)}, u32[]{:S(2)}) collective-permute-start(f32[136,128]{1,0:T(8,128)S(1)} %get-tuple-element.46), channel_id=1, source_target_pairs={{0,16},{8,24},{16,0},{24,8},{1,17},{9,25},{17,1},{25,9},{2,18},{10... | collective-permute-start | bytes 208904 | tf_op jit(solution)/shard_map/ppermute | solution.py:700
  23.5 3.4 %copy-start.7 = (bf16[128,256]{1,0:T(8,128)(2,1)S(1)}, bf16[128,256]{1,0:T(8,128)(2,1)}, u32[]{:S(2)}) copy-start(bf16[128,256]{1,0:T(8,128)(2,1)} %get-tuple-element.61.refs_7_) | copy-start | bytes 196612
  23.5 3.4 %copy-start.8 = (bf16[128,256]{1,0:T(8,128)(2,1)S(1)}, bf16[128,256]{1,0:T(8,128)(2,1)}, u32[]{:S(2)}) copy-start(bf16[128,256]{1,0:T(8,128)(2,1)} %get-tuple-element.62.refs_8_) | copy-start | bytes 196612
  27.5 6.6 %collective-permute-start.8 = (f32[64,256]{1,0:T(8,128)S(1)}, f32[64,256]{1,0:T(8,128)S(1)}, u32[]{:S(2)}, u32[]{:S(2)}) collective-permute-start(f32[64,256]{1,0:T(8,128)S(1)} %get-tuple-element.64), channel_id=1, source_target_pairs={{0,2},{2,4},{4,6},{6,0},{1,3},{3,5},{5,7},{7,1},{8,10},{10,12},{12... | collective-permute-start | bytes 196616 | tf_op jit(solution)/shard_map/ppermute | solution.py:734
  29.2 6.8 %collective-permute-start.9 = (f32[64,256]{1,0:T(8,128)S(1)}, f32[64,256]{1,0:T(8,128)S(1)}, u32[]{:S(2)}, u32[]{:S(2)}) collective-permute-start(f32[64,256]{1,0:T(8,128)S(1)} %get-tuple-element.65), channel_id=1, source_target_pairs={{0,4},{2,6},{4,0},{6,2},{1,5},{3,7},{5,1},{7,3},{8,12},{10,14},{12... | collective-permute-start | bytes 196616 | tf_op jit(solution)/shard_map/ppermute | solution.py:734
  31.7 4.8 %collective-permute-start.10 = (f32[64,256]{1,0:T(8,128)S(1)}, f32[64,256]{1,0:T(8,128)S(1)}, u32[]{:S(2)}, u32[]{:S(2)}) collective-permute-start(f32[64,256]{1,0:T(8,128)S(1)} %get-tuple-element.66), channel_id=1, source_target_pairs={{0,6},{2,0},{4,2},{6,4},{1,7},{3,1},{5,3},{7,5},{8,14},{10,8},{12,... | collective-permute-start | bytes 196616 | tf_op jit(solution)/shard_map/ppermute | solution.py:734

commit v6 on v4

--- a/solution.py
+++ b/solution.py
@@ -106,6 +106,7 @@
         places + [message.at[base : base + half, 0:D]],
         semaphores,
     )
+    flip = (iota((T, T), 0) + iota((T, T), 1) == T - 1).astype(f32).astype(bf16)
     for copy in copies[:9]:
         copy.wait()
     (inproj, tok, emb, prenorm, stepmap, bias, rates, skip, outnorm) = places
@@ -115,7 +116,6 @@
     inner = dot_split(normed, split2(inproj[pl.ds(1, D, stride=2), :]))
     message[0:V, 0:ch] = gate
     message[0:V, ch : 2 * ch] = inner
-    flip = (iota((T, T), 0) + iota((T, T), 1) == T - 1).astype(f32).astype(bf16)
     tokens = jnp.broadcast_to(tok[...].astype(f32), (8, T)).astype(bf16)
     message[V : V + 1, 0:T] = dot(tokens, flip)[0:1]
     message[V + 1 : V + 2, 0:ch] = outnorm[...]
@@ -130,6 +130,15 @@
     copies[9].wait()
 
 
+def head_line(dims, values):
+    V, D, hl, ch, nh, ns, T, N = dims
+    head_of = iota((1, ch), 1) // (ch // hl)
+    line = jnp.zeros((1, ch), f32)
+    for head in range(hl):
+        line = jnp.where(head_of == head, values[head], line)
+    return line
+
+
 def prepare_kernel(dims, *refs):
     V, D, hl, ch, nh, ns, T, N = dims
     H, P = nh * hl, ch // hl
@@ -140,9 +149,10 @@
         return taken
 
     emb, prenorm, statemap, complement, outproj = take(5)
-    prenorm2, inproj2, statemap2, stepmap2, bias2, rates2, skip2, outnorm2, outproj2 = take(9)
+    prenorm2, inproj2, statemap2, stepmap2 = take(4)
+    bias2, rates2, skip2, outnorm2 = take(4)
     pairs, small, choose_out, own_high, own_low = take(5)
-    state_high, state_low, rest_high, rest_low, out_high, out_low = take(6)
+    state_high, state_low, rest_high, rest_low = take(4)
     normed = split2(rms(emb[...]) * prenorm[...])
     write = dot_split(normed, split2(statemap[pl.ds(0, D, stride=2), :]))
     read = dot_split(normed, split2(statemap[pl.ds(1, D, stride=2), :]))
@@ -169,14 +179,10 @@
     gate = inproj2[pl.ds(0, D, stride=2), :] * gain_wide
     read2 = statemap2[pl.ds(1, D, stride=2), :] * gain_wide
     rest_high[...], rest_low[...] = weights(jnp.concatenate([gate, read2], axis=1))
-    out_gain = jnp.transpose(jnp.broadcast_to(outnorm2[...], (128, ch)))
-    out_high[...], out_low[...] = split2(outproj2[...] * out_gain[:, 0:1])
-    lane_head = iota((1, ch), 1) // P
-    for place, ref in ((0, bias2), (1, rates2), (2, skip2)):
-        line = jnp.zeros((1, ch), f32)
-        for head in range(hl):
-            line = jnp.where(lane_head == head, ref[head], line)
-        small[place : place + 1, :] = line
+    small[0:1, :] = head_line(dims, bias2)
+    small[1:2, :] = head_line(dims, rates2)
+    small[2:3, :] = head_line(dims, skip2)
+    small[3:4, :] = outnorm2[...]
 
 
 def shift_rows(value, amount, fill):
@@ -389,9 +395,9 @@
         taken, refs[:] = refs[:number], refs[number:]
         return taken
 
-    high, low, scale, write, inner, stepped, total, small, choose = take(9)
-    rest_high, rest_low = take(2)
-    base, out_read, out_gate, own, hidden_ref = take(5)
+    high, low, scale, write, inner, stepped, total, choose = take(8)
+    rest_high, rest_low, small, outproj2 = take(4)
+    base, out_read, out_gate, own, out_high, out_low, hidden_ref = take(7)
     rows = dot_split((high[...], low[...]), (rest_high[...], rest_low[...]))
     out_gate[...] = silu(rows[:, 0:ch] * scale[...])
     read = rows[:, ch:] * scale[...]
@@ -417,6 +423,8 @@
     share = T // nh
     hidden_ref[...] = high[...].astype(f32) + low[...].astype(f32)
     place = pl.multiple_of(lax.axis_index("head") * share, 8)
+    out_gain = jnp.transpose(jnp.broadcast_to(small[3:4, :], (128, ch)))
+    out_high[...], out_low[...] = split2(outproj2[...] * out_gain[:, 0:1])
     own[...] = dot_right_exact(hidden_ref[pl.ds(place, share), :], choose[...])
 
 
@@ -526,8 +534,7 @@
     def flat(value):
         return value.reshape(-1, value.shape[-1])
 
-    def cost(flops):
-        return pl.CostEstimate(flops=flops, bytes_accessed=4 * T * D, transcendentals=T * D)
+    heavy = pl.CostEstimate(flops=960 * T * D * D, bytes_accessed=4 * T * D, transcendentals=T * D)
 
     head_rows = V + 2 + 3 * hl
     half = ch // 2
@@ -552,6 +559,7 @@
         scratch_shapes=[room(value) for value in fetched]
         + [pltpu.SemaphoreType.DMA((len(fetched) + 1,))],
         compiler_params=pltpu.CompilerParams(vmem_limit_bytes=TABLES_LIMIT),
+        cost_estimate=heavy,
         name="tables",
     )(*fetched, outproj_first)
 
@@ -569,7 +577,6 @@
         rates_second,
         skipgain_second,
         line(outnorm_second),
-        outproj_second,
     ]
     (
         pair_table,
@@ -581,8 +588,6 @@
         state_low,
         rest_high,
         rest_low,
-        proj_high,
-        proj_low,
     ) = pl.pallas_call(
         functools.partial(prepare_kernel, dims),
         out_shape=(
@@ -592,12 +597,11 @@
             *halves(ch, D),
             *halves(D, 2 * ch + N),
             *halves(D, ch + N),
-            *halves(ch, D),
         ),
-        in_specs=[vmem] * 9 + [smem] * 3 + [vmem] * 2,
-        out_specs=(vmem,) * 11,
+        in_specs=[vmem] * 9 + [smem] * 3 + [vmem],
+        out_specs=(vmem,) * 9,
         compiler_params=params,
-        cost_estimate=cost(6 * T * D * D * 4),
+        cost_estimate=heavy,
         name="prepare",
     )(*prepared)
 
@@ -620,7 +624,7 @@
         out_specs=(vmem,) * 3,
         scratch_shapes=[pltpu.VMEM((max(ns, 8), T), f32)],
         compiler_params=params,
-        cost_estimate=cost(6 * T * D * D * 16),
+        cost_estimate=heavy,
         name="mix",
     )(*messages[::-1], embedding, pair_table)
 
@@ -652,14 +656,14 @@
         *others[::-1],
     )
 
-    base, read, gate, own = pl.pallas_call(
+    base, read, gate, own, proj_high, proj_low = pl.pallas_call(
         functools.partial(block_kernel, dims),
-        out_shape=(shape(T, ch), shape(T, N), shape(T, ch), shape(share, D)),
-        in_specs=[vmem] * 11,
-        out_specs=(vmem,) * 4,
+        out_shape=(shape(T, ch), shape(T, N), shape(T, ch), shape(share, D), *halves(ch, D)),
+        in_specs=[vmem] * 12,
+        out_specs=(vmem,) * 6,
         scratch_shapes=[pltpu.VMEM((T, D), f32)],
         compiler_params=params,
-        cost_estimate=cost(6 * T * D * D * 8),
+        cost_estimate=heavy,
         name="block",
     )(
         hidden_high,
@@ -669,10 +673,11 @@
         inner,
         stepped,
         total,
-        small,
         choose,
         rest_high,
         rest_low,
+        small,
+        outproj_second,
     )
 
     prefix = None

time: 35.7 us -> 35.3 us (0.989)
  local copies, waits for them, and re-layouts: 3.52 us -> 0.65 us
  waiting for transfers between devices: 8.38 us -> 9.72 us
  starting transfers between devices: 14.2 us -> 15.2 us
    unnamed x30, local copies, waits for them, and re-layouts: 3.52 us -> 0.65 us
    ppermute x3, waiting for transfers between devices: 0.01 us -> 2.39 us  [per_device(): messages.append(lax.ppermute(sent, ('seq', 'head'), pairs))]
    ppermute x3, starting transfers between devices: 3.89 us -> 4.67 us  [per_device(): result = result + lax.ppermute(parts[k], 'head', pairs)]
    ppermute x2, waiting for transfers between devices: 3.37 us -> 2.77 us  [per_device(): lax.ppermute(state, 'seq', [(seq, seq ^ 2 ** bit) for seq in range(ns)])]
    ppermute x3, waiting for transfers between devices: 5 us -> 4.55 us  [per_device(): result = result + lax.ppermute(parts[k], 'head', pairs)]
  transfers between devices with their start and end apart: 11 -> 11, of which waited for: 5 -> 6; matrix products, arithmetic and copies ran while one was open for 0% -> 0% of each run, Pallas kernels for 12% -> 13%
where the time goes in v6:
time: 35.3 us; the launch traced here: 35.2 us
  starting transfers between devices  15.2 us (43%)
  waiting for transfers between devices  9.72 us (28%)
  Pallas kernels  8.75 us (25%)
  local copies, waits for them, and re-layouts  0.65 us (2%)
  other arithmetic  0.65 us (2%)
    ppermute x3, starting transfers between devices, per_device(): messages.append(lax.ppermute(sent, ('seq', 'head'), pairs))  8.29 us
    ppermute x3, starting transfers between devices, per_device(): result = result + lax.ppermute(parts[k], 'head', pairs)  4.67 us
    ppermute x3, waiting for transfers between devices, per_device(): result = result + lax.ppermute(parts[k], 'head', pairs)  4.55 us
    ppermute x2, waiting for transfers between devices, per_device(): lax.ppermute(state, 'seq', [(seq, seq ^ 2 ** bit) for seq in range(ns)])  2.77 us
    ppermute x3, waiting for transfers between devices, per_device(): messages.append(lax.ppermute(sent, ('seq', 'head'), pairs))  2.39 us
    pallas_call x1, Pallas kernels, per_device(): pl.pallas_call(functools.partial(tables_kernel, dims), out_shape=shape(he...  2.07 us
    pallas_call x1, Pallas kernels, per_device(): pl.pallas_call(functools.partial(mix_kernel, dims), out_shape=(*halves(T,...  1.85 us
    ppermute x2, starting transfers between devices, per_device(): lax.ppermute(state, 'seq', [(seq, seq ^ 2 ** bit) for seq in range(ns)])  1.64 us
  transfers between devices with their start and end apart: 11, of which 6 were waited for; matrix products, arithmetic and copies ran while one was open for 0% of the time, Pallas kernels for 13%

profile of v6, /device:TPU:0, one launch (start us, length us, event | category | flops | bytes accessed | tf_op | source)
XLA Modules:
  0.0 35.2 jit_solution(5061122775543160319)
XLA Ops:
  0.0 0.0 copy-start.9
  0.0 0.0 copy-start.10
  0.0 0.0 copy-start.12
  0.0 0.0 copy-start.13
  0.1 0.0 copy-start.14
  0.1 2.1 %tables.1.refs_3_ = f32[88,256]{1,0:T(8,128)} custom-call(f32[512,128]{1,0:T(8,128)} %bitcast.24, s32[1,256]{1,0:T(1,128)} %bitcast.26, f32[16,256]{1,0:T(8,128)} %refs_4_.3, f32[1,256]{1,0:T(1,128)} %bitcast.19, f32[2,256]{1,0:T(2,128)} %bitcast.25, f32[1,2]{1,0:T(1,128)} %bitcast.27, f32[1,2]{1,0:T(1,128)} %bitcast.28, f32[1,2]{1,0:T(1,128)} %bitcast.29, ...), custom_call_target="tpu_custom_call" | custom-call | flops 16106127360 | bytes 262144 | tf_op jit(solution)/shard_map/tables/pallas_call | solution.py:554
  2.1 2.5 %collective-permute-start.2 = (f32[88,256]{1,0:T(8,128)}, f32[88,256]{1,0:T(8,128)S(1)}, u32[]{:S(2)}, u32[]{:S(2)}) collective-permute-start(f32[88,256]{1,0:T(8,128)} %tables.1.refs_3_), channel_id=1, source_target_pairs={{0,10},{2,12},{4,14},{6,8},{8,18},{10,20},{12,22},{14,16},{16,26},... | collective-permute-start | bytes 270344 | tf_op jit(solution)/shard_map/ppermute | solution.py:616
  4.7 3.5 %collective-permute-start.1 = (f32[88,256]{1,0:T(8,128)}, f32[88,256]{1,0:T(8,128)S(1)}, u32[]{:S(2)}, u32[]{:S(2)}) collective-permute-start(f32[88,256]{1,0:T(8,128)} %tables.1.refs_3_), channel_id=1, source_target_pairs={{0,20},{2,22},{4,16},{6,18},{8,28},{10,30},{12,24},{14,26},{16,4},... | collective-permute-start | bytes 270344 | tf_op jit(solution)/shard_map/ppermute | solution.py:616
  8.2 2.2 %collective-permute-start = (f32[88,256]{1,0:T(8,128)}, f32[88,256]{1,0:T(8,128)S(1)}, u32[]{:S(2)}, u32[]{:S(2)}) collective-permute-start(f32[88,256]{1,0:T(8,128)} %tables.1.refs_3_), channel_id=1, source_target_pairs={{0,30},{2,24},{4,26},{6,28},{8,6},{10,0},{12,2},{14,4},{16,14},{18... | collective-permute-start | bytes 270344 | tf_op jit(solution)/shard_map/ppermute | solution.py:616
  10.4 0.0 copy-done
  10.4 0.0 copy-done.1
  10.5 0.0 copy-done.2
  10.5 0.0 copy-done.3
  10.5 0.0 copy-done.6
  10.5 0.0 copy-done.9
  10.5 0.0 copy-done.10
  10.5 0.0 copy-done.12
  10.5 0.0 copy-done.13
  10.5 0.0 copy-done.14
  10.5 0.6 %copy-done.7 = f32[256,2]{0,1:T(2,128)S(1)} copy-done((f32[256,2]{0,1:T(2,128)S(1)}, f32[256,2]{0,1:T(2,128)}, u32[]{:S(2)}) %copy-start.7) | copy-done | bytes 2072
  11.1 0.0 copy-done.8
  11.1 1.3 %prepare.1 = (f32[16,128]{1,0:T(8,128)S(1)}, f32[8,128]{1,0:T(8,128)S(1)}, bf16[256,256]{1,0:T(8,128)(2,1)S(1)}, bf16[128,256]{1,0:T(8,128)(2,1)S(1)}, bf16[128,...) custom-call(f32[16,256]{1,0:T(8,128)S(1)} %copy-done.6, ...), custom_call_target="tpu_custom_call" | custom-call | flops 16106127360 | bytes 262144 | tf_op jit(solution)/shard_map/prepare/pallas_call | solution.py:591
  12.4 0.0 collective-permute-done.2.refs_2_.refs_10_
  12.4 0.1 collective-permute-start.5
  12.5 2.4 %collective-permute-done.1.refs_1_.refs_9_ = f32[88,256]{1,0:T(8,128)S(1)} collective-permute-done((f32[88,256]{1,0:T(8,128)}, f32[88,256]{1,0:T(8,128)S(1)}, u32[]{:S(2)}, u32[]{:S(2)}) %collective-permute-start.1) | collective-permute-done | bytes 90144 | tf_op jit(solution)/shard_map/ppermute | solution.py:616
  14.9 0.1 collective-permute-start.4
  15.0 0.0 collective-permute-done.refs_0_.refs_8_
  15.0 0.5 %collective-permute-start.3 = (f32[88,256]{1,0:T(8,128)S(1)}, f32[88,256]{1,0:T(8,128)S(1)}, u32[]{:S(2)}, u32[]{:S(2)}) collective-permute-start(f32[88,256]{1,0:T(8,128)S(1)} %collective-permute-done.refs_0_.refs_8_), channel_id=1, source_target_pairs={{0,8},{8,0},{16,24},{24,16},{1,9},{9,1},{17,25},{25,17},{2,10},{10... | collective-permute-start | bytes 270344 | tf_op jit(solution)/shard_map/ppermute | solution.py:618
  15.4 0.0 copy-done.5
  15.4 1.8 %mix.1 = (bf16[256,512]{1,0:T(8,128)(2,1)S(1)}, bf16[256,512]{1,0:T(8,128)(2,1)S(1)}, f32[256,256]{1,0:T(8,128)S(1)}) custom-call(f32[88,256]{1,0:T(8,128)S(1)} %collective-permute-done.refs_0_.refs_8_, f32[88,256]{1,0:T(8,128)S(1)} %collective-permute-done.1.refs_1_.refs_9_, f32[88,256]{1,0:T(8,128)S(1)} %collective-permute-done.2.refs_2_.refs_10_, ...), custom_call_target="tpu_custom_call" | custom-call | flops 16106127360 | bytes 262144 | tf_op jit(solution)/shard_map/mix/pallas_call | solution.py:620
  17.3 0.0 collective-permute-done.5.refs_13_
  17.3 0.0 collective-permute-done.4.refs_12_
  17.3 0.0 collective-permute-done.3.refs_11_
  17.3 1.5 %project.1 = (f32[136,128]{1,0:T(8,128)S(1)}, bf16[256,256]{1,0:T(8,128)(2,1)S(1)}, bf16[256,256]{1,0:T(8,128)(2,1)S(1)}, f32[256,128]{1,0:T(8,128)S(1)}, f32[25...) custom-call(bf16[256,512]{1,0:T(8,128)(2,1)S(1)} %get-tuple-element.38.refs_0_, ...), custom_call_target="tpu_custom_call" | custom-call | tf_op jit(solution)/shard_map/project/pallas_call | solution.py:631
  18.9 0.0 copy-start.4
  18.9 0.1 collective-permute-start.6
  19.0 1.2 %collective-permute-done.6.refs_1_ = f32[136,128]{1,0:T(8,128)S(1)} collective-permute-done((f32[136,128]{1,0:T(8,128)S(1)}, f32[136,128]{1,0:T(8,128)S(1)}, u32[]{:S(2)}, u32[]{:S(2)}) %collective-permute-start.6) | collective-permute-done | bytes 69664 | tf_op jit(solution)/shard_map/ppermute | solution.py:686
  20.2 1.5 %collective-permute-start.7 = (f32[136,128]{1,0:T(8,128)S(1)}, f32[136,128]{1,0:T(8,128)S(1)}, u32[]{:S(2)}, u32[]{:S(2)}) collective-permute-start(f32[136,128]{1,0:T(8,128)S(1)} %get-tuple-element.48), channel_id=1, source_target_pairs={{0,16},{8,24},{16,0},{24,8},{1,17},{9,25},{17,1},{25,9},{2,18},{10... | collective-permute-start | bytes 208904 | tf_op jit(solution)/shard_map/ppermute | solution.py:686
  21.7 1.3 %block.1 = (f32[256,128]{1,0:T(8,128)S(1)}, f32[256,128]{1,0:T(8,128)S(1)}, f32[256,128]{1,0:T(8,128)S(1)}, f32[64,256]{1,0:T(8,128)S(1)}, bf16[128,256]{1,0:T(8,128)(2,1)S(1)}, /*index=5*/bf16[128,256]{1,0:T(8,128)(2,1)S(1)}) custom-call(bf16[256,256]{1,0:T(8,128)(2,1)S(1)} %get-tuple-element.49.refs_0_, bf16[256,256]{1,0:T(8,128)(2,1)S(1)} %get-tuple-element.50.refs_1_, ...), custom_call_target="tpu_custom_call" | custom-call | flops 16106127360 | bytes 262144 | tf_op jit(solution)/shard_map/block/pallas_call | solution.py:659
  23.0 1.6 %collective-permute-done.7.refs_1_ = f32[136,128]{1,0:T(8,128)S(1)} collective-permute-done((f32[136,128]{1,0:T(8,128)S(1)}, f32[136,128]{1,0:T(8,128)S(1)}, u32[]{:S(2)}, u32[]{:S(2)}) %collective-permute-start.7) | collective-permute-done | bytes 69664 | tf_op jit(solution)/shard_map/ppermute | solution.py:686
  24.6 0.7 %output.1 = (f32[64,256]{1,0:T(8,128)S(1)}, f32[64,256]{1,0:T(8,128)S(1)}, f32[64,256]{1,0:T(8,128)S(1)}, f32[64,256]{1,0:T(8,128)S(1)}) custom-call(f32[136,128]{1,0:T(8,128)S(1)} %get-tuple-element.47.refs_0_, f32[136,128]{1,0:T(8,128)S(1)} %collective-permute-done.7.refs_1_, f32[256,128]{1,0:T(8,128)S(1)} %get-tuple-element.59.refs_2_, ...), custom_call_target="tpu_custom_call" | custom-call | tf_op jit(solution)/shard_map/output/pallas_call | solution.py:708
  25.3 2.2 %collective-permute-start.8 = (f32[64,256]{1,0:T(8,128)S(1)}, f32[64,256]{1,0:T(8,128)S(1)}, u32[]{:S(2)}, u32[]{:S(2)}) collective-permute-start(f32[64,256]{1,0:T(8,128)S(1)} %get-tuple-element.66), channel_id=1, source_target_pairs={{0,2},{2,4},{4,6},{6,0},{1,3},{3,5},{5,7},{7,1},{8,10},{10,12},{12... | collective-permute-start | bytes 196616 | tf_op jit(solution)/shard_map/ppermute | solution.py:720
  27.5 2.4 %collective-permute-start.9 = (f32[64,256]{1,0:T(8,128)S(1)}, f32[64,256]{1,0:T(8,128)S(1)}, u32[]{:S(2)}, u32[]{:S(2)}) collective-permute-start(f32[64,256]{1,0:T(8,128)S(1)} %get-tuple-element.67), channel_id=1, source_target_pairs={{0,4},{2,6},{4,0},{6,2},{1,5},{3,7},{5,1},{7,3},{8,12},{10,14},{12... | collective-permute-start | bytes 196616 | tf_op jit(solution)/shard_map/ppermute | solution.py:720
  30.0 0.0 collective-permute-start.10
  30.0 2.0 %collective-permute-done.8 = f32[64,256]{1,0:T(8,128)S(1)} collective-permute-done((f32[64,256]{1,0:T(8,128)S(1)}, f32[64,256]{1,0:T(8,128)S(1)}, u32[]{:S(2)}, u32[]{:S(2)}) %collective-permute-start.8) | collective-permute-done | bytes 65568 | tf_op jit(solution)/shard_map/ppermute | solution.py:720
  32.0 2.1 %collective-permute-done.9 = f32[64,256]{1,0:T(8,128)S(1)} collective-permute-done((f32[64,256]{1,0:T(8,128)S(1)}, f32[64,256]{1,0:T(8,128)S(1)}, u32[]{:S(2)}, u32[]{:S(2)}) %collective-permute-start.9) | collective-permute-done | bytes 65568 | tf_op jit(solution)/shard_map/ppermute | solution.py:720
  34.1 0.4 %collective-permute-done.10 = f32[64,256]{1,0:T(8,128)S(1)} collective-permute-done((f32[64,256]{1,0:T(8,128)S(1)}, f32[64,256]{1,0:T(8,128)S(1)}, u32[]{:S(2)}, u32[]{:S(2)}) %collective-permute-start.10) | collective-permute-done | bytes 65568 | tf_op jit(solution)/shard_map/ppermute | solution.py:720
  34.5 0.6 %add_add_fusion = f32[64,256]{1,0:T(8,128)} fusion(f32[64,256]{1,0:T(8,128)S(1)} %collective-permute-done.10, f32[64,256]{1,0:T(8,128)S(1)} %collective-permute-done.9, f32[64,256]{1,0:T(8,128)S(1)} %get-tuple-element.65, f32[64,256]{1,0:T(8,128)S(1)} %collective-permute-done.8), kind=kLoop, calls=%fused_computation | loop fusion | flops 49152 | bytes 327680 | tf_op jit(solution)/shard_map/add | solution.py:720
  (12 shorter events, 0.0 us)
Async XLA Ops:
  0.0 10.4 %copy-start = (f32[256,2,128]{2,1,0:T(2,128)S(1)}, f32[256,2,128]{2,1,0:T(2,128)}, u32[]{:S(2)}) copy-start(f32[256,2,128]{2,1,0:T(2,128)} %param.26) | copy-start | bytes 786436
  0.0 10.4 %copy-start.1 = (f32[256,2,128]{2,1,0:T(2,128)S(1)}, f32[256,2,128]{2,1,0:T(2,128)}, u32[]{:S(2)}) copy-start(f32[256,2,128]{2,1,0:T(2,128)} %param.34) | copy-start | bytes 786436
  0.0 10.4 %copy-start.2 = (f32[256,2,128]{2,1,0:T(2,128)S(1)}, f32[256,2,128]{2,1,0:T(2,128)}, u32[]{:S(2)}) copy-start(f32[256,2,128]{2,1,0:T(2,128)} %param.35) | copy-start | bytes 786436
  0.0 10.5 %copy-start.3 = (f32[128,256]{1,0:T(8,128)S(1)}, f32[128,256]{1,0:T(8,128)}, u32[]{:S(2)}) copy-start(f32[128,256]{1,0:T(8,128)} %refs_4_.2) | copy-start | bytes 393220
  0.0 10.5 %copy-start.6 = (f32[16,256]{1,0:T(8,128)S(1)}, f32[16,256]{1,0:T(8,128)}, u32[]{:S(2)}) copy-start(f32[16,256]{1,0:T(8,128)} %refs_4_.3) | copy-start | bytes 49156
  0.0 10.5 %copy-start.9 = (s32[256]{0:T(256)S(1)}, s32[256]{0:T(256)}, u32[]{:S(2)}) copy-start(s32[256]{0:T(256)} %param.23) | copy-start | bytes 3076
  0.0 10.5 %copy-start.10 = (f32[256]{0:T(256)S(1)}, f32[256]{0:T(256)}, u32[]{:S(2)}) copy-start(f32[256]{0:T(256)} %param.33) | copy-start | bytes 3076
  0.0 10.5 %copy-start.12 = (f32[2]{0:T(128)S(1)}, f32[2]{0:T(128)}, u32[]{:S(2)}) copy-start(f32[2]{0:T(128)} %refs_10_.1) | copy-start | bytes 28
  0.0 10.5 %copy-start.13 = (f32[2]{0:T(128)S(1)}, f32[2]{0:T(128)}, u32[]{:S(2)}) copy-start(f32[2]{0:T(128)} %refs_11_.2) | copy-start | bytes 28
  0.1 10.5 %copy-start.14 = (f32[128]{0:T(128)S(1)}, f32[128]{0:T(128)}, u32[]{:S(2)}) copy-start(f32[128]{0:T(128)} %param.40) | copy-start | bytes 1540
  2.1 10.3 %collective-permute-start.2 = (f32[88,256]{1,0:T(8,128)}, f32[88,256]{1,0:T(8,128)S(1)}, u32[]{:S(2)}, u32[]{:S(2)}) collective-permute-start(f32[88,256]{1,0:T(8,128)} %tables.1.refs_3_), channel_id=1, source_target_pairs={{0,10},{2,12},{4,14},{6,8},{8,18},{10,20},{12,22},{14,16},{16,26},... | collective-permute-start | bytes 270344 | tf_op jit(solution)/shard_map/ppermute | solution.py:616
  4.7 10.2 %collective-permute-start.1 = (f32[88,256]{1,0:T(8,128)}, f32[88,256]{1,0:T(8,128)S(1)}, u32[]{:S(2)}, u32[]{:S(2)}) collective-permute-start(f32[88,256]{1,0:T(8,128)} %tables.1.refs_3_), channel_id=1, source_target_pairs={{0,20},{2,22},{4,16},{6,18},{8,28},{10,30},{12,24},{14,26},{16,4},... | collective-permute-start | bytes 270344 | tf_op jit(solution)/shard_map/ppermute | solution.py:616
  8.2 6.8 %collective-permute-start = (f32[88,256]{1,0:T(8,128)}, f32[88,256]{1,0:T(8,128)S(1)}, u32[]{:S(2)}, u32[]{:S(2)}) collective-permute-start(f32[88,256]{1,0:T(8,128)} %tables.1.refs_3_), channel_id=1, source_target_pairs={{0,30},{2,24},{4,26},{6,28},{8,6},{10,0},{12,2},{14,4},{16,14},{18... | collective-permute-start | bytes 270344 | tf_op jit(solution)/shard_map/ppermute | solution.py:616
  10.4 0.7 %copy-start.7 = (f32[256,2]{0,1:T(2,128)S(1)}, f32[256,2]{0,1:T(2,128)}, u32[]{:S(2)}) copy-start(f32[256,2]{0,1:T(2,128)} %param.36) | copy-start | bytes 6148
  10.4 0.7 %copy-start.8 = (f32[256]{0:T(256)S(1)}, f32[256]{0:T(256)}, u32[]{:S(2)}) copy-start(f32[256]{0:T(256)} %param.24) | copy-start | bytes 3076
  10.4 0.7 %copy-start.11 = (f32[2]{0:T(128)S(1)}, f32[2]{0:T(128)}, u32[]{:S(2)}) copy-start(f32[2]{0:T(128)} %refs_9_.3) | copy-start | bytes 28
  11.1 4.3 %copy-start.5 = (f32[88,256]{1,0:T(8,128)S(1)}, f32[88,256]{1,0:T(8,128)}, u32[]{:S(2)}) copy-start(f32[88,256]{1,0:T(8,128)} %tables.1.refs_3_) | copy-start | bytes 270340
  12.4 4.8 %collective-permute-start.5 = (f32[88,256]{1,0:T(8,128)S(1)}, f32[88,256]{1,0:T(8,128)S(1)}, u32[]{:S(2)}, u32[]{:S(2)}) collective-permute-start(f32[88,256]{1,0:T(8,128)S(1)} %collective-permute-done.2.refs_2_.refs_10_), channel_id=1, source_target_pairs={{0,8},{8,0},{16,24},{24,16},{1,9},{9,1},{17,25},{25,17},{2,10},{10... | collective-permute-start | bytes 270344 | tf_op jit(solution)/shard_map/ppermute | solution.py:618
  14.9 2.4 %collective-permute-start.4 = (f32[88,256]{1,0:T(8,128)S(1)}, f32[88,256]{1,0:T(8,128)S(1)}, u32[]{:S(2)}, u32[]{:S(2)}) collective-permute-start(f32[88,256]{1,0:T(8,128)S(1)} %collective-permute-done.1.refs_1_.refs_9_), channel_id=1, source_target_pairs={{0,8},{8,0},{16,24},{24,16},{1,9},{9,1},{17,25},{25,17},{2,10},{10... | collective-permute-start | bytes 270344 | tf_op jit(solution)/shard_map/ppermute | solution.py:618
  15.0 2.3 %collective-permute-start.3 = (f32[88,256]{1,0:T(8,128)S(1)}, f32[88,256]{1,0:T(8,128)S(1)}, u32[]{:S(2)}, u32[]{:S(2)}) collective-permute-start(f32[88,256]{1,0:T(8,128)S(1)} %collective-permute-done.refs_0_.refs_8_), channel_id=1, source_target_pairs={{0,8},{8,0},{16,24},{24,16},{1,9},{9,1},{17,25},{25,17},{2,10},{10... | collective-permute-start | bytes 270344 | tf_op jit(solution)/shard_map/ppermute | solution.py:618
  18.9 2.9 %copy-start.4 = (f32[128,256]{1,0:T(8,128)S(1)}, f32[128,256]{1,0:T(8,128)}, u32[]{:S(2)}) copy-start(f32[128,256]{1,0:T(8,128)} %refs_11_.3) | copy-start | bytes 393220
  18.9 1.3 %collective-permute-start.6 = (f32[136,128]{1,0:T(8,128)S(1)}, f32[136,128]{1,0:T(8,128)S(1)}, u32[]{:S(2)}, u32[]{:S(2)}) collective-permute-start(f32[136,128]{1,0:T(8,128)S(1)} %get-tuple-element.46.refs_0_), channel_id=1, source_target_pairs={{0,8},{8,0},{16,24},{24,16},{1,9},{9,1},{17,25},{25,17},{2,10},{10... | collective-permute-start | bytes 208904 | tf_op jit(solution)/shard_map/ppermute | solution.py:686
  20.2 4.4 %collective-permute-start.7 = (f32[136,128]{1,0:T(8,128)S(1)}, f32[136,128]{1,0:T(8,128)S(1)}, u32[]{:S(2)}, u32[]{:S(2)}) collective-permute-start(f32[136,128]{1,0:T(8,128)S(1)} %get-tuple-element.48), channel_id=1, source_target_pairs={{0,16},{8,24},{16,0},{24,8},{1,17},{9,25},{17,1},{25,9},{2,18},{10... | collective-permute-start | bytes 208904 | tf_op jit(solution)/shard_map/ppermute | solution.py:686
  25.3 6.7 %collective-permute-start.8 = (f32[64,256]{1,0:T(8,128)S(1)}, f32[64,256]{1,0:T(8,128)S(1)}, u32[]{:S(2)}, u32[]{:S(2)}) collective-permute-start(f32[64,256]{1,0:T(8,128)S(1)} %get-tuple-element.66), channel_id=1, source_target_pairs={{0,2},{2,4},{4,6},{6,0},{1,3},{3,5},{5,7},{7,1},{8,10},{10,12},{12... | collective-permute-start | bytes 196616 | tf_op jit(solution)/shard_map/ppermute | solution.py:720
  27.5 6.6 %collective-permute-start.9 = (f32[64,256]{1,0:T(8,128)S(1)}, f32[64,256]{1,0:T(8,128)S(1)}, u32[]{:S(2)}, u32[]{:S(2)}) collective-permute-start(f32[64,256]{1,0:T(8,128)S(1)} %get-tuple-element.67), channel_id=1, source_target_pairs={{0,4},{2,6},{4,0},{6,2},{1,5},{3,7},{5,1},{7,3},{8,12},{10,14},{12... | collective-permute-start | bytes 196616 | tf_op jit(solution)/shard_map/ppermute | solution.py:720
  30.0 4.6 %collective-permute-start.10 = (f32[64,256]{1,0:T(8,128)S(1)}, f32[64,256]{1,0:T(8,128)S(1)}, u32[]{:S(2)}, u32[]{:S(2)}) collective-permute-start(f32[64,256]{1,0:T(8,128)S(1)} %get-tuple-element.68), channel_id=1, source_target_pairs={{0,6},{2,0},{4,2},{6,4},{1,7},{3,1},{5,3},{7,5},{8,14},{10,8},{12,... | collective-permute-start | bytes 196616 | tf_op jit(solution)/shard_map/ppermute | solution.py:720

commit v7 on v6

--- a/solution.py
+++ b/solution.py
@@ -16,6 +16,15 @@
 MM = (((1,), (0,)), ((), ()))
 NT = (((1,), (1,)), ((), ()))
 TN = (((0,), (0,)), ((), ()))
+
+
+def partners(ns, nh):
+    count = max(ns, nh)
+    return [((ns - k) if 0 < k < ns else 0, k if k < nh else 0) for k in range(count)]
+
+
+def in_turn(count):
+    return sorted(range(1, count), key=lambda k: (-k.bit_length(), k))
 
 
 def iota(shape, axis):
@@ -219,14 +228,15 @@
         taken, refs[:] = refs[:number], refs[number:]
         return taken
 
-    packets = take(max(ns, nh))[::-1]
+    count = max(ns, nh)
+    packets = dict(zip(in_turn(count)[::-1] + [0], take(count)))
     emb, pairs = take(2)
     out_high, out_low, out_embedded = take(3)
     tokens = take(1)[0]
     mine = lax.axis_index("seq")
 
     for k in range(ns):
-        block = ns - 1 - lax.rem(mine - k + ns, ns)
+        block = ns - 1 - lax.bitwise_xor(mine, partners(ns, nh)[k][0])
         tokens[pl.ds(block, 1), :] = packets[k][V : V + 1, 0:T]
 
     def rows_of(place):
@@ -341,8 +351,9 @@
         return taken
 
     high, low, embedded, small, own_high, own_low, state_high, state_low = take(8)
-    nears = take(nh - 1)[::-1]
-    others = take(nh - 1)[::-1]
+    order = in_turn(nh)[::-1]
+    nears = dict(zip(order, take(nh - 1)))
+    others = dict(zip(order, take(nh - 1)))
     out_state, out_high, out_low, out_scale = take(4)
     out_write, out_inner, out_stepped, out_total = take(4)
     half = ch // 2
@@ -351,9 +362,9 @@
 
     pieces = []
     for k in range(1, nh):
-        near = nears[k - 1][base : base + half, 0:D]
-        other = others[k - 1][base : base + half, 0:D]
-        even = lax.rem(mine - k + ns * nh, 2) == 0
+        near = nears[k][base : base + half, 0:D]
+        other = others[k][base : base + half, 0:D]
+        even = lax.rem(lax.bitwise_xor(mine, partners(ns, nh)[k][0]), 2) == 0
         pieces.append(jnp.where(even, near, other))
         pieces.append(jnp.where(even, other, near))
     weights = split2(jnp.concatenate(pieces, axis=0))
@@ -478,7 +489,7 @@
     partial_ref[...] = dot_split(split2(value), (proj_high[...], proj_low[...]))
     mine = lax.axis_index("head")
     for k in range(nh):
-        place = pl.multiple_of(lax.rem(mine + k, nh) * share, 8)
+        place = pl.multiple_of(lax.bitwise_xor(mine, k) * share, 8)
         part = partial_ref[pl.ds(place, share), :]
         outs[k][...] = part + own[...] if k == 0 else part
 
@@ -605,28 +616,31 @@
         name="prepare",
     )(*prepared)
 
-    messages = [message]
-    for k in range(1, max(ns, nh)):
+    count = max(ns, nh)
+    messages = {0: message}
+    for k in in_turn(count):
+        seq_bits, head_bits = partners(ns, nh)[k]
         pairs = [
-            (seq * nh + head, ((seq + k) % ns) * nh + (head + k) % nh)
+            (seq * nh + head, (seq ^ seq_bits) * nh + (head ^ head_bits))
             for seq in range(ns)
             for head in range(nh)
         ]
         sent = message if k < nh else message[0:head_rows]
-        messages.append(lax.ppermute(sent, ("seq", "head"), pairs))
+        messages[k] = lax.ppermute(sent, ("seq", "head"), pairs)
     swap = [(seq, seq ^ 1) for seq in range(ns)]
-    others = [lax.ppermute(messages[k], "seq", swap) for k in range(1, nh)]
+    order = in_turn(nh)[::-1]
+    others = [lax.ppermute(messages[k], "seq", swap) for k in order]
 
     mixed_high, mixed_low, embedded = pl.pallas_call(
         functools.partial(mix_kernel, dims),
         out_shape=(*halves(T, nh * ch), shape(T, D)),
-        in_specs=[vmem] * (len(messages) + 2),
+        in_specs=[vmem] * (count + 2),
         out_specs=(vmem,) * 3,
         scratch_shapes=[pltpu.VMEM((max(ns, 8), T), f32)],
         compiler_params=params,
         cost_estimate=heavy,
         name="mix",
-    )(*messages[::-1], embedding, pair_table)
+    )(*[messages[k] for k in in_turn(count)[::-1] + [0]], embedding, pair_table)
 
     state, hidden_high, hidden_low, scale, write, inner, stepped, total = pl.pallas_call(
         functools.partial(project_kernel, dims),
@@ -652,8 +666,8 @@
         own_low,
         state_high,
         state_low,
-        *messages[1:nh][::-1],
-        *others[::-1],
+        *[messages[k] for k in order],
+        *others,
     )
 
     base, read, gate, own, proj_high, proj_low = pl.pallas_call(
@@ -715,8 +729,8 @@
         name="output",
     )(prefix, came, read, base, total, gate, own, proj_high, proj_low)
     result = parts[0]
-    for k in range(1, nh):
-        pairs = [(source, (source + k) % nh) for source in range(nh)]
+    for k in in_turn(nh):
+        pairs = [(source, source ^ k) for source in range(nh)]
         result = result + lax.ppermute(parts[k], "head", pairs)
     return result
 

time: 35.3 us -> 35.6 us (level)
  waiting for transfers between devices: 9.72 us -> 13.4 us
  starting transfers between devices: 15.2 us -> 11.8 us
    ppermute x6, waiting for transfers between devices: 2.4 us -> 5.43 us  [the longest x3 5.42 us: per_device(): messages[k] = lax.ppermute(sent, ('seq', 'head'), pairs)]
    ppermute x6, starting transfers between devices: 8.87 us -> 6.38 us  [the longest x3 5.75 us: per_device(): messages[k] = lax.ppermute(sent, ('seq', 'head'), pairs)]
    ppermute x3, starting transfers between devices: 4.67 us -> 4.02 us  [per_device(): result = result + lax.ppermute(parts[k], 'head', pairs)]
    ppermute x2, waiting for transfers between devices: 2.77 us -> 3.19 us  [per_device(): lax.ppermute(state, 'seq', [(seq, seq ^ 2 ** bit) for seq in range(ns)])]
where the time goes in v7:
time: 35.6 us; the launch traced here: 35.4 us
  waiting for transfers between devices  13.4 us (38%)
  starting transfers between devices  11.8 us (33%)
  Pallas kernels  8.75 us (25%)
  local copies, waits for them, and re-layouts  0.65 us (2%)
  other arithmetic  0.65 us (2%)
    ppermute x3, starting transfers between devices, per_device(): messages[k] = lax.ppermute(sent, ('seq', 'head'), pairs)  5.75 us
    ppermute x3, waiting for transfers between devices, per_device(): messages[k] = lax.ppermute(sent, ('seq', 'head'), pairs)  5.42 us
    ppermute x3, waiting for transfers between devices, per_device(): result = result + lax.ppermute(parts[k], 'head', pairs)  4.77 us
    ppermute x3, starting transfers between devices, per_device(): result = result + lax.ppermute(parts[k], 'head', pairs)  4.02 us
    ppermute x2, waiting for transfers between devices, per_device(): lax.ppermute(state, 'seq', [(seq, seq ^ 2 ** bit) for seq in range(ns)])  3.19 us
    pallas_call x1, Pallas kernels, per_device(): pl.pallas_call(functools.partial(tables_kernel, dims), out_shape=shape(he...  2.07 us
    pallas_call x1, Pallas kernels, per_device(): pl.pallas_call(functools.partial(mix_kernel, dims), out_shape=(*halves(T,...  1.85 us
    pallas_call x1, Pallas kernels, per_device(): pl.pallas_call(functools.partial(project_kernel, dims), out_shape=(shape(...  1.53 us
  transfers between devices with their start and end apart: 11, of which 6 were waited for; matrix products, arithmetic and copies ran while one was open for 0% of the time, Pallas kernels for 13%

profile of v7, /device:TPU:0, one launch (start us, length us, event | category | flops | bytes accessed | tf_op | source)
XLA Modules:
  0.0 35.4 jit_solution(5651859197636352435)
XLA Ops:
  0.0 0.0 copy-start.9
  0.0 0.0 copy-start.10
  0.0 0.0 copy-start.12
  0.0 0.0 copy-start.13
  0.1 0.0 copy-start.14
  0.1 2.1 %tables.1.refs_3_ = f32[88,256]{1,0:T(8,128)} custom-call(f32[512,128]{1,0:T(8,128)} %bitcast.24, s32[1,256]{1,0:T(1,128)} %bitcast.26, f32[16,256]{1,0:T(8,128)} %refs_4_.3, f32[1,256]{1,0:T(1,128)} %bitcast.19, f32[2,256]{1,0:T(2,128)} %bitcast.25, f32[1,2]{1,0:T(1,128)} %bitcast.27, f32[1,2]{1,0:T(1,128)} %bitcast.28, f32[1,2]{1,0:T(1,128)} %bitcast.29, ...), custom_call_target="tpu_custom_call" | custom-call | flops 16106127360 | bytes 262144 | tf_op jit(solution)/shard_map/tables/pallas_call | solution.py:565
  2.1 5.0 %collective-permute-start.2 = (f32[88,256]{1,0:T(8,128)}, f32[88,256]{1,0:T(8,128)S(1)}, u32[]{:S(2)}, u32[]{:S(2)}) collective-permute-start(f32[88,256]{1,0:T(8,128)} %tables.1.refs_3_), channel_id=1, source_target_pairs={{0,20},{2,22},{4,16},{6,18},{8,28},{10,30},{12,24},{14,26},{16,4},... | collective-permute-start | bytes 270344 | tf_op jit(solution)/shard_map/ppermute | solution.py:629
  7.2 0.5 %collective-permute-start.1 = (f32[88,256]{1,0:T(8,128)}, f32[88,256]{1,0:T(8,128)S(1)}, u32[]{:S(2)}, u32[]{:S(2)}) collective-permute-start(f32[88,256]{1,0:T(8,128)} %tables.1.refs_3_), channel_id=1, source_target_pairs={{0,14},{2,12},{4,10},{6,8},{8,6},{10,4},{12,2},{14,0},{16,30},{18,... | collective-permute-start | bytes 270344 | tf_op jit(solution)/shard_map/ppermute | solution.py:629
  7.7 0.2 collective-permute-start
  7.9 0.0 copy-done
  7.9 0.0 copy-done.1
  7.9 0.0 copy-done.2
  7.9 0.0 copy-done.3
  7.9 0.0 copy-done.6
  7.9 0.0 copy-done.9
  8.0 0.0 copy-done.10
  8.0 0.0 copy-done.12
  8.0 0.0 copy-done.13
  8.0 0.0 copy-done.14
  8.0 0.6 %copy-done.7 = f32[256,2]{0,1:T(2,128)S(1)} copy-done((f32[256,2]{0,1:T(2,128)S(1)}, f32[256,2]{0,1:T(2,128)}, u32[]{:S(2)}) %copy-start.7) | copy-done | bytes 2072
  8.6 0.0 copy-done.8
  8.6 0.0 copy-done.11
  8.6 1.3 %prepare.1 = (f32[16,128]{1,0:T(8,128)S(1)}, f32[8,128]{1,0:T(8,128)S(1)}, bf16[256,256]{1,0:T(8,128)(2,1)S(1)}, bf16[128,256]{1,0:T(8,128)(2,1)S(1)}, bf16[128,...) custom-call(f32[16,256]{1,0:T(8,128)S(1)} %copy-done.6, ...), custom_call_target="tpu_custom_call" | custom-call | flops 16106127360 | bytes 262144 | tf_op jit(solution)/shard_map/prepare/pallas_call | solution.py:602
  9.9 4.5 %collective-permute-done.2.refs_2_.refs_10_ = f32[88,256]{1,0:T(8,128)S(1)} collective-permute-done((f32[88,256]{1,0:T(8,128)}, f32[88,256]{1,0:T(8,128)S(1)}, u32[]{:S(2)}, u32[]{:S(2)}) %collective-permute-start.2) | collective-permute-done | bytes 90144 | tf_op jit(solution)/shard_map/ppermute | solution.py:629
  14.4 0.0 collective-permute-start.5
  14.4 0.0 collective-permute-done.1.refs_1_.refs_9_
  14.4 0.5 %collective-permute-start.4 = (f32[88,256]{1,0:T(8,128)S(1)}, f32[88,256]{1,0:T(8,128)S(1)}, u32[]{:S(2)}, u32[]{:S(2)}) collective-permute-start(f32[88,256]{1,0:T(8,128)S(1)} %collective-permute-done.1.refs_1_.refs_9_), channel_id=1, source_target_pairs={{0,8},{8,0},{16,24},{24,16},{1,9},{9,1},{17,25},{25,17},{2,10},{10... | collective-permute-start | bytes 270344 | tf_op jit(solution)/shard_map/ppermute | solution.py:632
  14.9 0.9 %collective-permute-done.refs_0_.refs_8_ = f32[88,256]{1,0:T(8,128)S(1)} collective-permute-done((f32[88,256]{1,0:T(8,128)}, f32[88,256]{1,0:T(8,128)S(1)}, u32[]{:S(2)}, u32[]{:S(2)}) %collective-permute-start) | collective-permute-done | bytes 90144 | tf_op jit(solution)/shard_map/ppermute | solution.py:629
  15.8 0.1 collective-permute-start.3
  16.0 1.9 %mix.1 = (bf16[256,512]{1,0:T(8,128)(2,1)S(1)}, bf16[256,512]{1,0:T(8,128)(2,1)S(1)}, f32[256,256]{1,0:T(8,128)S(1)}) custom-call(f32[88,256]{1,0:T(8,128)S(1)} %collective-permute-done.refs_0_.refs_8_, f32[88,256]{1,0:T(8,128)S(1)} %collective-permute-done.1.refs_1_.refs_9_, f32[88,256]{1,0:T(8,128)S(1)} %collective-permute-done.2.refs_2_.refs_10_, ...), custom_call_target="tpu_custom_call" | custom-call | flops 16106127360 | bytes 262144 | tf_op jit(solution)/shard_map/mix/pallas_call | solution.py:634
  17.8 0.0 collective-permute-done.5.refs_13_
  17.8 0.0 collective-permute-done.4.refs_12_
  17.8 0.0 collective-permute-done.3.refs_11_
  17.8 1.5 %project.1 = (f32[136,128]{1,0:T(8,128)S(1)}, bf16[256,256]{1,0:T(8,128)(2,1)S(1)}, bf16[256,256]{1,0:T(8,128)(2,1)S(1)}, f32[256,128]{1,0:T(8,128)S(1)}, f32[25...) custom-call(bf16[256,512]{1,0:T(8,128)(2,1)S(1)} %get-tuple-element.38.refs_0_, ...), custom_call_target="tpu_custom_call" | custom-call | tf_op jit(solution)/shard_map/project/pallas_call | solution.py:645
  19.4 0.0 copy-start.4
  19.4 0.5 %collective-permute-start.6 = (f32[136,128]{1,0:T(8,128)S(1)}, f32[136,128]{1,0:T(8,128)S(1)}, u32[]{:S(2)}, u32[]{:S(2)}) collective-permute-start(f32[136,128]{1,0:T(8,128)S(1)} %get-tuple-element.46.refs_0_), channel_id=1, source_target_pairs={{0,8},{8,0},{16,24},{24,16},{1,9},{9,1},{17,25},{25,17},{2,10},{10... | collective-permute-start | bytes 208904 | tf_op jit(solution)/shard_map/ppermute | solution.py:700
  19.9 0.9 %collective-permute-done.6.refs_1_ = f32[136,128]{1,0:T(8,128)S(1)} collective-permute-done((f32[136,128]{1,0:T(8,128)S(1)}, f32[136,128]{1,0:T(8,128)S(1)}, u32[]{:S(2)}, u32[]{:S(2)}) %collective-permute-start.6) | collective-permute-done | bytes 69664 | tf_op jit(solution)/shard_map/ppermute | solution.py:700
  20.8 0.9 %collective-permute-start.7 = (f32[136,128]{1,0:T(8,128)S(1)}, f32[136,128]{1,0:T(8,128)S(1)}, u32[]{:S(2)}, u32[]{:S(2)}) collective-permute-start(f32[136,128]{1,0:T(8,128)S(1)} %get-tuple-element.48), channel_id=1, source_target_pairs={{0,16},{8,24},{16,0},{24,8},{1,17},{9,25},{17,1},{25,9},{2,18},{10... | collective-permute-start | bytes 208904 | tf_op jit(solution)/shard_map/ppermute | solution.py:700
  21.7 1.3 %block.1 = (f32[256,128]{1,0:T(8,128)S(1)}, f32[256,128]{1,0:T(8,128)S(1)}, f32[256,128]{1,0:T(8,128)S(1)}, f32[64,256]{1,0:T(8,128)S(1)}, bf16[128,256]{1,0:T(8,128)(2,1)S(1)}, /*index=5*/bf16[128,256]{1,0:T(8,128)(2,1)S(1)}) custom-call(bf16[256,256]{1,0:T(8,128)(2,1)S(1)} %get-tuple-element.49.refs_0_, bf16[256,256]{1,0:T(8,128)(2,1)S(1)} %get-tuple-element.50.refs_1_, ...), custom_call_target="tpu_custom_call" | custom-call | flops 16106127360 | bytes 262144 | tf_op jit(solution)/shard_map/block/pallas_call | solution.py:673
  23.0 2.3 %collective-permute-done.7.refs_1_ = f32[136,128]{1,0:T(8,128)S(1)} collective-permute-done((f32[136,128]{1,0:T(8,128)S(1)}, f32[136,128]{1,0:T(8,128)S(1)}, u32[]{:S(2)}, u32[]{:S(2)}) %collective-permute-start.7) | collective-permute-done | bytes 69664 | tf_op jit(solution)/shard_map/ppermute | solution.py:700
  25.3 0.7 %output.1 = (f32[64,256]{1,0:T(8,128)S(1)}, f32[64,256]{1,0:T(8,128)S(1)}, f32[64,256]{1,0:T(8,128)S(1)}, f32[64,256]{1,0:T(8,128)S(1)}) custom-call(f32[136,128]{1,0:T(8,128)S(1)} %get-tuple-element.47.refs_0_, f32[136,128]{1,0:T(8,128)S(1)} %collective-permute-done.7.refs_1_, f32[256,128]{1,0:T(8,128)S(1)} %get-tuple-element.59.refs_2_, ...), custom_call_target="tpu_custom_call" | custom-call | tf_op jit(solution)/shard_map/output/pallas_call | solution.py:722
  26.0 2.7 %collective-permute-start.8 = (f32[64,256]{1,0:T(8,128)S(1)}, f32[64,256]{1,0:T(8,128)S(1)}, u32[]{:S(2)}, u32[]{:S(2)}) collective-permute-start(f32[64,256]{1,0:T(8,128)S(1)} %get-tuple-element.66), channel_id=1, source_target_pairs={{0,4},{2,6},{4,0},{6,2},{1,5},{3,7},{5,1},{7,3},{8,12},{10,14},{12... | collective-permute-start | bytes 196616 | tf_op jit(solution)/shard_map/ppermute | solution.py:734
  28.7 0.8 %collective-permute-start.9 = (f32[64,256]{1,0:T(8,128)S(1)}, f32[64,256]{1,0:T(8,128)S(1)}, u32[]{:S(2)}, u32[]{:S(2)}) collective-permute-start(f32[64,256]{1,0:T(8,128)S(1)} %get-tuple-element.67), channel_id=1, source_target_pairs={{0,6},{2,4},{4,2},{6,0},{1,7},{3,5},{5,3},{7,1},{8,14},{10,12},{12... | collective-permute-start | bytes 196616 | tf_op jit(solution)/shard_map/ppermute | solution.py:734
  29.5 0.5 %collective-permute-start.10 = (f32[64,256]{1,0:T(8,128)S(1)}, f32[64,256]{1,0:T(8,128)S(1)}, u32[]{:S(2)}, u32[]{:S(2)}) collective-permute-start(f32[64,256]{1,0:T(8,128)S(1)} %get-tuple-element.68), channel_id=1, source_target_pairs={{0,2},{2,0},{4,6},{6,4},{1,3},{3,1},{5,7},{7,5},{8,10},{10,8},{12,... | collective-permute-start | bytes 196616 | tf_op jit(solution)/shard_map/ppermute | solution.py:734
  30.0 2.9 %collective-permute-done.8 = f32[64,256]{1,0:T(8,128)S(1)} collective-permute-done((f32[64,256]{1,0:T(8,128)S(1)}, f32[64,256]{1,0:T(8,128)S(1)}, u32[]{:S(2)}, u32[]{:S(2)}) %collective-permute-start.8) | collective-permute-done | bytes 65568 | tf_op jit(solution)/shard_map/ppermute | solution.py:734
  33.0 1.8 %collective-permute-done.9 = f32[64,256]{1,0:T(8,128)S(1)} collective-permute-done((f32[64,256]{1,0:T(8,128)S(1)}, f32[64,256]{1,0:T(8,128)S(1)}, u32[]{:S(2)}, u32[]{:S(2)}) %collective-permute-start.9) | collective-permute-done | bytes 65568 | tf_op jit(solution)/shard_map/ppermute | solution.py:734
  34.8 0.0 collective-permute-done.10
  34.8 0.6 %add_add_fusion = f32[64,256]{1,0:T(8,128)} fusion(f32[64,256]{1,0:T(8,128)S(1)} %collective-permute-done.10, f32[64,256]{1,0:T(8,128)S(1)} %collective-permute-done.9, f32[64,256]{1,0:T(8,128)S(1)} %get-tuple-element.65, f32[64,256]{1,0:T(8,128)S(1)} %collective-permute-done.8), kind=kLoop, calls=%fused_computation | loop fusion | flops 49152 | bytes 327680 | tf_op jit(solution)/shard_map/add | solution.py:734
  (12 shorter events, 0.0 us)
Async XLA Ops:
  0.0 7.9 %copy-start = (f32[256,2,128]{2,1,0:T(2,128)S(1)}, f32[256,2,128]{2,1,0:T(2,128)}, u32[]{:S(2)}) copy-start(f32[256,2,128]{2,1,0:T(2,128)} %param.26) | copy-start | bytes 786436
  0.0 7.9 %copy-start.1 = (f32[256,2,128]{2,1,0:T(2,128)S(1)}, f32[256,2,128]{2,1,0:T(2,128)}, u32[]{:S(2)}) copy-start(f32[256,2,128]{2,1,0:T(2,128)} %param.34) | copy-start | bytes 786436
  0.0 7.9 %copy-start.2 = (f32[256,2,128]{2,1,0:T(2,128)S(1)}, f32[256,2,128]{2,1,0:T(2,128)}, u32[]{:S(2)}) copy-start(f32[256,2,128]{2,1,0:T(2,128)} %param.35) | copy-start | bytes 786436
  0.0 7.9 %copy-start.3 = (f32[128,256]{1,0:T(8,128)S(1)}, f32[128,256]{1,0:T(8,128)}, u32[]{:S(2)}) copy-start(f32[128,256]{1,0:T(8,128)} %refs_4_.2) | copy-start | bytes 393220
  0.0 7.9 %copy-start.6 = (f32[16,256]{1,0:T(8,128)S(1)}, f32[16,256]{1,0:T(8,128)}, u32[]{:S(2)}) copy-start(f32[16,256]{1,0:T(8,128)} %refs_4_.3) | copy-start | bytes 49156
  0.0 7.9 %copy-start.9 = (s32[256]{0:T(256)S(1)}, s32[256]{0:T(256)}, u32[]{:S(2)}) copy-start(s32[256]{0:T(256)} %param.23) | copy-start | bytes 3076
  0.0 7.9 %copy-start.10 = (f32[256]{0:T(256)S(1)}, f32[256]{0:T(256)}, u32[]{:S(2)}) copy-start(f32[256]{0:T(256)} %param.33) | copy-start | bytes 3076
  0.0 7.9 %copy-start.12 = (f32[2]{0:T(128)S(1)}, f32[2]{0:T(128)}, u32[]{:S(2)}) copy-start(f32[2]{0:T(128)} %refs_10_.1) | copy-start | bytes 28
  0.0 7.9 %copy-start.13 = (f32[2]{0:T(128)S(1)}, f32[2]{0:T(128)}, u32[]{:S(2)}) copy-start(f32[2]{0:T(128)} %refs_11_.2) | copy-start | bytes 28
  0.1 7.9 %copy-start.14 = (f32[128]{0:T(128)S(1)}, f32[128]{0:T(128)}, u32[]{:S(2)}) copy-start(f32[128]{0:T(128)} %param.40) | copy-start | bytes 1540
  2.1 12.2 %collective-permute-start.2 = (f32[88,256]{1,0:T(8,128)}, f32[88,256]{1,0:T(8,128)S(1)}, u32[]{:S(2)}, u32[]{:S(2)}) collective-permute-start(f32[88,256]{1,0:T(8,128)} %tables.1.refs_3_), channel_id=1, source_target_pairs={{0,20},{2,22},{4,16},{6,18},{8,28},{10,30},{12,24},{14,26},{16,4},... | collective-permute-start | bytes 270344 | tf_op jit(solution)/shard_map/ppermute | solution.py:629
  7.2 7.2 %collective-permute-start.1 = (f32[88,256]{1,0:T(8,128)}, f32[88,256]{1,0:T(8,128)S(1)}, u32[]{:S(2)}, u32[]{:S(2)}) collective-permute-start(f32[88,256]{1,0:T(8,128)} %tables.1.refs_3_), channel_id=1, source_target_pairs={{0,14},{2,12},{4,10},{6,8},{8,6},{10,4},{12,2},{14,0},{16,30},{18,... | collective-permute-start | bytes 270344 | tf_op jit(solution)/shard_map/ppermute | solution.py:629
  7.7 8.1 %collective-permute-start = (f32[88,256]{1,0:T(8,128)}, f32[88,256]{1,0:T(8,128)S(1)}, u32[]{:S(2)}, u32[]{:S(2)}) collective-permute-start(f32[88,256]{1,0:T(8,128)} %tables.1.refs_3_), channel_id=1, source_target_pairs={{0,26},{2,24},{4,30},{6,28},{8,18},{10,16},{12,22},{14,20},{16,10}... | collective-permute-start | bytes 270344 | tf_op jit(solution)/shard_map/ppermute | solution.py:629
  7.9 0.7 %copy-start.7 = (f32[256,2]{0,1:T(2,128)S(1)}, f32[256,2]{0,1:T(2,128)}, u32[]{:S(2)}) copy-start(f32[256,2]{0,1:T(2,128)} %param.36) | copy-start | bytes 6148
  7.9 0.7 %copy-start.8 = (f32[256]{0:T(256)S(1)}, f32[256]{0:T(256)}, u32[]{:S(2)}) copy-start(f32[256]{0:T(256)} %param.24) | copy-start | bytes 3076
  7.9 0.7 %copy-start.11 = (f32[2]{0:T(128)S(1)}, f32[2]{0:T(128)}, u32[]{:S(2)}) copy-start(f32[2]{0:T(128)} %refs_9_.3) | copy-start | bytes 28
  8.6 7.4 %copy-start.5 = (f32[88,256]{1,0:T(8,128)S(1)}, f32[88,256]{1,0:T(8,128)}, u32[]{:S(2)}) copy-start(f32[88,256]{1,0:T(8,128)} %tables.1.refs_3_) | copy-start | bytes 270340
  14.4 3.4 %collective-permute-start.5 = (f32[88,256]{1,0:T(8,128)S(1)}, f32[88,256]{1,0:T(8,128)S(1)}, u32[]{:S(2)}, u32[]{:S(2)}) collective-permute-start(f32[88,256]{1,0:T(8,128)S(1)} %collective-permute-done.2.refs_2_.refs_10_), channel_id=1, source_target_pairs={{0,8},{8,0},{16,24},{24,16},{1,9},{9,1},{17,25},{25,17},{2,10},{10... | collective-permute-start | bytes 270344 | tf_op jit(solution)/shard_map/ppermute | solution.py:632
  14.4 3.4 %collective-permute-start.4 = (f32[88,256]{1,0:T(8,128)S(1)}, f32[88,256]{1,0:T(8,128)S(1)}, u32[]{:S(2)}, u32[]{:S(2)}) collective-permute-start(f32[88,256]{1,0:T(8,128)S(1)} %collective-permute-done.1.refs_1_.refs_9_), channel_id=1, source_target_pairs={{0,8},{8,0},{16,24},{24,16},{1,9},{9,1},{17,25},{25,17},{2,10},{10... | collective-permute-start | bytes 270344 | tf_op jit(solution)/shard_map/ppermute | solution.py:632
  15.8 2.0 %collective-permute-start.3 = (f32[88,256]{1,0:T(8,128)S(1)}, f32[88,256]{1,0:T(8,128)S(1)}, u32[]{:S(2)}, u32[]{:S(2)}) collective-permute-start(f32[88,256]{1,0:T(8,128)S(1)} %collective-permute-done.refs_0_.refs_8_), channel_id=1, source_target_pairs={{0,8},{8,0},{16,24},{24,16},{1,9},{9,1},{17,25},{25,17},{2,10},{10... | collective-permute-start | bytes 270344 | tf_op jit(solution)/shard_map/ppermute | solution.py:632
  19.4 2.3 %copy-start.4 = (f32[128,256]{1,0:T(8,128)S(1)}, f32[128,256]{1,0:T(8,128)}, u32[]{:S(2)}) copy-start(f32[128,256]{1,0:T(8,128)} %refs_11_.3) | copy-start | bytes 393220
  19.4 1.4 %collective-permute-start.6 = (f32[136,128]{1,0:T(8,128)S(1)}, f32[136,128]{1,0:T(8,128)S(1)}, u32[]{:S(2)}, u32[]{:S(2)}) collective-permute-start(f32[136,128]{1,0:T(8,128)S(1)} %get-tuple-element.46.refs_0_), channel_id=1, source_target_pairs={{0,8},{8,0},{16,24},{24,16},{1,9},{9,1},{17,25},{25,17},{2,10},{10... | collective-permute-start | bytes 208904 | tf_op jit(solution)/shard_map/ppermute | solution.py:700
  20.8 4.5 %collective-permute-start.7 = (f32[136,128]{1,0:T(8,128)S(1)}, f32[136,128]{1,0:T(8,128)S(1)}, u32[]{:S(2)}, u32[]{:S(2)}) collective-permute-start(f32[136,128]{1,0:T(8,128)S(1)} %get-tuple-element.48), channel_id=1, source_target_pairs={{0,16},{8,24},{16,0},{24,8},{1,17},{9,25},{17,1},{25,9},{2,18},{10... | collective-permute-start | bytes 208904 | tf_op jit(solution)/shard_map/ppermute | solution.py:700
  26.0 7.0 %collective-permute-start.8 = (f32[64,256]{1,0:T(8,128)S(1)}, f32[64,256]{1,0:T(8,128)S(1)}, u32[]{:S(2)}, u32[]{:S(2)}) collective-permute-start(f32[64,256]{1,0:T(8,128)S(1)} %get-tuple-element.66), channel_id=1, source_target_pairs={{0,4},{2,6},{4,0},{6,2},{1,5},{3,7},{5,1},{7,3},{8,12},{10,14},{12... | collective-permute-start | bytes 196616 | tf_op jit(solution)/shard_map/ppermute | solution.py:734
  28.7 6.1 %collective-permute-start.9 = (f32[64,256]{1,0:T(8,128)S(1)}, f32[64,256]{1,0:T(8,128)S(1)}, u32[]{:S(2)}, u32[]{:S(2)}) collective-permute-start(f32[64,256]{1,0:T(8,128)S(1)} %get-tuple-element.67), channel_id=1, source_target_pairs={{0,6},{2,4},{4,2},{6,0},{1,7},{3,5},{5,3},{7,1},{8,14},{10,12},{12... | collective-permute-start | bytes 196616 | tf_op jit(solution)/shard_map/ppermute | solution.py:734
  29.5 5.3 %collective-permute-start.10 = (f32[64,256]{1,0:T(8,128)S(1)}, f32[64,256]{1,0:T(8,128)S(1)}, u32[]{:S(2)}, u32[]{:S(2)}) collective-permute-start(f32[64,256]{1,0:T(8,128)S(1)} %get-tuple-element.68), channel_id=1, source_target_pairs={{0,2},{2,0},{4,6},{6,4},{1,3},{3,1},{5,7},{7,5},{8,10},{10,8},{12,... | collective-permute-start | bytes 196616 | tf_op jit(solution)/shard_map/ppermute | solution.py:734

commit v8 on v7

--- a/solution.py
+++ b/solution.py
@@ -104,15 +104,14 @@
         return taken
 
     sources = take(9)
-    outproj_source, message = take(2)
+    outproj_source, message, part = take(3)
     places = take(9)
     semaphores = take(1)[0]
     half = ch // 2
-    base = V + 2 + 3 * hl
     core = lax.rem(lax.axis_index("seq"), 2)
     copies = fetch(
         sources + [outproj_source.at[pl.ds(pl.multiple_of(core * half, 8), half), :]],
-        places + [message.at[base : base + half, 0:D]],
+        places + [part],
         semaphores,
     )
     flip = (iota((T, T), 0) + iota((T, T), 1) == T - 1).astype(f32).astype(bf16)
@@ -356,15 +355,12 @@
     others = dict(zip(order, take(nh - 1)))
     out_state, out_high, out_low, out_scale = take(4)
     out_write, out_inner, out_stepped, out_total = take(4)
-    half = ch // 2
-    base = V + 2 + 3 * hl
     mine = lax.axis_index("seq")
 
+    even = lax.rem(mine, 2) == 0
     pieces = []
     for k in range(1, nh):
-        near = nears[k][base : base + half, 0:D]
-        other = others[k][base : base + half, 0:D]
-        even = lax.rem(lax.bitwise_xor(mine, partners(ns, nh)[k][0]), 2) == 0
+        near, other = nears[k][...], others[k][...]
         pieces.append(jnp.where(even, near, other))
         pieces.append(jnp.where(even, other, near))
     weights = split2(jnp.concatenate(pieces, axis=0))
@@ -549,7 +545,7 @@
 
     head_rows = V + 2 + 3 * hl
     half = ch // 2
-    width = max(2 * ch, T, D)
+    width = max(2 * ch, T)
     share = T // nh
     fetched = [
         flat(inproj_first),
@@ -562,11 +558,11 @@
         line(skipgain_first),
         line(outnorm_first),
     ]
-    message = pl.pallas_call(
+    message, part = pl.pallas_call(
         functools.partial(tables_kernel, dims),
-        out_shape=shape(head_rows + half, width),
+        out_shape=(shape(head_rows, width), shape(half, D)),
         in_specs=[anywhere] * (len(fetched) + 1),
-        out_specs=vmem,
+        out_specs=(vmem, vmem),
         scratch_shapes=[room(value) for value in fetched]
         + [pltpu.SemaphoreType.DMA((len(fetched) + 1,))],
         compiler_params=pltpu.CompilerParams(vmem_limit_bytes=TABLES_LIMIT),
@@ -625,12 +621,13 @@
             for seq in range(ns)
             for head in range(nh)
         ]
-        sent = message if k < nh else message[0:head_rows]
-        messages[k] = lax.ppermute(sent, ("seq", "head"), pairs)
+        messages[k] = lax.ppermute(message, ("seq", "head"), pairs)
     swap = [(seq, seq ^ 1) for seq in range(ns)]
     order = in_turn(nh)[::-1]
-    others = [lax.ppermute(messages[k], "seq", swap) for k in order]
-
+    nears = {
+        k: lax.ppermute(part, "head", [(head, head ^ k) for head in range(nh)])
+        for k in in_turn(nh)
+    }
     mixed_high, mixed_low, embedded = pl.pallas_call(
         functools.partial(mix_kernel, dims),
         out_shape=(*halves(T, nh * ch), shape(T, D)),
@@ -641,6 +638,13 @@
         cost_estimate=heavy,
         name="mix",
     )(*[messages[k] for k in in_turn(count)[::-1] + [0]], embedding, pair_table)
+
+    mixed = [mixed_high, mixed_low, embedded]
+    for place, k in enumerate(order):
+        place = place % len(mixed)
+        mixed[place], nears[k] = lax.optimization_barrier((mixed[place], nears[k]))
+    mixed_high, mixed_low, embedded = mixed
+    others = [lax.ppermute(nears[k], "seq", swap) for k in order]
 
     state, hidden_high, hidden_low, scale, write, inner, stepped, total = pl.pallas_call(
         functools.partial(project_kernel, dims),
@@ -666,7 +670,7 @@
         own_low,
         state_high,
         state_low,
-        *[messages[k] for k in order],
+        *[nears[k] for k in order],
         *others,
     )
 

time: 35.6 us -> 37.5 us (1.053)
  starting transfers between devices: 11.8 us -> 16.4 us
  waiting for transfers between devices: 13.4 us -> 10.6 us
    ppermute x6 -> x9, starting transfers between devices: 6.38 us -> 11.1 us  [the longest x3 5.75 us: per_device(): messages[k] = lax.ppermute(message, ('seq', 'head'), pairs)]
    ppermute x6 -> x9, waiting for transfers between devices: 5.43 us -> 3.56 us  [the longest x3 2.37 us: per_device(): lax.ppermute(part, 'head', [(head, head ^ k) for head in range(nh)])]
    ppermute x2, waiting for transfers between devices: 3.19 us -> 2.63 us  [per_device(): lax.ppermute(state, 'seq', [(seq, seq ^ 2 ** bit) for seq in range(ns)])]
    ppermute x3, starting transfers between devices: 4.02 us -> 3.55 us  [per_device(): result = result + lax.ppermute(parts[k], 'head', pairs)]
    ppermute x2, starting transfers between devices: 1.39 us -> 1.78 us  [per_device(): lax.ppermute(state, 'seq', [(seq, seq ^ 2 ** bit) for seq in range(ns)])]
  transfers between devices with their start and end apart: 11 -> 14, of which waited for: 6 -> 8; matrix products, arithmetic and copies ran while one was open for 0% -> 0% of each run, Pallas kernels for 13% -> 12%
where the time goes in v8:
time: 37.5 us; the launch traced here: 37.4 us
  starting transfers between devices  16.4 us (44%)
  waiting for transfers between devices  10.6 us (28%)
  Pallas kernels  8.74 us (23%)
  other arithmetic  0.65 us (2%)
  local copies, waits for them, and re-layouts  0.64 us (2%)
    ppermute x3, starting transfers between devices, per_device(): messages[k] = lax.ppermute(message, ('seq', 'head'), pairs)  5.75 us
    ppermute x3, starting transfers between devices, per_device(): lax.ppermute(part, 'head', [(head, head ^ k) for head in range(nh)])  4.79 us
    ppermute x3, waiting for transfers between devices, per_device(): result = result + lax.ppermute(parts[k], 'head', pairs)  4.45 us
    ppermute x3, starting transfers between devices, per_device(): result = result + lax.ppermute(parts[k], 'head', pairs)  3.55 us
    ppermute x2, waiting for transfers between devices, per_device(): lax.ppermute(state, 'seq', [(seq, seq ^ 2 ** bit) for seq in range(ns)])  2.63 us
    ppermute x3, waiting for transfers between devices, per_device(): lax.ppermute(part, 'head', [(head, head ^ k) for head in range(nh)])  2.37 us
    pallas_call x1, Pallas kernels, per_device(): pl.pallas_call(functools.partial(tables_kernel, dims), out_shape=(shape(h...  2.06 us
    pallas_call x1, Pallas kernels, per_device(): pl.pallas_call(functools.partial(mix_kernel, dims), out_shape=(*halves(T,...  1.85 us
  transfers between devices with their start and end apart: 14, of which 8 were waited for; matrix products, arithmetic and copies ran while one was open for 0% of the time, Pallas kernels for 12%

profile of v8, /device:TPU:0, one launch (start us, length us, event | category | flops | bytes accessed | tf_op | source)
XLA Modules:
  0.0 37.4 jit_solution(11636763526056437046)
XLA Ops:
  0.0 0.0 copy-start.9
  0.0 0.0 copy-start.10
  0.0 0.0 copy-start.11
  0.0 0.0 copy-start.12
  0.1 0.0 copy-start.13
  0.1 0.0 copy-start.14
  0.1 2.1 %tables.1 = (f32[24,256]{1,0:T(8,128)}, f32[64,256]{1,0:T(8,128)}) custom-call(f32[512,128]{1,0:T(8,128)} %bitcast.24, s32[1,256]{1,0:T(1,128)} %bitcast.26, f32[16,256]{1,0:T(8,128)} %refs_4_.3, f32[1,256]{1,0:T(1,128)} %bitcast.19, f32[2,256]{1,0:T(2,128)} %bitcast.25, f32[1,2]{1,0:T(1,128)} %bitcast.27, f32[1,2]{1,0:T(1,128)} %bitcast.28, ...), custom_call_target="tpu_custom_call" | custom-call | flops 16106127360 | bytes 262144 | tf_op jit(solution)/shard_map/tables/pallas_call | solution.py:561
  2.1 0.0 copy-start.6
  2.2 5.0 %collective-permute-start.2 = (f32[24,256]{1,0:T(8,128)}, f32[24,256]{1,0:T(8,128)S(1)}, u32[]{:S(2)}, u32[]{:S(2)}) collective-permute-start(f32[24,256]{1,0:T(8,128)} %get-tuple-element.45.refs_3_), channel_id=1, source_target_pairs={{0,20},{2,22},{4,16},{6,18},{8,28},{10,30},{12,24},{14,26},{16,4},... | collective-permute-start | bytes 73736 | tf_op jit(solution)/shard_map/ppermute | solution.py:624
  7.2 0.5 %collective-permute-start.1 = (f32[24,256]{1,0:T(8,128)}, f32[24,256]{1,0:T(8,128)S(1)}, u32[]{:S(2)}, u32[]{:S(2)}) collective-permute-start(f32[24,256]{1,0:T(8,128)} %get-tuple-element.45.refs_3_), channel_id=1, source_target_pairs={{0,14},{2,12},{4,10},{6,8},{8,6},{10,4},{12,2},{14,0},{16,30},{18,... | collective-permute-start | bytes 73736 | tf_op jit(solution)/shard_map/ppermute | solution.py:624
  7.7 0.2 collective-permute-start
  7.9 3.4 %collective-permute-start.5 = (f32[64,256]{1,0:T(8,128)}, f32[64,256]{1,0:T(8,128)S(1)}, u32[]{:S(2)}, u32[]{:S(2)}) collective-permute-start(f32[64,256]{1,0:T(8,128)} %get-tuple-element.48), channel_id=1, source_target_pairs={{0,4},{2,6},{4,0},{6,2},{1,5},{3,7},{5,1},{7,3},{8,12},{10,14},{12... | collective-permute-start | bytes 196616 | tf_op jit(solution)/shard_map/ppermute | solution.py:628
  11.3 1.3 %collective-permute-start.4 = (f32[64,256]{1,0:T(8,128)}, f32[64,256]{1,0:T(8,128)S(1)}, u32[]{:S(2)}, u32[]{:S(2)}) collective-permute-start(f32[64,256]{1,0:T(8,128)} %get-tuple-element.48), channel_id=1, source_target_pairs={{0,6},{2,4},{4,2},{6,0},{1,7},{3,5},{5,3},{7,1},{8,14},{10,12},{12... | collective-permute-start | bytes 196616 | tf_op jit(solution)/shard_map/ppermute | solution.py:628
  12.6 0.0 copy-done
  12.6 0.0 copy-done.1
  12.7 0.6 %copy-done.8 = f32[256]{0:T(256)S(1)} copy-done((f32[256]{0:T(256)S(1)}, f32[256]{0:T(256)}, u32[]{:S(2)}) %copy-start.8) | copy-done | bytes 1048
  13.3 1.3 %prepare.1 = (f32[16,128]{1,0:T(8,128)S(1)}, f32[8,128]{1,0:T(8,128)S(1)}, bf16[256,256]{1,0:T(8,128)(2,1)S(1)}, bf16[128,256]{1,0:T(8,128)(2,1)S(1)}, bf16[128,...) custom-call(f32[16,256]{1,0:T(8,128)S(1)} %copy-done.6, ...), custom_call_target="tpu_custom_call" | custom-call | flops 16106127360 | bytes 262144 | tf_op jit(solution)/shard_map/prepare/pallas_call | solution.py:598
  14.6 0.0 collective-permute-done.2.refs_2_
  14.6 0.0 copy-done.15
  14.6 0.1 collective-permute-start.3
  14.7 0.0 collective-permute-done.1.refs_1_
  14.7 0.0 collective-permute-done.refs_0_
  14.7 0.0 copy-done.5
  14.7 1.9 %mix.1 = (bf16[256,512]{1,0:T(8,128)(2,1)S(1)}, bf16[256,512]{1,0:T(8,128)(2,1)S(1)}, f32[256,256]{1,0:T(8,128)S(1)}) custom-call(f32[24,256]{1,0:T(8,128)S(1)} %collective-permute-done.refs_0_, f32[24,256]{1,0:T(8,128)S(1)} %collective-permute-done.1.refs_1_, f32[24,256]{1,0:T(8,128)S(1)} %collective-permute-done.2.refs_2_, f32[24,256]{1,0:T(8,128)S(1)} %copy-done.5, ...), custom_call_target="tpu_custom_call" | custom-call | flops 16106127360 | bytes 262144 | tf_op jit(solution)/shard_map/mix/pallas_call | solution.py:631
  16.6 2.4 %collective-permute-done.3.refs_8_ = f32[64,256]{1,0:T(8,128)S(1)} collective-permute-done((f32[64,256]{1,0:T(8,128)S(1)}, f32[64,256]{1,0:T(8,128)S(1)}, u32[]{:S(2)}, u32[]{:S(2)}) %collective-permute-start.3) | collective-permute-done | bytes 65568 | tf_op jit(solution)/shard_map/ppermute | solution.py:628
  19.0 0.0 collective-permute-done.4.refs_9_
  19.0 0.0 collective-permute-done.5.refs_10_
  19.0 0.0 collective-permute-start.8
  19.0 0.5 %collective-permute-start.7 = (f32[64,256]{1,0:T(8,128)S(1)}, f32[64,256]{1,0:T(8,128)S(1)}, u32[]{:S(2)}, u32[]{:S(2)}) collective-permute-start(f32[64,256]{1,0:T(8,128)S(1)} %collective-permute-done.4.refs_9_), channel_id=1, source_target_pairs={{0,8},{8,0},{16,24},{24,16},{1,9},{9,1},{17,25},{25,17},{2,10},{10... | collective-permute-start | bytes 196616 | tf_op jit(solution)/shard_map/ppermute | solution.py:647
  19.5 0.1 collective-permute-start.6
  19.6 0.7 %collective-permute-done.8.refs_13_ = f32[64,256]{1,0:T(8,128)S(1)} collective-permute-done((f32[64,256]{1,0:T(8,128)S(1)}, f32[64,256]{1,0:T(8,128)S(1)}, u32[]{:S(2)}, u32[]{:S(2)}) %collective-permute-start.8) | collective-permute-done | bytes 65568 | tf_op jit(solution)/shard_map/ppermute | solution.py:647
  20.2 0.2 collective-permute-done.7.refs_12_
  20.4 0.4 collective-permute-done.6.refs_11_
  20.7 1.5 %project.1 = (f32[136,128]{1,0:T(8,128)S(1)}, bf16[256,256]{1,0:T(8,128)(2,1)S(1)}, bf16[256,256]{1,0:T(8,128)(2,1)S(1)}, f32[256,128]{1,0:T(8,128)S(1)}, f32[25...) custom-call(bf16[256,512]{1,0:T(8,128)(2,1)S(1)} %get-tuple-element.49.refs_0_, ...), custom_call_target="tpu_custom_call" | custom-call | tf_op jit(solution)/shard_map/project/pallas_call | solution.py:649
  22.3 0.0 copy-start.4
  22.3 0.2 collective-permute-start.9
  22.5 1.1 %collective-permute-done.9.refs_1_ = f32[136,128]{1,0:T(8,128)S(1)} collective-permute-done((f32[136,128]{1,0:T(8,128)S(1)}, f32[136,128]{1,0:T(8,128)S(1)}, u32[]{:S(2)}, u32[]{:S(2)}) %collective-permute-start.9) | collective-permute-done | bytes 69664 | tf_op jit(solution)/shard_map/ppermute | solution.py:704
  23.6 1.6 %collective-permute-start.10 = (f32[136,128]{1,0:T(8,128)S(1)}, f32[136,128]{1,0:T(8,128)S(1)}, u32[]{:S(2)}, u32[]{:S(2)}) collective-permute-start(f32[136,128]{1,0:T(8,128)S(1)} %get-tuple-element.64), channel_id=1, source_target_pairs={{0,16},{8,24},{16,0},{24,8},{1,17},{9,25},{17,1},{25,9},{2,18},{10... | collective-permute-start | bytes 208904 | tf_op jit(solution)/shard_map/ppermute | solution.py:704
  25.2 1.3 %block.1 = (f32[256,128]{1,0:T(8,128)S(1)}, f32[256,128]{1,0:T(8,128)S(1)}, f32[256,128]{1,0:T(8,128)S(1)}, f32[64,256]{1,0:T(8,128)S(1)}, bf16[128,256]{1,0:T(8,128)(2,1)S(1)}, /*index=5*/bf16[128,256]{1,0:T(8,128)(2,1)S(1)}) custom-call(bf16[256,256]{1,0:T(8,128)(2,1)S(1)} %get-tuple-element.65.refs_0_, bf16[256,256]{1,0:T(8,128)(2,1)S(1)} %get-tuple-element.66.refs_1_, ...), custom_call_target="tpu_custom_call" | custom-call | flops 16106127360 | bytes 262144 | tf_op jit(solution)/shard_map/block/pallas_call | solution.py:677
  26.5 1.5 %collective-permute-done.10.refs_1_ = f32[136,128]{1,0:T(8,128)S(1)} collective-permute-done((f32[136,128]{1,0:T(8,128)S(1)}, f32[136,128]{1,0:T(8,128)S(1)}, u32[]{:S(2)}, u32[]{:S(2)}) %collective-permute-start.10) | collective-permute-done | bytes 69664 | tf_op jit(solution)/shard_map/ppermute | solution.py:704
  28.0 0.7 %output.1 = (f32[64,256]{1,0:T(8,128)S(1)}, f32[64,256]{1,0:T(8,128)S(1)}, f32[64,256]{1,0:T(8,128)S(1)}, f32[64,256]{1,0:T(8,128)S(1)}) custom-call(f32[136,128]{1,0:T(8,128)S(1)} %get-tuple-element.63.refs_0_, f32[136,128]{1,0:T(8,128)S(1)} %collective-permute-done.10.refs_1_, f32[256,128]{1,0:T(8,128)S(1)} %get-tuple-element.75.refs_2_, ...), custom_call_target="tpu_custom_call" | custom-call | tf_op jit(solution)/shard_map/output/pallas_call | solution.py:726
  28.7 1.1 %collective-permute-start.11 = (f32[64,256]{1,0:T(8,128)S(1)}, f32[64,256]{1,0:T(8,128)S(1)}, u32[]{:S(2)}, u32[]{:S(2)}) collective-permute-start(f32[64,256]{1,0:T(8,128)S(1)} %get-tuple-element.82), channel_id=1, source_target_pairs={{0,4},{2,6},{4,0},{6,2},{1,5},{3,7},{5,1},{7,3},{8,12},{10,14},{12... | collective-permute-start | bytes 196616 | tf_op jit(solution)/shard_map/ppermute | solution.py:738
  29.8 1.5 %collective-permute-start.12 = (f32[64,256]{1,0:T(8,128)S(1)}, f32[64,256]{1,0:T(8,128)S(1)}, u32[]{:S(2)}, u32[]{:S(2)}) collective-permute-start(f32[64,256]{1,0:T(8,128)S(1)} %get-tuple-element.83), channel_id=1, source_target_pairs={{0,6},{2,4},{4,2},{6,0},{1,7},{3,5},{5,3},{7,1},{8,14},{10,12},{12... | collective-permute-start | bytes 196616 | tf_op jit(solution)/shard_map/ppermute | solution.py:738
  31.3 0.9 %collective-permute-start.13 = (f32[64,256]{1,0:T(8,128)S(1)}, f32[64,256]{1,0:T(8,128)S(1)}, u32[]{:S(2)}, u32[]{:S(2)}) collective-permute-start(f32[64,256]{1,0:T(8,128)S(1)} %get-tuple-element.84), channel_id=1, source_target_pairs={{0,2},{2,0},{4,6},{6,4},{1,3},{3,1},{5,7},{7,5},{8,10},{10,8},{12,... | collective-permute-start | bytes 196616 | tf_op jit(solution)/shard_map/ppermute | solution.py:738
  32.3 3.9 %collective-permute-done.11 = f32[64,256]{1,0:T(8,128)S(1)} collective-permute-done((f32[64,256]{1,0:T(8,128)S(1)}, f32[64,256]{1,0:T(8,128)S(1)}, u32[]{:S(2)}, u32[]{:S(2)}) %collective-permute-start.11) | collective-permute-done | bytes 65568 | tf_op jit(solution)/shard_map/ppermute | solution.py:738
  36.2 0.0 collective-permute-done.12
  36.2 0.5 %collective-permute-done.13 = f32[64,256]{1,0:T(8,128)S(1)} collective-permute-done((f32[64,256]{1,0:T(8,128)S(1)}, f32[64,256]{1,0:T(8,128)S(1)}, u32[]{:S(2)}, u32[]{:S(2)}) %collective-permute-start.13) | collective-permute-done | bytes 65568 | tf_op jit(solution)/shard_map/ppermute | solution.py:738
  36.7 0.6 %add_add_fusion = f32[64,256]{1,0:T(8,128)} fusion(f32[64,256]{1,0:T(8,128)S(1)} %collective-permute-done.13, f32[64,256]{1,0:T(8,128)S(1)} %collective-permute-done.12, f32[64,256]{1,0:T(8,128)S(1)} %get-tuple-element.81, f32[64,256]{1,0:T(8,128)S(1)} %collective-permute-done.11), kind=kLoop, calls=%fused_computation | loop fusion | flops 49152 | bytes 327680 | tf_op jit(solution)/shard_map/add | solution.py:738
  (20 shorter events, 0.1 us)
Async XLA Ops:
  0.0 12.6 %copy-start = (f32[256,2,128]{2,1,0:T(2,128)S(1)}, f32[256,2,128]{2,1,0:T(2,128)}, u32[]{:S(2)}) copy-start(f32[256,2,128]{2,1,0:T(2,128)} %param.26) | copy-start | bytes 786436
  0.0 12.6 %copy-start.1 = (f32[256,2,128]{2,1,0:T(2,128)S(1)}, f32[256,2,128]{2,1,0:T(2,128)}, u32[]{:S(2)}) copy-start(f32[256,2,128]{2,1,0:T(2,128)} %param.34) | copy-start | bytes 786436
  0.0 12.6 %copy-start.2 = (f32[256,2,128]{2,1,0:T(2,128)S(1)}, f32[256,2,128]{2,1,0:T(2,128)}, u32[]{:S(2)}) copy-start(f32[256,2,128]{2,1,0:T(2,128)} %param.35) | copy-start | bytes 786436
  0.0 12.6 %copy-start.3 = (f32[128,256]{1,0:T(8,128)S(1)}, f32[128,256]{1,0:T(8,128)}, u32[]{:S(2)}) copy-start(f32[128,256]{1,0:T(8,128)} %refs_4_.2) | copy-start | bytes 393220
  0.0 12.6 %copy-start.7 = (f32[256,2]{0,1:T(2,128)S(1)}, f32[256,2]{0,1:T(2,128)}, u32[]{:S(2)}) copy-start(f32[256,2]{0,1:T(2,128)} %param.36) | copy-start | bytes 6148
  0.0 12.6 %copy-start.9 = (s32[256]{0:T(256)S(1)}, s32[256]{0:T(256)}, u32[]{:S(2)}) copy-start(s32[256]{0:T(256)} %param.23) | copy-start | bytes 3076
  0.0 12.6 %copy-start.10 = (f32[256]{0:T(256)S(1)}, f32[256]{0:T(256)}, u32[]{:S(2)}) copy-start(f32[256]{0:T(256)} %param.33) | copy-start | bytes 3076
  0.0 12.6 %copy-start.11 = (f32[2]{0:T(128)S(1)}, f32[2]{0:T(128)}, u32[]{:S(2)}) copy-start(f32[2]{0:T(128)} %refs_9_.3) | copy-start | bytes 28
  0.0 12.6 %copy-start.12 = (f32[2]{0:T(128)S(1)}, f32[2]{0:T(128)}, u32[]{:S(2)}) copy-start(f32[2]{0:T(128)} %refs_10_.1) | copy-start | bytes 28
  0.1 12.6 %copy-start.13 = (f32[2]{0:T(128)S(1)}, f32[2]{0:T(128)}, u32[]{:S(2)}) copy-start(f32[2]{0:T(128)} %refs_11_.2) | copy-start | bytes 28
  0.1 12.6 %copy-start.14 = (f32[128]{0:T(128)S(1)}, f32[128]{0:T(128)}, u32[]{:S(2)}) copy-start(f32[128]{0:T(128)} %param.40) | copy-start | bytes 1540
  2.1 10.6 %copy-start.6 = (f32[16,256]{1,0:T(8,128)S(1)}, f32[16,256]{1,0:T(8,128)}, u32[]{:S(2)}) copy-start(f32[16,256]{1,0:T(8,128)} %refs_4_.3) | copy-start | bytes 49156
  2.2 12.5 %collective-permute-start.2 = (f32[24,256]{1,0:T(8,128)}, f32[24,256]{1,0:T(8,128)S(1)}, u32[]{:S(2)}, u32[]{:S(2)}) collective-permute-start(f32[24,256]{1,0:T(8,128)} %get-tuple-element.45.refs_3_), channel_id=1, source_target_pairs={{0,20},{2,22},{4,16},{6,18},{8,28},{10,30},{12,24},{14,26},{16,4},... | collective-permute-start | bytes 73736 | tf_op jit(solution)/shard_map/ppermute | solution.py:624
  7.2 7.5 %collective-permute-start.1 = (f32[24,256]{1,0:T(8,128)}, f32[24,256]{1,0:T(8,128)S(1)}, u32[]{:S(2)}, u32[]{:S(2)}) collective-permute-start(f32[24,256]{1,0:T(8,128)} %get-tuple-element.45.refs_3_), channel_id=1, source_target_pairs={{0,14},{2,12},{4,10},{6,8},{8,6},{10,4},{12,2},{14,0},{16,30},{18,... | collective-permute-start | bytes 73736 | tf_op jit(solution)/shard_map/ppermute | solution.py:624
  7.7 7.0 %collective-permute-start = (f32[24,256]{1,0:T(8,128)}, f32[24,256]{1,0:T(8,128)S(1)}, u32[]{:S(2)}, u32[]{:S(2)}) collective-permute-start(f32[24,256]{1,0:T(8,128)} %get-tuple-element.45.refs_3_), channel_id=1, source_target_pairs={{0,26},{2,24},{4,30},{6,28},{8,18},{10,16},{12,22},{14,20},{16,10}... | collective-permute-start | bytes 73736 | tf_op jit(solution)/shard_map/ppermute | solution.py:624
  7.9 11.1 %collective-permute-start.5 = (f32[64,256]{1,0:T(8,128)}, f32[64,256]{1,0:T(8,128)S(1)}, u32[]{:S(2)}, u32[]{:S(2)}) collective-permute-start(f32[64,256]{1,0:T(8,128)} %get-tuple-element.48), channel_id=1, source_target_pairs={{0,4},{2,6},{4,0},{6,2},{1,5},{3,7},{5,1},{7,3},{8,12},{10,14},{12... | collective-permute-start | bytes 196616 | tf_op jit(solution)/shard_map/ppermute | solution.py:628
  11.3 7.7 %collective-permute-start.4 = (f32[64,256]{1,0:T(8,128)}, f32[64,256]{1,0:T(8,128)S(1)}, u32[]{:S(2)}, u32[]{:S(2)}) collective-permute-start(f32[64,256]{1,0:T(8,128)} %get-tuple-element.48), channel_id=1, source_target_pairs={{0,6},{2,4},{4,2},{6,0},{1,7},{3,5},{5,3},{7,1},{8,14},{10,12},{12... | collective-permute-start | bytes 196616 | tf_op jit(solution)/shard_map/ppermute | solution.py:628
  12.6 0.7 %copy-start.8 = (f32[256]{0:T(256)S(1)}, f32[256]{0:T(256)}, u32[]{:S(2)}) copy-start(f32[256]{0:T(256)} %param.24) | copy-start | bytes 3076
  13.3 1.3 %copy-start.15 = (f32[64,256]{1,0:T(8,128)S(1)}, f32[64,256]{1,0:T(8,128)}, u32[]{:S(2)}) copy-start(f32[64,256]{1,0:T(8,128)} %get-tuple-element.48) | copy-start | bytes 196612
  13.3 1.4 %copy-start.5 = (f32[24,256]{1,0:T(8,128)S(1)}, f32[24,256]{1,0:T(8,128)}, u32[]{:S(2)}) copy-start(f32[24,256]{1,0:T(8,128)} %get-tuple-element.45.refs_3_) | copy-start | bytes 73732
  14.6 4.3 %collective-permute-start.3 = (f32[64,256]{1,0:T(8,128)S(1)}, f32[64,256]{1,0:T(8,128)S(1)}, u32[]{:S(2)}, u32[]{:S(2)}) collective-permute-start(f32[64,256]{1,0:T(8,128)S(1)} %copy-done.15), channel_id=1, source_target_pairs={{0,2},{2,0},{4,6},{6,4},{1,3},{3,1},{5,7},{7,5},{8,10},{10,8},{12,... | collective-permute-start | bytes 196616 | tf_op jit(solution)/shard_map/ppermute | solution.py:628
  19.0 1.3 %collective-permute-start.8 = (f32[64,256]{1,0:T(8,128)S(1)}, f32[64,256]{1,0:T(8,128)S(1)}, u32[]{:S(2)}, u32[]{:S(2)}) collective-permute-start(f32[64,256]{1,0:T(8,128)S(1)} %collective-permute-done.5.refs_10_), channel_id=1, source_target_pairs={{0,8},{8,0},{16,24},{24,16},{1,9},{9,1},{17,25},{25,17},{2,10},{10... | collective-permute-start | bytes 196616 | tf_op jit(solution)/shard_map/ppermute | solution.py:647
  19.0 1.4 %collective-permute-start.7 = (f32[64,256]{1,0:T(8,128)S(1)}, f32[64,256]{1,0:T(8,128)S(1)}, u32[]{:S(2)}, u32[]{:S(2)}) collective-permute-start(f32[64,256]{1,0:T(8,128)S(1)} %collective-permute-done.4.refs_9_), channel_id=1, source_target_pairs={{0,8},{8,0},{16,24},{24,16},{1,9},{9,1},{17,25},{25,17},{2,10},{10... | collective-permute-start | bytes 196616 | tf_op jit(solution)/shard_map/ppermute | solution.py:647
  19.5 1.3 %collective-permute-start.6 = (f32[64,256]{1,0:T(8,128)S(1)}, f32[64,256]{1,0:T(8,128)S(1)}, u32[]{:S(2)}, u32[]{:S(2)}) collective-permute-start(f32[64,256]{1,0:T(8,128)S(1)} %collective-permute-done.3.refs_8_), channel_id=1, source_target_pairs={{0,8},{8,0},{16,24},{24,16},{1,9},{9,1},{17,25},{25,17},{2,10},{10... | collective-permute-start | bytes 196616 | tf_op jit(solution)/shard_map/ppermute | solution.py:647
  22.3 2.9 %copy-start.4 = (f32[128,256]{1,0:T(8,128)S(1)}, f32[128,256]{1,0:T(8,128)}, u32[]{:S(2)}) copy-start(f32[128,256]{1,0:T(8,128)} %refs_11_.3) | copy-start | bytes 393220
  22.3 1.3 %collective-permute-start.9 = (f32[136,128]{1,0:T(8,128)S(1)}, f32[136,128]{1,0:T(8,128)S(1)}, u32[]{:S(2)}, u32[]{:S(2)}) collective-permute-start(f32[136,128]{1,0:T(8,128)S(1)} %get-tuple-element.62.refs_0_), channel_id=1, source_target_pairs={{0,8},{8,0},{16,24},{24,16},{1,9},{9,1},{17,25},{25,17},{2,10},{10... | collective-permute-start | bytes 208904 | tf_op jit(solution)/shard_map/ppermute | solution.py:704
  23.6 4.4 %collective-permute-start.10 = (f32[136,128]{1,0:T(8,128)S(1)}, f32[136,128]{1,0:T(8,128)S(1)}, u32[]{:S(2)}, u32[]{:S(2)}) collective-permute-start(f32[136,128]{1,0:T(8,128)S(1)} %get-tuple-element.64), channel_id=1, source_target_pairs={{0,16},{8,24},{16,0},{24,8},{1,17},{9,25},{17,1},{25,9},{2,18},{10... | collective-permute-start | bytes 208904 | tf_op jit(solution)/shard_map/ppermute | solution.py:704
  28.7 7.5 %collective-permute-start.11 = (f32[64,256]{1,0:T(8,128)S(1)}, f32[64,256]{1,0:T(8,128)S(1)}, u32[]{:S(2)}, u32[]{:S(2)}) collective-permute-start(f32[64,256]{1,0:T(8,128)S(1)} %get-tuple-element.82), channel_id=1, source_target_pairs={{0,4},{2,6},{4,0},{6,2},{1,5},{3,7},{5,1},{7,3},{8,12},{10,14},{12... | collective-permute-start | bytes 196616 | tf_op jit(solution)/shard_map/ppermute | solution.py:738
  29.8 6.4 %collective-permute-start.12 = (f32[64,256]{1,0:T(8,128)S(1)}, f32[64,256]{1,0:T(8,128)S(1)}, u32[]{:S(2)}, u32[]{:S(2)}) collective-permute-start(f32[64,256]{1,0:T(8,128)S(1)} %get-tuple-element.83), channel_id=1, source_target_pairs={{0,6},{2,4},{4,2},{6,0},{1,7},{3,5},{5,3},{7,1},{8,14},{10,12},{12... | collective-permute-start | bytes 196616 | tf_op jit(solution)/shard_map/ppermute | solution.py:738
  31.3 5.4 %collective-permute-start.13 = (f32[64,256]{1,0:T(8,128)S(1)}, f32[64,256]{1,0:T(8,128)S(1)}, u32[]{:S(2)}, u32[]{:S(2)}) collective-permute-start(f32[64,256]{1,0:T(8,128)S(1)} %get-tuple-element.84), channel_id=1, source_target_pairs={{0,2},{2,0},{4,6},{6,4},{1,3},{3,1},{5,7},{7,5},{8,10},{10,8},{12,... | collective-permute-start | bytes 196616 | tf_op jit(solution)/shard_map/ppermute | solution.py:738

commit v9 on v7

--- a/solution.py
+++ b/solution.py
@@ -48,9 +48,14 @@
 
 
 def dot_split(left, right, dims=MM):
-    return (
-        dot(left[0], right[1], dims) + dot(left[1], right[0], dims)
-    ) + dot(left[0], right[0], dims)
+    axis = 1 if dims == TN else 0
+    size = left[0].shape[axis]
+    if size % 16:
+        return (dot(left[0], right[1], dims) + dot(left[1], right[0], dims)) + dot(
+            left[0], right[0], dims
+        )
+    both = dot(jnp.concatenate([left[1], left[0]], axis=axis), right[0], dims)
+    return (dot(left[0], right[1], dims) + both[0:size]) + both[size:]
 
 
 def dot3(left, right, dims=MM):
@@ -121,10 +126,10 @@
     (inproj, tok, emb, prenorm, stepmap, bias, rates, skip, outnorm) = places
     normed = split2(rms(emb[...]) * prenorm[...])
     raw_t = dot_split(split2(stepmap[...]), normed, NT)
-    gate = dot_split(normed, split2(inproj[pl.ds(0, D, stride=2), :]))
-    inner = dot_split(normed, split2(inproj[pl.ds(1, D, stride=2), :]))
-    message[0:V, 0:ch] = gate
-    message[0:V, ch : 2 * ch] = inner
+    weights = jnp.concatenate(
+        [inproj[pl.ds(0, D, stride=2), :], inproj[pl.ds(1, D, stride=2), :]], axis=1
+    )
+    message[0:V, 0 : 2 * ch] = dot_split(normed, split2(weights))
     tokens = jnp.broadcast_to(tok[...].astype(f32), (8, T)).astype(bf16)
     message[V : V + 1, 0:T] = dot(tokens, flip)[0:1]
     message[V + 1 : V + 2, 0:ch] = outnorm[...]
@@ -244,18 +249,14 @@
         return jnp.concatenate([packets[k][low : low + hl, 0:V] for k in range(nh)], axis=0)
 
     step_t, log_t, skip_t = rows_of(0), rows_of(1), rows_of(2)
-    spread_heads = (iota((H, LV), 1) // V == iota((H, LV), 0)).astype(f32).astype(bf16)
-
-    def widen(value):
-        high, middle, low = split3(value)
-        return (dot(low, spread_heads, TN) + dot(middle, spread_heads, TN)) + dot(
-            high, spread_heads, TN
-        )
-
+    narrow = split3(jnp.concatenate([step_t, log_t, skip_t], axis=1))
+    narrow = jnp.concatenate([part.astype(f32) for part in narrow], axis=0).astype(bf16)
+    spread_heads = (iota((3 * H, LV), 1) // V == iota((3 * H, LV), 0) % H).astype(f32).astype(bf16)
+    wide = dot(narrow, spread_heads, TN)
     own = iota((V, LV), 1) % V == iota((V, LV), 0)
-    decay_table = jnp.exp(widen(log_t))
-    step_table = jnp.where(own, widen(step_t), 0.0)
-    gain_table = jnp.where(own, widen(skip_t), 0.0)
+    decay_table = jnp.exp(wide[V : 2 * V])
+    step_table = jnp.where(own, wide[0:V], 0.0)
+    gain_table = jnp.where(own, wide[2 * V : 3 * V], 0.0)
     gates = jnp.concatenate([packets[k][0:V, 0:ch] for k in range(nh)], axis=1)
     inners = jnp.concatenate([packets[k][0:V, ch : 2 * ch] for k in range(nh)], axis=1)
     gains = jnp.concatenate([packets[k][V + 1 : V + 2, 0:ch] for k in range(nh)], axis=1)
@@ -271,29 +272,36 @@
     first, second = iota((T, T), 0), iota((T, T), 1)
     later = (first > second).astype(f32).astype(bf16)
     sooner = (first < second).astype(f32).astype(bf16)
-    logs3 = split3(logs)
-    after = dot(logs3[2], later) + dot(logs3[1], later) + dot(logs3[0], later)
-    before = dot(logs3[2], sooner) + dot(logs3[1], sooner) + dot(logs3[0], sooner)
-    totals = jnp.sum(logs, axis=1, keepdims=True)
-    total_rows = jnp.broadcast_to(totals, (ns * H, 128))
+    size = ns * H
+    sums = dot(
+        jnp.concatenate(split3(logs)[::-1], axis=0), jnp.concatenate([later, sooner], axis=1)
+    )
+    sums = (sums[0:size] + sums[size : 2 * size]) + sums[2 * size :]
+    after, before = sums[:, 0:T], sums[:, T:]
+    totals = jnp.broadcast_to(jnp.sum(logs, axis=1, keepdims=True), (size, 128))
+    piece = iota((size, 128), 1)
+    high, middle, low = [part.astype(f32) for part in split3(totals)]
+    totals = jnp.where(
+        piece == 0, high, jnp.where(piece == 1, middle, jnp.where(piece == 2, low, 0.0))
+    )
     row, column = iota((ns * H, ns * H), 0), iota((ns * H, ns * H), 1)
     row_block, column_block = row // H, column // H
     between = ((row_block < column_block) & (column_block < mine)) | (
         (row_block > column_block) & (column_block > mine)
     )
     between = (between & (row % H == column % H)).astype(f32).astype(bf16)
-    gap = dot_left_exact(between, total_rows)[:, 0:1]
+    gap = jnp.sum(dot(between, totals.astype(bf16)), axis=1, keepdims=True)
     block_of = iota((ns * H, T), 0) // H
     weight_up = jnp.where(block_of < mine, jnp.exp(after + gap), 0.0)
     weight_down = jnp.where(block_of > mine, jnp.exp(before + gap), 0.0)
-    entering = jnp.zeros((2 * H, LV), f32)
+    entering = jnp.zeros((4 * H, LV), f32)
     for block in range(ns):
-        both = jnp.concatenate(
-            [weight_up[block * H : (block + 1) * H], weight_down[block * H : (block + 1) * H]],
-            axis=0,
+        rows = slice(block * H, (block + 1) * H)
+        both = jnp.concatenate([weight_up[rows], weight_down[rows]], axis=0)
+        entering = entering + dot(
+            jnp.concatenate(split2(both), axis=0), onehots[block], NT
         )
-        high, low = split2(both)
-        entering = entering + (dot(low, onehots[block], NT) + dot(high, onehots[block], NT))
+    entering = entering[2 * H :] + entering[0 : 2 * H]
     diagonal = iota((H, LV), 1) // V == iota((H, LV), 0)
     step_row = jnp.sum(step_table, axis=0, keepdims=True)
     enter_up = step_row * jnp.sum(
@@ -332,9 +340,14 @@
     wide = max(ch, 256)
     group = (iota((wide, wide), 0) // P == iota((wide, wide), 1) // P).astype(f32).astype(bf16)
     high, low = split2(value * value)
-    for start in range(0, C, wide):
+    starts = list(range(0, C, wide))
+    rows = 2 * T
+    stacked = [half[:, start : start + wide] for start in starts for half in (low, high)]
+    squares = dot(jnp.concatenate(stacked, axis=0), group)
+    for number, start in enumerate(starts):
+        place = 2 * number * rows
+        square = squares[place : place + rows] + squares[place + rows : place + 2 * rows]
         stop = start + wide
-        square = dot(low[:, start:stop], group) + dot(high[:, start:stop], group)
         normed = value[:, start:stop] * lax.rsqrt(square * (1.0 / P) + epsilon)
         out_high[:, start:stop], out_low[:, start:stop] = split2(
             (normed[0:T] + normed[T : 2 * T]) * gains[:, start:stop]
@@ -383,7 +396,9 @@
     step = softplus(rows[:, ch : 2 * ch] + small[0:1, :])
     stepped = inner * step
     upto = (iota((T, T), 0) >= iota((T, T), 1)).astype(f32).astype(bf16)
-    total = dot_left_exact(upto, -small[1:2, :] * step)
+    log_high, log_middle, log_low = split3(-small[1:2, :] * step)
+    total = dot(upto, jnp.concatenate([log_low, log_middle], axis=1))
+    total = (total[:, 0:ch] + total[:, ch:]) + dot(upto, log_high)
     end = total[T - 1 : T, :]
     state = dot3(stepped * jnp.exp(end - total), write, TN)
     out_state[0:ch, :] = state
@@ -408,12 +423,14 @@
 
     high, low, scale, write, inner, stepped, total, choose = take(8)
     rest_high, rest_low, small, outproj2 = take(4)
-    base, out_read, out_gate, own, out_high, out_low, hidden_ref = take(7)
+    base, read_high, read_low, out_fade, out_gate, own, out_high, out_low, hidden_ref = take(9)
     rows = dot_split((high[...], low[...]), (rest_high[...], rest_low[...]))
     out_gate[...] = silu(rows[:, 0:ch] * scale[...])
     read = rows[:, ch:] * scale[...]
-    out_read[...] = read
-    products = dot3(read, write[...], NT)
+    read = split2(read)
+    read_high[...], read_low[...] = read
+    out_fade[...] = jnp.exp(total[...])
+    products = dot_split(read, split2(write[...]), NT)
     stepped_high, stepped_low = split2(stepped[...])
     select = (iota((8, ch), 1) == iota((8, ch), 0) * P).astype(f32).astype(bf16)
     total_high, total_middle, total_low = split3(total[...])
@@ -477,13 +494,13 @@
 def output_kernel(dims, bit, *refs):
     V, D, hl, ch, nh, ns, T, N = dims
     P = ch // hl
-    prefix, came, read, base, total, gate, own, proj_high, proj_low = refs[:9]
-    outs, partial_ref = refs[9 : 9 + nh], refs[9 + nh]
+    prefix, came, read_high, read_low, base, fade, gate, own, proj_high, proj_low = refs[:10]
+    outs, partial_ref = refs[10 : 10 + nh], refs[10 + nh]
     entering = prefix_joined(dims, bit, prefix, came)
-    value = (base[...] + dot3(read[...], entering, NT) * jnp.exp(total[...])) * gate[...]
+    value = (base[...] + dot_split((read_high[...], read_low[...]), split2(entering), NT) * fade[...]) * gate[...]
     group = (iota((ch, ch), 0) // P == iota((ch, ch), 1) // P).astype(f32).astype(bf16)
-    high, low = split2(value * value)
-    square = dot(low, group) + dot(high, group)
+    square = dot(jnp.concatenate(split2(value * value), axis=0), group)
+    square = square[T:] + square[0:T]
     value = value * lax.rsqrt(square * (1.0 / P) + epsilon)
     share = T // nh
     partial_ref[...] = dot_split(split2(value), (proj_high[...], proj_low[...]))
@@ -670,11 +687,18 @@
         *others,
     )
 
-    base, read, gate, own, proj_high, proj_low = pl.pallas_call(
+    base, read_high, read_low, fade, gate, own, proj_high, proj_low = pl.pallas_call(
         functools.partial(block_kernel, dims),
-        out_shape=(shape(T, ch), shape(T, N), shape(T, ch), shape(share, D), *halves(ch, D)),
+        out_shape=(
+            shape(T, ch),
+            *halves(T, N),
+            shape(T, ch),
+            shape(T, ch),
+            shape(share, D),
+            *halves(ch, D),
+        ),
         in_specs=[vmem] * 12,
-        out_specs=(vmem,) * 6,
+        out_specs=(vmem,) * 8,
         scratch_shapes=[pltpu.VMEM((T, D), f32)],
         compiler_params=params,
         cost_estimate=heavy,
@@ -722,12 +746,12 @@
     parts = pl.pallas_call(
         functools.partial(output_kernel, dims, bits - 1),
         out_shape=(shape(share, D),) * nh,
-        in_specs=[vmem] * 9,
+        in_specs=[vmem] * 10,
         out_specs=(vmem,) * nh,
         scratch_shapes=[pltpu.VMEM((T, D), f32)],
         compiler_params=params,
         name="output",
-    )(prefix, came, read, base, total, gate, own, proj_high, proj_low)
+    )(prefix, came, read_high, read_low, base, fade, gate, own, proj_high, proj_low)
     result = parts[0]
     for k in in_turn(nh):
         pairs = [(source, source ^ k) for source in range(nh)]

time: 35.6 us -> 35.6 us (level)
  transfers between devices with their start and end apart: 11 -> 11, of which waited for: 6 -> 6; matrix products, arithmetic and copies ran while one was open for 0% -> 0% of each run, Pallas kernels for 13% -> 12%
where the time goes in v9:
time: 35.6 us; the launch traced here: 35.4 us
  waiting for transfers between devices  13.5 us (38%)
  starting transfers between devices  11.8 us (33%)
  Pallas kernels  8.61 us (24%)
  local copies, waits for them, and re-layouts  0.65 us (2%)
  other arithmetic  0.65 us (2%)
    ppermute x3, starting transfers between devices, per_device(): messages[k] = lax.ppermute(sent, ('seq', 'head'), pairs)  5.75 us
    ppermute x3, waiting for transfers between devices, per_device(): messages[k] = lax.ppermute(sent, ('seq', 'head'), pairs)  5.43 us
    ppermute x3, waiting for transfers between devices, per_device(): result = result + lax.ppermute(parts[k], 'head', pairs)  4.77 us
    ppermute x3, starting transfers between devices, per_device(): result = result + lax.ppermute(parts[k], 'head', pairs)  4.02 us
    ppermute x2, waiting for transfers between devices, per_device(): lax.ppermute(state, 'seq', [(seq, seq ^ 2 ** bit) for seq in range(ns)])  3.31 us
    pallas_call x1, Pallas kernels, per_device(): pl.pallas_call(functools.partial(tables_kernel, dims), out_shape=shape(he...  2.03 us
    pallas_call x1, Pallas kernels, per_device(): pl.pallas_call(functools.partial(mix_kernel, dims), out_shape=(*halves(T,...  1.9 us
    pallas_call x1, Pallas kernels, per_device(): pl.pallas_call(functools.partial(project_kernel, dims), out_shape=(shape(...  1.51 us
  transfers between devices with their start and end apart: 11, of which 6 were waited for; matrix products, arithmetic and copies ran while one was open for 0% of the time, Pallas kernels for 12%

profile of v9, /device:TPU:0, one launch (start us, length us, event | category | flops | bytes accessed | tf_op | source)
XLA Modules:
  0.0 35.4 jit_solution(14999096131809428901)
XLA Ops:
  0.0 0.0 copy-start.9
  0.0 0.0 copy-start.10
  0.0 0.0 copy-start.12
  0.0 0.0 copy-start.13
  0.1 0.0 copy-start.14
  0.1 2.0 %tables.1.refs_3_ = f32[88,256]{1,0:T(8,128)} custom-call(f32[512,128]{1,0:T(8,128)} %bitcast.24, s32[1,256]{1,0:T(1,128)} %bitcast.26, f32[16,256]{1,0:T(8,128)} %refs_4_.3, f32[1,256]{1,0:T(1,128)} %bitcast.19, f32[2,256]{1,0:T(2,128)} %bitcast.25, f32[1,2]{1,0:T(1,128)} %bitcast.27, f32[1,2]{1,0:T(1,128)} %bitcast.28, f32[1,2]{1,0:T(1,128)} %bitcast.29, ...), custom_call_target="tpu_custom_call" | custom-call | flops 16106127360 | bytes 262144 | tf_op jit(solution)/shard_map/tables/pallas_call | solution.py:582
  2.1 5.0 %collective-permute-start.2 = (f32[88,256]{1,0:T(8,128)}, f32[88,256]{1,0:T(8,128)S(1)}, u32[]{:S(2)}, u32[]{:S(2)}) collective-permute-start(f32[88,256]{1,0:T(8,128)} %tables.1.refs_3_), channel_id=1, source_target_pairs={{0,20},{2,22},{4,16},{6,18},{8,28},{10,30},{12,24},{14,26},{16,4},... | collective-permute-start | bytes 270344 | tf_op jit(solution)/shard_map/ppermute | solution.py:646
  7.1 0.5 %collective-permute-start.1 = (f32[88,256]{1,0:T(8,128)}, f32[88,256]{1,0:T(8,128)S(1)}, u32[]{:S(2)}, u32[]{:S(2)}) collective-permute-start(f32[88,256]{1,0:T(8,128)} %tables.1.refs_3_), channel_id=1, source_target_pairs={{0,14},{2,12},{4,10},{6,8},{8,6},{10,4},{12,2},{14,0},{16,30},{18,... | collective-permute-start | bytes 270344 | tf_op jit(solution)/shard_map/ppermute | solution.py:646
  7.7 0.2 collective-permute-start
  7.9 0.0 copy-done.1
  7.9 0.0 copy-done.2
  7.9 0.0 copy-done.3
  7.9 0.0 copy-done.6
  7.9 0.0 copy-done.9
  7.9 0.0 copy-done.10
  7.9 0.0 copy-done.12
  7.9 0.0 copy-done.13
  7.9 0.0 copy-done.14
  8.0 0.6 %copy-done.7 = f32[256,2]{0,1:T(2,128)S(1)} copy-done((f32[256,2]{0,1:T(2,128)S(1)}, f32[256,2]{0,1:T(2,128)}, u32[]{:S(2)}) %copy-start.7) | copy-done | bytes 2072
  8.5 0.0 copy-done.8
  8.5 0.0 copy-done.11
  8.6 1.3 %prepare.1 = (f32[16,128]{1,0:T(8,128)S(1)}, f32[8,128]{1,0:T(8,128)S(1)}, bf16[256,256]{1,0:T(8,128)(2,1)S(1)}, bf16[128,256]{1,0:T(8,128)(2,1)S(1)}, bf16[128,...) custom-call(f32[16,256]{1,0:T(8,128)S(1)} %copy-done.6, ...), custom_call_target="tpu_custom_call" | custom-call | flops 16106127360 | bytes 262144 | tf_op jit(solution)/shard_map/prepare/pallas_call | solution.py:619
  9.8 4.5 %collective-permute-done.2.refs_2_.refs_10_ = f32[88,256]{1,0:T(8,128)S(1)} collective-permute-done((f32[88,256]{1,0:T(8,128)}, f32[88,256]{1,0:T(8,128)S(1)}, u32[]{:S(2)}, u32[]{:S(2)}) %collective-permute-start.2) | collective-permute-done | bytes 90144 | tf_op jit(solution)/shard_map/ppermute | solution.py:646
  14.3 0.0 collective-permute-start.5
  14.3 0.0 collective-permute-done.1.refs_1_.refs_9_
  14.3 0.5 %collective-permute-start.4 = (f32[88,256]{1,0:T(8,128)S(1)}, f32[88,256]{1,0:T(8,128)S(1)}, u32[]{:S(2)}, u32[]{:S(2)}) collective-permute-start(f32[88,256]{1,0:T(8,128)S(1)} %collective-permute-done.1.refs_1_.refs_9_), channel_id=1, source_target_pairs={{0,8},{8,0},{16,24},{24,16},{1,9},{9,1},{17,25},{25,17},{2,10},{10... | collective-permute-start | bytes 270344 | tf_op jit(solution)/shard_map/ppermute | solution.py:649
  14.9 0.9 %collective-permute-done.refs_0_.refs_8_ = f32[88,256]{1,0:T(8,128)S(1)} collective-permute-done((f32[88,256]{1,0:T(8,128)}, f32[88,256]{1,0:T(8,128)S(1)}, u32[]{:S(2)}, u32[]{:S(2)}) %collective-permute-start) | collective-permute-done | bytes 90144 | tf_op jit(solution)/shard_map/ppermute | solution.py:646
  15.8 0.1 collective-permute-start.3
  15.9 0.0 copy-done.5
  15.9 1.9 %mix.1 = (bf16[256,512]{1,0:T(8,128)(2,1)S(1)}, bf16[256,512]{1,0:T(8,128)(2,1)S(1)}, f32[256,256]{1,0:T(8,128)S(1)}) custom-call(f32[88,256]{1,0:T(8,128)S(1)} %collective-permute-done.refs_0_.refs_8_, f32[88,256]{1,0:T(8,128)S(1)} %collective-permute-done.1.refs_1_.refs_9_, f32[88,256]{1,0:T(8,128)S(1)} %collective-permute-done.2.refs_2_.refs_10_, ...), custom_call_target="tpu_custom_call" | custom-call | flops 16106127360 | bytes 262144 | tf_op jit(solution)/shard_map/mix/pallas_call | solution.py:651
  17.8 0.0 collective-permute-done.5.refs_13_
  17.8 0.0 collective-permute-done.4.refs_12_
  17.8 0.0 collective-permute-done.3.refs_11_
  17.9 1.5 %project.1 = (f32[136,128]{1,0:T(8,128)S(1)}, bf16[256,256]{1,0:T(8,128)(2,1)S(1)}, bf16[256,256]{1,0:T(8,128)(2,1)S(1)}, f32[256,128]{1,0:T(8,128)S(1)}, f32[25...) custom-call(bf16[256,512]{1,0:T(8,128)(2,1)S(1)} %get-tuple-element.40.refs_0_, ...), custom_call_target="tpu_custom_call" | custom-call | tf_op jit(solution)/shard_map/project/pallas_call | solution.py:662
  19.4 0.0 copy-start.4
  19.4 0.5 %collective-permute-start.6 = (f32[136,128]{1,0:T(8,128)S(1)}, f32[136,128]{1,0:T(8,128)S(1)}, u32[]{:S(2)}, u32[]{:S(2)}) collective-permute-start(f32[136,128]{1,0:T(8,128)S(1)} %get-tuple-element.48.refs_0_), channel_id=1, source_target_pairs={{0,8},{8,0},{16,24},{24,16},{1,9},{9,1},{17,25},{25,17},{2,10},{10... | collective-permute-start | bytes 208904 | tf_op jit(solution)/shard_map/ppermute | solution.py:724
  19.8 0.9 %collective-permute-done.6.refs_1_ = f32[136,128]{1,0:T(8,128)S(1)} collective-permute-done((f32[136,128]{1,0:T(8,128)S(1)}, f32[136,128]{1,0:T(8,128)S(1)}, u32[]{:S(2)}, u32[]{:S(2)}) %collective-permute-start.6) | collective-permute-done | bytes 69664 | tf_op jit(solution)/shard_map/ppermute | solution.py:724
  20.8 0.9 %collective-permute-start.7 = (f32[136,128]{1,0:T(8,128)S(1)}, f32[136,128]{1,0:T(8,128)S(1)}, u32[]{:S(2)}, u32[]{:S(2)}) collective-permute-start(f32[136,128]{1,0:T(8,128)S(1)} %get-tuple-element.50), channel_id=1, source_target_pairs={{0,16},{8,24},{16,0},{24,8},{1,17},{9,25},{17,1},{25,9},{2,18},{10... | collective-permute-start | bytes 208904 | tf_op jit(solution)/shard_map/ppermute | solution.py:724
  21.7 1.2 %block.1 = (f32[256,128]{1,0:T(8,128)S(1)}, bf16[256,128]{1,0:T(8,128)(2,1)S(1)}, bf16[256,128]{1,0:T(8,128)(2,1)S(1)}, f32[256,128]{1,0:T(8,128)S(1)}, f32[256,...) custom-call(bf16[256,256]{1,0:T(8,128)(2,1)S(1)} %get-tuple-element.51.refs, ...), custom_call_target="tpu_custom_call" | custom-call | flops 16106127360 | bytes 262144 | tf_op jit(solution)/shard_map/block/pallas_call | solution.py:690
  22.9 2.4 %collective-permute-done.7.refs_1_ = f32[136,128]{1,0:T(8,128)S(1)} collective-permute-done((f32[136,128]{1,0:T(8,128)S(1)}, f32[136,128]{1,0:T(8,128)S(1)}, u32[]{:S(2)}, u32[]{:S(2)}) %collective-permute-start.7) | collective-permute-done | bytes 69664 | tf_op jit(solution)/shard_map/ppermute | solution.py:724
  25.3 0.7 %output.1 = (f32[64,256]{1,0:T(8,128)S(1)}, f32[64,256]{1,0:T(8,128)S(1)}, f32[64,256]{1,0:T(8,128)S(1)}, f32[64,256]{1,0:T(8,128)S(1)}) custom-call(f32[136,128]{1,0:T(8,128)S(1)} %get-tuple-element.49.refs_0_, f32[136,128]{1,0:T(8,128)S(1)} %collective-permute-done.7.refs_1_, bf16[256,128]{1,0:T(8,128)(2,1)S(1)} %get-tuple-element.61.refs_2_, ...), custom_call_target="tpu_custom_call" | custom-call | tf_op jit(solution)/shard_map/output/pallas_call | solution.py:746
  26.0 2.7 %collective-permute-start.8 = (f32[64,256]{1,0:T(8,128)S(1)}, f32[64,256]{1,0:T(8,128)S(1)}, u32[]{:S(2)}, u32[]{:S(2)}) collective-permute-start(f32[64,256]{1,0:T(8,128)S(1)} %get-tuple-element.70), channel_id=1, source_target_pairs={{0,4},{2,6},{4,0},{6,2},{1,5},{3,7},{5,1},{7,3},{8,12},{10,14},{12... | collective-permute-start | bytes 196616 | tf_op jit(solution)/shard_map/ppermute | solution.py:758
  28.7 0.8 %collective-permute-start.9 = (f32[64,256]{1,0:T(8,128)S(1)}, f32[64,256]{1,0:T(8,128)S(1)}, u32[]{:S(2)}, u32[]{:S(2)}) collective-permute-start(f32[64,256]{1,0:T(8,128)S(1)} %get-tuple-element.71), channel_id=1, source_target_pairs={{0,6},{2,4},{4,2},{6,0},{1,7},{3,5},{5,3},{7,1},{8,14},{10,12},{12... | collective-permute-start | bytes 196616 | tf_op jit(solution)/shard_map/ppermute | solution.py:758
  29.5 0.5 %collective-permute-start.10 = (f32[64,256]{1,0:T(8,128)S(1)}, f32[64,256]{1,0:T(8,128)S(1)}, u32[]{:S(2)}, u32[]{:S(2)}) collective-permute-start(f32[64,256]{1,0:T(8,128)S(1)} %get-tuple-element.72), channel_id=1, source_target_pairs={{0,2},{2,0},{4,6},{6,4},{1,3},{3,1},{5,7},{7,5},{8,10},{10,8},{12,... | collective-permute-start | bytes 196616 | tf_op jit(solution)/shard_map/ppermute | solution.py:758
  30.0 2.9 %collective-permute-done.8 = f32[64,256]{1,0:T(8,128)S(1)} collective-permute-done((f32[64,256]{1,0:T(8,128)S(1)}, f32[64,256]{1,0:T(8,128)S(1)}, u32[]{:S(2)}, u32[]{:S(2)}) %collective-permute-start.8) | collective-permute-done | bytes 65568 | tf_op jit(solution)/shard_map/ppermute | solution.py:758
  33.0 1.8 %collective-permute-done.9 = f32[64,256]{1,0:T(8,128)S(1)} collective-permute-done((f32[64,256]{1,0:T(8,128)S(1)}, f32[64,256]{1,0:T(8,128)S(1)}, u32[]{:S(2)}, u32[]{:S(2)}) %collective-permute-start.9) | collective-permute-done | bytes 65568 | tf_op jit(solution)/shard_map/ppermute | solution.py:758
  34.8 0.0 collective-permute-done.10
  34.8 0.6 %add_add_fusion = f32[64,256]{1,0:T(8,128)} fusion(f32[64,256]{1,0:T(8,128)S(1)} %collective-permute-done.10, f32[64,256]{1,0:T(8,128)S(1)} %collective-permute-done.9, f32[64,256]{1,0:T(8,128)S(1)} %get-tuple-element.69, f32[64,256]{1,0:T(8,128)S(1)} %collective-permute-done.8), kind=kLoop, calls=%fused_computation | loop fusion | flops 49152 | bytes 327680 | tf_op jit(solution)/shard_map/add | solution.py:758
  (12 shorter events, 0.0 us)
Async XLA Ops:
  0.0 7.9 %copy-start = (f32[256,2,128]{2,1,0:T(2,128)S(1)}, f32[256,2,128]{2,1,0:T(2,128)}, u32[]{:S(2)}) copy-start(f32[256,2,128]{2,1,0:T(2,128)} %param.26) | copy-start | bytes 786436
  0.0 7.9 %copy-start.1 = (f32[256,2,128]{2,1,0:T(2,128)S(1)}, f32[256,2,128]{2,1,0:T(2,128)}, u32[]{:S(2)}) copy-start(f32[256,2,128]{2,1,0:T(2,128)} %param.34) | copy-start | bytes 786436
  0.0 7.9 %copy-start.2 = (f32[256,2,128]{2,1,0:T(2,128)S(1)}, f32[256,2,128]{2,1,0:T(2,128)}, u32[]{:S(2)}) copy-start(f32[256,2,128]{2,1,0:T(2,128)} %param.35) | copy-start | bytes 786436
  0.0 7.9 %copy-start.3 = (f32[128,256]{1,0:T(8,128)S(1)}, f32[128,256]{1,0:T(8,128)}, u32[]{:S(2)}) copy-start(f32[128,256]{1,0:T(8,128)} %refs_4_.2) | copy-start | bytes 393220
  0.0 7.9 %copy-start.6 = (f32[16,256]{1,0:T(8,128)S(1)}, f32[16,256]{1,0:T(8,128)}, u32[]{:S(2)}) copy-start(f32[16,256]{1,0:T(8,128)} %refs_4_.3) | copy-start | bytes 49156
  0.0 7.9 %copy-start.9 = (s32[256]{0:T(256)S(1)}, s32[256]{0:T(256)}, u32[]{:S(2)}) copy-start(s32[256]{0:T(256)} %param.23) | copy-start | bytes 3076
  0.0 7.9 %copy-start.10 = (f32[256]{0:T(256)S(1)}, f32[256]{0:T(256)}, u32[]{:S(2)}) copy-start(f32[256]{0:T(256)} %param.33) | copy-start | bytes 3076
  0.0 7.9 %copy-start.12 = (f32[2]{0:T(128)S(1)}, f32[2]{0:T(128)}, u32[]{:S(2)}) copy-start(f32[2]{0:T(128)} %refs_10_.1) | copy-start | bytes 28
  0.0 7.9 %copy-start.13 = (f32[2]{0:T(128)S(1)}, f32[2]{0:T(128)}, u32[]{:S(2)}) copy-start(f32[2]{0:T(128)} %refs_11_.2) | copy-start | bytes 28
  0.1 7.9 %copy-start.14 = (f32[128]{0:T(128)S(1)}, f32[128]{0:T(128)}, u32[]{:S(2)}) copy-start(f32[128]{0:T(128)} %param.40) | copy-start | bytes 1540
  2.1 12.2 %collective-permute-start.2 = (f32[88,256]{1,0:T(8,128)}, f32[88,256]{1,0:T(8,128)S(1)}, u32[]{:S(2)}, u32[]{:S(2)}) collective-permute-start(f32[88,256]{1,0:T(8,128)} %tables.1.refs_3_), channel_id=1, source_target_pairs={{0,20},{2,22},{4,16},{6,18},{8,28},{10,30},{12,24},{14,26},{16,4},... | collective-permute-start | bytes 270344 | tf_op jit(solution)/shard_map/ppermute | solution.py:646
  7.1 7.2 %collective-permute-start.1 = (f32[88,256]{1,0:T(8,128)}, f32[88,256]{1,0:T(8,128)S(1)}, u32[]{:S(2)}, u32[]{:S(2)}) collective-permute-start(f32[88,256]{1,0:T(8,128)} %tables.1.refs_3_), channel_id=1, source_target_pairs={{0,14},{2,12},{4,10},{6,8},{8,6},{10,4},{12,2},{14,0},{16,30},{18,... | collective-permute-start | bytes 270344 | tf_op jit(solution)/shard_map/ppermute | solution.py:646
  7.7 8.1 %collective-permute-start = (f32[88,256]{1,0:T(8,128)}, f32[88,256]{1,0:T(8,128)S(1)}, u32[]{:S(2)}, u32[]{:S(2)}) collective-permute-start(f32[88,256]{1,0:T(8,128)} %tables.1.refs_3_), channel_id=1, source_target_pairs={{0,26},{2,24},{4,30},{6,28},{8,18},{10,16},{12,22},{14,20},{16,10}... | collective-permute-start | bytes 270344 | tf_op jit(solution)/shard_map/ppermute | solution.py:646
  7.9 0.7 %copy-start.7 = (f32[256,2]{0,1:T(2,128)S(1)}, f32[256,2]{0,1:T(2,128)}, u32[]{:S(2)}) copy-start(f32[256,2]{0,1:T(2,128)} %param.36) | copy-start | bytes 6148
  7.9 0.7 %copy-start.8 = (f32[256]{0:T(256)S(1)}, f32[256]{0:T(256)}, u32[]{:S(2)}) copy-start(f32[256]{0:T(256)} %param.24) | copy-start | bytes 3076
  7.9 0.7 %copy-start.11 = (f32[2]{0:T(128)S(1)}, f32[2]{0:T(128)}, u32[]{:S(2)}) copy-start(f32[2]{0:T(128)} %refs_9_.3) | copy-start | bytes 28
  8.6 7.4 %copy-start.5 = (f32[88,256]{1,0:T(8,128)S(1)}, f32[88,256]{1,0:T(8,128)}, u32[]{:S(2)}) copy-start(f32[88,256]{1,0:T(8,128)} %tables.1.refs_3_) | copy-start | bytes 270340
  14.3 3.5 %collective-permute-start.5 = (f32[88,256]{1,0:T(8,128)S(1)}, f32[88,256]{1,0:T(8,128)S(1)}, u32[]{:S(2)}, u32[]{:S(2)}) collective-permute-start(f32[88,256]{1,0:T(8,128)S(1)} %collective-permute-done.2.refs_2_.refs_10_), channel_id=1, source_target_pairs={{0,8},{8,0},{16,24},{24,16},{1,9},{9,1},{17,25},{25,17},{2,10},{10... | collective-permute-start | bytes 270344 | tf_op jit(solution)/shard_map/ppermute | solution.py:649
  14.3 3.5 %collective-permute-start.4 = (f32[88,256]{1,0:T(8,128)S(1)}, f32[88,256]{1,0:T(8,128)S(1)}, u32[]{:S(2)}, u32[]{:S(2)}) collective-permute-start(f32[88,256]{1,0:T(8,128)S(1)} %collective-permute-done.1.refs_1_.refs_9_), channel_id=1, source_target_pairs={{0,8},{8,0},{16,24},{24,16},{1,9},{9,1},{17,25},{25,17},{2,10},{10... | collective-permute-start | bytes 270344 | tf_op jit(solution)/shard_map/ppermute | solution.py:649
  15.8 2.1 %collective-permute-start.3 = (f32[88,256]{1,0:T(8,128)S(1)}, f32[88,256]{1,0:T(8,128)S(1)}, u32[]{:S(2)}, u32[]{:S(2)}) collective-permute-start(f32[88,256]{1,0:T(8,128)S(1)} %collective-permute-done.refs_0_.refs_8_), channel_id=1, source_target_pairs={{0,8},{8,0},{16,24},{24,16},{1,9},{9,1},{17,25},{25,17},{2,10},{10... | collective-permute-start | bytes 270344 | tf_op jit(solution)/shard_map/ppermute | solution.py:649
  19.4 2.3 %copy-start.4 = (f32[128,256]{1,0:T(8,128)S(1)}, f32[128,256]{1,0:T(8,128)}, u32[]{:S(2)}) copy-start(f32[128,256]{1,0:T(8,128)} %refs_11_.3) | copy-start | bytes 393220
  19.4 1.4 %collective-permute-start.6 = (f32[136,128]{1,0:T(8,128)S(1)}, f32[136,128]{1,0:T(8,128)S(1)}, u32[]{:S(2)}, u32[]{:S(2)}) collective-permute-start(f32[136,128]{1,0:T(8,128)S(1)} %get-tuple-element.48.refs_0_), channel_id=1, source_target_pairs={{0,8},{8,0},{16,24},{24,16},{1,9},{9,1},{17,25},{25,17},{2,10},{10... | collective-permute-start | bytes 208904 | tf_op jit(solution)/shard_map/ppermute | solution.py:724
  20.8 4.5 %collective-permute-start.7 = (f32[136,128]{1,0:T(8,128)S(1)}, f32[136,128]{1,0:T(8,128)S(1)}, u32[]{:S(2)}, u32[]{:S(2)}) collective-permute-start(f32[136,128]{1,0:T(8,128)S(1)} %get-tuple-element.50), channel_id=1, source_target_pairs={{0,16},{8,24},{16,0},{24,8},{1,17},{9,25},{17,1},{25,9},{2,18},{10... | collective-permute-start | bytes 208904 | tf_op jit(solution)/shard_map/ppermute | solution.py:724
  26.0 7.0 %collective-permute-start.8 = (f32[64,256]{1,0:T(8,128)S(1)}, f32[64,256]{1,0:T(8,128)S(1)}, u32[]{:S(2)}, u32[]{:S(2)}) collective-permute-start(f32[64,256]{1,0:T(8,128)S(1)} %get-tuple-element.70), channel_id=1, source_target_pairs={{0,4},{2,6},{4,0},{6,2},{1,5},{3,7},{5,1},{7,3},{8,12},{10,14},{12... | collective-permute-start | bytes 196616 | tf_op jit(solution)/shard_map/ppermute | solution.py:758
  28.7 6.1 %collective-permute-start.9 = (f32[64,256]{1,0:T(8,128)S(1)}, f32[64,256]{1,0:T(8,128)S(1)}, u32[]{:S(2)}, u32[]{:S(2)}) collective-permute-start(f32[64,256]{1,0:T(8,128)S(1)} %get-tuple-element.71), channel_id=1, source_target_pairs={{0,6},{2,4},{4,2},{6,0},{1,7},{3,5},{5,3},{7,1},{8,14},{10,12},{12... | collective-permute-start | bytes 196616 | tf_op jit(solution)/shard_map/ppermute | solution.py:758
  29.5 5.3 %collective-permute-start.10 = (f32[64,256]{1,0:T(8,128)S(1)}, f32[64,256]{1,0:T(8,128)S(1)}, u32[]{:S(2)}, u32[]{:S(2)}) collective-permute-start(f32[64,256]{1,0:T(8,128)S(1)} %get-tuple-element.72), channel_id=1, source_target_pairs={{0,2},{2,0},{4,6},{6,4},{1,3},{3,1},{5,7},{7,5},{8,10},{10,8},{12,... | collective-permute-start | bytes 196616 | tf_op jit(solution)/shard_map/ppermute | solution.py:758

commit v10 on v9

--- a/solution.py
+++ b/solution.py
@@ -100,6 +100,9 @@
     return copies
 
 
+PIECES = 4
+
+
 def tables_kernel(dims, *refs):
     V, D, hl, ch, nh, ns, T, N = dims
     refs = list(refs)
@@ -113,35 +116,54 @@
     places = take(9)
     semaphores = take(1)[0]
     half = ch // 2
-    base = V + 2 + 3 * hl
+    top = top_rows(dims)
     core = lax.rem(lax.axis_index("seq"), 2)
+    (inproj, tok, emb, prenorm, stepmap, bias, rates, skip, outnorm) = places
+    size = inproj.shape[0] // PIECES
+    pieces = [pl.ds(number * size, size) for number in range(PIECES)]
+    rows = pl.ds(pl.multiple_of(core * half, 8), half)
+    wide = [(place, pl.ds(place * ch, ch)) for place in range(D // ch)]
     copies = fetch(
-        sources + [outproj_source.at[pl.ds(pl.multiple_of(core * half, 8), half), :]],
-        places + [message.at[base : base + half, 0:D]],
+        [sources[0].at[piece, :] for piece in pieces]
+        + sources[1:]
+        + [outproj_source.at[rows, columns] for _, columns in wide],
+        [inproj.at[piece, :] for piece in pieces]
+        + places[1:]
+        + [message.at[pl.ds(top + place * half, half), :] for place, _ in wide],
         semaphores,
     )
-    flip = (iota((T, T), 0) + iota((T, T), 1) == T - 1).astype(f32).astype(bf16)
-    for copy in copies[:9]:
+    flip = (iota((T, 1), 0) + iota((1, T), 1) == T - 1).astype(f32).astype(bf16)
+    for copy in copies[PIECES : PIECES + 8]:
         copy.wait()
-    (inproj, tok, emb, prenorm, stepmap, bias, rates, skip, outnorm) = places
     normed = split2(rms(emb[...]) * prenorm[...])
     raw_t = dot_split(split2(stepmap[...]), normed, NT)
+    tokens = jnp.broadcast_to(tok[...].astype(f32), (8, T)).astype(bf16)
+    tokens = dot(tokens, flip)
+    for place in range(T // ch):
+        message[2 * V + place : 2 * V + place + 1, :] = tokens[0:1, place * ch : (place + 1) * ch]
+    row = 2 * V + T // ch
+    message[row : row + 1, :] = outnorm[...]
+    for head in range(hl):
+        line = softplus(raw_t[head : head + 1, :] + bias[:, head : head + 1])
+        row = row + 1
+        message[row : row + 1, 0:V] = line
+        message[row : row + 1, V : 2 * V] = -rates[:, head : head + 1] * line
+        message[row : row + 1, 2 * V : 3 * V] = jnp.broadcast_to(skip[:, head : head + 1], (1, V))
+    for copy in copies[:PIECES]:
+        copy.wait()
     weights = jnp.concatenate(
         [inproj[pl.ds(0, D, stride=2), :], inproj[pl.ds(1, D, stride=2), :]], axis=1
     )
-    message[0:V, 0 : 2 * ch] = dot_split(normed, split2(weights))
-    tokens = jnp.broadcast_to(tok[...].astype(f32), (8, T)).astype(bf16)
-    message[V : V + 1, 0:T] = dot(tokens, flip)[0:1]
-    message[V + 1 : V + 2, 0:ch] = outnorm[...]
-    for head in range(hl):
-        line = softplus(raw_t[head : head + 1, :] + bias[:, head : head + 1])
-        row = V + 2 + head
-        message[row : row + 1, 0:V] = line
-        message[row + hl : row + hl + 1, 0:V] = -rates[:, head : head + 1] * line
-        message[row + 2 * hl : row + 2 * hl + 1, 0:V] = jnp.broadcast_to(
-            skip[:, head : head + 1], (1, V)
-        )
-    copies[9].wait()
+    both = dot_split(normed, split2(weights))
+    message[0:V, :] = both[:, 0:ch]
+    message[V : 2 * V, :] = both[:, ch:]
+    for copy in copies[PIECES + 8 :]:
+        copy.wait()
+
+
+def top_rows(dims):
+    V, D, hl, ch, nh, ns, T, N = dims
+    return 2 * V + -(-(T // ch + 1 + hl) // 8) * 8
 
 
 def head_line(dims, values):
@@ -167,12 +189,13 @@
     bias2, rates2, skip2, outnorm2 = take(4)
     pairs, small, choose_out, own_high, own_low = take(5)
     state_high, state_low, rest_high, rest_low = take(4)
+    triangles, upto, groups, blocks = take(4)
     normed = split2(rms(emb[...]) * prenorm[...])
     write = dot_split(normed, split2(statemap[pl.ds(0, D, stride=2), :]))
     read = dot_split(normed, split2(statemap[pl.ds(1, D, stride=2), :]))
     pairs[...] = dot3(read, jnp.concatenate([write] * H, axis=0), NT)
     own_high[...], own_low[...] = split2(outproj[...])
-    choose = (complement[...] == iota((D, D), 0)).astype(f32).astype(bf16)
+    choose = (complement[...] == iota((D, 1), 0)).astype(f32).astype(bf16)
     choose_out[...] = choose
     gain = jnp.transpose(jnp.broadcast_to(prenorm2[...], (128, D)))
 
@@ -197,6 +220,14 @@
     small[1:2, :] = head_line(dims, rates2)
     small[2:3, :] = head_line(dims, skip2)
     small[3:4, :] = outnorm2[...]
+    row, column = iota((T, 1), 0), iota((1, T), 1)
+    triangles[:, 0:T] = (row > column).astype(f32).astype(bf16)
+    triangles[:, T:] = (row < column).astype(f32).astype(bf16)
+    upto[...] = (row >= column).astype(f32).astype(bf16)
+    size = groups.shape[0]
+    groups[...] = (iota((size, 1), 0) // P == iota((1, size), 1) // P).astype(f32).astype(bf16)
+    rows, columns = blocks.shape
+    blocks[...] = (iota((rows, 1), 0) // V == iota((1, columns), 1) // P).astype(f32).astype(bf16)
 
 
 def shift_rows(value, amount, fill):
@@ -207,9 +238,12 @@
             return jnp.concatenate([empty, value[: size - amount]], axis=0)
         return jnp.concatenate([value[-amount:], empty], axis=0)
     rolled = pltpu.roll(value, amount % size, 0)
-    row = iota(value.shape, 0)
-    have = (row >= amount) if amount > 0 else (row < size + amount)
-    return jnp.where(have, rolled, fill)
+    row = iota((8,) + value.shape[1:], 0)
+    if amount > 0:
+        edge = jnp.where(row >= amount, rolled[0:8], fill)
+        return jnp.concatenate([edge, rolled[8:]], axis=0)
+    edge = jnp.where(row < 8 + amount, rolled[size - 8 :], fill)
+    return jnp.concatenate([rolled[: size - 8], edge], axis=0)
 
 
 def scan_rows(decay, value, sign):
@@ -235,33 +269,34 @@
 
     count = max(ns, nh)
     packets = dict(zip(in_turn(count)[::-1] + [0], take(count)))
-    emb, pairs = take(2)
+    emb, pairs, triangles, groups, blocks = take(5)
     out_high, out_low, out_embedded = take(3)
     tokens = take(1)[0]
     mine = lax.axis_index("seq")
 
     for k in range(ns):
         block = ns - 1 - lax.bitwise_xor(mine, partners(ns, nh)[k][0])
-        tokens[pl.ds(block, 1), :] = packets[k][V : V + 1, 0:T]
-
-    def rows_of(place):
-        low = V + 2 + place * hl
-        return jnp.concatenate([packets[k][low : low + hl, 0:V] for k in range(nh)], axis=0)
-
-    step_t, log_t, skip_t = rows_of(0), rows_of(1), rows_of(2)
-    narrow = split3(jnp.concatenate([step_t, log_t, skip_t], axis=1))
-    narrow = jnp.concatenate([part.astype(f32) for part in narrow], axis=0).astype(bf16)
-    spread_heads = (iota((3 * H, LV), 1) // V == iota((3 * H, LV), 0) % H).astype(f32).astype(bf16)
+        row = 2 * V
+        pieces = [packets[k][row + place : row + place + 1, :] for place in range(T // ch)]
+        tokens[pl.ds(block, 1), :] = jnp.concatenate(pieces, axis=1)
+
+    first = 2 * V + T // ch + 1
+    steps = jnp.concatenate(
+        [packets[k][first : first + hl, 0 : 3 * V] for k in range(nh)], axis=0
+    )
+    log_t = steps[:, V : 2 * V]
+    narrow = jnp.concatenate([part.astype(f32) for part in split3(steps)], axis=0).astype(bf16)
+    spread_heads = (iota((1, LV), 1) // V == iota((3 * H, 1), 0) % H).astype(f32).astype(bf16)
     wide = dot(narrow, spread_heads, TN)
-    own = iota((V, LV), 1) % V == iota((V, LV), 0)
+    own = iota((1, LV), 1) % V == iota((V, 1), 0)
     decay_table = jnp.exp(wide[V : 2 * V])
     step_table = jnp.where(own, wide[0:V], 0.0)
     gain_table = jnp.where(own, wide[2 * V : 3 * V], 0.0)
-    gates = jnp.concatenate([packets[k][0:V, 0:ch] for k in range(nh)], axis=1)
-    inners = jnp.concatenate([packets[k][0:V, ch : 2 * ch] for k in range(nh)], axis=1)
-    gains = jnp.concatenate([packets[k][V + 1 : V + 2, 0:ch] for k in range(nh)], axis=1)
-
-    token_row = (iota((LV, T), 0) % V).astype(f32)
+    gates = jnp.concatenate([packets[k][0:V, :] for k in range(nh)], axis=1)
+    inners = jnp.concatenate([packets[k][V : 2 * V, :] for k in range(nh)], axis=1)
+    gains = jnp.concatenate([packets[k][first - 1 : first, :] for k in range(nh)], axis=1)
+
+    token_row = (iota((LV, 1), 0) % V).astype(f32)
     log_split = jnp.concatenate(split3(log_t), axis=1)
     onehots, logs = [], []
     for block in range(ns):
@@ -269,29 +304,24 @@
         onehots.append(onehot)
         logs.append(dot(log_split, onehot[0 : 3 * V, :]))
     logs = jnp.concatenate(logs, axis=0)
-    first, second = iota((T, T), 0), iota((T, T), 1)
-    later = (first > second).astype(f32).astype(bf16)
-    sooner = (first < second).astype(f32).astype(bf16)
     size = ns * H
-    sums = dot(
-        jnp.concatenate(split3(logs)[::-1], axis=0), jnp.concatenate([later, sooner], axis=1)
-    )
+    sums = dot(jnp.concatenate(split3(logs)[::-1], axis=0), triangles[...])
     sums = (sums[0:size] + sums[size : 2 * size]) + sums[2 * size :]
     after, before = sums[:, 0:T], sums[:, T:]
     totals = jnp.broadcast_to(jnp.sum(logs, axis=1, keepdims=True), (size, 128))
-    piece = iota((size, 128), 1)
+    piece = iota((1, 128), 1)
     high, middle, low = [part.astype(f32) for part in split3(totals)]
     totals = jnp.where(
         piece == 0, high, jnp.where(piece == 1, middle, jnp.where(piece == 2, low, 0.0))
     )
-    row, column = iota((ns * H, ns * H), 0), iota((ns * H, ns * H), 1)
+    row, column = iota((ns * H, 1), 0), iota((1, ns * H), 1)
     row_block, column_block = row // H, column // H
     between = ((row_block < column_block) & (column_block < mine)) | (
         (row_block > column_block) & (column_block > mine)
     )
     between = (between & (row % H == column % H)).astype(f32).astype(bf16)
     gap = jnp.sum(dot(between, totals.astype(bf16)), axis=1, keepdims=True)
-    block_of = iota((ns * H, T), 0) // H
+    block_of = iota((ns * H, 1), 0) // H
     weight_up = jnp.where(block_of < mine, jnp.exp(after + gap), 0.0)
     weight_down = jnp.where(block_of > mine, jnp.exp(before + gap), 0.0)
     entering = jnp.zeros((4 * H, LV), f32)
@@ -302,7 +332,7 @@
             jnp.concatenate(split2(both), axis=0), onehots[block], NT
         )
     entering = entering[2 * H :] + entering[0 : 2 * H]
-    diagonal = iota((H, LV), 1) // V == iota((H, LV), 0)
+    diagonal = iota((1, LV), 1) // V == iota((H, 1), 0)
     step_row = jnp.sum(step_table, axis=0, keepdims=True)
     enter_up = step_row * jnp.sum(
         jnp.where(diagonal, entering[0:H], 0.0), axis=0, keepdims=True
@@ -316,20 +346,24 @@
     )
     looked = jnp.concatenate(split3(looked), axis=0)
     token = tokens[pl.ds(mine, 1), :]
-    onehot = (token == (iota((3 * V, T), 0) % V).astype(f32)).astype(f32).astype(bf16)
+    onehot = (token == token_row[0 : 3 * V]).astype(f32).astype(bf16)
     rows = dot(onehot, looked, TN)
     decay, step = rows[:, 0:LV], rows[:, LV : 2 * LV]
     pair, gain = rows[:, 2 * LV : 3 * LV], rows[:, 3 * LV : 4 * LV]
     silu_rows = rows[:, 4 * LV : 4 * LV + C]
     out_embedded[...] = rows[:, 4 * LV + C :]
 
-    position = iota((T, LV), 0)
-    up = scan_rows(decay, jnp.where(position == 0, step + decay * enter_up, step), 1)
-    down = scan_rows(decay, jnp.where(position == T - 1, step + decay * enter_down, step), -1)
-
-    tiled = jnp.concatenate([inners] * H, axis=0)
-    spread = jnp.where(iota((LV, C), 0) // V == iota((LV, C), 1) // P, tiled, 0.0)
-    spread_high, spread_low = split2(spread)
+    edge = iota((8, 1), 0)
+    begin = jnp.where(edge == 0, decay[0:8] * enter_up, 0.0)
+    up = scan_rows(decay, jnp.concatenate([step[0:8] + begin, step[8:]], axis=0), 1)
+    begin = jnp.where(edge == 7, decay[T - 8 :] * enter_down, 0.0)
+    down = scan_rows(
+        decay, jnp.concatenate([step[: T - 8], step[T - 8 :] + begin], axis=0), -1
+    )
+
+    spread_high, spread_low = [
+        jnp.concatenate([part] * H, axis=0) * blocks[...] for part in split2(inners)
+    ]
     both = jnp.concatenate([up * pair + gain, down * pair + gain], axis=0)
     high, low = split2(both)
     value = dot(high, spread_low) + dot(
@@ -337,13 +371,12 @@
         jnp.concatenate([spread_high, spread_high], axis=0),
     )
     value = value * jnp.concatenate([silu_rows, silu_rows], axis=0)
-    wide = max(ch, 256)
-    group = (iota((wide, wide), 0) // P == iota((wide, wide), 1) // P).astype(f32).astype(bf16)
+    wide = groups.shape[0]
     high, low = split2(value * value)
     starts = list(range(0, C, wide))
     rows = 2 * T
     stacked = [half[:, start : start + wide] for start in starts for half in (low, high)]
-    squares = dot(jnp.concatenate(stacked, axis=0), group)
+    squares = dot(jnp.concatenate(stacked, axis=0), groups[...])
     for number, start in enumerate(starts):
         place = 2 * number * rows
         square = squares[place : place + rows] + squares[place + rows : place + 2 * rows]
@@ -363,20 +396,28 @@
         taken, refs[:] = refs[:number], refs[number:]
         return taken
 
-    high, low, embedded, small, own_high, own_low, state_high, state_low = take(8)
+    high, low, embedded, small, own_high, own_low, state_high, state_low, upto = take(9)
     order = in_turn(nh)[::-1]
     nears = dict(zip(order, take(nh - 1)))
     others = dict(zip(order, take(nh - 1)))
     out_state, out_high, out_low, out_scale = take(4)
     out_write, out_inner, out_stepped, out_total = take(4)
     half = ch // 2
-    base = V + 2 + 3 * hl
+    base = top_rows(dims)
     mine = lax.axis_index("seq")
 
     pieces = []
     for k in range(1, nh):
-        near = nears[k][base : base + half, 0:D]
-        other = others[k][base : base + half, 0:D]
+        near, other = [
+            jnp.concatenate(
+                [
+                    ref[base + place * half : base + (place + 1) * half, :]
+                    for place in range(D // ch)
+                ],
+                axis=1,
+            )
+            for ref in (nears[k], others[k])
+        ]
         even = lax.rem(lax.bitwise_xor(mine, partners(ns, nh)[k][0]), 2) == 0
         pieces.append(jnp.where(even, near, other))
         pieces.append(jnp.where(even, other, near))
@@ -395,10 +436,9 @@
     inner, write = rows[:, 0:ch], rows[:, 2 * ch :]
     step = softplus(rows[:, ch : 2 * ch] + small[0:1, :])
     stepped = inner * step
-    upto = (iota((T, T), 0) >= iota((T, T), 1)).astype(f32).astype(bf16)
     log_high, log_middle, log_low = split3(-small[1:2, :] * step)
-    total = dot(upto, jnp.concatenate([log_low, log_middle], axis=1))
-    total = (total[:, 0:ch] + total[:, ch:]) + dot(upto, log_high)
+    total = dot(upto[...], jnp.concatenate([log_low, log_middle], axis=1))
+    total = (total[:, 0:ch] + total[:, ch:]) + dot(upto[...], log_high)
     end = total[T - 1 : T, :]
     state = dot3(stepped * jnp.exp(end - total), write, TN)
     out_state[0:ch, :] = state
@@ -437,7 +477,7 @@
     total_t = (dot(select, total_low, NT) + dot(select, total_middle, NT)) + dot(
         select, total_high, NT
     )
-    allowed = iota((T, T), 0) >= iota((T, T), 1)
+    allowed = iota((T, 1), 0) >= iota((1, T), 1)
     parts = []
     for head in range(hl):
         start, stop = head * P, (head + 1) * P
@@ -495,11 +535,11 @@
     V, D, hl, ch, nh, ns, T, N = dims
     P = ch // hl
     prefix, came, read_high, read_low, base, fade, gate, own, proj_high, proj_low = refs[:10]
-    outs, partial_ref = refs[10 : 10 + nh], refs[10 + nh]
+    groups, outs, partial_ref = refs[10], refs[11 : 11 + nh], refs[11 + nh]
     entering = prefix_joined(dims, bit, prefix, came)
-    value = (base[...] + dot_split((read_high[...], read_low[...]), split2(entering), NT) * fade[...]) * gate[...]
-    group = (iota((ch, ch), 0) // P == iota((ch, ch), 1) // P).astype(f32).astype(bf16)
-    square = dot(jnp.concatenate(split2(value * value), axis=0), group)
+    carried = dot_split((read_high[...], read_low[...]), split2(entering), NT)
+    value = (base[...] + carried * fade[...]) * gate[...]
+    square = dot(jnp.concatenate(split2(value * value), axis=0), groups[0:ch, 0:ch])
     square = square[T:] + square[0:T]
     value = value * lax.rsqrt(square * (1.0 / P) + epsilon)
     share = T // nh
@@ -564,9 +604,7 @@
 
     heavy = pl.CostEstimate(flops=960 * T * D * D, bytes_accessed=4 * T * D, transcendentals=T * D)
 
-    head_rows = V + 2 + 3 * hl
     half = ch // 2
-    width = max(2 * ch, T, D)
     share = T // nh
     fetched = [
         flat(inproj_first),
@@ -581,11 +619,11 @@
     ]
     message = pl.pallas_call(
         functools.partial(tables_kernel, dims),
-        out_shape=shape(head_rows + half, width),
+        out_shape=shape(top_rows(dims) + half * (D // ch), ch),
         in_specs=[anywhere] * (len(fetched) + 1),
         out_specs=vmem,
         scratch_shapes=[room(value) for value in fetched]
-        + [pltpu.SemaphoreType.DMA((len(fetched) + 1,))],
+        + [pltpu.SemaphoreType.DMA((len(fetched) - 1 + PIECES + D // ch,))],
         compiler_params=pltpu.CompilerParams(vmem_limit_bytes=TABLES_LIMIT),
         cost_estimate=heavy,
         name="tables",
@@ -616,6 +654,10 @@
         state_low,
         rest_high,
         rest_low,
+        triangles,
+        upto,
+        groups,
+        blocks,
     ) = pl.pallas_call(
         functools.partial(prepare_kernel, dims),
         out_shape=(
@@ -625,9 +667,13 @@
             *halves(ch, D),
             *halves(D, 2 * ch + N),
             *halves(D, ch + N),
+            shape(T, 2 * T, dtype=bf16),
+            shape(T, T, dtype=bf16),
+            shape(2 * ch, 2 * ch, dtype=bf16),
+            shape(LV, nh * ch, dtype=bf16),
         ),
         in_specs=[vmem] * 9 + [smem] * 3 + [vmem],
-        out_specs=(vmem,) * 9,
+        out_specs=(vmem,) * 13,
         compiler_params=params,
         cost_estimate=heavy,
         name="prepare",
@@ -642,7 +688,7 @@
             for seq in range(ns)
             for head in range(nh)
         ]
-        sent = message if k < nh else message[0:head_rows]
+        sent = message if k < nh else message[0 : top_rows(dims)]
         messages[k] = lax.ppermute(sent, ("seq", "head"), pairs)
     swap = [(seq, seq ^ 1) for seq in range(ns)]
     order = in_turn(nh)[::-1]
@@ -651,13 +697,20 @@
     mixed_high, mixed_low, embedded = pl.pallas_call(
         functools.partial(mix_kernel, dims),
         out_shape=(*halves(T, nh * ch), shape(T, D)),
-        in_specs=[vmem] * (count + 2),
+        in_specs=[vmem] * (count + 5),
         out_specs=(vmem,) * 3,
         scratch_shapes=[pltpu.VMEM((max(ns, 8), T), f32)],
         compiler_params=params,
         cost_estimate=heavy,
         name="mix",
-    )(*[messages[k] for k in in_turn(count)[::-1] + [0]], embedding, pair_table)
+    )(
+        *[messages[k] for k in in_turn(count)[::-1] + [0]],
+        embedding,
+        pair_table,
+        triangles,
+        groups,
+        blocks,
+    )
 
     state, hidden_high, hidden_low, scale, write, inner, stepped, total = pl.pallas_call(
         functools.partial(project_kernel, dims),
@@ -670,7 +723,7 @@
             shape(T, ch),
             shape(T, ch),
         ),
-        in_specs=[vmem] * (8 + 2 * (nh - 1)),
+        in_specs=[vmem] * (9 + 2 * (nh - 1)),
         out_specs=(vmem,) * 8,
         compiler_params=params,
         name="project",
@@ -683,6 +736,7 @@
         own_low,
         state_high,
         state_low,
+        upto,
         *[messages[k] for k in order],
         *others,
     )
@@ -746,12 +800,24 @@
     parts = pl.pallas_call(
         functools.partial(output_kernel, dims, bits - 1),
         out_shape=(shape(share, D),) * nh,
-        in_specs=[vmem] * 10,
+        in_specs=[vmem] * 11,
         out_specs=(vmem,) * nh,
         scratch_shapes=[pltpu.VMEM((T, D), f32)],
         compiler_params=params,
         name="output",
-    )(prefix, came, read_high, read_low, base, fade, gate, own, proj_high, proj_low)
+    )(
+        prefix,
+        came,
+        read_high,
+        read_low,
+        base,
+        fade,
+        gate,
+        own,
+        proj_high,
+        proj_low,
+        groups,
+    )
     result = parts[0]
     for k in in_turn(nh):
         pairs = [(source, source ^ k) for source in range(nh)]

time: 35.6 us -> 35.3 us (level)
  waiting for transfers between devices: 13.5 us -> 13.1 us
  transfers between devices with their start and end apart: 11 -> 11, of which waited for: 6 -> 7; matrix products, arithmetic and copies ran while one was open for 0% -> 0% of each run, Pallas kernels for 12% -> 12%
where the time goes in v10:
time: 35.3 us; the launch traced here: 35.2 us
  waiting for transfers between devices  13.1 us (37%)
  starting transfers between devices  11.8 us (33%)
  Pallas kernels  8.76 us (25%)
  local copies, waits for them, and re-layouts  0.65 us (2%)
  other arithmetic  0.65 us (2%)
    ppermute x3, starting transfers between devices, per_device(): messages[k] = lax.ppermute(sent, ('seq', 'head'), pairs)  5.75 us
    ppermute x3, waiting for transfers between devices, per_device(): messages[k] = lax.ppermute(sent, ('seq', 'head'), pairs)  5.14 us
    ppermute x3, waiting for transfers between devices, per_device(): result = result + lax.ppermute(parts[k], 'head', pairs)  4.75 us
    ppermute x3, starting transfers between devices, per_device(): result = result + lax.ppermute(parts[k], 'head', pairs)  4.02 us
    ppermute x2, waiting for transfers between devices, per_device(): lax.ppermute(state, 'seq', [(seq, seq ^ 2 ** bit) for seq in range(ns)])  3.23 us
    pallas_call x1, Pallas kernels, per_device(): pl.pallas_call(functools.partial(tables_kernel, dims), out_shape=shape(to...  2.18 us
    pallas_call x1, Pallas kernels, per_device(): pl.pallas_call(functools.partial(mix_kernel, dims), out_shape=(*halves(T,...  1.84 us
    pallas_call x1, Pallas kernels, per_device(): pl.pallas_call(functools.partial(project_kernel, dims), out_shape=(shape(...  1.5 us
  transfers between devices with their start and end apart: 11, of which 7 were waited for; matrix products, arithmetic and copies ran while one was open for 0% of the time, Pallas kernels for 12%

profile of v10, /device:TPU:0, one launch (start us, length us, event | category | flops | bytes accessed | tf_op | source)
XLA Modules:
  0.0 35.2 jit_solution(1263055761740783380)
XLA Ops:
  0.0 0.0 copy-start.9
  0.0 0.0 copy-start.10
  0.0 0.0 copy-start.12
  0.0 0.0 copy-start.13
  0.1 0.0 copy-start.14
  0.1 2.2 %tables.1.refs_3_ = f32[168,128]{1,0:T(8,128)} custom-call(f32[512,128]{1,0:T(8,128)} %bitcast.24, s32[1,256]{1,0:T(1,128)} %bitcast.26, f32[16,256]{1,0:T(8,128)} %refs_4_.3, f32[1,256]{1,0:T(1,128)} %bitcast.19, f32[2,256]{1,0:T(2,128)} %bitcast.25, f32[1,2]{1,0:T(1,128)} %bitcast.27, f32[1,2]{1,0:T(1,128)} %bitcast.28, f32[1,2]{1,0:T(1,128)} %bitcast.29, ...), custom_call_target="tpu_custom_call" | custom-call | flops 16106127360 | bytes 262144 | tf_op jit(solution)/shard_map/tables/pallas_call | solution.py:620
  2.2 5.0 %collective-permute-start.2 = (f32[168,128]{1,0:T(8,128)}, f32[168,128]{1,0:T(8,128)S(1)}, u32[]{:S(2)}, u32[]{:S(2)}) collective-permute-start(f32[168,128]{1,0:T(8,128)} %tables.1.refs_3_), channel_id=1, source_target_pairs={{0,20},{2,22},{4,16},{6,18},{8,28},{10,30},{12,24},{14,26},{16,4},... | collective-permute-start | bytes 258056 | tf_op jit(solution)/shard_map/ppermute | solution.py:692
  7.3 0.5 %collective-permute-start.1 = (f32[168,128]{1,0:T(8,128)}, f32[168,128]{1,0:T(8,128)S(1)}, u32[]{:S(2)}, u32[]{:S(2)}) collective-permute-start(f32[168,128]{1,0:T(8,128)} %tables.1.refs_3_), channel_id=1, source_target_pairs={{0,14},{2,12},{4,10},{6,8},{8,6},{10,4},{12,2},{14,0},{16,30},{18,... | collective-permute-start | bytes 258056 | tf_op jit(solution)/shard_map/ppermute | solution.py:692
  7.8 0.2 collective-permute-start
  8.0 0.0 copy-done
  8.0 0.0 copy-done.1
  8.0 0.0 copy-done.2
  8.0 0.0 copy-done.3
  8.0 0.0 copy-done.6
  8.1 0.0 copy-done.9
  8.1 0.0 copy-done.10
  8.1 0.0 copy-done.12
  8.1 0.0 copy-done.13
  8.1 0.0 copy-done.14
  8.1 0.6 %copy-done.7 = f32[256,2]{0,1:T(2,128)S(1)} copy-done((f32[256,2]{0,1:T(2,128)S(1)}, f32[256,2]{0,1:T(2,128)}, u32[]{:S(2)}) %copy-start.7) | copy-done | bytes 2072
  8.7 0.0 copy-done.8
  8.7 0.0 copy-done.11
  8.7 1.4 %prepare.1 = (f32[16,128]{1,0:T(8,128)S(1)}, f32[8,128]{1,0:T(8,128)S(1)}, bf16[256,256]{1,0:T(8,128)(2,1)S(1)}, bf16[128,256]{1,0:T(8,128)(2,1)S(1)}, bf16[128,...) custom-call(f32[16,256]{1,0:T(8,128)S(1)} %copy-done.6, ...), custom_call_target="tpu_custom_call" | custom-call | flops 16106127360 | bytes 262144 | tf_op jit(solution)/shard_map/prepare/pallas_call | solution.py:661
  10.1 4.0 %collective-permute-done.2.refs_2_.refs_11_ = f32[168,128]{1,0:T(8,128)S(1)} collective-permute-done((f32[168,128]{1,0:T(8,128)}, f32[168,128]{1,0:T(8,128)S(1)}, u32[]{:S(2)}, u32[]{:S(2)}) %collective-permute-start.2) | collective-permute-done | bytes 86048 | tf_op jit(solution)/shard_map/ppermute | solution.py:692
  14.1 0.0 collective-permute-start.5
  14.1 0.1 collective-permute-done.1.refs_1_.refs_10_
  14.2 0.4 %collective-permute-start.4 = (f32[168,128]{1,0:T(8,128)S(1)}, f32[168,128]{1,0:T(8,128)S(1)}, u32[]{:S(2)}, u32[]{:S(2)}) collective-permute-start(f32[168,128]{1,0:T(8,128)S(1)} %collective-permute-done.1.refs_1_.refs_10_), channel_id=1, source_target_pairs={{0,8},{8,0},{16,24},{24,16},{1,9},{9,1},{17,25},{25,17},{2,10},{10... | collective-permute-start | bytes 258056 | tf_op jit(solution)/shard_map/ppermute | solution.py:695
  14.6 1.0 %collective-permute-done.refs_0_.refs_9_ = f32[168,128]{1,0:T(8,128)S(1)} collective-permute-done((f32[168,128]{1,0:T(8,128)}, f32[168,128]{1,0:T(8,128)S(1)}, u32[]{:S(2)}, u32[]{:S(2)}) %collective-permute-start) | collective-permute-done | bytes 86048 | tf_op jit(solution)/shard_map/ppermute | solution.py:692
  15.6 0.1 collective-permute-start.3
  15.7 1.8 %mix.1 = (bf16[256,512]{1,0:T(8,128)(2,1)S(1)}, bf16[256,512]{1,0:T(8,128)(2,1)S(1)}, f32[256,256]{1,0:T(8,128)S(1)}) custom-call(f32[168,128]{1,0:T(8,128)S(1)} %collective-permute-done.refs_0_.refs_9_, f32[168,128]{1,0:T(8,128)S(1)} %collective-permute-done.1.refs_1_.refs_10_, f32[168,128]{1,0:T(8,128)S(1)} %collective-permute-done.2.refs_2_.refs_11_, ...), custom_call_target="tpu_custom_call" | custom-call | flops 16106127360 | bytes 262144 | tf_op jit(solution)/shard_map/mix/pallas_call | solution.py:697
  17.6 0.0 collective-permute-done.5.refs_14_
  17.6 0.0 collective-permute-done.4.refs_13_
  17.6 0.0 collective-permute-done.3.refs_12_
  17.6 1.5 %project.1 = (f32[136,128]{1,0:T(8,128)S(1)}, bf16[256,256]{1,0:T(8,128)(2,1)S(1)}, bf16[256,256]{1,0:T(8,128)(2,1)S(1)}, f32[256,128]{1,0:T(8,128)S(1)}, f32[25...) custom-call(bf16[256,512]{1,0:T(8,128)(2,1)S(1)} %get-tuple-element.47.refs_0_, ...), custom_call_target="tpu_custom_call" | custom-call | tf_op jit(solution)/shard_map/project/pallas_call | solution.py:715
  19.1 0.0 copy-start.4
  19.1 0.5 %collective-permute-start.6 = (f32[136,128]{1,0:T(8,128)S(1)}, f32[136,128]{1,0:T(8,128)S(1)}, u32[]{:S(2)}, u32[]{:S(2)}) collective-permute-start(f32[136,128]{1,0:T(8,128)S(1)} %get-tuple-element.56.refs_0_), channel_id=1, source_target_pairs={{0,8},{8,0},{16,24},{24,16},{1,9},{9,1},{17,25},{25,17},{2,10},{10... | collective-permute-start | bytes 208904 | tf_op jit(solution)/shard_map/ppermute | solution.py:778
  19.6 0.9 %collective-permute-done.6.refs_1_ = f32[136,128]{1,0:T(8,128)S(1)} collective-permute-done((f32[136,128]{1,0:T(8,128)S(1)}, f32[136,128]{1,0:T(8,128)S(1)}, u32[]{:S(2)}, u32[]{:S(2)}) %collective-permute-start.6) | collective-permute-done | bytes 69664 | tf_op jit(solution)/shard_map/ppermute | solution.py:778
  20.5 1.0 %collective-permute-start.7 = (f32[136,128]{1,0:T(8,128)S(1)}, f32[136,128]{1,0:T(8,128)S(1)}, u32[]{:S(2)}, u32[]{:S(2)}) collective-permute-start(f32[136,128]{1,0:T(8,128)S(1)} %get-tuple-element.58), channel_id=1, source_target_pairs={{0,16},{8,24},{16,0},{24,8},{1,17},{9,25},{17,1},{25,9},{2,18},{10... | collective-permute-start | bytes 208904 | tf_op jit(solution)/shard_map/ppermute | solution.py:778
  21.5 1.2 %block.1 = (f32[256,128]{1,0:T(8,128)S(1)}, bf16[256,128]{1,0:T(8,128)(2,1)S(1)}, bf16[256,128]{1,0:T(8,128)(2,1)S(1)}, f32[256,128]{1,0:T(8,128)S(1)}, f32[256,...) custom-call(bf16[256,256]{1,0:T(8,128)(2,1)S(1)} %get-tuple-element.59.refs, ...), custom_call_target="tpu_custom_call" | custom-call | flops 16106127360 | bytes 262144 | tf_op jit(solution)/shard_map/block/pallas_call | solution.py:744
  22.7 2.3 %collective-permute-done.7.refs_1_ = f32[136,128]{1,0:T(8,128)S(1)} collective-permute-done((f32[136,128]{1,0:T(8,128)S(1)}, f32[136,128]{1,0:T(8,128)S(1)}, u32[]{:S(2)}, u32[]{:S(2)}) %collective-permute-start.7) | collective-permute-done | bytes 69664 | tf_op jit(solution)/shard_map/ppermute | solution.py:778
  25.0 0.7 %output.1 = (f32[64,256]{1,0:T(8,128)S(1)}, f32[64,256]{1,0:T(8,128)S(1)}, f32[64,256]{1,0:T(8,128)S(1)}, f32[64,256]{1,0:T(8,128)S(1)}) custom-call(f32[136,128]{1,0:T(8,128)S(1)} %get-tuple-element.57.refs_0_, f32[136,128]{1,0:T(8,128)S(1)} %collective-permute-done.7.refs_1_, bf16[256,128]{1,0:T(8,128)(2,1)S(1)} %get-tuple-element.69.refs_2_, ...), custom_call_target="tpu_custom_call" | custom-call | tf_op jit(solution)/shard_map/output/pallas_call | solution.py:800
  25.7 2.7 %collective-permute-start.8 = (f32[64,256]{1,0:T(8,128)S(1)}, f32[64,256]{1,0:T(8,128)S(1)}, u32[]{:S(2)}, u32[]{:S(2)}) collective-permute-start(f32[64,256]{1,0:T(8,128)S(1)} %get-tuple-element.78), channel_id=1, source_target_pairs={{0,4},{2,6},{4,0},{6,2},{1,5},{3,7},{5,1},{7,3},{8,12},{10,14},{12... | collective-permute-start | bytes 196616 | tf_op jit(solution)/shard_map/ppermute | solution.py:824
  28.4 0.8 %collective-permute-start.9 = (f32[64,256]{1,0:T(8,128)S(1)}, f32[64,256]{1,0:T(8,128)S(1)}, u32[]{:S(2)}, u32[]{:S(2)}) collective-permute-start(f32[64,256]{1,0:T(8,128)S(1)} %get-tuple-element.79), channel_id=1, source_target_pairs={{0,6},{2,4},{4,2},{6,0},{1,7},{3,5},{5,3},{7,1},{8,14},{10,12},{12... | collective-permute-start | bytes 196616 | tf_op jit(solution)/shard_map/ppermute | solution.py:824
  29.3 0.5 %collective-permute-start.10 = (f32[64,256]{1,0:T(8,128)S(1)}, f32[64,256]{1,0:T(8,128)S(1)}, u32[]{:S(2)}, u32[]{:S(2)}) collective-permute-start(f32[64,256]{1,0:T(8,128)S(1)} %get-tuple-element.80), channel_id=1, source_target_pairs={{0,2},{2,0},{4,6},{6,4},{1,3},{3,1},{5,7},{7,5},{8,10},{10,8},{12,... | collective-permute-start | bytes 196616 | tf_op jit(solution)/shard_map/ppermute | solution.py:824
  29.8 2.9 %collective-permute-done.8 = f32[64,256]{1,0:T(8,128)S(1)} collective-permute-done((f32[64,256]{1,0:T(8,128)S(1)}, f32[64,256]{1,0:T(8,128)S(1)}, u32[]{:S(2)}, u32[]{:S(2)}) %collective-permute-start.8) | collective-permute-done | bytes 65568 | tf_op jit(solution)/shard_map/ppermute | solution.py:824
  32.7 1.8 %collective-permute-done.9 = f32[64,256]{1,0:T(8,128)S(1)} collective-permute-done((f32[64,256]{1,0:T(8,128)S(1)}, f32[64,256]{1,0:T(8,128)S(1)}, u32[]{:S(2)}, u32[]{:S(2)}) %collective-permute-start.9) | collective-permute-done | bytes 65568 | tf_op jit(solution)/shard_map/ppermute | solution.py:824
  34.5 0.0 collective-permute-done.10
  34.5 0.6 %add_add_fusion = f32[64,256]{1,0:T(8,128)} fusion(f32[64,256]{1,0:T(8,128)S(1)} %collective-permute-done.10, f32[64,256]{1,0:T(8,128)S(1)} %collective-permute-done.9, f32[64,256]{1,0:T(8,128)S(1)} %get-tuple-element.77, f32[64,256]{1,0:T(8,128)S(1)} %collective-permute-done.8), kind=kLoop, calls=%fused_computation | loop fusion | flops 49152 | bytes 327680 | tf_op jit(solution)/shard_map/add | solution.py:824
  (12 shorter events, 0.0 us)
Async XLA Ops:
  0.0 8.0 %copy-start = (f32[256,2,128]{2,1,0:T(2,128)S(1)}, f32[256,2,128]{2,1,0:T(2,128)}, u32[]{:S(2)}) copy-start(f32[256,2,128]{2,1,0:T(2,128)} %param.26) | copy-start | bytes 786436
  0.0 8.0 %copy-start.1 = (f32[256,2,128]{2,1,0:T(2,128)S(1)}, f32[256,2,128]{2,1,0:T(2,128)}, u32[]{:S(2)}) copy-start(f32[256,2,128]{2,1,0:T(2,128)} %param.34) | copy-start | bytes 786436
  0.0 8.0 %copy-start.2 = (f32[256,2,128]{2,1,0:T(2,128)S(1)}, f32[256,2,128]{2,1,0:T(2,128)}, u32[]{:S(2)}) copy-start(f32[256,2,128]{2,1,0:T(2,128)} %param.35) | copy-start | bytes 786436
  0.0 8.0 %copy-start.3 = (f32[128,256]{1,0:T(8,128)S(1)}, f32[128,256]{1,0:T(8,128)}, u32[]{:S(2)}) copy-start(f32[128,256]{1,0:T(8,128)} %refs_4_.2) | copy-start | bytes 393220
  0.0 8.0 %copy-start.6 = (f32[16,256]{1,0:T(8,128)S(1)}, f32[16,256]{1,0:T(8,128)}, u32[]{:S(2)}) copy-start(f32[16,256]{1,0:T(8,128)} %refs_4_.3) | copy-start | bytes 49156
  0.0 8.0 %copy-start.9 = (s32[256]{0:T(256)S(1)}, s32[256]{0:T(256)}, u32[]{:S(2)}) copy-start(s32[256]{0:T(256)} %param.23) | copy-start | bytes 3076
  0.0 8.0 %copy-start.10 = (f32[256]{0:T(256)S(1)}, f32[256]{0:T(256)}, u32[]{:S(2)}) copy-start(f32[256]{0:T(256)} %param.33) | copy-start | bytes 3076
  0.0 8.0 %copy-start.12 = (f32[2]{0:T(128)S(1)}, f32[2]{0:T(128)}, u32[]{:S(2)}) copy-start(f32[2]{0:T(128)} %refs_10_.1) | copy-start | bytes 28
  0.0 8.0 %copy-start.13 = (f32[2]{0:T(128)S(1)}, f32[2]{0:T(128)}, u32[]{:S(2)}) copy-start(f32[2]{0:T(128)} %refs_11_.2) | copy-start | bytes 28
  0.1 8.0 %copy-start.14 = (f32[128]{0:T(128)S(1)}, f32[128]{0:T(128)}, u32[]{:S(2)}) copy-start(f32[128]{0:T(128)} %param.40) | copy-start | bytes 1540
  2.2 11.8 %collective-permute-start.2 = (f32[168,128]{1,0:T(8,128)}, f32[168,128]{1,0:T(8,128)S(1)}, u32[]{:S(2)}, u32[]{:S(2)}) collective-permute-start(f32[168,128]{1,0:T(8,128)} %tables.1.refs_3_), channel_id=1, source_target_pairs={{0,20},{2,22},{4,16},{6,18},{8,28},{10,30},{12,24},{14,26},{16,4},... | collective-permute-start | bytes 258056 | tf_op jit(solution)/shard_map/ppermute | solution.py:692
  7.3 6.9 %collective-permute-start.1 = (f32[168,128]{1,0:T(8,128)}, f32[168,128]{1,0:T(8,128)S(1)}, u32[]{:S(2)}, u32[]{:S(2)}) collective-permute-start(f32[168,128]{1,0:T(8,128)} %tables.1.refs_3_), channel_id=1, source_target_pairs={{0,14},{2,12},{4,10},{6,8},{8,6},{10,4},{12,2},{14,0},{16,30},{18,... | collective-permute-start | bytes 258056 | tf_op jit(solution)/shard_map/ppermute | solution.py:692
  7.8 7.8 %collective-permute-start = (f32[168,128]{1,0:T(8,128)}, f32[168,128]{1,0:T(8,128)S(1)}, u32[]{:S(2)}, u32[]{:S(2)}) collective-permute-start(f32[168,128]{1,0:T(8,128)} %tables.1.refs_3_), channel_id=1, source_target_pairs={{0,26},{2,24},{4,30},{6,28},{8,18},{10,16},{12,22},{14,20},{16,10}... | collective-permute-start | bytes 258056 | tf_op jit(solution)/shard_map/ppermute | solution.py:692
  8.0 0.7 %copy-start.7 = (f32[256,2]{0,1:T(2,128)S(1)}, f32[256,2]{0,1:T(2,128)}, u32[]{:S(2)}) copy-start(f32[256,2]{0,1:T(2,128)} %param.36) | copy-start | bytes 6148
  8.0 0.7 %copy-start.8 = (f32[256]{0:T(256)S(1)}, f32[256]{0:T(256)}, u32[]{:S(2)}) copy-start(f32[256]{0:T(256)} %param.24) | copy-start | bytes 3076
  8.0 0.7 %copy-start.11 = (f32[2]{0:T(128)S(1)}, f32[2]{0:T(128)}, u32[]{:S(2)}) copy-start(f32[2]{0:T(128)} %refs_9_.3) | copy-start | bytes 28
  8.7 7.0 %copy-start.5 = (f32[168,128]{1,0:T(8,128)S(1)}, f32[168,128]{1,0:T(8,128)}, u32[]{:S(2)}) copy-start(f32[168,128]{1,0:T(8,128)} %tables.1.refs_3_) | copy-start | bytes 258052
  14.1 3.5 %collective-permute-start.5 = (f32[168,128]{1,0:T(8,128)S(1)}, f32[168,128]{1,0:T(8,128)S(1)}, u32[]{:S(2)}, u32[]{:S(2)}) collective-permute-start(f32[168,128]{1,0:T(8,128)S(1)} %collective-permute-done.2.refs_2_.refs_11_), channel_id=1, source_target_pairs={{0,8},{8,0},{16,24},{24,16},{1,9},{9,1},{17,25},{25,17},{2,10},{10... | collective-permute-start | bytes 258056 | tf_op jit(solution)/shard_map/ppermute | solution.py:695
  14.2 3.4 %collective-permute-start.4 = (f32[168,128]{1,0:T(8,128)S(1)}, f32[168,128]{1,0:T(8,128)S(1)}, u32[]{:S(2)}, u32[]{:S(2)}) collective-permute-start(f32[168,128]{1,0:T(8,128)S(1)} %collective-permute-done.1.refs_1_.refs_10_), channel_id=1, source_target_pairs={{0,8},{8,0},{16,24},{24,16},{1,9},{9,1},{17,25},{25,17},{2,10},{10... | collective-permute-start | bytes 258056 | tf_op jit(solution)/shard_map/ppermute | solution.py:695
  15.6 2.0 %collective-permute-start.3 = (f32[168,128]{1,0:T(8,128)S(1)}, f32[168,128]{1,0:T(8,128)S(1)}, u32[]{:S(2)}, u32[]{:S(2)}) collective-permute-start(f32[168,128]{1,0:T(8,128)S(1)} %collective-permute-done.refs_0_.refs_9_), channel_id=1, source_target_pairs={{0,8},{8,0},{16,24},{24,16},{1,9},{9,1},{17,25},{25,17},{2,10},{10... | collective-permute-start | bytes 258056 | tf_op jit(solution)/shard_map/ppermute | solution.py:695
  19.1 2.4 %copy-start.4 = (f32[128,256]{1,0:T(8,128)S(1)}, f32[128,256]{1,0:T(8,128)}, u32[]{:S(2)}) copy-start(f32[128,256]{1,0:T(8,128)} %refs_11_.3) | copy-start | bytes 393220
  19.1 1.4 %collective-permute-start.6 = (f32[136,128]{1,0:T(8,128)S(1)}, f32[136,128]{1,0:T(8,128)S(1)}, u32[]{:S(2)}, u32[]{:S(2)}) collective-permute-start(f32[136,128]{1,0:T(8,128)S(1)} %get-tuple-element.56.refs_0_), channel_id=1, source_target_pairs={{0,8},{8,0},{16,24},{24,16},{1,9},{9,1},{17,25},{25,17},{2,10},{10... | collective-permute-start | bytes 208904 | tf_op jit(solution)/shard_map/ppermute | solution.py:778
  20.5 4.5 %collective-permute-start.7 = (f32[136,128]{1,0:T(8,128)S(1)}, f32[136,128]{1,0:T(8,128)S(1)}, u32[]{:S(2)}, u32[]{:S(2)}) collective-permute-start(f32[136,128]{1,0:T(8,128)S(1)} %get-tuple-element.58), channel_id=1, source_target_pairs={{0,16},{8,24},{16,0},{24,8},{1,17},{9,25},{17,1},{25,9},{2,18},{10... | collective-permute-start | bytes 208904 | tf_op jit(solution)/shard_map/ppermute | solution.py:778
  25.7 7.0 %collective-permute-start.8 = (f32[64,256]{1,0:T(8,128)S(1)}, f32[64,256]{1,0:T(8,128)S(1)}, u32[]{:S(2)}, u32[]{:S(2)}) collective-permute-start(f32[64,256]{1,0:T(8,128)S(1)} %get-tuple-element.78), channel_id=1, source_target_pairs={{0,4},{2,6},{4,0},{6,2},{1,5},{3,7},{5,1},{7,3},{8,12},{10,14},{12... | collective-permute-start | bytes 196616 | tf_op jit(solution)/shard_map/ppermute | solution.py:824
  28.4 6.1 %collective-permute-start.9 = (f32[64,256]{1,0:T(8,128)S(1)}, f32[64,256]{1,0:T(8,128)S(1)}, u32[]{:S(2)}, u32[]{:S(2)}) collective-permute-start(f32[64,256]{1,0:T(8,128)S(1)} %get-tuple-element.79), channel_id=1, source_target_pairs={{0,6},{2,4},{4,2},{6,0},{1,7},{3,5},{5,3},{7,1},{8,14},{10,12},{12... | collective-permute-start | bytes 196616 | tf_op jit(solution)/shard_map/ppermute | solution.py:824
  29.3 5.2 %collective-permute-start.10 = (f32[64,256]{1,0:T(8,128)S(1)}, f32[64,256]{1,0:T(8,128)S(1)}, u32[]{:S(2)}, u32[]{:S(2)}) collective-permute-start(f32[64,256]{1,0:T(8,128)S(1)} %get-tuple-element.80), channel_id=1, source_target_pairs={{0,2},{2,0},{4,6},{6,4},{1,3},{3,1},{5,7},{7,5},{8,10},{10,8},{12,... | collective-permute-start | bytes 196616 | tf_op jit(solution)/shard_map/ppermute | solution.py:824

commit v11 on v10

--- a/solution.py
+++ b/solution.py
@@ -100,7 +100,7 @@
     return copies
 
 
-PIECES = 4
+PIECES = 1
 
 
 def tables_kernel(dims, *refs):
@@ -222,7 +222,8 @@
     small[3:4, :] = outnorm2[...]
     row, column = iota((T, 1), 0), iota((1, T), 1)
     triangles[:, 0:T] = (row > column).astype(f32).astype(bf16)
-    triangles[:, T:] = (row < column).astype(f32).astype(bf16)
+    triangles[:, T : 2 * T] = (row < column).astype(f32).astype(bf16)
+    triangles[:, 2 * T :] = jnp.ones((T, 128), bf16)
     upto[...] = (row >= column).astype(f32).astype(bf16)
     size = groups.shape[0]
     groups[...] = (iota((size, 1), 0) // P == iota((1, size), 1) // P).astype(f32).astype(bf16)
@@ -251,10 +252,9 @@
     amount = 1
     while amount < size:
         value = value + decay * shift_rows(value, sign * amount, 0.0)
-        if 2 * amount < size:
-            decay = decay * shift_rows(decay, sign * amount, 1.0)
+        decay = decay * shift_rows(decay, sign * amount, 1.0)
         amount *= 2
-    return value
+    return value, decay
 
 
 def mix_kernel(dims, *refs):
@@ -307,27 +307,25 @@
     size = ns * H
     sums = dot(jnp.concatenate(split3(logs)[::-1], axis=0), triangles[...])
     sums = (sums[0:size] + sums[size : 2 * size]) + sums[2 * size :]
-    after, before = sums[:, 0:T], sums[:, T:]
-    totals = jnp.broadcast_to(jnp.sum(logs, axis=1, keepdims=True), (size, 128))
-    piece = iota((1, 128), 1)
-    high, middle, low = [part.astype(f32) for part in split3(totals)]
-    totals = jnp.where(
-        piece == 0, high, jnp.where(piece == 1, middle, jnp.where(piece == 2, low, 0.0))
-    )
-    row, column = iota((ns * H, 1), 0), iota((1, ns * H), 1)
-    row_block, column_block = row // H, column // H
-    between = ((row_block < column_block) & (column_block < mine)) | (
-        (row_block > column_block) & (column_block > mine)
-    )
-    between = (between & (row % H == column % H)).astype(f32).astype(bf16)
-    gap = jnp.sum(dot(between, totals.astype(bf16)), axis=1, keepdims=True)
-    block_of = iota((ns * H, 1), 0) // H
-    weight_up = jnp.where(block_of < mine, jnp.exp(after + gap), 0.0)
-    weight_down = jnp.where(block_of > mine, jnp.exp(before + gap), 0.0)
+    blocks_of = [sums[block * H : (block + 1) * H] for block in range(ns)]
+    weight_up, weight_down = [None] * ns, [None] * ns
+    gap = jnp.zeros((H, 128), f32)
+    for block in reversed(range(ns)):
+        wide = jnp.concatenate([gap] * (T // 128), axis=1)
+        weight_up[block] = jnp.where(
+            block < mine, jnp.exp(blocks_of[block][:, 0:T] + wide), 0.0
+        )
+        gap = jnp.where(block < mine, gap + blocks_of[block][:, 2 * T :], gap)
+    gap = jnp.zeros((H, 128), f32)
+    for block in range(ns):
+        wide = jnp.concatenate([gap] * (T // 128), axis=1)
+        weight_down[block] = jnp.where(
+            block > mine, jnp.exp(blocks_of[block][:, T : 2 * T] + wide), 0.0
+        )
+        gap = jnp.where(block > mine, gap + blocks_of[block][:, 2 * T :], gap)
     entering = jnp.zeros((4 * H, LV), f32)
     for block in range(ns):
-        rows = slice(block * H, (block + 1) * H)
-        both = jnp.concatenate([weight_up[rows], weight_down[rows]], axis=0)
+        both = jnp.concatenate([weight_up[block], weight_down[block]], axis=0)
         entering = entering + dot(
             jnp.concatenate(split2(both), axis=0), onehots[block], NT
         )
@@ -353,23 +351,32 @@
     silu_rows = rows[:, 4 * LV : 4 * LV + C]
     out_embedded[...] = rows[:, 4 * LV + C :]
 
-    edge = iota((8, 1), 0)
-    begin = jnp.where(edge == 0, decay[0:8] * enter_up, 0.0)
-    up = scan_rows(decay, jnp.concatenate([step[0:8] + begin, step[8:]], axis=0), 1)
-    begin = jnp.where(edge == 7, decay[T - 8 :] * enter_down, 0.0)
-    down = scan_rows(
-        decay, jnp.concatenate([step[: T - 8], step[T - 8 :] + begin], axis=0), -1
-    )
+    up, fade = scan_rows(decay, step, 1)
+    up = up + fade * enter_up
+    down, fade = scan_rows(decay, step, -1)
+    down = down + fade * enter_down
 
     spread_high, spread_low = [
         jnp.concatenate([part] * H, axis=0) * blocks[...] for part in split2(inners)
     ]
     both = jnp.concatenate([up * pair + gain, down * pair + gain], axis=0)
-    high, low = split2(both)
-    value = dot(high, spread_low) + dot(
-        jnp.concatenate([low, high], axis=1),
-        jnp.concatenate([spread_high, spread_high], axis=0),
-    )
+    high = both.astype(bf16)
+    high_wide = high.astype(f32)
+    low_turned = pltpu.roll(both - high_wide, LV // 2, 1)
+    lower = iota((1, LV), 1) < LV // 2
+    value = []
+    for side in (0, 1):
+        mixed = jnp.where(lower == (side == 0), high_wide, low_turned).astype(bf16)
+        rows = slice(side * LV // 2, (side + 1) * LV // 2)
+        columns = slice(side * C // 2, (side + 1) * C // 2)
+        weight, rest = spread_high[rows, columns], spread_low[:, columns]
+        value.append(
+            dot(
+                jnp.concatenate([mixed, high], axis=1),
+                jnp.concatenate([weight, weight, rest], axis=0),
+            )
+        )
+    value = jnp.concatenate(value, axis=1)
     value = value * jnp.concatenate([silu_rows, silu_rows], axis=0)
     wide = groups.shape[0]
     high, low = split2(value * value)
@@ -667,7 +674,7 @@
             *halves(ch, D),
             *halves(D, 2 * ch + N),
             *halves(D, ch + N),
-            shape(T, 2 * T, dtype=bf16),
+            shape(T, 2 * T + 128, dtype=bf16),
             shape(T, T, dtype=bf16),
             shape(2 * ch, 2 * ch, dtype=bf16),
             shape(LV, nh * ch, dtype=bf16),

time: 35.3 us -> 35 us (level)
  no operation moved by 1% of the time
where the time goes in v11:
time: 35 us; the launch traced here: 34.8 us
  waiting for transfers between devices  13.1 us (37%)
  starting transfers between devices  11.7 us (33%)
  Pallas kernels  8.43 us (24%)
  local copies, waits for them, and re-layouts  0.65 us (2%)
  other arithmetic  0.65 us (2%)
    ppermute x3, starting transfers between devices, per_device(): messages[k] = lax.ppermute(sent, ('seq', 'head'), pairs)  5.75 us
    ppermute x3, waiting for transfers between devices, per_device(): messages[k] = lax.ppermute(sent, ('seq', 'head'), pairs)  5.15 us
    ppermute x3, waiting for transfers between devices, per_device(): result = result + lax.ppermute(parts[k], 'head', pairs)  4.75 us
    ppermute x3, starting transfers between devices, per_device(): result = result + lax.ppermute(parts[k], 'head', pairs)  4 us
    ppermute x2, waiting for transfers between devices, per_device(): lax.ppermute(state, 'seq', [(seq, seq ^ 2 ** bit) for seq in range(ns)])  3.24 us
    pallas_call x1, Pallas kernels, per_device(): pl.pallas_call(functools.partial(tables_kernel, dims), out_shape=shape(to...  2.1 us
    pallas_call x1, Pallas kernels, per_device(): pl.pallas_call(functools.partial(mix_kernel, dims), out_shape=(*halves(T,...  1.59 us
    pallas_call x1, Pallas kernels, per_device(): pl.pallas_call(functools.partial(project_kernel, dims), out_shape=(shape(...  1.5 us
  transfers between devices with their start and end apart: 11, of which 7 were waited for; matrix products, arithmetic and copies ran while one was open for 0% of the time, Pallas kernels for 12%

profile of v11, /device:TPU:0, one launch (start us, length us, event | category | flops | bytes accessed | tf_op | source)
XLA Modules:
  0.0 34.8 jit_solution(1390359208371888539)
XLA Ops:
  0.0 0.0 copy-start.9
  0.0 0.0 copy-start.10
  0.0 0.0 copy-start.12
  0.0 0.0 copy-start.13
  0.1 0.0 copy-start.14
  0.1 2.1 %tables.1.refs_3_ = f32[168,128]{1,0:T(8,128)} custom-call(f32[512,128]{1,0:T(8,128)} %bitcast.24, s32[1,256]{1,0:T(1,128)} %bitcast.26, f32[16,256]{1,0:T(8,128)} %refs_4_.3, f32[1,256]{1,0:T(1,128)} %bitcast.19, f32[2,256]{1,0:T(2,128)} %bitcast.25, f32[1,2]{1,0:T(1,128)} %bitcast.27, f32[1,2]{1,0:T(1,128)} %bitcast.28, f32[1,2]{1,0:T(1,128)} %bitcast.29, ...), custom_call_target="tpu_custom_call" | custom-call | flops 16106127360 | bytes 262144 | tf_op jit(solution)/shard_map/tables/pallas_call | solution.py:627
  2.2 5.0 %collective-permute-start.2 = (f32[168,128]{1,0:T(8,128)}, f32[168,128]{1,0:T(8,128)S(1)}, u32[]{:S(2)}, u32[]{:S(2)}) collective-permute-start(f32[168,128]{1,0:T(8,128)} %tables.1.refs_3_), channel_id=1, source_target_pairs={{0,20},{2,22},{4,16},{6,18},{8,28},{10,30},{12,24},{14,26},{16,4},... | collective-permute-start | bytes 258056 | tf_op jit(solution)/shard_map/ppermute | solution.py:699
  7.2 0.5 %collective-permute-start.1 = (f32[168,128]{1,0:T(8,128)}, f32[168,128]{1,0:T(8,128)S(1)}, u32[]{:S(2)}, u32[]{:S(2)}) collective-permute-start(f32[168,128]{1,0:T(8,128)} %tables.1.refs_3_), channel_id=1, source_target_pairs={{0,14},{2,12},{4,10},{6,8},{8,6},{10,4},{12,2},{14,0},{16,30},{18,... | collective-permute-start | bytes 258056 | tf_op jit(solution)/shard_map/ppermute | solution.py:699
  7.7 0.2 collective-permute-start
  7.9 0.0 copy-done
  7.9 0.0 copy-done.1
  7.9 0.0 copy-done.2
  8.0 0.0 copy-done.3
  8.0 0.0 copy-done.6
  8.0 0.0 copy-done.9
  8.0 0.0 copy-done.10
  8.0 0.0 copy-done.12
  8.0 0.0 copy-done.13
  8.0 0.6 %copy-done.7 = f32[256,2]{0,1:T(2,128)S(1)} copy-done((f32[256,2]{0,1:T(2,128)S(1)}, f32[256,2]{0,1:T(2,128)}, u32[]{:S(2)}) %copy-start.7) | copy-done | bytes 2072
  8.6 0.0 copy-done.8
  8.6 0.0 copy-done.11
  8.6 1.3 %prepare.1 = (f32[16,128]{1,0:T(8,128)S(1)}, f32[8,128]{1,0:T(8,128)S(1)}, bf16[256,256]{1,0:T(8,128)(2,1)S(1)}, bf16[128,256]{1,0:T(8,128)(2,1)S(1)}, bf16[128,...) custom-call(f32[16,256]{1,0:T(8,128)S(1)} %copy-done.6, ...), custom_call_target="tpu_custom_call" | custom-call | flops 16106127360 | bytes 262144 | tf_op jit(solution)/shard_map/prepare/pallas_call | solution.py:668
  10.0 4.0 %collective-permute-done.2.refs_2_.refs_11_ = f32[168,128]{1,0:T(8,128)S(1)} collective-permute-done((f32[168,128]{1,0:T(8,128)}, f32[168,128]{1,0:T(8,128)S(1)}, u32[]{:S(2)}, u32[]{:S(2)}) %collective-permute-start.2) | collective-permute-done | bytes 86048 | tf_op jit(solution)/shard_map/ppermute | solution.py:699
  14.0 0.0 collective-permute-start.5
  14.0 0.1 collective-permute-done.1.refs_1_.refs_10_
  14.1 0.4 %collective-permute-start.4 = (f32[168,128]{1,0:T(8,128)S(1)}, f32[168,128]{1,0:T(8,128)S(1)}, u32[]{:S(2)}, u32[]{:S(2)}) collective-permute-start(f32[168,128]{1,0:T(8,128)S(1)} %collective-permute-done.1.refs_1_.refs_10_), channel_id=1, source_target_pairs={{0,8},{8,0},{16,24},{24,16},{1,9},{9,1},{17,25},{25,17},{2,10},{10... | collective-permute-start | bytes 258056 | tf_op jit(solution)/shard_map/ppermute | solution.py:702
  14.5 1.0 %collective-permute-done.refs_0_.refs_9_ = f32[168,128]{1,0:T(8,128)S(1)} collective-permute-done((f32[168,128]{1,0:T(8,128)}, f32[168,128]{1,0:T(8,128)S(1)}, u32[]{:S(2)}, u32[]{:S(2)}) %collective-permute-start) | collective-permute-done | bytes 86048 | tf_op jit(solution)/shard_map/ppermute | solution.py:699
  15.5 0.1 collective-permute-start.3
  15.6 0.0 copy-done.5
  15.6 1.6 %mix.1 = (bf16[256,512]{1,0:T(8,128)(2,1)S(1)}, bf16[256,512]{1,0:T(8,128)(2,1)S(1)}, f32[256,256]{1,0:T(8,128)S(1)}) custom-call(f32[168,128]{1,0:T(8,128)S(1)} %collective-permute-done.refs_0_.refs_9_, f32[168,128]{1,0:T(8,128)S(1)} %collective-permute-done.1.refs_1_.refs_10_, f32[168,128]{1,0:T(8,128)S(1)} %collective-permute-done.2.refs_2_.refs_11_, ...), custom_call_target="tpu_custom_call" | custom-call | flops 16106127360 | bytes 262144 | tf_op jit(solution)/shard_map/mix/pallas_call | solution.py:704
  17.2 0.0 collective-permute-done.5.refs_14_
  17.2 0.0 collective-permute-done.4.refs_13_
  17.3 0.0 collective-permute-done.3.refs_12_
  17.3 1.5 %project.1 = (f32[136,128]{1,0:T(8,128)S(1)}, bf16[256,256]{1,0:T(8,128)(2,1)S(1)}, bf16[256,256]{1,0:T(8,128)(2,1)S(1)}, f32[256,128]{1,0:T(8,128)S(1)}, f32[25...) custom-call(bf16[256,512]{1,0:T(8,128)(2,1)S(1)} %get-tuple-element.47.refs_0_, ...), custom_call_target="tpu_custom_call" | custom-call | tf_op jit(solution)/shard_map/project/pallas_call | solution.py:722
  18.8 0.0 copy-start.4
  18.8 0.5 %collective-permute-start.6 = (f32[136,128]{1,0:T(8,128)S(1)}, f32[136,128]{1,0:T(8,128)S(1)}, u32[]{:S(2)}, u32[]{:S(2)}) collective-permute-start(f32[136,128]{1,0:T(8,128)S(1)} %get-tuple-element.56.refs_0_), channel_id=1, source_target_pairs={{0,8},{8,0},{16,24},{24,16},{1,9},{9,1},{17,25},{25,17},{2,10},{10... | collective-permute-start | bytes 208904 | tf_op jit(solution)/shard_map/ppermute | solution.py:785
  19.3 0.9 %collective-permute-done.6.refs_1_ = f32[136,128]{1,0:T(8,128)S(1)} collective-permute-done((f32[136,128]{1,0:T(8,128)S(1)}, f32[136,128]{1,0:T(8,128)S(1)}, u32[]{:S(2)}, u32[]{:S(2)}) %collective-permute-start.6) | collective-permute-done | bytes 69664 | tf_op jit(solution)/shard_map/ppermute | solution.py:785
  20.2 1.0 %collective-permute-start.7 = (f32[136,128]{1,0:T(8,128)S(1)}, f32[136,128]{1,0:T(8,128)S(1)}, u32[]{:S(2)}, u32[]{:S(2)}) collective-permute-start(f32[136,128]{1,0:T(8,128)S(1)} %get-tuple-element.58), channel_id=1, source_target_pairs={{0,16},{8,24},{16,0},{24,8},{1,17},{9,25},{17,1},{25,9},{2,18},{10... | collective-permute-start | bytes 208904 | tf_op jit(solution)/shard_map/ppermute | solution.py:785
  21.2 1.2 %block.1 = (f32[256,128]{1,0:T(8,128)S(1)}, bf16[256,128]{1,0:T(8,128)(2,1)S(1)}, bf16[256,128]{1,0:T(8,128)(2,1)S(1)}, f32[256,128]{1,0:T(8,128)S(1)}, f32[256,...) custom-call(bf16[256,256]{1,0:T(8,128)(2,1)S(1)} %get-tuple-element.59.refs, ...), custom_call_target="tpu_custom_call" | custom-call | flops 16106127360 | bytes 262144 | tf_op jit(solution)/shard_map/block/pallas_call | solution.py:751
  22.4 2.3 %collective-permute-done.7.refs_1_ = f32[136,128]{1,0:T(8,128)S(1)} collective-permute-done((f32[136,128]{1,0:T(8,128)S(1)}, f32[136,128]{1,0:T(8,128)S(1)}, u32[]{:S(2)}, u32[]{:S(2)}) %collective-permute-start.7) | collective-permute-done | bytes 69664 | tf_op jit(solution)/shard_map/ppermute | solution.py:785
  24.7 0.7 %output.1 = (f32[64,256]{1,0:T(8,128)S(1)}, f32[64,256]{1,0:T(8,128)S(1)}, f32[64,256]{1,0:T(8,128)S(1)}, f32[64,256]{1,0:T(8,128)S(1)}) custom-call(f32[136,128]{1,0:T(8,128)S(1)} %get-tuple-element.57.refs_0_, f32[136,128]{1,0:T(8,128)S(1)} %collective-permute-done.7.refs_1_, bf16[256,128]{1,0:T(8,128)(2,1)S(1)} %get-tuple-element.69.refs_2_, ...), custom_call_target="tpu_custom_call" | custom-call | tf_op jit(solution)/shard_map/output/pallas_call | solution.py:807
  25.4 2.7 %collective-permute-start.8 = (f32[64,256]{1,0:T(8,128)S(1)}, f32[64,256]{1,0:T(8,128)S(1)}, u32[]{:S(2)}, u32[]{:S(2)}) collective-permute-start(f32[64,256]{1,0:T(8,128)S(1)} %get-tuple-element.78), channel_id=1, source_target_pairs={{0,4},{2,6},{4,0},{6,2},{1,5},{3,7},{5,1},{7,3},{8,12},{10,14},{12... | collective-permute-start | bytes 196616 | tf_op jit(solution)/shard_map/ppermute | solution.py:831
  28.1 0.8 %collective-permute-start.9 = (f32[64,256]{1,0:T(8,128)S(1)}, f32[64,256]{1,0:T(8,128)S(1)}, u32[]{:S(2)}, u32[]{:S(2)}) collective-permute-start(f32[64,256]{1,0:T(8,128)S(1)} %get-tuple-element.79), channel_id=1, source_target_pairs={{0,6},{2,4},{4,2},{6,0},{1,7},{3,5},{5,3},{7,1},{8,14},{10,12},{12... | collective-permute-start | bytes 196616 | tf_op jit(solution)/shard_map/ppermute | solution.py:831
  28.9 0.5 %collective-permute-start.10 = (f32[64,256]{1,0:T(8,128)S(1)}, f32[64,256]{1,0:T(8,128)S(1)}, u32[]{:S(2)}, u32[]{:S(2)}) collective-permute-start(f32[64,256]{1,0:T(8,128)S(1)} %get-tuple-element.80), channel_id=1, source_target_pairs={{0,2},{2,0},{4,6},{6,4},{1,3},{3,1},{5,7},{7,5},{8,10},{10,8},{12,... | collective-permute-start | bytes 196616 | tf_op jit(solution)/shard_map/ppermute | solution.py:831
  29.4 2.9 %collective-permute-done.8 = f32[64,256]{1,0:T(8,128)S(1)} collective-permute-done((f32[64,256]{1,0:T(8,128)S(1)}, f32[64,256]{1,0:T(8,128)S(1)}, u32[]{:S(2)}, u32[]{:S(2)}) %collective-permute-start.8) | collective-permute-done | bytes 65568 | tf_op jit(solution)/shard_map/ppermute | solution.py:831
  32.4 1.8 %collective-permute-done.9 = f32[64,256]{1,0:T(8,128)S(1)} collective-permute-done((f32[64,256]{1,0:T(8,128)S(1)}, f32[64,256]{1,0:T(8,128)S(1)}, u32[]{:S(2)}, u32[]{:S(2)}) %collective-permute-start.9) | collective-permute-done | bytes 65568 | tf_op jit(solution)/shard_map/ppermute | solution.py:831
  34.2 0.0 collective-permute-done.10
  34.2 0.6 %add_add_fusion = f32[64,256]{1,0:T(8,128)} fusion(f32[64,256]{1,0:T(8,128)S(1)} %collective-permute-done.10, f32[64,256]{1,0:T(8,128)S(1)} %collective-permute-done.9, f32[64,256]{1,0:T(8,128)S(1)} %get-tuple-element.77, f32[64,256]{1,0:T(8,128)S(1)} %collective-permute-done.8), kind=kLoop, calls=%fused_computation | loop fusion | flops 49152 | bytes 327680 | tf_op jit(solution)/shard_map/add | solution.py:831
  (12 shorter events, 0.0 us)
Async XLA Ops:
  0.0 7.9 %copy-start = (f32[256,2,128]{2,1,0:T(2,128)S(1)}, f32[256,2,128]{2,1,0:T(2,128)}, u32[]{:S(2)}) copy-start(f32[256,2,128]{2,1,0:T(2,128)} %param.26) | copy-start | bytes 786436
  0.0 7.9 %copy-start.1 = (f32[256,2,128]{2,1,0:T(2,128)S(1)}, f32[256,2,128]{2,1,0:T(2,128)}, u32[]{:S(2)}) copy-start(f32[256,2,128]{2,1,0:T(2,128)} %param.34) | copy-start | bytes 786436
  0.0 7.9 %copy-start.2 = (f32[256,2,128]{2,1,0:T(2,128)S(1)}, f32[256,2,128]{2,1,0:T(2,128)}, u32[]{:S(2)}) copy-start(f32[256,2,128]{2,1,0:T(2,128)} %param.35) | copy-start | bytes 786436
  0.0 8.0 %copy-start.3 = (f32[128,256]{1,0:T(8,128)S(1)}, f32[128,256]{1,0:T(8,128)}, u32[]{:S(2)}) copy-start(f32[128,256]{1,0:T(8,128)} %refs_4_.2) | copy-start | bytes 393220
  0.0 8.0 %copy-start.6 = (f32[16,256]{1,0:T(8,128)S(1)}, f32[16,256]{1,0:T(8,128)}, u32[]{:S(2)}) copy-start(f32[16,256]{1,0:T(8,128)} %refs_4_.3) | copy-start | bytes 49156
  0.0 8.0 %copy-start.9 = (s32[256]{0:T(256)S(1)}, s32[256]{0:T(256)}, u32[]{:S(2)}) copy-start(s32[256]{0:T(256)} %param.23) | copy-start | bytes 3076
  0.0 8.0 %copy-start.10 = (f32[256]{0:T(256)S(1)}, f32[256]{0:T(256)}, u32[]{:S(2)}) copy-start(f32[256]{0:T(256)} %param.33) | copy-start | bytes 3076
  0.0 8.0 %copy-start.12 = (f32[2]{0:T(128)S(1)}, f32[2]{0:T(128)}, u32[]{:S(2)}) copy-start(f32[2]{0:T(128)} %refs_10_.1) | copy-start | bytes 28
  0.0 8.0 %copy-start.13 = (f32[2]{0:T(128)S(1)}, f32[2]{0:T(128)}, u32[]{:S(2)}) copy-start(f32[2]{0:T(128)} %refs_11_.2) | copy-start | bytes 28
  0.1 8.0 %copy-start.14 = (f32[128]{0:T(128)S(1)}, f32[128]{0:T(128)}, u32[]{:S(2)}) copy-start(f32[128]{0:T(128)} %param.40) | copy-start | bytes 1540
  2.2 11.8 %collective-permute-start.2 = (f32[168,128]{1,0:T(8,128)}, f32[168,128]{1,0:T(8,128)S(1)}, u32[]{:S(2)}, u32[]{:S(2)}) collective-permute-start(f32[168,128]{1,0:T(8,128)} %tables.1.refs_3_), channel_id=1, source_target_pairs={{0,20},{2,22},{4,16},{6,18},{8,28},{10,30},{12,24},{14,26},{16,4},... | collective-permute-start | bytes 258056 | tf_op jit(solution)/shard_map/ppermute | solution.py:699
  7.2 6.9 %collective-permute-start.1 = (f32[168,128]{1,0:T(8,128)}, f32[168,128]{1,0:T(8,128)S(1)}, u32[]{:S(2)}, u32[]{:S(2)}) collective-permute-start(f32[168,128]{1,0:T(8,128)} %tables.1.refs_3_), channel_id=1, source_target_pairs={{0,14},{2,12},{4,10},{6,8},{8,6},{10,4},{12,2},{14,0},{16,30},{18,... | collective-permute-start | bytes 258056 | tf_op jit(solution)/shard_map/ppermute | solution.py:699
  7.7 7.8 %collective-permute-start = (f32[168,128]{1,0:T(8,128)}, f32[168,128]{1,0:T(8,128)S(1)}, u32[]{:S(2)}, u32[]{:S(2)}) collective-permute-start(f32[168,128]{1,0:T(8,128)} %tables.1.refs_3_), channel_id=1, source_target_pairs={{0,26},{2,24},{4,30},{6,28},{8,18},{10,16},{12,22},{14,20},{16,10}... | collective-permute-start | bytes 258056 | tf_op jit(solution)/shard_map/ppermute | solution.py:699
  7.9 0.7 %copy-start.7 = (f32[256,2]{0,1:T(2,128)S(1)}, f32[256,2]{0,1:T(2,128)}, u32[]{:S(2)}) copy-start(f32[256,2]{0,1:T(2,128)} %param.36) | copy-start | bytes 6148
  7.9 0.7 %copy-start.8 = (f32[256]{0:T(256)S(1)}, f32[256]{0:T(256)}, u32[]{:S(2)}) copy-start(f32[256]{0:T(256)} %param.24) | copy-start | bytes 3076
  7.9 0.7 %copy-start.11 = (f32[2]{0:T(128)S(1)}, f32[2]{0:T(128)}, u32[]{:S(2)}) copy-start(f32[2]{0:T(128)} %refs_9_.3) | copy-start | bytes 28
  8.6 7.0 %copy-start.5 = (f32[168,128]{1,0:T(8,128)S(1)}, f32[168,128]{1,0:T(8,128)}, u32[]{:S(2)}) copy-start(f32[168,128]{1,0:T(8,128)} %tables.1.refs_3_) | copy-start | bytes 258052
  14.0 3.3 %collective-permute-start.5 = (f32[168,128]{1,0:T(8,128)S(1)}, f32[168,128]{1,0:T(8,128)S(1)}, u32[]{:S(2)}, u32[]{:S(2)}) collective-permute-start(f32[168,128]{1,0:T(8,128)S(1)} %collective-permute-done.2.refs_2_.refs_11_), channel_id=1, source_target_pairs={{0,8},{8,0},{16,24},{24,16},{1,9},{9,1},{17,25},{25,17},{2,10},{10... | collective-permute-start | bytes 258056 | tf_op jit(solution)/shard_map/ppermute | solution.py:702
  14.1 3.1 %collective-permute-start.4 = (f32[168,128]{1,0:T(8,128)S(1)}, f32[168,128]{1,0:T(8,128)S(1)}, u32[]{:S(2)}, u32[]{:S(2)}) collective-permute-start(f32[168,128]{1,0:T(8,128)S(1)} %collective-permute-done.1.refs_1_.refs_10_), channel_id=1, source_target_pairs={{0,8},{8,0},{16,24},{24,16},{1,9},{9,1},{17,25},{25,17},{2,10},{10... | collective-permute-start | bytes 258056 | tf_op jit(solution)/shard_map/ppermute | solution.py:702
  15.5 1.7 %collective-permute-start.3 = (f32[168,128]{1,0:T(8,128)S(1)}, f32[168,128]{1,0:T(8,128)S(1)}, u32[]{:S(2)}, u32[]{:S(2)}) collective-permute-start(f32[168,128]{1,0:T(8,128)S(1)} %collective-permute-done.refs_0_.refs_9_), channel_id=1, source_target_pairs={{0,8},{8,0},{16,24},{24,16},{1,9},{9,1},{17,25},{25,17},{2,10},{10... | collective-permute-start | bytes 258056 | tf_op jit(solution)/shard_map/ppermute | solution.py:702
  18.8 2.4 %copy-start.4 = (f32[128,256]{1,0:T(8,128)S(1)}, f32[128,256]{1,0:T(8,128)}, u32[]{:S(2)}) copy-start(f32[128,256]{1,0:T(8,128)} %refs_11_.3) | copy-start | bytes 393220
  18.8 1.4 %collective-permute-start.6 = (f32[136,128]{1,0:T(8,128)S(1)}, f32[136,128]{1,0:T(8,128)S(1)}, u32[]{:S(2)}, u32[]{:S(2)}) collective-permute-start(f32[136,128]{1,0:T(8,128)S(1)} %get-tuple-element.56.refs_0_), channel_id=1, source_target_pairs={{0,8},{8,0},{16,24},{24,16},{1,9},{9,1},{17,25},{25,17},{2,10},{10... | collective-permute-start | bytes 208904 | tf_op jit(solution)/shard_map/ppermute | solution.py:785
  20.2 4.5 %collective-permute-start.7 = (f32[136,128]{1,0:T(8,128)S(1)}, f32[136,128]{1,0:T(8,128)S(1)}, u32[]{:S(2)}, u32[]{:S(2)}) collective-permute-start(f32[136,128]{1,0:T(8,128)S(1)} %get-tuple-element.58), channel_id=1, source_target_pairs={{0,16},{8,24},{16,0},{24,8},{1,17},{9,25},{17,1},{25,9},{2,18},{10... | collective-permute-start | bytes 208904 | tf_op jit(solution)/shard_map/ppermute | solution.py:785
  25.4 6.9 %collective-permute-start.8 = (f32[64,256]{1,0:T(8,128)S(1)}, f32[64,256]{1,0:T(8,128)S(1)}, u32[]{:S(2)}, u32[]{:S(2)}) collective-permute-start(f32[64,256]{1,0:T(8,128)S(1)} %get-tuple-element.78), channel_id=1, source_target_pairs={{0,4},{2,6},{4,0},{6,2},{1,5},{3,7},{5,1},{7,3},{8,12},{10,14},{12... | collective-permute-start | bytes 196616 | tf_op jit(solution)/shard_map/ppermute | solution.py:831
  28.1 6.1 %collective-permute-start.9 = (f32[64,256]{1,0:T(8,128)S(1)}, f32[64,256]{1,0:T(8,128)S(1)}, u32[]{:S(2)}, u32[]{:S(2)}) collective-permute-start(f32[64,256]{1,0:T(8,128)S(1)} %get-tuple-element.79), channel_id=1, source_target_pairs={{0,6},{2,4},{4,2},{6,0},{1,7},{3,5},{5,3},{7,1},{8,14},{10,12},{12... | collective-permute-start | bytes 196616 | tf_op jit(solution)/shard_map/ppermute | solution.py:831
  28.9 5.2 %collective-permute-start.10 = (f32[64,256]{1,0:T(8,128)S(1)}, f32[64,256]{1,0:T(8,128)S(1)}, u32[]{:S(2)}, u32[]{:S(2)}) collective-permute-start(f32[64,256]{1,0:T(8,128)S(1)} %get-tuple-element.80), channel_id=1, source_target_pairs={{0,2},{2,0},{4,6},{6,4},{1,3},{3,1},{5,7},{7,5},{8,10},{10,8},{12,... | collective-permute-start | bytes 196616 | tf_op jit(solution)/shard_map/ppermute | solution.py:831

commit v12 on v11

--- a/solution.py
+++ b/solution.py
@@ -11,7 +11,6 @@
 f32 = jnp.float32
 bf16 = jnp.bfloat16
 LIMIT = 48 * 1024 * 1024
-TABLES_LIMIT = 60 * 1000 * 1000
 
 MM = (((1,), (0,)), ((), ()))
 NT = (((1,), (1,)), ((), ()))
@@ -171,7 +170,7 @@
     head_of = iota((1, ch), 1) // (ch // hl)
     line = jnp.zeros((1, ch), f32)
     for head in range(hl):
-        line = jnp.where(head_of == head, values[head], line)
+        line = jnp.where(head_of == head, values[:, head : head + 1], line)
     return line
 
 
@@ -184,42 +183,15 @@
         taken, refs[:] = refs[:number], refs[number:]
         return taken
 
-    emb, prenorm, statemap, complement, outproj = take(5)
-    prenorm2, inproj2, statemap2, stepmap2 = take(4)
-    bias2, rates2, skip2, outnorm2 = take(4)
+    sources = take(14)
     pairs, small, choose_out, own_high, own_low = take(5)
-    state_high, state_low, rest_high, rest_low = take(4)
+    state_high, state_low, rest_high, rest_low, out_high, out_low = take(6)
     triangles, upto, groups, blocks = take(4)
-    normed = split2(rms(emb[...]) * prenorm[...])
-    write = dot_split(normed, split2(statemap[pl.ds(0, D, stride=2), :]))
-    read = dot_split(normed, split2(statemap[pl.ds(1, D, stride=2), :]))
-    pairs[...] = dot3(read, jnp.concatenate([write] * H, axis=0), NT)
-    own_high[...], own_low[...] = split2(outproj[...])
-    choose = (complement[...] == iota((D, 1), 0)).astype(f32).astype(bf16)
-    choose_out[...] = choose
-    gain = jnp.transpose(jnp.broadcast_to(prenorm2[...], (128, D)))
-
-    def weights(values):
-        return split2(dot_left_exact(choose, values))
-
-    gain_wide = gain[:, 0:1]
-    inner = inproj2[pl.ds(1, D, stride=2), :] * gain_wide
-    step = jnp.transpose(
-        jnp.concatenate(
-            [jnp.broadcast_to(stepmap2[head : head + 1, :], (P, D)) for head in range(hl)], axis=0
-        )
-    )
-    write2 = statemap2[pl.ds(0, D, stride=2), :] * gain_wide
-    state_high[...], state_low[...] = weights(
-        jnp.concatenate([inner, step * gain_wide, write2], axis=1)
-    )
-    gate = inproj2[pl.ds(0, D, stride=2), :] * gain_wide
-    read2 = statemap2[pl.ds(1, D, stride=2), :] * gain_wide
-    rest_high[...], rest_low[...] = weights(jnp.concatenate([gate, read2], axis=1))
-    small[0:1, :] = head_line(dims, bias2)
-    small[1:2, :] = head_line(dims, rates2)
-    small[2:3, :] = head_line(dims, skip2)
-    small[3:4, :] = outnorm2[...]
+    places = take(14)
+    semaphores = take(1)[0]
+    copies = fetch(sources, places, semaphores)
+    inproj2, statemap2, statemap, outproj, outproj2, emb, prenorm, complement = places[:8]
+    prenorm2, stepmap2, bias2, rates2, skip2, outnorm2 = places[8:]
     row, column = iota((T, 1), 0), iota((1, T), 1)
     triangles[:, 0:T] = (row > column).astype(f32).astype(bf16)
     triangles[:, T : 2 * T] = (row < column).astype(f32).astype(bf16)
@@ -229,6 +201,39 @@
     groups[...] = (iota((size, 1), 0) // P == iota((1, size), 1) // P).astype(f32).astype(bf16)
     rows, columns = blocks.shape
     blocks[...] = (iota((rows, 1), 0) // V == iota((1, columns), 1) // P).astype(f32).astype(bf16)
+    for copy in copies:
+        copy.wait()
+    normed = split2(rms(emb[...]) * prenorm[...])
+    write = dot_split(normed, split2(statemap[pl.ds(0, D, stride=2), :]))
+    read = dot_split(normed, split2(statemap[pl.ds(1, D, stride=2), :]))
+    pairs[...] = dot3(read, jnp.concatenate([write] * H, axis=0), NT)
+    own_high[...], own_low[...] = split2(outproj[...])
+    choose = (complement[...] == iota((D, 1), 0)).astype(f32).astype(bf16)
+    choose_out[...] = choose
+    gain = jnp.transpose(jnp.broadcast_to(prenorm2[...], (128, D)))
+
+    def weights(values):
+        return split2(dot_left_exact(choose, values))
+
+    gain_wide = gain[:, 0:1]
+    inner = inproj2[pl.ds(1, D, stride=2), :] * gain_wide
+    step = jnp.transpose(
+        jnp.concatenate(
+            [jnp.broadcast_to(stepmap2[head : head + 1, :], (P, D)) for head in range(hl)], axis=0
+        )
+    )
+    write2 = statemap2[pl.ds(0, D, stride=2), :] * gain_wide
+    state_high[...], state_low[...] = weights(
+        jnp.concatenate([inner, step * gain_wide, write2], axis=1)
+    )
+    gate = inproj2[pl.ds(0, D, stride=2), :] * gain_wide
+    read2 = statemap2[pl.ds(1, D, stride=2), :] * gain_wide
+    rest_high[...], rest_low[...] = weights(jnp.concatenate([gate, read2], axis=1))
+    small[0:1, :] = head_line(dims, bias2)
+    small[1:2, :] = head_line(dims, rates2)
+    small[2:3, :] = head_line(dims, skip2)
+    out_gain = jnp.transpose(jnp.broadcast_to(outnorm2[...], (128, ch)))
+    out_high[...], out_low[...] = split2(outproj2[...] * out_gain[:, 0:1])
 
 
 def shift_rows(value, amount, fill):
@@ -469,8 +474,8 @@
         return taken
 
     high, low, scale, write, inner, stepped, total, choose = take(8)
-    rest_high, rest_low, small, outproj2 = take(4)
-    base, read_high, read_low, out_fade, out_gate, own, out_high, out_low, hidden_ref = take(9)
+    rest_high, rest_low, small = take(3)
+    base, read_high, read_low, out_fade, out_gate, own, hidden_ref = take(7)
     rows = dot_split((high[...], low[...]), (rest_high[...], rest_low[...]))
     out_gate[...] = silu(rows[:, 0:ch] * scale[...])
     read = rows[:, ch:] * scale[...]
@@ -498,8 +503,6 @@
     share = T // nh
     hidden_ref[...] = high[...].astype(f32) + low[...].astype(f32)
     place = pl.multiple_of(lax.axis_index("head") * share, 8)
-    out_gain = jnp.transpose(jnp.broadcast_to(small[3:4, :], (128, ch)))
-    out_high[...], out_low[...] = split2(outproj2[...] * out_gain[:, 0:1])
     own[...] = dot_right_exact(hidden_ref[pl.ds(place, share), :], choose[...])
 
 
@@ -590,7 +593,6 @@
     LV = nh * hl * V
     dims = (V, D, hl, ch, nh, ns, T, N)
     vmem = pl.BlockSpec(memory_space=pltpu.VMEM)
-    smem = pl.BlockSpec(memory_space=pltpu.SMEM)
     anywhere = pl.BlockSpec(memory_space=pl.ANY)
     params = pltpu.CompilerParams(vmem_limit_bytes=LIMIT)
 
@@ -602,6 +604,9 @@
 
     def room(value):
         return pltpu.VMEM(value.shape, value.dtype)
+
+    def kept(values):
+        return [pltpu.with_memory_space_constraint(value, pltpu.HBM) for value in values]
 
     def line(value):
         return value.reshape(1, -1)
@@ -626,29 +631,29 @@
     ]
     message = pl.pallas_call(
         functools.partial(tables_kernel, dims),
-        out_shape=shape(top_rows(dims) + half * (D // ch), ch),
+        out_shape=pltpu.VMEM((top_rows(dims) + half * (D // ch), ch), f32),
         in_specs=[anywhere] * (len(fetched) + 1),
         out_specs=vmem,
         scratch_shapes=[room(value) for value in fetched]
         + [pltpu.SemaphoreType.DMA((len(fetched) - 1 + PIECES + D // ch,))],
-        compiler_params=pltpu.CompilerParams(vmem_limit_bytes=TABLES_LIMIT),
-        cost_estimate=heavy,
+        compiler_params=params,
         name="tables",
-    )(*fetched, outproj_first)
+    )(*kept([*fetched, outproj_first]))
 
     prepared = [
+        flat(inproj_second),
+        flat(statemap_second),
+        flat(statemap_first),
+        outproj_first,
+        outproj_second,
         embedding,
         line(prenorm_first),
-        flat(statemap_first),
         line(complement),
-        outproj_first,
         line(prenorm_second),
-        flat(inproj_second),
-        flat(statemap_second),
         stepmap_second.T,
-        stepbias_second,
-        rates_second,
-        skipgain_second,
+        line(stepbias_second),
+        line(rates_second),
+        line(skipgain_second),
         line(outnorm_second),
     ]
     (
@@ -661,6 +666,8 @@
         state_low,
         rest_high,
         rest_low,
+        proj_high,
+        proj_low,
         triangles,
         upto,
         groups,
@@ -674,17 +681,20 @@
             *halves(ch, D),
             *halves(D, 2 * ch + N),
             *halves(D, ch + N),
+            *halves(ch, D),
             shape(T, 2 * T + 128, dtype=bf16),
             shape(T, T, dtype=bf16),
             shape(2 * ch, 2 * ch, dtype=bf16),
             shape(LV, nh * ch, dtype=bf16),
         ),
-        in_specs=[vmem] * 9 + [smem] * 3 + [vmem],
-        out_specs=(vmem,) * 13,
+        in_specs=[anywhere] * len(prepared),
+        out_specs=(vmem,) * 15,
+        scratch_shapes=[room(value) for value in prepared]
+        + [pltpu.SemaphoreType.DMA((len(prepared),))],
         compiler_params=params,
         cost_estimate=heavy,
         name="prepare",
-    )(*prepared)
+    )(*kept(prepared))
 
     count = max(ns, nh)
     messages = {0: message}
@@ -748,7 +758,7 @@
         *others,
     )
 
-    base, read_high, read_low, fade, gate, own, proj_high, proj_low = pl.pallas_call(
+    base, read_high, read_low, fade, gate, own = pl.pallas_call(
         functools.partial(block_kernel, dims),
         out_shape=(
             shape(T, ch),
@@ -756,10 +766,9 @@
             shape(T, ch),
             shape(T, ch),
             shape(share, D),
-            *halves(ch, D),
         ),
-        in_specs=[vmem] * 12,
-        out_specs=(vmem,) * 8,
+        in_specs=[vmem] * 11,
+        out_specs=(vmem,) * 6,
         scratch_shapes=[pltpu.VMEM((T, D), f32)],
         compiler_params=params,
         cost_estimate=heavy,
@@ -776,7 +785,6 @@
         rest_high,
         rest_low,
         small,
-        outproj_second,
     )
 
     prefix = None

time: 35 us -> 34 us (0.971)
  local copies, waits for them, and re-layouts: 0.65 us -> 0.01 us
    pallas_call x1, Pallas kernels: 1.35 us -> 2.07 us  [per_device(): pl.pallas_call(functools.partial(prepare_kernel, dims), out_shape=(shape(...]
    pallas_call x1, Pallas kernels: 2.1 us -> 1.43 us  [per_device(): pl.pallas_call(functools.partial(tables_kernel, dims), out_shape=pltpu.VM...]
    unnamed x30 -> x2, local copies, waits for them, and re-layouts: 0.65 us -> 0.01 us
  transfers between devices with their start and end apart: 11 -> 11, of which waited for: 7 -> 7; matrix products, arithmetic and copies ran while one was open for 0% -> 0% of each run, Pallas kernels for 12% -> 14%
where the time goes in v12:
time: 34 us; the launch traced here: 33.9 us
  waiting for transfers between devices  13 us (38%)
  starting transfers between devices  11.7 us (34%)
  Pallas kernels  8.41 us (25%)
  other arithmetic  0.65 us (2%)
    ppermute x3, starting transfers between devices, per_device(): messages[k] = lax.ppermute(sent, ('seq', 'head'), pairs)  5.74 us
    ppermute x3, waiting for transfers between devices, per_device(): messages[k] = lax.ppermute(sent, ('seq', 'head'), pairs)  4.9 us
    ppermute x3, waiting for transfers between devices, per_device(): result = result + lax.ppermute(parts[k], 'head', pairs)  4.75 us
    ppermute x3, starting transfers between devices, per_device(): result = result + lax.ppermute(parts[k], 'head', pairs)  4.02 us
    ppermute x2, waiting for transfers between devices, per_device(): lax.ppermute(state, 'seq', [(seq, seq ^ 2 ** bit) for seq in range(ns)])  3.32 us
    pallas_call x1, Pallas kernels, per_device(): pl.pallas_call(functools.partial(prepare_kernel, dims), out_shape=(shape(...  2.07 us
    pallas_call x1, Pallas kernels, per_device(): pl.pallas_call(functools.partial(mix_kernel, dims), out_shape=(*halves(T,...  1.59 us
    pallas_call x1, Pallas kernels, per_device(): pl.pallas_call(functools.partial(project_kernel, dims), out_shape=(shape(...  1.51 us
  transfers between devices with their start and end apart: 11, of which 7 were waited for; matrix products, arithmetic and copies ran while one was open for 0% of the time, Pallas kernels for 14%

profile of v12, /device:TPU:0, one launch (start us, length us, event | category | flops | bytes accessed | tf_op | source)
XLA Modules:
  0.0 33.9 jit_solution(9696213120593465746)
XLA Ops:
  0.0 1.4 %tables.1.refs_3_ = f32[168,128]{1,0:T(8,128)S(1)} custom-call(f32[512,128]{1,0:T(8,128)} %bitcast.18, s32[1,256]{1,0:T(1,128)} %bitcast.20, f32[16,256]{1,0:T(8,128)} %refs_4_.3, f32[1,256]{1,0:T(1,128)} %bitcast.21, f32[2,256]{1,0:T(2,128)} %bitcast.19, f32[1,2]{1,0:T(1,128)} %bitcast.23, f32[1,2]{1,0:T(1,128)} %bitcast.24, f32[1,2]{1,0:T(1,128)} %bitcast.25, ...), custom_call_target="tpu_custom_call" | custom-call | tf_op jit(solution)/shard_map/tables/pallas_call | solution.py:632
  1.4 5.0 %collective-permute-start.2 = (f32[168,128]{1,0:T(8,128)S(1)}, f32[168,128]{1,0:T(8,128)S(1)}, u32[]{:S(2)}, u32[]{:S(2)}) collective-permute-start(f32[168,128]{1,0:T(8,128)S(1)} %tables.1.refs_3_), channel_id=1, source_target_pairs={{0,20},{2,22},{4,16},{6,18},{8,28},{10,30},{12,24},{14,26},{16,4},... | collective-permute-start | bytes 258056 | tf_op jit(solution)/shard_map/ppermute | solution.py:709
  6.5 0.5 %collective-permute-start.1 = (f32[168,128]{1,0:T(8,128)S(1)}, f32[168,128]{1,0:T(8,128)S(1)}, u32[]{:S(2)}, u32[]{:S(2)}) collective-permute-start(f32[168,128]{1,0:T(8,128)S(1)} %tables.1.refs_3_), channel_id=1, source_target_pairs={{0,14},{2,12},{4,10},{6,8},{8,6},{10,4},{12,2},{14,0},{16,30},{18,... | collective-permute-start | bytes 258056 | tf_op jit(solution)/shard_map/ppermute | solution.py:709
  7.0 0.2 collective-permute-start
  7.2 0.0 copy-start
  7.2 2.1 %prepare.1 = (f32[16,128]{1,0:T(8,128)S(1)}, f32[8,128]{1,0:T(8,128)S(1)}, bf16[256,256]{1,0:T(8,128)(2,1)S(1)}, bf16[128,256]{1,0:T(8,128)(2,1)S(1)}, bf16[128,...) custom-call(f32[512,128]{1,0:T(8,128)} %bitcast.27, ...), custom_call_target="tpu_custom_call" | custom-call | flops 16106127360 | bytes 262144 | tf_op jit(solution)/shard_map/prepare/pallas_call | solution.py:675
  9.3 3.8 %collective-permute-done.2.refs_2_.refs_11_ = f32[168,128]{1,0:T(8,128)S(1)} collective-permute-done((f32[168,128]{1,0:T(8,128)S(1)}, f32[168,128]{1,0:T(8,128)S(1)}, u32[]{:S(2)}, u32[]{:S(2)}) %collective-permute-start.2) | collective-permute-done | bytes 86048 | tf_op jit(solution)/shard_map/ppermute | solution.py:709
  13.0 0.0 collective-permute-start.5
  13.0 0.1 collective-permute-done.1.refs_1_.refs_10_
  13.1 0.4 %collective-permute-start.4 = (f32[168,128]{1,0:T(8,128)S(1)}, f32[168,128]{1,0:T(8,128)S(1)}, u32[]{:S(2)}, u32[]{:S(2)}) collective-permute-start(f32[168,128]{1,0:T(8,128)S(1)} %collective-permute-done.1.refs_1_.refs_10_), channel_id=1, source_target_pairs={{0,8},{8,0},{16,24},{24,16},{1,9},{9,1},{17,25},{25,17},{2,10},{10... | collective-permute-start | bytes 258056 | tf_op jit(solution)/shard_map/ppermute | solution.py:712
  13.5 1.0 %collective-permute-done.refs_0_.refs_9_ = f32[168,128]{1,0:T(8,128)S(1)} collective-permute-done((f32[168,128]{1,0:T(8,128)S(1)}, f32[168,128]{1,0:T(8,128)S(1)}, u32[]{:S(2)}, u32[]{:S(2)}) %collective-permute-start) | collective-permute-done | bytes 86048 | tf_op jit(solution)/shard_map/ppermute | solution.py:709
  14.6 0.1 collective-permute-start.3
  14.7 0.0 copy-done
  14.7 1.6 %mix.1 = (bf16[256,512]{1,0:T(8,128)(2,1)S(1)}, bf16[256,512]{1,0:T(8,128)(2,1)S(1)}, f32[256,256]{1,0:T(8,128)S(1)}) custom-call(f32[168,128]{1,0:T(8,128)S(1)} %collective-permute-done.refs_0_.refs_9_, f32[168,128]{1,0:T(8,128)S(1)} %collective-permute-done.1.refs_1_.refs_10_, f32[168,128]{1,0:T(8,128)S(1)} %collective-permute-done.2.refs_2_.refs_11_, ...), custom_call_target="tpu_custom_call" | custom-call | flops 16106127360 | bytes 262144 | tf_op jit(solution)/shard_map/mix/pallas_call | solution.py:714
  16.3 0.0 collective-permute-done.5.refs_14_
  16.3 0.0 collective-permute-done.4.refs_13_
  16.3 0.0 collective-permute-done.3.refs_12_
  16.3 1.5 %project.1 = (f32[136,128]{1,0:T(8,128)S(1)}, bf16[256,256]{1,0:T(8,128)(2,1)S(1)}, bf16[256,256]{1,0:T(8,128)(2,1)S(1)}, f32[256,128]{1,0:T(8,128)S(1)}, f32[25...) custom-call(bf16[256,512]{1,0:T(8,128)(2,1)S(1)} %get-tuple-element.47.refs_0_, ...), custom_call_target="tpu_custom_call" | custom-call | tf_op jit(solution)/shard_map/project/pallas_call | solution.py:732
  17.8 0.5 %collective-permute-start.6 = (f32[136,128]{1,0:T(8,128)S(1)}, f32[136,128]{1,0:T(8,128)S(1)}, u32[]{:S(2)}, u32[]{:S(2)}) collective-permute-start(f32[136,128]{1,0:T(8,128)S(1)} %get-tuple-element.56.refs_0_), channel_id=1, source_target_pairs={{0,8},{8,0},{16,24},{24,16},{1,9},{9,1},{17,25},{25,17},{2,10},{10... | collective-permute-start | bytes 208904 | tf_op jit(solution)/shard_map/ppermute | solution.py:793
  18.3 0.9 %collective-permute-done.6.refs_1_ = f32[136,128]{1,0:T(8,128)S(1)} collective-permute-done((f32[136,128]{1,0:T(8,128)S(1)}, f32[136,128]{1,0:T(8,128)S(1)}, u32[]{:S(2)}, u32[]{:S(2)}) %collective-permute-start.6) | collective-permute-done | bytes 69664 | tf_op jit(solution)/shard_map/ppermute | solution.py:793
  19.2 1.0 %collective-permute-start.7 = (f32[136,128]{1,0:T(8,128)S(1)}, f32[136,128]{1,0:T(8,128)S(1)}, u32[]{:S(2)}, u32[]{:S(2)}) collective-permute-start(f32[136,128]{1,0:T(8,128)S(1)} %get-tuple-element.58), channel_id=1, source_target_pairs={{0,16},{8,24},{16,0},{24,8},{1,17},{9,25},{17,1},{25,9},{2,18},{10... | collective-permute-start | bytes 208904 | tf_op jit(solution)/shard_map/ppermute | solution.py:793
  20.2 1.1 %block.1 = (f32[256,128]{1,0:T(8,128)S(1)}, bf16[256,128]{1,0:T(8,128)(2,1)S(1)}, bf16[256,128]{1,0:T(8,128)(2,1)S(1)}, f32[256,128]{1,0:T(8,128)S(1)}, f32[256,128]{1,0:T(8,128)S(1)}, /*index=5*/f32[64,256]{1,0:T(8,128)S(1)}) custom-call(bf16[256,256]{1,0:T(8,128)(2,1)S(1)} %get-tuple-element.59.refs_0_, bf16[256,256]{1,0:T(8,128)(2,1)S(1)} %get-tuple-element.60.refs_1_, ...), custom_call_target="tpu_custom_call" | custom-call | flops 16106127360 | bytes 262144 | tf_op jit(solution)/shard_map/block/pallas_call | solution.py:761
  21.3 2.4 %collective-permute-done.7.refs_1_ = f32[136,128]{1,0:T(8,128)S(1)} collective-permute-done((f32[136,128]{1,0:T(8,128)S(1)}, f32[136,128]{1,0:T(8,128)S(1)}, u32[]{:S(2)}, u32[]{:S(2)}) %collective-permute-start.7) | collective-permute-done | bytes 69664 | tf_op jit(solution)/shard_map/ppermute | solution.py:793
  23.7 0.7 %output.1 = (f32[64,256]{1,0:T(8,128)S(1)}, f32[64,256]{1,0:T(8,128)S(1)}, f32[64,256]{1,0:T(8,128)S(1)}, f32[64,256]{1,0:T(8,128)S(1)}) custom-call(f32[136,128]{1,0:T(8,128)S(1)} %get-tuple-element.57.refs_0_, f32[136,128]{1,0:T(8,128)S(1)} %collective-permute-done.7.refs_1_, bf16[256,128]{1,0:T(8,128)(2,1)S(1)} %get-tuple-element.69.refs_2_, ...), custom_call_target="tpu_custom_call" | custom-call | tf_op jit(solution)/shard_map/output/pallas_call | solution.py:815
  24.4 2.7 %collective-permute-start.8 = (f32[64,256]{1,0:T(8,128)S(1)}, f32[64,256]{1,0:T(8,128)S(1)}, u32[]{:S(2)}, u32[]{:S(2)}) collective-permute-start(f32[64,256]{1,0:T(8,128)S(1)} %get-tuple-element.78), channel_id=1, source_target_pairs={{0,4},{2,6},{4,0},{6,2},{1,5},{3,7},{5,1},{7,3},{8,12},{10,14},{12... | collective-permute-start | bytes 196616 | tf_op jit(solution)/shard_map/ppermute | solution.py:839
  27.1 0.8 %collective-permute-start.9 = (f32[64,256]{1,0:T(8,128)S(1)}, f32[64,256]{1,0:T(8,128)S(1)}, u32[]{:S(2)}, u32[]{:S(2)}) collective-permute-start(f32[64,256]{1,0:T(8,128)S(1)} %get-tuple-element.79), channel_id=1, source_target_pairs={{0,6},{2,4},{4,2},{6,0},{1,7},{3,5},{5,3},{7,1},{8,14},{10,12},{12... | collective-permute-start | bytes 196616 | tf_op jit(solution)/shard_map/ppermute | solution.py:839
  28.0 0.5 %collective-permute-start.10 = (f32[64,256]{1,0:T(8,128)S(1)}, f32[64,256]{1,0:T(8,128)S(1)}, u32[]{:S(2)}, u32[]{:S(2)}) collective-permute-start(f32[64,256]{1,0:T(8,128)S(1)} %get-tuple-element.80), channel_id=1, source_target_pairs={{0,2},{2,0},{4,6},{6,4},{1,3},{3,1},{5,7},{7,5},{8,10},{10,8},{12,... | collective-permute-start | bytes 196616 | tf_op jit(solution)/shard_map/ppermute | solution.py:839
  28.5 2.9 %collective-permute-done.8 = f32[64,256]{1,0:T(8,128)S(1)} collective-permute-done((f32[64,256]{1,0:T(8,128)S(1)}, f32[64,256]{1,0:T(8,128)S(1)}, u32[]{:S(2)}, u32[]{:S(2)}) %collective-permute-start.8) | collective-permute-done | bytes 65568 | tf_op jit(solution)/shard_map/ppermute | solution.py:839
  31.4 1.8 %collective-permute-done.9 = f32[64,256]{1,0:T(8,128)S(1)} collective-permute-done((f32[64,256]{1,0:T(8,128)S(1)}, f32[64,256]{1,0:T(8,128)S(1)}, u32[]{:S(2)}, u32[]{:S(2)}) %collective-permute-start.9) | collective-permute-done | bytes 65568 | tf_op jit(solution)/shard_map/ppermute | solution.py:839
  33.2 0.0 collective-permute-done.10
  33.2 0.6 %add_add_fusion = f32[64,256]{1,0:T(8,128)} fusion(f32[64,256]{1,0:T(8,128)S(1)} %collective-permute-done.10, f32[64,256]{1,0:T(8,128)S(1)} %collective-permute-done.9, f32[64,256]{1,0:T(8,128)S(1)} %get-tuple-element.77, f32[64,256]{1,0:T(8,128)S(1)} %collective-permute-done.8), kind=kLoop, calls=%fused_computation | loop fusion | flops 49152 | bytes 327680 | tf_op jit(solution)/shard_map/add | solution.py:839
  (1 shorter events, 0.0 us)
Async XLA Ops:
  1.4 11.6 %collective-permute-start.2 = (f32[168,128]{1,0:T(8,128)S(1)}, f32[168,128]{1,0:T(8,128)S(1)}, u32[]{:S(2)}, u32[]{:S(2)}) collective-permute-start(f32[168,128]{1,0:T(8,128)S(1)} %tables.1.refs_3_), channel_id=1, source_target_pairs={{0,20},{2,22},{4,16},{6,18},{8,28},{10,30},{12,24},{14,26},{16,4},... | collective-permute-start | bytes 258056 | tf_op jit(solution)/shard_map/ppermute | solution.py:709
  6.5 6.7 %collective-permute-start.1 = (f32[168,128]{1,0:T(8,128)S(1)}, f32[168,128]{1,0:T(8,128)S(1)}, u32[]{:S(2)}, u32[]{:S(2)}) collective-permute-start(f32[168,128]{1,0:T(8,128)S(1)} %tables.1.refs_3_), channel_id=1, source_target_pairs={{0,14},{2,12},{4,10},{6,8},{8,6},{10,4},{12,2},{14,0},{16,30},{18,... | collective-permute-start | bytes 258056 | tf_op jit(solution)/shard_map/ppermute | solution.py:709
  7.0 7.6 %collective-permute-start = (f32[168,128]{1,0:T(8,128)S(1)}, f32[168,128]{1,0:T(8,128)S(1)}, u32[]{:S(2)}, u32[]{:S(2)}) collective-permute-start(f32[168,128]{1,0:T(8,128)S(1)} %tables.1.refs_3_), channel_id=1, source_target_pairs={{0,26},{2,24},{4,30},{6,28},{8,18},{10,16},{12,22},{14,20},{16,10}... | collective-permute-start | bytes 258056 | tf_op jit(solution)/shard_map/ppermute | solution.py:709
  7.2 7.5 %copy-start = (f32[16,256]{1,0:T(8,128)S(1)}, f32[16,256]{1,0:T(8,128)}, u32[]{:S(2)}) copy-start(f32[16,256]{1,0:T(8,128)} %refs_4_.3) | copy-start | bytes 49156
  13.0 3.2 %collective-permute-start.5 = (f32[168,128]{1,0:T(8,128)S(1)}, f32[168,128]{1,0:T(8,128)S(1)}, u32[]{:S(2)}, u32[]{:S(2)}) collective-permute-start(f32[168,128]{1,0:T(8,128)S(1)} %collective-permute-done.2.refs_2_.refs_11_), channel_id=1, source_target_pairs={{0,8},{8,0},{16,24},{24,16},{1,9},{9,1},{17,25},{25,17},{2,10},{10... | collective-permute-start | bytes 258056 | tf_op jit(solution)/shard_map/ppermute | solution.py:712
  13.1 3.1 %collective-permute-start.4 = (f32[168,128]{1,0:T(8,128)S(1)}, f32[168,128]{1,0:T(8,128)S(1)}, u32[]{:S(2)}, u32[]{:S(2)}) collective-permute-start(f32[168,128]{1,0:T(8,128)S(1)} %collective-permute-done.1.refs_1_.refs_10_), channel_id=1, source_target_pairs={{0,8},{8,0},{16,24},{24,16},{1,9},{9,1},{17,25},{25,17},{2,10},{10... | collective-permute-start | bytes 258056 | tf_op jit(solution)/shard_map/ppermute | solution.py:712
  14.6 1.7 %collective-permute-start.3 = (f32[168,128]{1,0:T(8,128)S(1)}, f32[168,128]{1,0:T(8,128)S(1)}, u32[]{:S(2)}, u32[]{:S(2)}) collective-permute-start(f32[168,128]{1,0:T(8,128)S(1)} %collective-permute-done.refs_0_.refs_9_), channel_id=1, source_target_pairs={{0,8},{8,0},{16,24},{24,16},{1,9},{9,1},{17,25},{25,17},{2,10},{10... | collective-permute-start | bytes 258056 | tf_op jit(solution)/shard_map/ppermute | solution.py:712
  17.8 1.4 %collective-permute-start.6 = (f32[136,128]{1,0:T(8,128)S(1)}, f32[136,128]{1,0:T(8,128)S(1)}, u32[]{:S(2)}, u32[]{:S(2)}) collective-permute-start(f32[136,128]{1,0:T(8,128)S(1)} %get-tuple-element.56.refs_0_), channel_id=1, source_target_pairs={{0,8},{8,0},{16,24},{24,16},{1,9},{9,1},{17,25},{25,17},{2,10},{10... | collective-permute-start | bytes 208904 | tf_op jit(solution)/shard_map/ppermute | solution.py:793
  19.2 4.5 %collective-permute-start.7 = (f32[136,128]{1,0:T(8,128)S(1)}, f32[136,128]{1,0:T(8,128)S(1)}, u32[]{:S(2)}, u32[]{:S(2)}) collective-permute-start(f32[136,128]{1,0:T(8,128)S(1)} %get-tuple-element.58), channel_id=1, source_target_pairs={{0,16},{8,24},{16,0},{24,8},{1,17},{9,25},{17,1},{25,9},{2,18},{10... | collective-permute-start | bytes 208904 | tf_op jit(solution)/shard_map/ppermute | solution.py:793
  24.4 7.0 %collective-permute-start.8 = (f32[64,256]{1,0:T(8,128)S(1)}, f32[64,256]{1,0:T(8,128)S(1)}, u32[]{:S(2)}, u32[]{:S(2)}) collective-permute-start(f32[64,256]{1,0:T(8,128)S(1)} %get-tuple-element.78), channel_id=1, source_target_pairs={{0,4},{2,6},{4,0},{6,2},{1,5},{3,7},{5,1},{7,3},{8,12},{10,14},{12... | collective-permute-start | bytes 196616 | tf_op jit(solution)/shard_map/ppermute | solution.py:839
  27.1 6.1 %collective-permute-start.9 = (f32[64,256]{1,0:T(8,128)S(1)}, f32[64,256]{1,0:T(8,128)S(1)}, u32[]{:S(2)}, u32[]{:S(2)}) collective-permute-start(f32[64,256]{1,0:T(8,128)S(1)} %get-tuple-element.79), channel_id=1, source_target_pairs={{0,6},{2,4},{4,2},{6,0},{1,7},{3,5},{5,3},{7,1},{8,14},{10,12},{12... | collective-permute-start | bytes 196616 | tf_op jit(solution)/shard_map/ppermute | solution.py:839
  28.0 5.2 %collective-permute-start.10 = (f32[64,256]{1,0:T(8,128)S(1)}, f32[64,256]{1,0:T(8,128)S(1)}, u32[]{:S(2)}, u32[]{:S(2)}) collective-permute-start(f32[64,256]{1,0:T(8,128)S(1)} %get-tuple-element.80), channel_id=1, source_target_pairs={{0,2},{2,0},{4,6},{6,4},{1,3},{3,1},{5,7},{7,5},{8,10},{10,8},{12,... | collective-permute-start | bytes 196616 | tf_op jit(solution)/shard_map/ppermute | solution.py:839

commit v13 on v12

--- a/solution.py
+++ b/solution.py
@@ -43,6 +43,13 @@
 
 
 def dot(left, right, dims=MM):
+    rows = left.shape[0]
+    if dims != TN and rows >= 256:
+        parts = [left[: rows // 2], left[rows // 2 :]]
+        return jnp.concatenate(
+            [lax.dot_general(part, right, dims, preferred_element_type=f32) for part in parts],
+            axis=0,
+        )
     return lax.dot_general(left, right, dims, preferred_element_type=f32)
 
 
@@ -559,6 +566,28 @@
         place = pl.multiple_of(lax.bitwise_xor(mine, k) * share, 8)
         part = partial_ref[pl.ds(place, share), :]
         outs[k][...] = part + own[...] if k == 0 else part
+
+
+QUARTERS = 4
+
+
+def finish_kernel(dims, *refs):
+    V, D, hl, ch, nh, ns, T, N = dims
+    parts, (out, total, semaphores) = refs[:nh][::-1], refs[nh:]
+    size = out.shape[0] // QUARTERS
+    copies = []
+    for quarter in range(QUARTERS):
+        rows = pl.ds(quarter * size, size)
+        value = parts[0][rows, :]
+        for part in parts[1:]:
+            value = value + part[rows, :]
+        total[rows, :] = value
+        copies.append(
+            pltpu.make_async_copy(total.at[rows, :], out.at[rows, :], semaphores.at[quarter])
+        )
+        copies[-1].start()
+    for copy in copies:
+        copy.wait()
 
 
 def per_device(
@@ -833,11 +862,19 @@
         proj_low,
         groups,
     )
-    result = parts[0]
-    for k in in_turn(nh):
-        pairs = [(source, source ^ k) for source in range(nh)]
-        result = result + lax.ppermute(parts[k], "head", pairs)
-    return result
+    arrived = [
+        lax.ppermute(parts[k], "head", [(source, source ^ k) for source in range(nh)])
+        for k in in_turn(nh)
+    ]
+    return pl.pallas_call(
+        functools.partial(finish_kernel, dims),
+        out_shape=shape(share, D),
+        in_specs=[vmem] * nh,
+        out_specs=anywhere,
+        scratch_shapes=[pltpu.VMEM((share, D), f32), pltpu.SemaphoreType.DMA((QUARTERS,))],
+        compiler_params=params,
+        name="finish",
+    )(*arrived, parts[0])
 
 
 def solution(mesh):

time: 34 us -> 34.1 us (level)
  Pallas kernels: 8.41 us -> 9.18 us
  other arithmetic: 0.65 us -> 0 us
    pallas_call x0 -> x1, Pallas kernels: none -> 0.66 us  [per_device(): pl.pallas_call(functools.partial(finish_kernel, dims), out_shape=shape(sh...]
    add x1 -> x0, other arithmetic: 0.65 us -> none  [per_device(): result = result + lax.ppermute(parts[k], 'head', pairs)]
where the time goes in v13:
time: 34.1 us; the launch traced here: 34 us
  waiting for transfers between devices  13 us (38%)
  starting transfers between devices  11.7 us (34%)
  Pallas kernels  9.18 us (27%)
    ppermute x3, starting transfers between devices, per_device(): messages[k] = lax.ppermute(sent, ('seq', 'head'), pairs)  5.74 us
    ppermute x3, waiting for transfers between devices, per_device(): messages[k] = lax.ppermute(sent, ('seq', 'head'), pairs)  4.88 us
    ppermute x3, waiting for transfers between devices, per_device(): lax.ppermute(parts[k], 'head', [(source, source ^ k) for source in range(...  4.75 us
    ppermute x3, starting transfers between devices, per_device(): lax.ppermute(parts[k], 'head', [(source, source ^ k) for source in range(...  4.02 us
    ppermute x2, waiting for transfers between devices, per_device(): lax.ppermute(state, 'seq', [(seq, seq ^ 2 ** bit) for seq in range(ns)])  3.33 us
    pallas_call x1, Pallas kernels, per_device(): pl.pallas_call(functools.partial(prepare_kernel, dims), out_shape=(shape(...  2.09 us
    pallas_call x1, Pallas kernels, per_device(): pl.pallas_call(functools.partial(mix_kernel, dims), out_shape=(*halves(T,...  1.66 us
    pallas_call x1, Pallas kernels, per_device(): pl.pallas_call(functools.partial(project_kernel, dims), out_shape=(shape(...  1.52 us
  transfers between devices with their start and end apart: 11, of which 7 were waited for; matrix products, arithmetic and copies ran while one was open for 0% of the time, Pallas kernels for 14%

profile of v13, /device:TPU:0, one launch (start us, length us, event | category | flops | bytes accessed | tf_op | source)
XLA Modules:
  0.0 34.0 jit_solution(9309354970932864746)
XLA Ops:
  0.0 1.4 %tables.1.refs_3_ = f32[168,128]{1,0:T(8,128)S(1)} custom-call(f32[512,128]{1,0:T(8,128)} %bitcast.18, s32[1,256]{1,0:T(1,128)} %bitcast.20, f32[16,256]{1,0:T(8,128)} %refs_4_.3, f32[1,256]{1,0:T(1,128)} %bitcast.21, f32[2,256]{1,0:T(2,128)} %bitcast.19, f32[1,2]{1,0:T(1,128)} %bitcast.23, f32[1,2]{1,0:T(1,128)} %bitcast.24, f32[1,2]{1,0:T(1,128)} %bitcast.25, ...), custom_call_target="tpu_custom_call" | custom-call | tf_op jit(solution)/shard_map/tables/pallas_call | solution.py:661
  1.4 5.0 %collective-permute-start.2 = (f32[168,128]{1,0:T(8,128)S(1)}, f32[168,128]{1,0:T(8,128)S(1)}, u32[]{:S(2)}, u32[]{:S(2)}) collective-permute-start(f32[168,128]{1,0:T(8,128)S(1)} %tables.1.refs_3_), channel_id=1, source_target_pairs={{0,20},{2,22},{4,16},{6,18},{8,28},{10,30},{12,24},{14,26},{16,4},... | collective-permute-start | bytes 258056 | tf_op jit(solution)/shard_map/ppermute | solution.py:738
  6.5 0.5 %collective-permute-start.1 = (f32[168,128]{1,0:T(8,128)S(1)}, f32[168,128]{1,0:T(8,128)S(1)}, u32[]{:S(2)}, u32[]{:S(2)}) collective-permute-start(f32[168,128]{1,0:T(8,128)S(1)} %tables.1.refs_3_), channel_id=1, source_target_pairs={{0,14},{2,12},{4,10},{6,8},{8,6},{10,4},{12,2},{14,0},{16,30},{18,... | collective-permute-start | bytes 258056 | tf_op jit(solution)/shard_map/ppermute | solution.py:738
  7.0 0.2 collective-permute-start
  7.2 0.0 copy-start
  7.2 2.1 %prepare.1 = (f32[16,128]{1,0:T(8,128)S(1)}, f32[8,128]{1,0:T(8,128)S(1)}, bf16[256,256]{1,0:T(8,128)(2,1)S(1)}, bf16[128,256]{1,0:T(8,128)(2,1)S(1)}, bf16[128,...) custom-call(f32[512,128]{1,0:T(8,128)} %bitcast.27, ...), custom_call_target="tpu_custom_call" | custom-call | flops 16106127360 | bytes 262144 | tf_op jit(solution)/shard_map/prepare/pallas_call | solution.py:704
  9.3 3.7 %collective-permute-done.2.refs_2_.refs_11_ = f32[168,128]{1,0:T(8,128)S(1)} collective-permute-done((f32[168,128]{1,0:T(8,128)S(1)}, f32[168,128]{1,0:T(8,128)S(1)}, u32[]{:S(2)}, u32[]{:S(2)}) %collective-permute-start.2) | collective-permute-done | bytes 86048 | tf_op jit(solution)/shard_map/ppermute | solution.py:738
  13.0 0.0 collective-permute-start.5
  13.0 0.1 collective-permute-done.1.refs_1_.refs_10_
  13.1 0.4 %collective-permute-start.4 = (f32[168,128]{1,0:T(8,128)S(1)}, f32[168,128]{1,0:T(8,128)S(1)}, u32[]{:S(2)}, u32[]{:S(2)}) collective-permute-start(f32[168,128]{1,0:T(8,128)S(1)} %collective-permute-done.1.refs_1_.refs_10_), channel_id=1, source_target_pairs={{0,8},{8,0},{16,24},{24,16},{1,9},{9,1},{17,25},{25,17},{2,10},{10... | collective-permute-start | bytes 258056 | tf_op jit(solution)/shard_map/ppermute | solution.py:741
  13.5 1.0 %collective-permute-done.refs_0_.refs_9_ = f32[168,128]{1,0:T(8,128)S(1)} collective-permute-done((f32[168,128]{1,0:T(8,128)S(1)}, f32[168,128]{1,0:T(8,128)S(1)}, u32[]{:S(2)}, u32[]{:S(2)}) %collective-permute-start) | collective-permute-done | bytes 86048 | tf_op jit(solution)/shard_map/ppermute | solution.py:738
  14.6 0.1 collective-permute-start.3
  14.7 0.0 copy-done
  14.7 1.7 %mix.1 = (bf16[256,512]{1,0:T(8,128)(2,1)S(1)}, bf16[256,512]{1,0:T(8,128)(2,1)S(1)}, f32[256,256]{1,0:T(8,128)S(1)}) custom-call(f32[168,128]{1,0:T(8,128)S(1)} %collective-permute-done.refs_0_.refs_9_, f32[168,128]{1,0:T(8,128)S(1)} %collective-permute-done.1.refs_1_.refs_10_, f32[168,128]{1,0:T(8,128)S(1)} %collective-permute-done.2.refs_2_.refs_11_, ...), custom_call_target="tpu_custom_call" | custom-call | flops 16106127360 | bytes 262144 | tf_op jit(solution)/shard_map/mix/pallas_call | solution.py:743
  16.3 0.0 collective-permute-done.5.refs_14_
  16.4 0.0 collective-permute-done.4.refs_13_
  16.4 0.0 collective-permute-done.3.refs_12_
  16.4 1.5 %project.1 = (f32[136,128]{1,0:T(8,128)S(1)}, bf16[256,256]{1,0:T(8,128)(2,1)S(1)}, bf16[256,256]{1,0:T(8,128)(2,1)S(1)}, f32[256,128]{1,0:T(8,128)S(1)}, f32[25...) custom-call(bf16[256,512]{1,0:T(8,128)(2,1)S(1)} %get-tuple-element.47.refs_0_, ...), custom_call_target="tpu_custom_call" | custom-call | tf_op jit(solution)/shard_map/project/pallas_call | solution.py:761
  17.9 0.5 %collective-permute-start.6 = (f32[136,128]{1,0:T(8,128)S(1)}, f32[136,128]{1,0:T(8,128)S(1)}, u32[]{:S(2)}, u32[]{:S(2)}) collective-permute-start(f32[136,128]{1,0:T(8,128)S(1)} %get-tuple-element.56.refs_0_), channel_id=1, source_target_pairs={{0,8},{8,0},{16,24},{24,16},{1,9},{9,1},{17,25},{25,17},{2,10},{10... | collective-permute-start | bytes 208904 | tf_op jit(solution)/shard_map/ppermute | solution.py:822
  18.4 0.9 %collective-permute-done.6.refs_1_ = f32[136,128]{1,0:T(8,128)S(1)} collective-permute-done((f32[136,128]{1,0:T(8,128)S(1)}, f32[136,128]{1,0:T(8,128)S(1)}, u32[]{:S(2)}, u32[]{:S(2)}) %collective-permute-start.6) | collective-permute-done | bytes 69664 | tf_op jit(solution)/shard_map/ppermute | solution.py:822
  19.3 1.0 %collective-permute-start.7 = (f32[136,128]{1,0:T(8,128)S(1)}, f32[136,128]{1,0:T(8,128)S(1)}, u32[]{:S(2)}, u32[]{:S(2)}) collective-permute-start(f32[136,128]{1,0:T(8,128)S(1)} %get-tuple-element.58), channel_id=1, source_target_pairs={{0,16},{8,24},{16,0},{24,8},{1,17},{9,25},{17,1},{25,9},{2,18},{10... | collective-permute-start | bytes 208904 | tf_op jit(solution)/shard_map/ppermute | solution.py:822
  20.3 1.1 %block.1 = (f32[256,128]{1,0:T(8,128)S(1)}, bf16[256,128]{1,0:T(8,128)(2,1)S(1)}, bf16[256,128]{1,0:T(8,128)(2,1)S(1)}, f32[256,128]{1,0:T(8,128)S(1)}, f32[256,128]{1,0:T(8,128)S(1)}, /*index=5*/f32[64,256]{1,0:T(8,128)S(1)}) custom-call(bf16[256,256]{1,0:T(8,128)(2,1)S(1)} %get-tuple-element.59.refs_0_, bf16[256,256]{1,0:T(8,128)(2,1)S(1)} %get-tuple-element.60.refs_1_, ...), custom_call_target="tpu_custom_call" | custom-call | flops 16106127360 | bytes 262144 | tf_op jit(solution)/shard_map/block/pallas_call | solution.py:790
  21.4 2.4 %collective-permute-done.7.refs_1_ = f32[136,128]{1,0:T(8,128)S(1)} collective-permute-done((f32[136,128]{1,0:T(8,128)S(1)}, f32[136,128]{1,0:T(8,128)S(1)}, u32[]{:S(2)}, u32[]{:S(2)}) %collective-permute-start.7) | collective-permute-done | bytes 69664 | tf_op jit(solution)/shard_map/ppermute | solution.py:822
  23.8 0.7 %output.1 = (f32[64,256]{1,0:T(8,128)S(1)}, f32[64,256]{1,0:T(8,128)S(1)}, f32[64,256]{1,0:T(8,128)S(1)}, f32[64,256]{1,0:T(8,128)S(1)}) custom-call(f32[136,128]{1,0:T(8,128)S(1)} %get-tuple-element.57.refs_0_, f32[136,128]{1,0:T(8,128)S(1)} %collective-permute-done.7.refs_1_, bf16[256,128]{1,0:T(8,128)(2,1)S(1)} %get-tuple-element.69.refs_2_, ...), custom_call_target="tpu_custom_call" | custom-call | tf_op jit(solution)/shard_map/output/pallas_call | solution.py:844
  24.5 2.7 %collective-permute-start.8 = (f32[64,256]{1,0:T(8,128)S(1)}, f32[64,256]{1,0:T(8,128)S(1)}, u32[]{:S(2)}, u32[]{:S(2)}) collective-permute-start(f32[64,256]{1,0:T(8,128)S(1)} %get-tuple-element.77), channel_id=1, source_target_pairs={{0,4},{2,6},{4,0},{6,2},{1,5},{3,7},{5,1},{7,3},{8,12},{10,14},{12... | collective-permute-start | bytes 196616 | tf_op jit(solution)/shard_map/ppermute | solution.py:866
  27.2 0.8 %collective-permute-start.9 = (f32[64,256]{1,0:T(8,128)S(1)}, f32[64,256]{1,0:T(8,128)S(1)}, u32[]{:S(2)}, u32[]{:S(2)}) collective-permute-start(f32[64,256]{1,0:T(8,128)S(1)} %get-tuple-element.78), channel_id=1, source_target_pairs={{0,6},{2,4},{4,2},{6,0},{1,7},{3,5},{5,3},{7,1},{8,14},{10,12},{12... | collective-permute-start | bytes 196616 | tf_op jit(solution)/shard_map/ppermute | solution.py:866
  28.1 0.5 %collective-permute-start.10 = (f32[64,256]{1,0:T(8,128)S(1)}, f32[64,256]{1,0:T(8,128)S(1)}, u32[]{:S(2)}, u32[]{:S(2)}) collective-permute-start(f32[64,256]{1,0:T(8,128)S(1)} %get-tuple-element.79), channel_id=1, source_target_pairs={{0,2},{2,0},{4,6},{6,4},{1,3},{3,1},{5,7},{7,5},{8,10},{10,8},{12,... | collective-permute-start | bytes 196616 | tf_op jit(solution)/shard_map/ppermute | solution.py:866
  28.6 2.9 %collective-permute-done.8.refs_0_ = f32[64,256]{1,0:T(8,128)S(1)} collective-permute-done((f32[64,256]{1,0:T(8,128)S(1)}, f32[64,256]{1,0:T(8,128)S(1)}, u32[]{:S(2)}, u32[]{:S(2)}) %collective-permute-start.8) | collective-permute-done | bytes 65568 | tf_op jit(solution)/shard_map/ppermute | solution.py:866
  31.5 1.8 %collective-permute-done.9.refs_1_ = f32[64,256]{1,0:T(8,128)S(1)} collective-permute-done((f32[64,256]{1,0:T(8,128)S(1)}, f32[64,256]{1,0:T(8,128)S(1)}, u32[]{:S(2)}, u32[]{:S(2)}) %collective-permute-start.9) | collective-permute-done | bytes 65568 | tf_op jit(solution)/shard_map/ppermute | solution.py:866
  33.3 0.0 collective-permute-done.10.refs_2_
  33.3 0.7 %finish.1 = f32[64,256]{1,0:T(8,128)} custom-call(f32[64,256]{1,0:T(8,128)S(1)} %collective-permute-done.8.refs_0_, f32[64,256]{1,0:T(8,128)S(1)} %collective-permute-done.9.refs_1_, f32[64,256]{1,0:T(8,128)S(1)} %collective-permute-done.10.refs_2_, f32[64,256]{1,0:T(8,128)S(1)} %get-tuple-element.80.refs_3_), custom_call_target="tpu_custom_call" | custom-call | tf_op jit(solution)/shard_map/finish/pallas_call | solution.py:869
  (1 shorter events, 0.0 us)
Async XLA Ops:
  1.4 11.6 %collective-permute-start.2 = (f32[168,128]{1,0:T(8,128)S(1)}, f32[168,128]{1,0:T(8,128)S(1)}, u32[]{:S(2)}, u32[]{:S(2)}) collective-permute-start(f32[168,128]{1,0:T(8,128)S(1)} %tables.1.refs_3_), channel_id=1, source_target_pairs={{0,20},{2,22},{4,16},{6,18},{8,28},{10,30},{12,24},{14,26},{16,4},... | collective-permute-start | bytes 258056 | tf_op jit(solution)/shard_map/ppermute | solution.py:738
  6.5 6.7 %collective-permute-start.1 = (f32[168,128]{1,0:T(8,128)S(1)}, f32[168,128]{1,0:T(8,128)S(1)}, u32[]{:S(2)}, u32[]{:S(2)}) collective-permute-start(f32[168,128]{1,0:T(8,128)S(1)} %tables.1.refs_3_), channel_id=1, source_target_pairs={{0,14},{2,12},{4,10},{6,8},{8,6},{10,4},{12,2},{14,0},{16,30},{18,... | collective-permute-start | bytes 258056 | tf_op jit(solution)/shard_map/ppermute | solution.py:738
  7.0 7.6 %collective-permute-start = (f32[168,128]{1,0:T(8,128)S(1)}, f32[168,128]{1,0:T(8,128)S(1)}, u32[]{:S(2)}, u32[]{:S(2)}) collective-permute-start(f32[168,128]{1,0:T(8,128)S(1)} %tables.1.refs_3_), channel_id=1, source_target_pairs={{0,26},{2,24},{4,30},{6,28},{8,18},{10,16},{12,22},{14,20},{16,10}... | collective-permute-start | bytes 258056 | tf_op jit(solution)/shard_map/ppermute | solution.py:738
  7.2 7.5 %copy-start = (f32[16,256]{1,0:T(8,128)S(1)}, f32[16,256]{1,0:T(8,128)}, u32[]{:S(2)}) copy-start(f32[16,256]{1,0:T(8,128)} %refs_4_.3) | copy-start | bytes 49156
  13.0 3.3 %collective-permute-start.5 = (f32[168,128]{1,0:T(8,128)S(1)}, f32[168,128]{1,0:T(8,128)S(1)}, u32[]{:S(2)}, u32[]{:S(2)}) collective-permute-start(f32[168,128]{1,0:T(8,128)S(1)} %collective-permute-done.2.refs_2_.refs_11_), channel_id=1, source_target_pairs={{0,8},{8,0},{16,24},{24,16},{1,9},{9,1},{17,25},{25,17},{2,10},{10... | collective-permute-start | bytes 258056 | tf_op jit(solution)/shard_map/ppermute | solution.py:741
  13.1 3.2 %collective-permute-start.4 = (f32[168,128]{1,0:T(8,128)S(1)}, f32[168,128]{1,0:T(8,128)S(1)}, u32[]{:S(2)}, u32[]{:S(2)}) collective-permute-start(f32[168,128]{1,0:T(8,128)S(1)} %collective-permute-done.1.refs_1_.refs_10_), channel_id=1, source_target_pairs={{0,8},{8,0},{16,24},{24,16},{1,9},{9,1},{17,25},{25,17},{2,10},{10... | collective-permute-start | bytes 258056 | tf_op jit(solution)/shard_map/ppermute | solution.py:741
  14.6 1.8 %collective-permute-start.3 = (f32[168,128]{1,0:T(8,128)S(1)}, f32[168,128]{1,0:T(8,128)S(1)}, u32[]{:S(2)}, u32[]{:S(2)}) collective-permute-start(f32[168,128]{1,0:T(8,128)S(1)} %collective-permute-done.refs_0_.refs_9_), channel_id=1, source_target_pairs={{0,8},{8,0},{16,24},{24,16},{1,9},{9,1},{17,25},{25,17},{2,10},{10... | collective-permute-start | bytes 258056 | tf_op jit(solution)/shard_map/ppermute | solution.py:741
  17.9 1.4 %collective-permute-start.6 = (f32[136,128]{1,0:T(8,128)S(1)}, f32[136,128]{1,0:T(8,128)S(1)}, u32[]{:S(2)}, u32[]{:S(2)}) collective-permute-start(f32[136,128]{1,0:T(8,128)S(1)} %get-tuple-element.56.refs_0_), channel_id=1, source_target_pairs={{0,8},{8,0},{16,24},{24,16},{1,9},{9,1},{17,25},{25,17},{2,10},{10... | collective-permute-start | bytes 208904 | tf_op jit(solution)/shard_map/ppermute | solution.py:822
  19.3 4.5 %collective-permute-start.7 = (f32[136,128]{1,0:T(8,128)S(1)}, f32[136,128]{1,0:T(8,128)S(1)}, u32[]{:S(2)}, u32[]{:S(2)}) collective-permute-start(f32[136,128]{1,0:T(8,128)S(1)} %get-tuple-element.58), channel_id=1, source_target_pairs={{0,16},{8,24},{16,0},{24,8},{1,17},{9,25},{17,1},{25,9},{2,18},{10... | collective-permute-start | bytes 208904 | tf_op jit(solution)/shard_map/ppermute | solution.py:822
  24.5 7.0 %collective-permute-start.8 = (f32[64,256]{1,0:T(8,128)S(1)}, f32[64,256]{1,0:T(8,128)S(1)}, u32[]{:S(2)}, u32[]{:S(2)}) collective-permute-start(f32[64,256]{1,0:T(8,128)S(1)} %get-tuple-element.77), channel_id=1, source_target_pairs={{0,4},{2,6},{4,0},{6,2},{1,5},{3,7},{5,1},{7,3},{8,12},{10,14},{12... | collective-permute-start | bytes 196616 | tf_op jit(solution)/shard_map/ppermute | solution.py:866
  27.2 6.1 %collective-permute-start.9 = (f32[64,256]{1,0:T(8,128)S(1)}, f32[64,256]{1,0:T(8,128)S(1)}, u32[]{:S(2)}, u32[]{:S(2)}) collective-permute-start(f32[64,256]{1,0:T(8,128)S(1)} %get-tuple-element.78), channel_id=1, source_target_pairs={{0,6},{2,4},{4,2},{6,0},{1,7},{3,5},{5,3},{7,1},{8,14},{10,12},{12... | collective-permute-start | bytes 196616 | tf_op jit(solution)/shard_map/ppermute | solution.py:866
  28.1 5.2 %collective-permute-start.10 = (f32[64,256]{1,0:T(8,128)S(1)}, f32[64,256]{1,0:T(8,128)S(1)}, u32[]{:S(2)}, u32[]{:S(2)}) collective-permute-start(f32[64,256]{1,0:T(8,128)S(1)} %get-tuple-element.79), channel_id=1, source_target_pairs={{0,2},{2,0},{4,6},{6,4},{1,3},{3,1},{5,7},{7,5},{8,10},{10,8},{12,... | collective-permute-start | bytes 196616 | tf_op jit(solution)/shard_map/ppermute | solution.py:866

commit v14 on v12

--- a/solution.py
+++ b/solution.py
@@ -19,11 +19,13 @@
 
 def partners(ns, nh):
     count = max(ns, nh)
-    return [((ns - k) if 0 < k < ns else 0, k if k < nh else 0) for k in range(count)]
+    return [
+        (k % (ns - 1) + 1 if 0 < k < ns else 0, k if k < nh else 0) for k in range(count)
+    ]
 
 
 def in_turn(count):
-    return sorted(range(1, count), key=lambda k: (-k.bit_length(), k))
+    return list(range(1, count))[::-1]
 
 
 def iota(shape, axis):

time: 34 us -> 34.4 us (1.012)
  starting transfers between devices: 11.7 us -> 12.3 us
    ppermute x3, waiting for transfers between devices: 4.75 us -> 3.93 us  [per_device(): result = result + lax.ppermute(parts[k], 'head', pairs)]
    ppermute x2, starting transfers between devices: 1.48 us -> 0.77 us  [per_device(): lax.ppermute(state, 'seq', [(seq, seq ^ 2 ** bit) for seq in range(ns)])]
    ppermute x2, waiting for transfers between devices: 3.32 us -> 3.85 us  [per_device(): lax.ppermute(state, 'seq', [(seq, seq ^ 2 ** bit) for seq in range(ns)])]
    ppermute x3, starting transfers between devices: 0.51 us -> 0.97 us  [per_device(): others = [lax.ppermute(messages[k], 'seq', swap) for k in order]]
    ppermute x3, starting transfers between devices: 4.02 us -> 4.45 us  [per_device(): result = result + lax.ppermute(parts[k], 'head', pairs)]
    ppermute x3, starting transfers between devices: 5.74 us -> 6.09 us  [per_device(): messages[k] = lax.ppermute(sent, ('seq', 'head'), pairs)]
  transfers between devices with their start and end apart: 11 -> 11, of which waited for: 7 -> 5; matrix products, arithmetic and copies ran while one was open for 0% -> 0% of each run, Pallas kernels for 14% -> 14%
where the time goes in v14:
time: 34.4 us; the launch traced here: 34.3 us
  waiting for transfers between devices  12.8 us (37%)
  starting transfers between devices  12.3 us (36%)
  Pallas kernels  8.42 us (24%)
  other arithmetic  0.65 us (2%)
    ppermute x3, starting transfers between devices, per_device(): messages[k] = lax.ppermute(sent, ('seq', 'head'), pairs)  6.09 us
    ppermute x3, waiting for transfers between devices, per_device(): messages[k] = lax.ppermute(sent, ('seq', 'head'), pairs)  5.04 us
    ppermute x3, starting transfers between devices, per_device(): result = result + lax.ppermute(parts[k], 'head', pairs)  4.45 us
    ppermute x3, waiting for transfers between devices, per_device(): result = result + lax.ppermute(parts[k], 'head', pairs)  3.93 us
    ppermute x2, waiting for transfers between devices, per_device(): lax.ppermute(state, 'seq', [(seq, seq ^ 2 ** bit) for seq in range(ns)])  3.85 us
    pallas_call x1, Pallas kernels, per_device(): pl.pallas_call(functools.partial(prepare_kernel, dims), out_shape=(shape(...  2.07 us
    pallas_call x1, Pallas kernels, per_device(): pl.pallas_call(functools.partial(mix_kernel, dims), out_shape=(*halves(T,...  1.6 us
    pallas_call x1, Pallas kernels, per_device(): pl.pallas_call(functools.partial(project_kernel, dims), out_shape=(shape(...  1.51 us
  transfers between devices with their start and end apart: 11, of which 5 were waited for; matrix products, arithmetic and copies ran while one was open for 0% of the time, Pallas kernels for 14%

profile of v14, /device:TPU:0, one launch (start us, length us, event | category | flops | bytes accessed | tf_op | source)
XLA Modules:
  0.0 34.3 jit_solution(1654517864666879896)
XLA Ops:
  0.0 1.4 %tables.1.refs_3_ = f32[168,128]{1,0:T(8,128)S(1)} custom-call(f32[512,128]{1,0:T(8,128)} %bitcast.18, s32[1,256]{1,0:T(1,128)} %bitcast.20, f32[16,256]{1,0:T(8,128)} %refs_4_.3, f32[1,256]{1,0:T(1,128)} %bitcast.21, f32[2,256]{1,0:T(2,128)} %bitcast.19, f32[1,2]{1,0:T(1,128)} %bitcast.23, f32[1,2]{1,0:T(1,128)} %bitcast.24, f32[1,2]{1,0:T(1,128)} %bitcast.25, ...), custom_call_target="tpu_custom_call" | custom-call | tf_op jit(solution)/shard_map/tables/pallas_call | solution.py:634
  1.4 4.6 %collective-permute-start.2 = (f32[168,128]{1,0:T(8,128)S(1)}, f32[168,128]{1,0:T(8,128)S(1)}, u32[]{:S(2)}, u32[]{:S(2)}) collective-permute-start(f32[168,128]{1,0:T(8,128)S(1)} %tables.1.refs_3_), channel_id=1, source_target_pairs={{0,14},{2,12},{4,10},{6,8},{8,6},{10,4},{12,2},{14,0},{16,30},{18,... | collective-permute-start | bytes 258056 | tf_op jit(solution)/shard_map/ppermute | solution.py:711
  6.0 0.6 %collective-permute-start.1 = (f32[168,128]{1,0:T(8,128)S(1)}, f32[168,128]{1,0:T(8,128)S(1)}, u32[]{:S(2)}, u32[]{:S(2)}) collective-permute-start(f32[168,128]{1,0:T(8,128)S(1)} %tables.1.refs_3_), channel_id=1, source_target_pairs={{0,28},{2,30},{4,24},{6,26},{8,20},{10,22},{12,16},{14,18},{16,12}... | collective-permute-start | bytes 258056 | tf_op jit(solution)/shard_map/ppermute | solution.py:711
  6.6 0.9 %collective-permute-start = (f32[168,128]{1,0:T(8,128)S(1)}, f32[168,128]{1,0:T(8,128)S(1)}, u32[]{:S(2)}, u32[]{:S(2)}) collective-permute-start(f32[168,128]{1,0:T(8,128)S(1)} %tables.1.refs_3_), channel_id=1, source_target_pairs={{0,18},{2,16},{4,22},{6,20},{8,26},{10,24},{12,30},{14,28},{16,2},... | collective-permute-start | bytes 258056 | tf_op jit(solution)/shard_map/ppermute | solution.py:711
  7.5 0.0 copy-start
  7.5 2.1 %prepare.1 = (f32[16,128]{1,0:T(8,128)S(1)}, f32[8,128]{1,0:T(8,128)S(1)}, bf16[256,256]{1,0:T(8,128)(2,1)S(1)}, bf16[128,256]{1,0:T(8,128)(2,1)S(1)}, bf16[128,...) custom-call(f32[512,128]{1,0:T(8,128)} %bitcast.27, ...), custom_call_target="tpu_custom_call" | custom-call | flops 16106127360 | bytes 262144 | tf_op jit(solution)/shard_map/prepare/pallas_call | solution.py:677
  9.6 0.0 collective-permute-done.2.refs_2_.refs_11_
  9.6 0.5 %collective-permute-start.5 = (f32[168,128]{1,0:T(8,128)S(1)}, f32[168,128]{1,0:T(8,128)S(1)}, u32[]{:S(2)}, u32[]{:S(2)}) collective-permute-start(f32[168,128]{1,0:T(8,128)S(1)} %collective-permute-done.2.refs_2_.refs_11_), channel_id=1, source_target_pairs={{0,8},{8,0},{16,24},{24,16},{1,9},{9,1},{17,25},{25,17},{2,10},{10... | collective-permute-start | bytes 258056 | tf_op jit(solution)/shard_map/ppermute | solution.py:714
  10.1 5.0 %collective-permute-done.1.refs_1_.refs_10_ = f32[168,128]{1,0:T(8,128)S(1)} collective-permute-done((f32[168,128]{1,0:T(8,128)S(1)}, f32[168,128]{1,0:T(8,128)S(1)}, u32[]{:S(2)}, u32[]{:S(2)}) %collective-permute-start.1) | collective-permute-done | bytes 86048 | tf_op jit(solution)/shard_map/ppermute | solution.py:711
  15.1 0.1 collective-permute-start.4
  15.2 0.0 collective-permute-done.refs_0_.refs_9_
  15.2 0.4 %collective-permute-start.3 = (f32[168,128]{1,0:T(8,128)S(1)}, f32[168,128]{1,0:T(8,128)S(1)}, u32[]{:S(2)}, u32[]{:S(2)}) collective-permute-start(f32[168,128]{1,0:T(8,128)S(1)} %collective-permute-done.refs_0_.refs_9_), channel_id=1, source_target_pairs={{0,8},{8,0},{16,24},{24,16},{1,9},{9,1},{17,25},{25,17},{2,10},{10... | collective-permute-start | bytes 258056 | tf_op jit(solution)/shard_map/ppermute | solution.py:714
  15.6 0.0 copy-done
  15.6 1.6 %mix.1 = (bf16[256,512]{1,0:T(8,128)(2,1)S(1)}, bf16[256,512]{1,0:T(8,128)(2,1)S(1)}, f32[256,256]{1,0:T(8,128)S(1)}) custom-call(f32[168,128]{1,0:T(8,128)S(1)} %collective-permute-done.refs_0_.refs_9_, f32[168,128]{1,0:T(8,128)S(1)} %collective-permute-done.1.refs_1_.refs_10_, f32[168,128]{1,0:T(8,128)S(1)} %collective-permute-done.2.refs_2_.refs_11_, ...), custom_call_target="tpu_custom_call" | custom-call | flops 16106127360 | bytes 262144 | tf_op jit(solution)/shard_map/mix/pallas_call | solution.py:716
  17.2 0.0 collective-permute-done.5.refs_14_
  17.3 0.0 collective-permute-done.4.refs_13_
  17.3 0.0 collective-permute-done.3.refs_12_
  17.3 1.5 %project.1 = (f32[136,128]{1,0:T(8,128)S(1)}, bf16[256,256]{1,0:T(8,128)(2,1)S(1)}, bf16[256,256]{1,0:T(8,128)(2,1)S(1)}, f32[256,128]{1,0:T(8,128)S(1)}, f32[25...) custom-call(bf16[256,512]{1,0:T(8,128)(2,1)S(1)} %get-tuple-element.47.refs_0_, ...), custom_call_target="tpu_custom_call" | custom-call | tf_op jit(solution)/shard_map/project/pallas_call | solution.py:734
  18.8 0.2 collective-permute-start.6
  19.0 1.1 %collective-permute-done.6.refs_1_ = f32[136,128]{1,0:T(8,128)S(1)} collective-permute-done((f32[136,128]{1,0:T(8,128)S(1)}, f32[136,128]{1,0:T(8,128)S(1)}, u32[]{:S(2)}, u32[]{:S(2)}) %collective-permute-start.6) | collective-permute-done | bytes 69664 | tf_op jit(solution)/shard_map/ppermute | solution.py:795
  20.2 0.6 %collective-permute-start.7 = (f32[136,128]{1,0:T(8,128)S(1)}, f32[136,128]{1,0:T(8,128)S(1)}, u32[]{:S(2)}, u32[]{:S(2)}) collective-permute-start(f32[136,128]{1,0:T(8,128)S(1)} %get-tuple-element.58), channel_id=1, source_target_pairs={{0,16},{8,24},{16,0},{24,8},{1,17},{9,25},{17,1},{25,9},{2,18},{10... | collective-permute-start | bytes 208904 | tf_op jit(solution)/shard_map/ppermute | solution.py:795
  20.7 1.1 %block.1 = (f32[256,128]{1,0:T(8,128)S(1)}, bf16[256,128]{1,0:T(8,128)(2,1)S(1)}, bf16[256,128]{1,0:T(8,128)(2,1)S(1)}, f32[256,128]{1,0:T(8,128)S(1)}, f32[256,128]{1,0:T(8,128)S(1)}, /*index=5*/f32[64,256]{1,0:T(8,128)S(1)}) custom-call(bf16[256,256]{1,0:T(8,128)(2,1)S(1)} %get-tuple-element.59.refs_0_, bf16[256,256]{1,0:T(8,128)(2,1)S(1)} %get-tuple-element.60.refs_1_, ...), custom_call_target="tpu_custom_call" | custom-call | flops 16106127360 | bytes 262144 | tf_op jit(solution)/shard_map/block/pallas_call | solution.py:763
  21.8 2.7 %collective-permute-done.7.refs_1_ = f32[136,128]{1,0:T(8,128)S(1)} collective-permute-done((f32[136,128]{1,0:T(8,128)S(1)}, f32[136,128]{1,0:T(8,128)S(1)}, u32[]{:S(2)}, u32[]{:S(2)}) %collective-permute-start.7) | collective-permute-done | bytes 69664 | tf_op jit(solution)/shard_map/ppermute | solution.py:795
  24.5 0.7 %output.1 = (f32[64,256]{1,0:T(8,128)S(1)}, f32[64,256]{1,0:T(8,128)S(1)}, f32[64,256]{1,0:T(8,128)S(1)}, f32[64,256]{1,0:T(8,128)S(1)}) custom-call(f32[136,128]{1,0:T(8,128)S(1)} %get-tuple-element.57.refs_0_, f32[136,128]{1,0:T(8,128)S(1)} %collective-permute-done.7.refs_1_, bf16[256,128]{1,0:T(8,128)(2,1)S(1)} %get-tuple-element.69.refs_2_, ...), custom_call_target="tpu_custom_call" | custom-call | tf_op jit(solution)/shard_map/output/pallas_call | solution.py:817
  25.2 2.7 %collective-permute-start.8 = (f32[64,256]{1,0:T(8,128)S(1)}, f32[64,256]{1,0:T(8,128)S(1)}, u32[]{:S(2)}, u32[]{:S(2)}) collective-permute-start(f32[64,256]{1,0:T(8,128)S(1)} %get-tuple-element.78), channel_id=1, source_target_pairs={{0,6},{2,4},{4,2},{6,0},{1,7},{3,5},{5,3},{7,1},{8,14},{10,12},{12... | collective-permute-start | bytes 196616 | tf_op jit(solution)/shard_map/ppermute | solution.py:841
  27.9 0.0 collective-permute-start.9
  27.9 1.8 %collective-permute-start.10 = (f32[64,256]{1,0:T(8,128)S(1)}, f32[64,256]{1,0:T(8,128)S(1)}, u32[]{:S(2)}, u32[]{:S(2)}) collective-permute-start(f32[64,256]{1,0:T(8,128)S(1)} %get-tuple-element.80), channel_id=1, source_target_pairs={{0,2},{2,0},{4,6},{6,4},{1,3},{3,1},{5,7},{7,5},{8,10},{10,8},{12,... | collective-permute-start | bytes 196616 | tf_op jit(solution)/shard_map/ppermute | solution.py:841
  29.7 1.8 %collective-permute-done.8 = f32[64,256]{1,0:T(8,128)S(1)} collective-permute-done((f32[64,256]{1,0:T(8,128)S(1)}, f32[64,256]{1,0:T(8,128)S(1)}, u32[]{:S(2)}, u32[]{:S(2)}) %collective-permute-start.8) | collective-permute-done | bytes 65568 | tf_op jit(solution)/shard_map/ppermute | solution.py:841
  31.5 2.2 %collective-permute-done.9 = f32[64,256]{1,0:T(8,128)S(1)} collective-permute-done((f32[64,256]{1,0:T(8,128)S(1)}, f32[64,256]{1,0:T(8,128)S(1)}, u32[]{:S(2)}, u32[]{:S(2)}) %collective-permute-start.9) | collective-permute-done | bytes 65568 | tf_op jit(solution)/shard_map/ppermute | solution.py:841
  33.6 0.0 collective-permute-done.10
  33.6 0.6 %add_add_fusion = f32[64,256]{1,0:T(8,128)} fusion(f32[64,256]{1,0:T(8,128)S(1)} %collective-permute-done.10, f32[64,256]{1,0:T(8,128)S(1)} %collective-permute-done.9, f32[64,256]{1,0:T(8,128)S(1)} %get-tuple-element.77, f32[64,256]{1,0:T(8,128)S(1)} %collective-permute-done.8), kind=kLoop, calls=%fused_computation | loop fusion | flops 49152 | bytes 327680 | tf_op jit(solution)/shard_map/add | solution.py:841
  (1 shorter events, 0.0 us)
Async XLA Ops:
  1.4 8.2 %collective-permute-start.2 = (f32[168,128]{1,0:T(8,128)S(1)}, f32[168,128]{1,0:T(8,128)S(1)}, u32[]{:S(2)}, u32[]{:S(2)}) collective-permute-start(f32[168,128]{1,0:T(8,128)S(1)} %tables.1.refs_3_), channel_id=1, source_target_pairs={{0,14},{2,12},{4,10},{6,8},{8,6},{10,4},{12,2},{14,0},{16,30},{18,... | collective-permute-start | bytes 258056 | tf_op jit(solution)/shard_map/ppermute | solution.py:711
  6.0 9.1 %collective-permute-start.1 = (f32[168,128]{1,0:T(8,128)S(1)}, f32[168,128]{1,0:T(8,128)S(1)}, u32[]{:S(2)}, u32[]{:S(2)}) collective-permute-start(f32[168,128]{1,0:T(8,128)S(1)} %tables.1.refs_3_), channel_id=1, source_target_pairs={{0,28},{2,30},{4,24},{6,26},{8,20},{10,22},{12,16},{14,18},{16,12}... | collective-permute-start | bytes 258056 | tf_op jit(solution)/shard_map/ppermute | solution.py:711
  6.6 8.6 %collective-permute-start = (f32[168,128]{1,0:T(8,128)S(1)}, f32[168,128]{1,0:T(8,128)S(1)}, u32[]{:S(2)}, u32[]{:S(2)}) collective-permute-start(f32[168,128]{1,0:T(8,128)S(1)} %tables.1.refs_3_), channel_id=1, source_target_pairs={{0,18},{2,16},{4,22},{6,20},{8,26},{10,24},{12,30},{14,28},{16,2},... | collective-permute-start | bytes 258056 | tf_op jit(solution)/shard_map/ppermute | solution.py:711
  7.5 8.1 %copy-start = (f32[16,256]{1,0:T(8,128)S(1)}, f32[16,256]{1,0:T(8,128)}, u32[]{:S(2)}) copy-start(f32[16,256]{1,0:T(8,128)} %refs_4_.3) | copy-start | bytes 49156
  9.6 7.6 %collective-permute-start.5 = (f32[168,128]{1,0:T(8,128)S(1)}, f32[168,128]{1,0:T(8,128)S(1)}, u32[]{:S(2)}, u32[]{:S(2)}) collective-permute-start(f32[168,128]{1,0:T(8,128)S(1)} %collective-permute-done.2.refs_2_.refs_11_), channel_id=1, source_target_pairs={{0,8},{8,0},{16,24},{24,16},{1,9},{9,1},{17,25},{25,17},{2,10},{10... | collective-permute-start | bytes 258056 | tf_op jit(solution)/shard_map/ppermute | solution.py:714
  15.1 2.1 %collective-permute-start.4 = (f32[168,128]{1,0:T(8,128)S(1)}, f32[168,128]{1,0:T(8,128)S(1)}, u32[]{:S(2)}, u32[]{:S(2)}) collective-permute-start(f32[168,128]{1,0:T(8,128)S(1)} %collective-permute-done.1.refs_1_.refs_10_), channel_id=1, source_target_pairs={{0,8},{8,0},{16,24},{24,16},{1,9},{9,1},{17,25},{25,17},{2,10},{10... | collective-permute-start | bytes 258056 | tf_op jit(solution)/shard_map/ppermute | solution.py:714
  15.2 2.0 %collective-permute-start.3 = (f32[168,128]{1,0:T(8,128)S(1)}, f32[168,128]{1,0:T(8,128)S(1)}, u32[]{:S(2)}, u32[]{:S(2)}) collective-permute-start(f32[168,128]{1,0:T(8,128)S(1)} %collective-permute-done.refs_0_.refs_9_), channel_id=1, source_target_pairs={{0,8},{8,0},{16,24},{24,16},{1,9},{9,1},{17,25},{25,17},{2,10},{10... | collective-permute-start | bytes 258056 | tf_op jit(solution)/shard_map/ppermute | solution.py:714
  18.8 1.3 %collective-permute-start.6 = (f32[136,128]{1,0:T(8,128)S(1)}, f32[136,128]{1,0:T(8,128)S(1)}, u32[]{:S(2)}, u32[]{:S(2)}) collective-permute-start(f32[136,128]{1,0:T(8,128)S(1)} %get-tuple-element.56.refs_0_), channel_id=1, source_target_pairs={{0,8},{8,0},{16,24},{24,16},{1,9},{9,1},{17,25},{25,17},{2,10},{10... | collective-permute-start | bytes 208904 | tf_op jit(solution)/shard_map/ppermute | solution.py:795
  20.2 4.4 %collective-permute-start.7 = (f32[136,128]{1,0:T(8,128)S(1)}, f32[136,128]{1,0:T(8,128)S(1)}, u32[]{:S(2)}, u32[]{:S(2)}) collective-permute-start(f32[136,128]{1,0:T(8,128)S(1)} %get-tuple-element.58), channel_id=1, source_target_pairs={{0,16},{8,24},{16,0},{24,8},{1,17},{9,25},{17,1},{25,9},{2,18},{10... | collective-permute-start | bytes 208904 | tf_op jit(solution)/shard_map/ppermute | solution.py:795
  25.2 6.2 %collective-permute-start.8 = (f32[64,256]{1,0:T(8,128)S(1)}, f32[64,256]{1,0:T(8,128)S(1)}, u32[]{:S(2)}, u32[]{:S(2)}) collective-permute-start(f32[64,256]{1,0:T(8,128)S(1)} %get-tuple-element.78), channel_id=1, source_target_pairs={{0,6},{2,4},{4,2},{6,0},{1,7},{3,5},{5,3},{7,1},{8,14},{10,12},{12... | collective-permute-start | bytes 196616 | tf_op jit(solution)/shard_map/ppermute | solution.py:841
  27.9 5.7 %collective-permute-start.9 = (f32[64,256]{1,0:T(8,128)S(1)}, f32[64,256]{1,0:T(8,128)S(1)}, u32[]{:S(2)}, u32[]{:S(2)}) collective-permute-start(f32[64,256]{1,0:T(8,128)S(1)} %get-tuple-element.79), channel_id=1, source_target_pairs={{0,4},{2,6},{4,0},{6,2},{1,5},{3,7},{5,1},{7,3},{8,12},{10,14},{12... | collective-permute-start | bytes 196616 | tf_op jit(solution)/shard_map/ppermute | solution.py:841
  27.9 5.7 %collective-permute-start.10 = (f32[64,256]{1,0:T(8,128)S(1)}, f32[64,256]{1,0:T(8,128)S(1)}, u32[]{:S(2)}, u32[]{:S(2)}) collective-permute-start(f32[64,256]{1,0:T(8,128)S(1)} %get-tuple-element.80), channel_id=1, source_target_pairs={{0,2},{2,0},{4,6},{6,4},{1,3},{3,1},{5,7},{7,5},{8,10},{10,8},{12,... | collective-permute-start | bytes 196616 | tf_op jit(solution)/shard_map/ppermute | solution.py:841

commit v15 on v12

--- a/solution.py
+++ b/solution.py
@@ -17,13 +17,35 @@
 TN = (((0,), (0,)), ((), ()))
 
 
+def shifts(count):
+    found = []
+    for step in range(1, count):
+        for shift in (step, count - step):
+            if shift not in found:
+                found.append(shift)
+    return found
+
+
+def moved(place, shift, count):
+    half = count // 2
+    position = place % half * 2 + place // half
+    position = (position + shift) % count
+    return position // 2 + position % 2 * half
+
+
 def partners(ns, nh):
-    count = max(ns, nh)
-    return [((ns - k) if 0 < k < ns else 0, k if k < nh else 0) for k in range(count)]
+    bits = list(range(1, ns))
+    if ns > 2:
+        bits[:2] = [2, 1]
+    heads = shifts(nh)
+    count = max(len(bits), len(heads))
+    bits += [0] * (count - len(bits))
+    heads += [0] * (count - len(heads))
+    return [(0, 0)] + list(zip(bits, heads))
 
 
 def in_turn(count):
-    return sorted(range(1, count), key=lambda k: (-k.bit_length(), k))
+    return list(range(1, count))
 
 
 def iota(shape, axis):
@@ -556,7 +578,11 @@
     partial_ref[...] = dot_split(split2(value), (proj_high[...], proj_low[...]))
     mine = lax.axis_index("head")
     for k in range(nh):
-        place = pl.multiple_of(lax.bitwise_xor(mine, k) * share, 8)
+        shift = 0 if k == 0 else shifts(nh)[k - 1]
+        position = lax.rem(mine, nh // 2) * 2 + lax.div(mine, nh // 2)
+        position = lax.rem(position + shift, nh)
+        to = lax.div(position, 2) + lax.rem(position, 2) * (nh // 2)
+        place = pl.multiple_of(to * share, 8)
         part = partial_ref[pl.ds(place, share), :]
         outs[k][...] = part + own[...] if k == 0 else part
 
@@ -699,9 +725,9 @@
     count = max(ns, nh)
     messages = {0: message}
     for k in in_turn(count):
-        seq_bits, head_bits = partners(ns, nh)[k]
+        seq_bits, shift = partners(ns, nh)[k]
         pairs = [
-            (seq * nh + head, (seq ^ seq_bits) * nh + (head ^ head_bits))
+            (seq * nh + head, (seq ^ seq_bits) * nh + moved(head, shift, nh))
             for seq in range(ns)
             for head in range(nh)
         ]
@@ -835,7 +861,8 @@
     )
     result = parts[0]
     for k in in_turn(nh):
-        pairs = [(source, source ^ k) for source in range(nh)]
+        shift = shifts(nh)[k - 1]
+        pairs = [(source, moved(source, shift, nh)) for source in range(nh)]
         result = result + lax.ppermute(parts[k], "head", pairs)
     return result
 

time: 34 us -> 34.1 us (level)
    ppermute x2, waiting for transfers between devices: 3.32 us -> 3.73 us  [per_device(): lax.ppermute(state, 'seq', [(seq, seq ^ 2 ** bit) for seq in range(ns)])]
    ppermute x2, starting transfers between devices: 1.48 us -> 1.13 us  [per_device(): lax.ppermute(state, 'seq', [(seq, seq ^ 2 ** bit) for seq in range(ns)])]
  transfers between devices with their start and end apart: 11 -> 11, of which waited for: 7 -> 6; matrix products, arithmetic and copies ran while one was open for 0% -> 0% of each run, Pallas kernels for 14% -> 14%
where the time goes in v15:
time: 34.1 us; the launch traced here: 33.9 us
  waiting for transfers between devices  13.2 us (39%)
  starting transfers between devices  11.6 us (34%)
  Pallas kernels  8.41 us (25%)
  other arithmetic  0.65 us (2%)
    ppermute x3, starting transfers between devices, per_device(): messages[k] = lax.ppermute(sent, ('seq', 'head'), pairs)  5.73 us
    ppermute x3, waiting for transfers between devices, per_device(): result = result + lax.ppermute(parts[k], 'head', pairs)  4.85 us
    ppermute x3, waiting for transfers between devices, per_device(): messages[k] = lax.ppermute(sent, ('seq', 'head'), pairs)  4.59 us
    ppermute x3, starting transfers between devices, per_device(): result = result + lax.ppermute(parts[k], 'head', pairs)  4.06 us
    ppermute x2, waiting for transfers between devices, per_device(): lax.ppermute(state, 'seq', [(seq, seq ^ 2 ** bit) for seq in range(ns)])  3.73 us
    pallas_call x1, Pallas kernels, per_device(): pl.pallas_call(functools.partial(prepare_kernel, dims), out_shape=(shape(...  2.08 us
    pallas_call x1, Pallas kernels, per_device(): pl.pallas_call(functools.partial(mix_kernel, dims), out_shape=(*halves(T,...  1.6 us
    pallas_call x1, Pallas kernels, per_device(): pl.pallas_call(functools.partial(project_kernel, dims), out_shape=(shape(...  1.51 us
  transfers between devices with their start and end apart: 11, of which 6 were waited for; matrix products, arithmetic and copies ran while one was open for 0% of the time, Pallas kernels for 14%

profile of v15, /device:TPU:0, one launch (start us, length us, event | category | flops | bytes accessed | tf_op | source)
XLA Modules:
  0.0 33.9 jit_solution(15409442110629886187)
XLA Ops:
  0.0 1.4 %tables.1.refs_3_ = f32[168,128]{1,0:T(8,128)S(1)} custom-call(f32[512,128]{1,0:T(8,128)} %bitcast.18, s32[1,256]{1,0:T(1,128)} %bitcast.20, f32[16,256]{1,0:T(8,128)} %refs_4_.3, f32[1,256]{1,0:T(1,128)} %bitcast.21, f32[2,256]{1,0:T(2,128)} %bitcast.19, f32[1,2]{1,0:T(1,128)} %bitcast.23, f32[1,2]{1,0:T(1,128)} %bitcast.24, f32[1,2]{1,0:T(1,128)} %bitcast.25, ...), custom_call_target="tpu_custom_call" | custom-call | tf_op jit(solution)/shard_map/tables/pallas_call | solution.py:658
  1.4 5.0 %collective-permute-start.2 = (f32[168,128]{1,0:T(8,128)S(1)}, f32[168,128]{1,0:T(8,128)S(1)}, u32[]{:S(2)}, u32[]{:S(2)}) collective-permute-start(f32[168,128]{1,0:T(8,128)S(1)} %tables.1.refs_3_), channel_id=1, source_target_pairs={{0,20},{2,22},{4,18},{6,16},{8,28},{10,30},{12,26},{14,24},{16,4},... | collective-permute-start | bytes 258056 | tf_op jit(solution)/shard_map/ppermute | solution.py:735
  6.5 0.4 %collective-permute-start.1 = (f32[168,128]{1,0:T(8,128)S(1)}, f32[168,128]{1,0:T(8,128)S(1)}, u32[]{:S(2)}, u32[]{:S(2)}) collective-permute-start(f32[168,128]{1,0:T(8,128)S(1)} %tables.1.refs_3_), channel_id=1, source_target_pairs={{0,14},{2,12},{4,8},{6,10},{8,6},{10,4},{12,0},{14,2},{16,30},{18,... | collective-permute-start | bytes 258056 | tf_op jit(solution)/shard_map/ppermute | solution.py:735
  6.9 0.3 collective-permute-start
  7.2 0.0 copy-start
  7.2 2.1 %prepare.1 = (f32[16,128]{1,0:T(8,128)S(1)}, f32[8,128]{1,0:T(8,128)S(1)}, bf16[256,256]{1,0:T(8,128)(2,1)S(1)}, bf16[128,256]{1,0:T(8,128)(2,1)S(1)}, bf16[128,...) custom-call(f32[512,128]{1,0:T(8,128)} %bitcast.27, ...), custom_call_target="tpu_custom_call" | custom-call | flops 16106127360 | bytes 262144 | tf_op jit(solution)/shard_map/prepare/pallas_call | solution.py:701
  9.3 0.8 %collective-permute-done.2.refs_2_.refs_11_ = f32[168,128]{1,0:T(8,128)S(1)} collective-permute-done((f32[168,128]{1,0:T(8,128)S(1)}, f32[168,128]{1,0:T(8,128)S(1)}, u32[]{:S(2)}, u32[]{:S(2)}) %collective-permute-start.2) | collective-permute-done | bytes 86048 | tf_op jit(solution)/shard_map/ppermute | solution.py:735
  10.1 0.2 collective-permute-start.5
  10.3 3.7 %collective-permute-done.1.refs_1_.refs_10_ = f32[168,128]{1,0:T(8,128)S(1)} collective-permute-done((f32[168,128]{1,0:T(8,128)S(1)}, f32[168,128]{1,0:T(8,128)S(1)}, u32[]{:S(2)}, u32[]{:S(2)}) %collective-permute-start.1) | collective-permute-done | bytes 86048 | tf_op jit(solution)/shard_map/ppermute | solution.py:735
  14.0 0.5 %collective-permute-start.4 = (f32[168,128]{1,0:T(8,128)S(1)}, f32[168,128]{1,0:T(8,128)S(1)}, u32[]{:S(2)}, u32[]{:S(2)}) collective-permute-start(f32[168,128]{1,0:T(8,128)S(1)} %collective-permute-done.1.refs_1_.refs_10_), channel_id=1, source_target_pairs={{0,8},{8,0},{16,24},{24,16},{1,9},{9,1},{17,25},{25,17},{2,10},{10... | collective-permute-start | bytes 258056 | tf_op jit(solution)/shard_map/ppermute | solution.py:738
  14.5 0.0 collective-permute-done.refs_0_.refs_9_
  14.5 0.0 collective-permute-start.3
  14.5 0.0 copy-done
  14.5 1.6 %mix.1 = (bf16[256,512]{1,0:T(8,128)(2,1)S(1)}, bf16[256,512]{1,0:T(8,128)(2,1)S(1)}, f32[256,256]{1,0:T(8,128)S(1)}) custom-call(f32[168,128]{1,0:T(8,128)S(1)} %collective-permute-done.refs_0_.refs_9_, f32[168,128]{1,0:T(8,128)S(1)} %collective-permute-done.1.refs_1_.refs_10_, f32[168,128]{1,0:T(8,128)S(1)} %collective-permute-done.2.refs_2_.refs_11_, ...), custom_call_target="tpu_custom_call" | custom-call | flops 16106127360 | bytes 262144 | tf_op jit(solution)/shard_map/mix/pallas_call | solution.py:740
  16.2 0.0 collective-permute-done.5.refs_14_
  16.2 0.0 collective-permute-done.4.refs_13_
  16.2 0.0 collective-permute-done.3.refs_12_
  16.2 1.5 %project.1 = (f32[136,128]{1,0:T(8,128)S(1)}, bf16[256,256]{1,0:T(8,128)(2,1)S(1)}, bf16[256,256]{1,0:T(8,128)(2,1)S(1)}, f32[256,128]{1,0:T(8,128)S(1)}, f32[25...) custom-call(bf16[256,512]{1,0:T(8,128)(2,1)S(1)} %get-tuple-element.47.refs_0_, ...), custom_call_target="tpu_custom_call" | custom-call | tf_op jit(solution)/shard_map/project/pallas_call | solution.py:758
  17.7 0.5 %collective-permute-start.6 = (f32[136,128]{1,0:T(8,128)S(1)}, f32[136,128]{1,0:T(8,128)S(1)}, u32[]{:S(2)}, u32[]{:S(2)}) collective-permute-start(f32[136,128]{1,0:T(8,128)S(1)} %get-tuple-element.56.refs_0_), channel_id=1, source_target_pairs={{0,8},{8,0},{16,24},{24,16},{1,9},{9,1},{17,25},{25,17},{2,10},{10... | collective-permute-start | bytes 208904 | tf_op jit(solution)/shard_map/ppermute | solution.py:819
  18.2 0.9 %collective-permute-done.6.refs_1_ = f32[136,128]{1,0:T(8,128)S(1)} collective-permute-done((f32[136,128]{1,0:T(8,128)S(1)}, f32[136,128]{1,0:T(8,128)S(1)}, u32[]{:S(2)}, u32[]{:S(2)}) %collective-permute-start.6) | collective-permute-done | bytes 69664 | tf_op jit(solution)/shard_map/ppermute | solution.py:819
  19.2 0.6 %collective-permute-start.7 = (f32[136,128]{1,0:T(8,128)S(1)}, f32[136,128]{1,0:T(8,128)S(1)}, u32[]{:S(2)}, u32[]{:S(2)}) collective-permute-start(f32[136,128]{1,0:T(8,128)S(1)} %get-tuple-element.58), channel_id=1, source_target_pairs={{0,16},{8,24},{16,0},{24,8},{1,17},{9,25},{17,1},{25,9},{2,18},{10... | collective-permute-start | bytes 208904 | tf_op jit(solution)/shard_map/ppermute | solution.py:819
  19.8 1.1 %block.1 = (f32[256,128]{1,0:T(8,128)S(1)}, bf16[256,128]{1,0:T(8,128)(2,1)S(1)}, bf16[256,128]{1,0:T(8,128)(2,1)S(1)}, f32[256,128]{1,0:T(8,128)S(1)}, f32[256,128]{1,0:T(8,128)S(1)}, /*index=5*/f32[64,256]{1,0:T(8,128)S(1)}) custom-call(bf16[256,256]{1,0:T(8,128)(2,1)S(1)} %get-tuple-element.59.refs_0_, bf16[256,256]{1,0:T(8,128)(2,1)S(1)} %get-tuple-element.60.refs_1_, ...), custom_call_target="tpu_custom_call" | custom-call | flops 16106127360 | bytes 262144 | tf_op jit(solution)/shard_map/block/pallas_call | solution.py:787
  20.9 2.8 %collective-permute-done.7.refs_1_ = f32[136,128]{1,0:T(8,128)S(1)} collective-permute-done((f32[136,128]{1,0:T(8,128)S(1)}, f32[136,128]{1,0:T(8,128)S(1)}, u32[]{:S(2)}, u32[]{:S(2)}) %collective-permute-start.7) | collective-permute-done | bytes 69664 | tf_op jit(solution)/shard_map/ppermute | solution.py:819
  23.7 0.7 %output.1 = (f32[64,256]{1,0:T(8,128)S(1)}, f32[64,256]{1,0:T(8,128)S(1)}, f32[64,256]{1,0:T(8,128)S(1)}, f32[64,256]{1,0:T(8,128)S(1)}) custom-call(f32[136,128]{1,0:T(8,128)S(1)} %get-tuple-element.57.refs_0_, f32[136,128]{1,0:T(8,128)S(1)} %collective-permute-done.7.refs_1_, bf16[256,128]{1,0:T(8,128)(2,1)S(1)} %get-tuple-element.69.refs_2_, ...), custom_call_target="tpu_custom_call" | custom-call | tf_op jit(solution)/shard_map/output/pallas_call | solution.py:841
  24.4 2.7 %collective-permute-start.8 = (f32[64,256]{1,0:T(8,128)S(1)}, f32[64,256]{1,0:T(8,128)S(1)}, u32[]{:S(2)}, u32[]{:S(2)}) collective-permute-start(f32[64,256]{1,0:T(8,128)S(1)} %get-tuple-element.78), channel_id=1, source_target_pairs={{0,4},{2,6},{4,2},{6,0},{1,5},{3,7},{5,3},{7,1},{8,12},{10,14},{12... | collective-permute-start | bytes 196616 | tf_op jit(solution)/shard_map/ppermute | solution.py:866
  27.1 1.2 %collective-permute-start.9 = (f32[64,256]{1,0:T(8,128)S(1)}, f32[64,256]{1,0:T(8,128)S(1)}, u32[]{:S(2)}, u32[]{:S(2)}) collective-permute-start(f32[64,256]{1,0:T(8,128)S(1)} %get-tuple-element.79), channel_id=1, source_target_pairs={{0,6},{2,4},{4,0},{6,2},{1,7},{3,5},{5,1},{7,3},{8,14},{10,12},{12... | collective-permute-start | bytes 196616 | tf_op jit(solution)/shard_map/ppermute | solution.py:866
  28.2 0.2 collective-permute-start.10
  28.4 2.3 %collective-permute-done.8 = f32[64,256]{1,0:T(8,128)S(1)} collective-permute-done((f32[64,256]{1,0:T(8,128)S(1)}, f32[64,256]{1,0:T(8,128)S(1)}, u32[]{:S(2)}, u32[]{:S(2)}) %collective-permute-start.8) | collective-permute-done | bytes 65568 | tf_op jit(solution)/shard_map/ppermute | solution.py:866
  30.7 2.6 %collective-permute-done.9 = f32[64,256]{1,0:T(8,128)S(1)} collective-permute-done((f32[64,256]{1,0:T(8,128)S(1)}, f32[64,256]{1,0:T(8,128)S(1)}, u32[]{:S(2)}, u32[]{:S(2)}) %collective-permute-start.9) | collective-permute-done | bytes 65568 | tf_op jit(solution)/shard_map/ppermute | solution.py:866
  33.3 0.0 collective-permute-done.10
  33.3 0.6 %add_add_fusion = f32[64,256]{1,0:T(8,128)} fusion(f32[64,256]{1,0:T(8,128)S(1)} %collective-permute-done.10, f32[64,256]{1,0:T(8,128)S(1)} %collective-permute-done.9, f32[64,256]{1,0:T(8,128)S(1)} %get-tuple-element.77, f32[64,256]{1,0:T(8,128)S(1)} %collective-permute-done.8), kind=kLoop, calls=%fused_computation | loop fusion | flops 49152 | bytes 327680 | tf_op jit(solution)/shard_map/add | solution.py:866
  (1 shorter events, 0.0 us)
Async XLA Ops:
  1.4 8.7 %collective-permute-start.2 = (f32[168,128]{1,0:T(8,128)S(1)}, f32[168,128]{1,0:T(8,128)S(1)}, u32[]{:S(2)}, u32[]{:S(2)}) collective-permute-start(f32[168,128]{1,0:T(8,128)S(1)} %tables.1.refs_3_), channel_id=1, source_target_pairs={{0,20},{2,22},{4,18},{6,16},{8,28},{10,30},{12,26},{14,24},{16,4},... | collective-permute-start | bytes 258056 | tf_op jit(solution)/shard_map/ppermute | solution.py:735
  6.5 7.6 %collective-permute-start.1 = (f32[168,128]{1,0:T(8,128)S(1)}, f32[168,128]{1,0:T(8,128)S(1)}, u32[]{:S(2)}, u32[]{:S(2)}) collective-permute-start(f32[168,128]{1,0:T(8,128)S(1)} %tables.1.refs_3_), channel_id=1, source_target_pairs={{0,14},{2,12},{4,8},{6,10},{8,6},{10,4},{12,0},{14,2},{16,30},{18,... | collective-permute-start | bytes 258056 | tf_op jit(solution)/shard_map/ppermute | solution.py:735
  6.9 7.7 %collective-permute-start = (f32[168,128]{1,0:T(8,128)S(1)}, f32[168,128]{1,0:T(8,128)S(1)}, u32[]{:S(2)}, u32[]{:S(2)}) collective-permute-start(f32[168,128]{1,0:T(8,128)S(1)} %tables.1.refs_3_), channel_id=1, source_target_pairs={{0,26},{2,24},{4,30},{6,28},{8,18},{10,16},{12,22},{14,20},{16,10}... | collective-permute-start | bytes 258056 | tf_op jit(solution)/shard_map/ppermute | solution.py:735
  7.2 7.4 %copy-start = (f32[16,256]{1,0:T(8,128)S(1)}, f32[16,256]{1,0:T(8,128)}, u32[]{:S(2)}) copy-start(f32[16,256]{1,0:T(8,128)} %refs_4_.3) | copy-start | bytes 49156
  10.1 6.1 %collective-permute-start.5 = (f32[168,128]{1,0:T(8,128)S(1)}, f32[168,128]{1,0:T(8,128)S(1)}, u32[]{:S(2)}, u32[]{:S(2)}) collective-permute-start(f32[168,128]{1,0:T(8,128)S(1)} %collective-permute-done.2.refs_2_.refs_11_), channel_id=1, source_target_pairs={{0,8},{8,0},{16,24},{24,16},{1,9},{9,1},{17,25},{25,17},{2,10},{10... | collective-permute-start | bytes 258056 | tf_op jit(solution)/shard_map/ppermute | solution.py:738
  14.0 2.1 %collective-permute-start.4 = (f32[168,128]{1,0:T(8,128)S(1)}, f32[168,128]{1,0:T(8,128)S(1)}, u32[]{:S(2)}, u32[]{:S(2)}) collective-permute-start(f32[168,128]{1,0:T(8,128)S(1)} %collective-permute-done.1.refs_1_.refs_10_), channel_id=1, source_target_pairs={{0,8},{8,0},{16,24},{24,16},{1,9},{9,1},{17,25},{25,17},{2,10},{10... | collective-permute-start | bytes 258056 | tf_op jit(solution)/shard_map/ppermute | solution.py:738
  14.5 1.7 %collective-permute-start.3 = (f32[168,128]{1,0:T(8,128)S(1)}, f32[168,128]{1,0:T(8,128)S(1)}, u32[]{:S(2)}, u32[]{:S(2)}) collective-permute-start(f32[168,128]{1,0:T(8,128)S(1)} %collective-permute-done.refs_0_.refs_9_), channel_id=1, source_target_pairs={{0,8},{8,0},{16,24},{24,16},{1,9},{9,1},{17,25},{25,17},{2,10},{10... | collective-permute-start | bytes 258056 | tf_op jit(solution)/shard_map/ppermute | solution.py:738
  17.7 1.4 %collective-permute-start.6 = (f32[136,128]{1,0:T(8,128)S(1)}, f32[136,128]{1,0:T(8,128)S(1)}, u32[]{:S(2)}, u32[]{:S(2)}) collective-permute-start(f32[136,128]{1,0:T(8,128)S(1)} %get-tuple-element.56.refs_0_), channel_id=1, source_target_pairs={{0,8},{8,0},{16,24},{24,16},{1,9},{9,1},{17,25},{25,17},{2,10},{10... | collective-permute-start | bytes 208904 | tf_op jit(solution)/shard_map/ppermute | solution.py:819
  19.2 4.5 %collective-permute-start.7 = (f32[136,128]{1,0:T(8,128)S(1)}, f32[136,128]{1,0:T(8,128)S(1)}, u32[]{:S(2)}, u32[]{:S(2)}) collective-permute-start(f32[136,128]{1,0:T(8,128)S(1)} %get-tuple-element.58), channel_id=1, source_target_pairs={{0,16},{8,24},{16,0},{24,8},{1,17},{9,25},{17,1},{25,9},{2,18},{10... | collective-permute-start | bytes 208904 | tf_op jit(solution)/shard_map/ppermute | solution.py:819
  24.4 6.3 %collective-permute-start.8 = (f32[64,256]{1,0:T(8,128)S(1)}, f32[64,256]{1,0:T(8,128)S(1)}, u32[]{:S(2)}, u32[]{:S(2)}) collective-permute-start(f32[64,256]{1,0:T(8,128)S(1)} %get-tuple-element.78), channel_id=1, source_target_pairs={{0,4},{2,6},{4,2},{6,0},{1,5},{3,7},{5,3},{7,1},{8,12},{10,14},{12... | collective-permute-start | bytes 196616 | tf_op jit(solution)/shard_map/ppermute | solution.py:866
  27.1 6.2 %collective-permute-start.9 = (f32[64,256]{1,0:T(8,128)S(1)}, f32[64,256]{1,0:T(8,128)S(1)}, u32[]{:S(2)}, u32[]{:S(2)}) collective-permute-start(f32[64,256]{1,0:T(8,128)S(1)} %get-tuple-element.79), channel_id=1, source_target_pairs={{0,6},{2,4},{4,0},{6,2},{1,7},{3,5},{5,1},{7,3},{8,14},{10,12},{12... | collective-permute-start | bytes 196616 | tf_op jit(solution)/shard_map/ppermute | solution.py:866
  28.2 5.0 %collective-permute-start.10 = (f32[64,256]{1,0:T(8,128)S(1)}, f32[64,256]{1,0:T(8,128)S(1)}, u32[]{:S(2)}, u32[]{:S(2)}) collective-permute-start(f32[64,256]{1,0:T(8,128)S(1)} %get-tuple-element.80), channel_id=1, source_target_pairs={{0,2},{2,0},{4,6},{6,4},{1,3},{3,1},{5,7},{7,5},{8,10},{10,8},{12,... | collective-permute-start | bytes 196616 | tf_op jit(solution)/shard_map/ppermute | solution.py:866

commit v16 on v15

--- a/solution.py
+++ b/solution.py
@@ -816,7 +816,10 @@
     prefix = None
     bits = ns.bit_length() - 1
     for bit in range(bits):
-        came = lax.ppermute(state, "seq", [(seq, seq ^ 2**bit) for seq in range(ns)])
+        pairs = [
+            (seq, seq ^ 2**bit) for seq in range(ns) if bit < bits - 1 or not seq & 2**bit
+        ]
+        came = lax.ppermute(state, "seq", pairs)
         if bit == bits - 1:
             break
         given = [state] + ([] if prefix is None else [prefix]) + [came]

time: 34.1 us -> 34.3 us (level)
  starting transfers between devices: 11.6 us -> 14 us
  waiting for transfers between devices: 13.2 us -> 11 us
    ppermute x2, waiting for transfers between devices: 3.73 us -> 1.75 us  [per_device(): came = lax.ppermute(state, 'seq', pairs)]
    ppermute x2, starting transfers between devices: 1.13 us -> 2.97 us  [per_device(): came = lax.ppermute(state, 'seq', pairs)]
    ppermute x3, starting transfers between devices: 4.06 us -> 4.58 us  [per_device(): result = result + lax.ppermute(parts[k], 'head', pairs)]
  transfers between devices with their start and end apart: 11 -> 11, of which waited for: 6 -> 7; matrix products, arithmetic and copies ran while one was open for 0% -> 0% of each run, Pallas kernels for 14% -> 14%
where the time goes in v16:
time: 34.3 us; the launch traced here: 34.2 us
  starting transfers between devices  14 us (41%)
  waiting for transfers between devices  11 us (32%)
  Pallas kernels  8.42 us (25%)
  other arithmetic  0.65 us (2%)
    ppermute x3, starting transfers between devices, per_device(): messages[k] = lax.ppermute(sent, ('seq', 'head'), pairs)  5.73 us
    ppermute x3, waiting for transfers between devices, per_device(): result = result + lax.ppermute(parts[k], 'head', pairs)  4.68 us
    ppermute x3, waiting for transfers between devices, per_device(): messages[k] = lax.ppermute(sent, ('seq', 'head'), pairs)  4.59 us
    ppermute x3, starting transfers between devices, per_device(): result = result + lax.ppermute(parts[k], 'head', pairs)  4.58 us
    ppermute x2, starting transfers between devices, per_device(): came = lax.ppermute(state, 'seq', pairs)  2.97 us
    pallas_call x1, Pallas kernels, per_device(): pl.pallas_call(functools.partial(prepare_kernel, dims), out_shape=(shape(...  2.08 us
    ppermute x2, waiting for transfers between devices, per_device(): came = lax.ppermute(state, 'seq', pairs)  1.75 us
    pallas_call x1, Pallas kernels, per_device(): pl.pallas_call(functools.partial(mix_kernel, dims), out_shape=(*halves(T,...  1.6 us
  transfers between devices with their start and end apart: 11, of which 7 were waited for; matrix products, arithmetic and copies ran while one was open for 0% of the time, Pallas kernels for 14%

profile of v16, /device:TPU:0, one launch (start us, length us, event | category | flops | bytes accessed | tf_op | source)
XLA Modules:
  0.0 34.2 jit_solution(8023389343262688437)
XLA Ops:
  0.0 1.4 %tables.1.refs_3_ = f32[168,128]{1,0:T(8,128)S(1)} custom-call(f32[512,128]{1,0:T(8,128)} %bitcast.18, s32[1,256]{1,0:T(1,128)} %bitcast.20, f32[16,256]{1,0:T(8,128)} %refs_4_.3, f32[1,256]{1,0:T(1,128)} %bitcast.21, f32[2,256]{1,0:T(2,128)} %bitcast.19, f32[1,2]{1,0:T(1,128)} %bitcast.23, f32[1,2]{1,0:T(1,128)} %bitcast.24, f32[1,2]{1,0:T(1,128)} %bitcast.25, ...), custom_call_target="tpu_custom_call" | custom-call | tf_op jit(solution)/shard_map/tables/pallas_call | solution.py:658
  1.4 5.0 %collective-permute-start.2 = (f32[168,128]{1,0:T(8,128)S(1)}, f32[168,128]{1,0:T(8,128)S(1)}, u32[]{:S(2)}, u32[]{:S(2)}) collective-permute-start(f32[168,128]{1,0:T(8,128)S(1)} %tables.1.refs_3_), channel_id=1, source_target_pairs={{0,20},{2,22},{4,18},{6,16},{8,28},{10,30},{12,26},{14,24},{16,4},... | collective-permute-start | bytes 258056 | tf_op jit(solution)/shard_map/ppermute | solution.py:735
  6.5 0.4 %collective-permute-start.1 = (f32[168,128]{1,0:T(8,128)S(1)}, f32[168,128]{1,0:T(8,128)S(1)}, u32[]{:S(2)}, u32[]{:S(2)}) collective-permute-start(f32[168,128]{1,0:T(8,128)S(1)} %tables.1.refs_3_), channel_id=1, source_target_pairs={{0,14},{2,12},{4,8},{6,10},{8,6},{10,4},{12,0},{14,2},{16,30},{18,... | collective-permute-start | bytes 258056 | tf_op jit(solution)/shard_map/ppermute | solution.py:735
  6.9 0.3 collective-permute-start
  7.2 0.0 copy-start
  7.2 2.1 %prepare.1 = (f32[16,128]{1,0:T(8,128)S(1)}, f32[8,128]{1,0:T(8,128)S(1)}, bf16[256,256]{1,0:T(8,128)(2,1)S(1)}, bf16[128,256]{1,0:T(8,128)(2,1)S(1)}, bf16[128,...) custom-call(f32[512,128]{1,0:T(8,128)} %bitcast.27, ...), custom_call_target="tpu_custom_call" | custom-call | flops 16106127360 | bytes 262144 | tf_op jit(solution)/shard_map/prepare/pallas_call | solution.py:701
  9.3 0.8 %collective-permute-done.2.refs_2_.refs_11_ = f32[168,128]{1,0:T(8,128)S(1)} collective-permute-done((f32[168,128]{1,0:T(8,128)S(1)}, f32[168,128]{1,0:T(8,128)S(1)}, u32[]{:S(2)}, u32[]{:S(2)}) %collective-permute-start.2) | collective-permute-done | bytes 86048 | tf_op jit(solution)/shard_map/ppermute | solution.py:735
  10.1 0.2 collective-permute-start.5
  10.3 3.7 %collective-permute-done.1.refs_1_.refs_10_ = f32[168,128]{1,0:T(8,128)S(1)} collective-permute-done((f32[168,128]{1,0:T(8,128)S(1)}, f32[168,128]{1,0:T(8,128)S(1)}, u32[]{:S(2)}, u32[]{:S(2)}) %collective-permute-start.1) | collective-permute-done | bytes 86048 | tf_op jit(solution)/shard_map/ppermute | solution.py:735
  14.0 0.5 %collective-permute-start.4 = (f32[168,128]{1,0:T(8,128)S(1)}, f32[168,128]{1,0:T(8,128)S(1)}, u32[]{:S(2)}, u32[]{:S(2)}) collective-permute-start(f32[168,128]{1,0:T(8,128)S(1)} %collective-permute-done.1.refs_1_.refs_10_), channel_id=1, source_target_pairs={{0,8},{8,0},{16,24},{24,16},{1,9},{9,1},{17,25},{25,17},{2,10},{10... | collective-permute-start | bytes 258056 | tf_op jit(solution)/shard_map/ppermute | solution.py:738
  14.5 0.0 collective-permute-done.refs_0_.refs_9_
  14.5 0.0 collective-permute-start.3
  14.5 0.0 copy-done
  14.5 1.6 %mix.1 = (bf16[256,512]{1,0:T(8,128)(2,1)S(1)}, bf16[256,512]{1,0:T(8,128)(2,1)S(1)}, f32[256,256]{1,0:T(8,128)S(1)}) custom-call(f32[168,128]{1,0:T(8,128)S(1)} %collective-permute-done.refs_0_.refs_9_, f32[168,128]{1,0:T(8,128)S(1)} %collective-permute-done.1.refs_1_.refs_10_, f32[168,128]{1,0:T(8,128)S(1)} %collective-permute-done.2.refs_2_.refs_11_, ...), custom_call_target="tpu_custom_call" | custom-call | flops 16106127360 | bytes 262144 | tf_op jit(solution)/shard_map/mix/pallas_call | solution.py:740
  16.2 0.0 collective-permute-done.5.refs_14_
  16.2 0.0 collective-permute-done.4.refs_13_
  16.2 0.0 collective-permute-done.3.refs_12_
  16.2 1.5 %project.1 = (f32[136,128]{1,0:T(8,128)S(1)}, bf16[256,256]{1,0:T(8,128)(2,1)S(1)}, bf16[256,256]{1,0:T(8,128)(2,1)S(1)}, f32[256,128]{1,0:T(8,128)S(1)}, f32[25...) custom-call(bf16[256,512]{1,0:T(8,128)(2,1)S(1)} %get-tuple-element.47.refs_0_, ...), custom_call_target="tpu_custom_call" | custom-call | tf_op jit(solution)/shard_map/project/pallas_call | solution.py:758
  17.7 0.5 %collective-permute-start.6 = (f32[136,128]{1,0:T(8,128)S(1)}, f32[136,128]{1,0:T(8,128)S(1)}, u32[]{:S(2)}, u32[]{:S(2)}) collective-permute-start(f32[136,128]{1,0:T(8,128)S(1)} %get-tuple-element.56.refs_0_), channel_id=1, source_target_pairs={{0,8},{8,0},{16,24},{24,16},{1,9},{9,1},{17,25},{25,17},{2,10},{10... | collective-permute-start | bytes 208904 | tf_op jit(solution)/shard_map/ppermute | solution.py:822
  18.2 0.9 %collective-permute-done.6.refs_1_ = f32[136,128]{1,0:T(8,128)S(1)} collective-permute-done((f32[136,128]{1,0:T(8,128)S(1)}, f32[136,128]{1,0:T(8,128)S(1)}, u32[]{:S(2)}, u32[]{:S(2)}) %collective-permute-start.6) | collective-permute-done | bytes 69664 | tf_op jit(solution)/shard_map/ppermute | solution.py:822
  19.2 2.4 %collective-permute-start.7 = (f32[136,128]{1,0:T(8,128)S(1)}, f32[136,128]{1,0:T(8,128)S(1)}, u32[]{:S(2)}, u32[]{:S(2)}) collective-permute-start(f32[136,128]{1,0:T(8,128)S(1)} %get-tuple-element.58), channel_id=1, source_target_pairs={{0,16},{8,24},{1,17},{9,25},{2,18},{10,26},{3,19},{11,27},{4,20},{... | collective-permute-start | bytes 208904 | tf_op jit(solution)/shard_map/ppermute | solution.py:822
  21.6 1.1 %block.1 = (f32[256,128]{1,0:T(8,128)S(1)}, bf16[256,128]{1,0:T(8,128)(2,1)S(1)}, bf16[256,128]{1,0:T(8,128)(2,1)S(1)}, f32[256,128]{1,0:T(8,128)S(1)}, f32[256,128]{1,0:T(8,128)S(1)}, /*index=5*/f32[64,256]{1,0:T(8,128)S(1)}) custom-call(bf16[256,256]{1,0:T(8,128)(2,1)S(1)} %get-tuple-element.59.refs_0_, bf16[256,256]{1,0:T(8,128)(2,1)S(1)} %get-tuple-element.60.refs_1_, ...), custom_call_target="tpu_custom_call" | custom-call | flops 16106127360 | bytes 262144 | tf_op jit(solution)/shard_map/block/pallas_call | solution.py:787
  22.7 0.8 %collective-permute-done.7.refs_1_ = f32[136,128]{1,0:T(8,128)S(1)} collective-permute-done((f32[136,128]{1,0:T(8,128)S(1)}, f32[136,128]{1,0:T(8,128)S(1)}, u32[]{:S(2)}, u32[]{:S(2)}) %collective-permute-start.7) | collective-permute-done | bytes 69664 | tf_op jit(solution)/shard_map/ppermute | solution.py:822
  23.6 0.7 %output.1 = (f32[64,256]{1,0:T(8,128)S(1)}, f32[64,256]{1,0:T(8,128)S(1)}, f32[64,256]{1,0:T(8,128)S(1)}, f32[64,256]{1,0:T(8,128)S(1)}) custom-call(f32[136,128]{1,0:T(8,128)S(1)} %get-tuple-element.57.refs_0_, f32[136,128]{1,0:T(8,128)S(1)} %collective-permute-done.7.refs_1_, bf16[256,128]{1,0:T(8,128)(2,1)S(1)} %get-tuple-element.69.refs_2_, ...), custom_call_target="tpu_custom_call" | custom-call | tf_op jit(solution)/shard_map/output/pallas_call | solution.py:844
  24.3 2.9 %collective-permute-start.8 = (f32[64,256]{1,0:T(8,128)S(1)}, f32[64,256]{1,0:T(8,128)S(1)}, u32[]{:S(2)}, u32[]{:S(2)}) collective-permute-start(f32[64,256]{1,0:T(8,128)S(1)} %get-tuple-element.78), channel_id=1, source_target_pairs={{0,4},{2,6},{4,2},{6,0},{1,5},{3,7},{5,3},{7,1},{8,12},{10,14},{12... | collective-permute-start | bytes 196616 | tf_op jit(solution)/shard_map/ppermute | solution.py:869
  27.1 1.2 %collective-permute-start.9 = (f32[64,256]{1,0:T(8,128)S(1)}, f32[64,256]{1,0:T(8,128)S(1)}, u32[]{:S(2)}, u32[]{:S(2)}) collective-permute-start(f32[64,256]{1,0:T(8,128)S(1)} %get-tuple-element.79), channel_id=1, source_target_pairs={{0,6},{2,4},{4,0},{6,2},{1,7},{3,5},{5,1},{7,3},{8,14},{10,12},{12... | collective-permute-start | bytes 196616 | tf_op jit(solution)/shard_map/ppermute | solution.py:869
  28.3 0.5 %collective-permute-start.10 = (f32[64,256]{1,0:T(8,128)S(1)}, f32[64,256]{1,0:T(8,128)S(1)}, u32[]{:S(2)}, u32[]{:S(2)}) collective-permute-start(f32[64,256]{1,0:T(8,128)S(1)} %get-tuple-element.80), channel_id=1, source_target_pairs={{0,2},{2,0},{4,6},{6,4},{1,3},{3,1},{5,7},{7,5},{8,10},{10,8},{12,... | collective-permute-start | bytes 196616 | tf_op jit(solution)/shard_map/ppermute | solution.py:869
  28.8 1.7 %collective-permute-done.8 = f32[64,256]{1,0:T(8,128)S(1)} collective-permute-done((f32[64,256]{1,0:T(8,128)S(1)}, f32[64,256]{1,0:T(8,128)S(1)}, u32[]{:S(2)}, u32[]{:S(2)}) %collective-permute-start.8) | collective-permute-done | bytes 65568 | tf_op jit(solution)/shard_map/ppermute | solution.py:869
  30.5 2.4 %collective-permute-done.9 = f32[64,256]{1,0:T(8,128)S(1)} collective-permute-done((f32[64,256]{1,0:T(8,128)S(1)}, f32[64,256]{1,0:T(8,128)S(1)}, u32[]{:S(2)}, u32[]{:S(2)}) %collective-permute-start.9) | collective-permute-done | bytes 65568 | tf_op jit(solution)/shard_map/ppermute | solution.py:869
  32.9 0.6 %collective-permute-done.10 = f32[64,256]{1,0:T(8,128)S(1)} collective-permute-done((f32[64,256]{1,0:T(8,128)S(1)}, f32[64,256]{1,0:T(8,128)S(1)}, u32[]{:S(2)}, u32[]{:S(2)}) %collective-permute-start.10) | collective-permute-done | bytes 65568 | tf_op jit(solution)/shard_map/ppermute | solution.py:869
  33.5 0.6 %add_add_fusion = f32[64,256]{1,0:T(8,128)} fusion(f32[64,256]{1,0:T(8,128)S(1)} %collective-permute-done.10, f32[64,256]{1,0:T(8,128)S(1)} %collective-permute-done.9, f32[64,256]{1,0:T(8,128)S(1)} %get-tuple-element.77, f32[64,256]{1,0:T(8,128)S(1)} %collective-permute-done.8), kind=kLoop, calls=%fused_computation | loop fusion | flops 49152 | bytes 327680 | tf_op jit(solution)/shard_map/add | solution.py:869
  (1 shorter events, 0.0 us)
Async XLA Ops:
  1.4 8.7 %collective-permute-start.2 = (f32[168,128]{1,0:T(8,128)S(1)}, f32[168,128]{1,0:T(8,128)S(1)}, u32[]{:S(2)}, u32[]{:S(2)}) collective-permute-start(f32[168,128]{1,0:T(8,128)S(1)} %tables.1.refs_3_), channel_id=1, source_target_pairs={{0,20},{2,22},{4,18},{6,16},{8,28},{10,30},{12,26},{14,24},{16,4},... | collective-permute-start | bytes 258056 | tf_op jit(solution)/shard_map/ppermute | solution.py:735
  6.5 7.6 %collective-permute-start.1 = (f32[168,128]{1,0:T(8,128)S(1)}, f32[168,128]{1,0:T(8,128)S(1)}, u32[]{:S(2)}, u32[]{:S(2)}) collective-permute-start(f32[168,128]{1,0:T(8,128)S(1)} %tables.1.refs_3_), channel_id=1, source_target_pairs={{0,14},{2,12},{4,8},{6,10},{8,6},{10,4},{12,0},{14,2},{16,30},{18,... | collective-permute-start | bytes 258056 | tf_op jit(solution)/shard_map/ppermute | solution.py:735
  6.9 7.7 %collective-permute-start = (f32[168,128]{1,0:T(8,128)S(1)}, f32[168,128]{1,0:T(8,128)S(1)}, u32[]{:S(2)}, u32[]{:S(2)}) collective-permute-start(f32[168,128]{1,0:T(8,128)S(1)} %tables.1.refs_3_), channel_id=1, source_target_pairs={{0,26},{2,24},{4,30},{6,28},{8,18},{10,16},{12,22},{14,20},{16,10}... | collective-permute-start | bytes 258056 | tf_op jit(solution)/shard_map/ppermute | solution.py:735
  7.2 7.4 %copy-start = (f32[16,256]{1,0:T(8,128)S(1)}, f32[16,256]{1,0:T(8,128)}, u32[]{:S(2)}) copy-start(f32[16,256]{1,0:T(8,128)} %refs_4_.3) | copy-start | bytes 49156
  10.1 6.1 %collective-permute-start.5 = (f32[168,128]{1,0:T(8,128)S(1)}, f32[168,128]{1,0:T(8,128)S(1)}, u32[]{:S(2)}, u32[]{:S(2)}) collective-permute-start(f32[168,128]{1,0:T(8,128)S(1)} %collective-permute-done.2.refs_2_.refs_11_), channel_id=1, source_target_pairs={{0,8},{8,0},{16,24},{24,16},{1,9},{9,1},{17,25},{25,17},{2,10},{10... | collective-permute-start | bytes 258056 | tf_op jit(solution)/shard_map/ppermute | solution.py:738
  14.0 2.1 %collective-permute-start.4 = (f32[168,128]{1,0:T(8,128)S(1)}, f32[168,128]{1,0:T(8,128)S(1)}, u32[]{:S(2)}, u32[]{:S(2)}) collective-permute-start(f32[168,128]{1,0:T(8,128)S(1)} %collective-permute-done.1.refs_1_.refs_10_), channel_id=1, source_target_pairs={{0,8},{8,0},{16,24},{24,16},{1,9},{9,1},{17,25},{25,17},{2,10},{10... | collective-permute-start | bytes 258056 | tf_op jit(solution)/shard_map/ppermute | solution.py:738
  14.5 1.7 %collective-permute-start.3 = (f32[168,128]{1,0:T(8,128)S(1)}, f32[168,128]{1,0:T(8,128)S(1)}, u32[]{:S(2)}, u32[]{:S(2)}) collective-permute-start(f32[168,128]{1,0:T(8,128)S(1)} %collective-permute-done.refs_0_.refs_9_), channel_id=1, source_target_pairs={{0,8},{8,0},{16,24},{24,16},{1,9},{9,1},{17,25},{25,17},{2,10},{10... | collective-permute-start | bytes 258056 | tf_op jit(solution)/shard_map/ppermute | solution.py:738
  17.7 1.4 %collective-permute-start.6 = (f32[136,128]{1,0:T(8,128)S(1)}, f32[136,128]{1,0:T(8,128)S(1)}, u32[]{:S(2)}, u32[]{:S(2)}) collective-permute-start(f32[136,128]{1,0:T(8,128)S(1)} %get-tuple-element.56.refs_0_), channel_id=1, source_target_pairs={{0,8},{8,0},{16,24},{24,16},{1,9},{9,1},{17,25},{25,17},{2,10},{10... | collective-permute-start | bytes 208904 | tf_op jit(solution)/shard_map/ppermute | solution.py:822
  19.2 4.4 %collective-permute-start.7 = (f32[136,128]{1,0:T(8,128)S(1)}, f32[136,128]{1,0:T(8,128)S(1)}, u32[]{:S(2)}, u32[]{:S(2)}) collective-permute-start(f32[136,128]{1,0:T(8,128)S(1)} %get-tuple-element.58), channel_id=1, source_target_pairs={{0,16},{8,24},{1,17},{9,25},{2,18},{10,26},{3,19},{11,27},{4,20},{... | collective-permute-start | bytes 208904 | tf_op jit(solution)/shard_map/ppermute | solution.py:822
  24.3 6.3 %collective-permute-start.8 = (f32[64,256]{1,0:T(8,128)S(1)}, f32[64,256]{1,0:T(8,128)S(1)}, u32[]{:S(2)}, u32[]{:S(2)}) collective-permute-start(f32[64,256]{1,0:T(8,128)S(1)} %get-tuple-element.78), channel_id=1, source_target_pairs={{0,4},{2,6},{4,2},{6,0},{1,5},{3,7},{5,3},{7,1},{8,12},{10,14},{12... | collective-permute-start | bytes 196616 | tf_op jit(solution)/shard_map/ppermute | solution.py:869
  27.1 5.8 %collective-permute-start.9 = (f32[64,256]{1,0:T(8,128)S(1)}, f32[64,256]{1,0:T(8,128)S(1)}, u32[]{:S(2)}, u32[]{:S(2)}) collective-permute-start(f32[64,256]{1,0:T(8,128)S(1)} %get-tuple-element.79), channel_id=1, source_target_pairs={{0,6},{2,4},{4,0},{6,2},{1,7},{3,5},{5,1},{7,3},{8,14},{10,12},{12... | collective-permute-start | bytes 196616 | tf_op jit(solution)/shard_map/ppermute | solution.py:869
  28.3 5.2 %collective-permute-start.10 = (f32[64,256]{1,0:T(8,128)S(1)}, f32[64,256]{1,0:T(8,128)S(1)}, u32[]{:S(2)}, u32[]{:S(2)}) collective-permute-start(f32[64,256]{1,0:T(8,128)S(1)} %get-tuple-element.80), channel_id=1, source_target_pairs={{0,2},{2,0},{4,6},{6,4},{1,3},{3,1},{5,7},{7,5},{8,10},{10,8},{12,... | collective-permute-start | bytes 196616 | tf_op jit(solution)/shard_map/ppermute | solution.py:869

commit v17 on v12

--- a/solution.py
+++ b/solution.py
@@ -541,12 +541,36 @@
     return prefix[0:ch, :] + jnp.where(later, factor * came[0:ch, :], 0.0)
 
 
-def output_kernel(dims, bit, *refs):
+def entering_state(dims, bit, prefix, came):
+    V, D, hl, ch, nh, ns, T, N = dims
+    place = lax.rem(lax.div(lax.axis_index("seq"), 2**bit), 2 ** (len(came) // 2 + 1))
+    odd = lax.rem(place, 2) == 1
+
+    def fade(value):
+        return jnp.exp(state_rows(dims, value))
+
+    nearest, log = came[0][0:ch, :], came[0][ch : ch + hl, :]
+    if len(came) > 1:
+        nearest = jnp.where(odd, nearest, came[2][0:ch, :])
+        log = jnp.where(odd, log, came[2][ch : ch + hl, :])
+    entering = jnp.where(place > 0, nearest, 0.0)
+    if len(came) > 1:
+        second = jnp.where(place > 1, came[1][0:ch, :], 0.0)
+        third = jnp.where(place > 2, came[2][0:ch, :], 0.0)
+        entering = entering + fade(log) * (second + fade(came[1][ch : ch + hl, :]) * third)
+    if prefix is not None:
+        entering = prefix[0:ch, :] + fade(prefix[ch : ch + hl, :]) * entering
+    return entering
+
+
+def output_kernel(dims, bit, known, number, *refs):
     V, D, hl, ch, nh, ns, T, N = dims
     P = ch // hl
-    prefix, came, read_high, read_low, base, fade, gate, own, proj_high, proj_low = refs[:10]
-    groups, outs, partial_ref = refs[10], refs[11 : 11 + nh], refs[11 + nh]
-    entering = prefix_joined(dims, bit, prefix, came)
+    came, refs = refs[:number], refs[number:]
+    prefix, refs = (refs[0], refs[1:]) if known else (None, refs)
+    read_high, read_low, base, fade, gate, own, proj_high, proj_low, groups = refs[:9]
+    outs, partial_ref = refs[9 : 9 + nh], refs[9 + nh]
+    entering = entering_state(dims, bit, prefix, came)
     carried = dot_split((read_high[...], read_low[...]), split2(entering), NT)
     value = (base[...] + carried * fade[...]) * gate[...]
     square = dot(jnp.concatenate(split2(value * value), axis=0), groups[0:ch, 0:ch])
@@ -789,10 +813,9 @@
 
     prefix = None
     bits = ns.bit_length() - 1
-    for bit in range(bits):
+    direct = max(bits - 2, 0)
+    for bit in range(direct):
         came = lax.ppermute(state, "seq", [(seq, seq ^ 2**bit) for seq in range(ns)])
-        if bit == bits - 1:
-            break
         given = [state] + ([] if prefix is None else [prefix]) + [came]
 
         def join(bit, known, *refs):
@@ -809,20 +832,24 @@
             compiler_params=params,
             name="join",
         )(*given)
-    if prefix is None:
-        prefix = jnp.zeros_like(state)
+    came = {
+        k: lax.ppermute(state, "seq", [(seq, seq ^ k * 2**direct) for seq in range(ns)])
+        for k in range(1, ns // 2**direct)
+    }
+    came = [came[k] for k in sorted(came)]
+    known = [] if prefix is None else [prefix]
 
     parts = pl.pallas_call(
-        functools.partial(output_kernel, dims, bits - 1),
+        functools.partial(output_kernel, dims, direct, bool(known), len(came)),
         out_shape=(shape(share, D),) * nh,
-        in_specs=[vmem] * 11,
+        in_specs=[vmem] * (len(came) + len(known) + 9),
         out_specs=(vmem,) * nh,
         scratch_shapes=[pltpu.VMEM((T, D), f32)],
         compiler_params=params,
         name="output",
     )(
-        prefix,
-        came,
+        *came,
+        *known,
         read_high,
         read_low,
         base,

time: 34 us -> 34.4 us (1.012)
  starting transfers between devices: 11.7 us -> 12.4 us
    ppermute x2 -> x3, starting transfers between devices: 1.48 us -> 2.13 us  [per_device(): lax.ppermute(state, 'seq', [(seq, seq ^ k * 2 ** direct) for seq in range...]
    ppermute x2 -> x3, waiting for transfers between devices: 3.32 us -> 2.82 us  [per_device(): lax.ppermute(state, 'seq', [(seq, seq ^ k * 2 ** direct) for seq in range...]
    pallas_call x2 -> x1, Pallas kernels: 0.73 us -> 0.71 us  [per_device(): pl.pallas_call(functools.partial(output_kernel, dims, direct, bool(known)...]
  transfers between devices with their start and end apart: 11 -> 12, of which waited for: 7 -> 7; matrix products, arithmetic and copies ran while one was open for 0% -> 0% of each run, Pallas kernels for 14% -> 14%
where the time goes in v17:
time: 34.4 us; the launch traced here: 34.3 us
  waiting for transfers between devices  12.7 us (37%)
  starting transfers between devices  12.4 us (36%)
  Pallas kernels  8.38 us (24%)
  other arithmetic  0.65 us (2%)
    ppermute x3, starting transfers between devices, per_device(): messages[k] = lax.ppermute(sent, ('seq', 'head'), pairs)  5.74 us
    ppermute x3, waiting for transfers between devices, per_device(): result = result + lax.ppermute(parts[k], 'head', pairs)  4.99 us
    ppermute x3, waiting for transfers between devices, per_device(): messages[k] = lax.ppermute(sent, ('seq', 'head'), pairs)  4.9 us
    ppermute x3, starting transfers between devices, per_device(): result = result + lax.ppermute(parts[k], 'head', pairs)  4.05 us
    ppermute x3, waiting for transfers between devices, per_device(): lax.ppermute(state, 'seq', [(seq, seq ^ k * 2 ** direct) for seq in range...  2.82 us
    ppermute x3, starting transfers between devices, per_device(): lax.ppermute(state, 'seq', [(seq, seq ^ k * 2 ** direct) for seq in range...  2.13 us
    pallas_call x1, Pallas kernels, per_device(): pl.pallas_call(functools.partial(prepare_kernel, dims), out_shape=(shape(...  2.07 us
    pallas_call x1, Pallas kernels, per_device(): pl.pallas_call(functools.partial(mix_kernel, dims), out_shape=(*halves(T,...  1.59 us
  transfers between devices with their start and end apart: 12, of which 7 were waited for; matrix products, arithmetic and copies ran while one was open for 0% of the time, Pallas kernels for 14%

profile of v17, /device:TPU:0, one launch (start us, length us, event | category | flops | bytes accessed | tf_op | source)
XLA Modules:
  0.0 34.3 jit_solution(9650362493418693804)
XLA Ops:
  0.0 1.4 %tables.1.refs_3_ = f32[168,128]{1,0:T(8,128)S(1)} custom-call(f32[512,128]{1,0:T(8,128)} %bitcast.18, s32[1,256]{1,0:T(1,128)} %bitcast.20, f32[16,256]{1,0:T(8,128)} %refs_4_.3, f32[1,256]{1,0:T(1,128)} %bitcast.21, f32[2,256]{1,0:T(2,128)} %bitcast.19, f32[1,2]{1,0:T(1,128)} %bitcast.23, f32[1,2]{1,0:T(1,128)} %bitcast.24, f32[1,2]{1,0:T(1,128)} %bitcast.25, ...), custom_call_target="tpu_custom_call" | custom-call | tf_op jit(solution)/shard_map/tables/pallas_call | solution.py:656
  1.4 5.0 %collective-permute-start.2 = (f32[168,128]{1,0:T(8,128)S(1)}, f32[168,128]{1,0:T(8,128)S(1)}, u32[]{:S(2)}, u32[]{:S(2)}) collective-permute-start(f32[168,128]{1,0:T(8,128)S(1)} %tables.1.refs_3_), channel_id=1, source_target_pairs={{0,20},{2,22},{4,16},{6,18},{8,28},{10,30},{12,24},{14,26},{16,4},... | collective-permute-start | bytes 258056 | tf_op jit(solution)/shard_map/ppermute | solution.py:733
  6.5 0.5 %collective-permute-start.1 = (f32[168,128]{1,0:T(8,128)S(1)}, f32[168,128]{1,0:T(8,128)S(1)}, u32[]{:S(2)}, u32[]{:S(2)}) collective-permute-start(f32[168,128]{1,0:T(8,128)S(1)} %tables.1.refs_3_), channel_id=1, source_target_pairs={{0,14},{2,12},{4,10},{6,8},{8,6},{10,4},{12,2},{14,0},{16,30},{18,... | collective-permute-start | bytes 258056 | tf_op jit(solution)/shard_map/ppermute | solution.py:733
  7.0 0.2 collective-permute-start
  7.2 0.0 copy-start
  7.2 2.1 %prepare.1 = (f32[16,128]{1,0:T(8,128)S(1)}, f32[8,128]{1,0:T(8,128)S(1)}, bf16[256,256]{1,0:T(8,128)(2,1)S(1)}, bf16[128,256]{1,0:T(8,128)(2,1)S(1)}, bf16[128,...) custom-call(f32[512,128]{1,0:T(8,128)} %bitcast.27, ...), custom_call_target="tpu_custom_call" | custom-call | flops 16106127360 | bytes 262144 | tf_op jit(solution)/shard_map/prepare/pallas_call | solution.py:699
  9.3 3.8 %collective-permute-done.2.refs_2_.refs_11_ = f32[168,128]{1,0:T(8,128)S(1)} collective-permute-done((f32[168,128]{1,0:T(8,128)S(1)}, f32[168,128]{1,0:T(8,128)S(1)}, u32[]{:S(2)}, u32[]{:S(2)}) %collective-permute-start.2) | collective-permute-done | bytes 86048 | tf_op jit(solution)/shard_map/ppermute | solution.py:733
  13.0 0.0 collective-permute-start.5
  13.0 0.1 collective-permute-done.1.refs_1_.refs_10_
  13.1 0.4 %collective-permute-start.4 = (f32[168,128]{1,0:T(8,128)S(1)}, f32[168,128]{1,0:T(8,128)S(1)}, u32[]{:S(2)}, u32[]{:S(2)}) collective-permute-start(f32[168,128]{1,0:T(8,128)S(1)} %collective-permute-done.1.refs_1_.refs_10_), channel_id=1, source_target_pairs={{0,8},{8,0},{16,24},{24,16},{1,9},{9,1},{17,25},{25,17},{2,10},{10... | collective-permute-start | bytes 258056 | tf_op jit(solution)/shard_map/ppermute | solution.py:736
  13.5 1.0 %collective-permute-done.refs_0_.refs_9_ = f32[168,128]{1,0:T(8,128)S(1)} collective-permute-done((f32[168,128]{1,0:T(8,128)S(1)}, f32[168,128]{1,0:T(8,128)S(1)}, u32[]{:S(2)}, u32[]{:S(2)}) %collective-permute-start) | collective-permute-done | bytes 86048 | tf_op jit(solution)/shard_map/ppermute | solution.py:733
  14.6 0.1 collective-permute-start.3
  14.7 0.0 copy-done
  14.7 1.6 %mix.1 = (bf16[256,512]{1,0:T(8,128)(2,1)S(1)}, bf16[256,512]{1,0:T(8,128)(2,1)S(1)}, f32[256,256]{1,0:T(8,128)S(1)}) custom-call(f32[168,128]{1,0:T(8,128)S(1)} %collective-permute-done.refs_0_.refs_9_, f32[168,128]{1,0:T(8,128)S(1)} %collective-permute-done.1.refs_1_.refs_10_, f32[168,128]{1,0:T(8,128)S(1)} %collective-permute-done.2.refs_2_.refs_11_, ...), custom_call_target="tpu_custom_call" | custom-call | flops 16106127360 | bytes 262144 | tf_op jit(solution)/shard_map/mix/pallas_call | solution.py:738
  16.3 0.0 collective-permute-done.5.refs_14_
  16.3 0.0 collective-permute-done.4.refs_13_
  16.3 0.0 collective-permute-done.3.refs_12_
  16.3 1.5 %project.1 = (f32[136,128]{1,0:T(8,128)S(1)}, bf16[256,256]{1,0:T(8,128)(2,1)S(1)}, bf16[256,256]{1,0:T(8,128)(2,1)S(1)}, f32[256,128]{1,0:T(8,128)S(1)}, f32[25...) custom-call(bf16[256,512]{1,0:T(8,128)(2,1)S(1)} %get-tuple-element.45.refs_0_, ...), custom_call_target="tpu_custom_call" | custom-call | tf_op jit(solution)/shard_map/project/pallas_call | solution.py:756
  17.8 0.8 %collective-permute-start.8 = (f32[136,128]{1,0:T(8,128)S(1)}, f32[136,128]{1,0:T(8,128)S(1)}, u32[]{:S(2)}, u32[]{:S(2)}) collective-permute-start(f32[136,128]{1,0:T(8,128)S(1)} %get-tuple-element.54), channel_id=1, source_target_pairs={{0,24},{8,16},{16,8},{24,0},{1,25},{9,17},{17,9},{25,1},{2,26},{10... | collective-permute-start | bytes 208904 | tf_op jit(solution)/shard_map/ppermute | solution.py:836
  18.6 1.3 %collective-permute-start.7 = (f32[136,128]{1,0:T(8,128)S(1)}, f32[136,128]{1,0:T(8,128)S(1)}, u32[]{:S(2)}, u32[]{:S(2)}) collective-permute-start(f32[136,128]{1,0:T(8,128)S(1)} %get-tuple-element.54), channel_id=1, source_target_pairs={{0,16},{8,24},{16,0},{24,8},{1,17},{9,25},{17,1},{25,9},{2,18},{10... | collective-permute-start | bytes 208904 | tf_op jit(solution)/shard_map/ppermute | solution.py:836
  19.9 0.0 collective-permute-start.6
  19.9 1.1 %block.1 = (f32[256,128]{1,0:T(8,128)S(1)}, bf16[256,128]{1,0:T(8,128)(2,1)S(1)}, bf16[256,128]{1,0:T(8,128)(2,1)S(1)}, f32[256,128]{1,0:T(8,128)S(1)}, f32[256,128]{1,0:T(8,128)S(1)}, /*index=5*/f32[64,256]{1,0:T(8,128)S(1)}) custom-call(bf16[256,256]{1,0:T(8,128)(2,1)S(1)} %get-tuple-element.55.refs_0_, bf16[256,256]{1,0:T(8,128)(2,1)S(1)} %get-tuple-element.56.refs_1_, ...), custom_call_target="tpu_custom_call" | custom-call | flops 16106127360 | bytes 262144 | tf_op jit(solution)/shard_map/block/pallas_call | solution.py:785
  21.0 0.8 %collective-permute-done.8.refs_2_ = f32[136,128]{1,0:T(8,128)S(1)} collective-permute-done((f32[136,128]{1,0:T(8,128)S(1)}, f32[136,128]{1,0:T(8,128)S(1)}, u32[]{:S(2)}, u32[]{:S(2)}) %collective-permute-start.8) | collective-permute-done | bytes 69664 | tf_op jit(solution)/shard_map/ppermute | solution.py:836
  21.8 2.0 %collective-permute-done.7.refs_1_ = f32[136,128]{1,0:T(8,128)S(1)} collective-permute-done((f32[136,128]{1,0:T(8,128)S(1)}, f32[136,128]{1,0:T(8,128)S(1)}, u32[]{:S(2)}, u32[]{:S(2)}) %collective-permute-start.7) | collective-permute-done | bytes 69664 | tf_op jit(solution)/shard_map/ppermute | solution.py:836
  23.8 0.0 collective-permute-done.6.refs_0_
  23.8 0.7 %output.1 = (f32[64,256]{1,0:T(8,128)S(1)}, f32[64,256]{1,0:T(8,128)S(1)}, f32[64,256]{1,0:T(8,128)S(1)}, f32[64,256]{1,0:T(8,128)S(1)}) custom-call(f32[136,128]{1,0:T(8,128)S(1)} %collective-permute-done.6.refs_0_, f32[136,128]{1,0:T(8,128)S(1)} %collective-permute-done.7.refs_1_, f32[136,128]{1,0:T(8,128)S(1)} %collective-permute-done.8.refs_2_, ...), custom_call_target="tpu_custom_call" | custom-call | tf_op jit(solution)/shard_map/output/pallas_call | solution.py:842
  24.6 2.9 %collective-permute-start.9 = (f32[64,256]{1,0:T(8,128)S(1)}, f32[64,256]{1,0:T(8,128)S(1)}, u32[]{:S(2)}, u32[]{:S(2)}) collective-permute-start(f32[64,256]{1,0:T(8,128)S(1)} %get-tuple-element.74), channel_id=1, source_target_pairs={{0,4},{2,6},{4,0},{6,2},{1,5},{3,7},{5,1},{7,3},{8,12},{10,14},{12... | collective-permute-start | bytes 196616 | tf_op jit(solution)/shard_map/ppermute | solution.py:866
  27.4 0.7 %collective-permute-start.10 = (f32[64,256]{1,0:T(8,128)S(1)}, f32[64,256]{1,0:T(8,128)S(1)}, u32[]{:S(2)}, u32[]{:S(2)}) collective-permute-start(f32[64,256]{1,0:T(8,128)S(1)} %get-tuple-element.75), channel_id=1, source_target_pairs={{0,6},{2,4},{4,2},{6,0},{1,7},{3,5},{5,3},{7,1},{8,14},{10,12},{12... | collective-permute-start | bytes 196616 | tf_op jit(solution)/shard_map/ppermute | solution.py:866
  28.1 0.5 %collective-permute-start.11 = (f32[64,256]{1,0:T(8,128)S(1)}, f32[64,256]{1,0:T(8,128)S(1)}, u32[]{:S(2)}, u32[]{:S(2)}) collective-permute-start(f32[64,256]{1,0:T(8,128)S(1)} %get-tuple-element.76), channel_id=1, source_target_pairs={{0,2},{2,0},{4,6},{6,4},{1,3},{3,1},{5,7},{7,5},{8,10},{10,8},{12,... | collective-permute-start | bytes 196616 | tf_op jit(solution)/shard_map/ppermute | solution.py:866
  28.6 3.6 %collective-permute-done.9 = f32[64,256]{1,0:T(8,128)S(1)} collective-permute-done((f32[64,256]{1,0:T(8,128)S(1)}, f32[64,256]{1,0:T(8,128)S(1)}, u32[]{:S(2)}, u32[]{:S(2)}) %collective-permute-start.9) | collective-permute-done | bytes 65568 | tf_op jit(solution)/shard_map/ppermute | solution.py:866
  32.2 1.4 %collective-permute-done.10 = f32[64,256]{1,0:T(8,128)S(1)} collective-permute-done((f32[64,256]{1,0:T(8,128)S(1)}, f32[64,256]{1,0:T(8,128)S(1)}, u32[]{:S(2)}, u32[]{:S(2)}) %collective-permute-start.10) | collective-permute-done | bytes 65568 | tf_op jit(solution)/shard_map/ppermute | solution.py:866
  33.6 0.0 collective-permute-done.11
  33.6 0.6 %add_add_fusion = f32[64,256]{1,0:T(8,128)} fusion(f32[64,256]{1,0:T(8,128)S(1)} %collective-permute-done.11, f32[64,256]{1,0:T(8,128)S(1)} %collective-permute-done.10, f32[64,256]{1,0:T(8,128)S(1)} %get-tuple-element.73, f32[64,256]{1,0:T(8,128)S(1)} %collective-permute-done.9), kind=kLoop, calls=%fused_computation | loop fusion | flops 49152 | bytes 327680 | tf_op jit(solution)/shard_map/add | solution.py:866
Async XLA Ops:
  1.4 11.6 %collective-permute-start.2 = (f32[168,128]{1,0:T(8,128)S(1)}, f32[168,128]{1,0:T(8,128)S(1)}, u32[]{:S(2)}, u32[]{:S(2)}) collective-permute-start(f32[168,128]{1,0:T(8,128)S(1)} %tables.1.refs_3_), channel_id=1, source_target_pairs={{0,20},{2,22},{4,16},{6,18},{8,28},{10,30},{12,24},{14,26},{16,4},... | collective-permute-start | bytes 258056 | tf_op jit(solution)/shard_map/ppermute | solution.py:733
  6.5 6.7 %collective-permute-start.1 = (f32[168,128]{1,0:T(8,128)S(1)}, f32[168,128]{1,0:T(8,128)S(1)}, u32[]{:S(2)}, u32[]{:S(2)}) collective-permute-start(f32[168,128]{1,0:T(8,128)S(1)} %tables.1.refs_3_), channel_id=1, source_target_pairs={{0,14},{2,12},{4,10},{6,8},{8,6},{10,4},{12,2},{14,0},{16,30},{18,... | collective-permute-start | bytes 258056 | tf_op jit(solution)/shard_map/ppermute | solution.py:733
  7.0 7.6 %collective-permute-start = (f32[168,128]{1,0:T(8,128)S(1)}, f32[168,128]{1,0:T(8,128)S(1)}, u32[]{:S(2)}, u32[]{:S(2)}) collective-permute-start(f32[168,128]{1,0:T(8,128)S(1)} %tables.1.refs_3_), channel_id=1, source_target_pairs={{0,26},{2,24},{4,30},{6,28},{8,18},{10,16},{12,22},{14,20},{16,10}... | collective-permute-start | bytes 258056 | tf_op jit(solution)/shard_map/ppermute | solution.py:733
  7.2 7.5 %copy-start = (f32[16,256]{1,0:T(8,128)S(1)}, f32[16,256]{1,0:T(8,128)}, u32[]{:S(2)}) copy-start(f32[16,256]{1,0:T(8,128)} %refs_4_.3) | copy-start | bytes 49156
  13.0 3.2 %collective-permute-start.5 = (f32[168,128]{1,0:T(8,128)S(1)}, f32[168,128]{1,0:T(8,128)S(1)}, u32[]{:S(2)}, u32[]{:S(2)}) collective-permute-start(f32[168,128]{1,0:T(8,128)S(1)} %collective-permute-done.2.refs_2_.refs_11_), channel_id=1, source_target_pairs={{0,8},{8,0},{16,24},{24,16},{1,9},{9,1},{17,25},{25,17},{2,10},{10... | collective-permute-start | bytes 258056 | tf_op jit(solution)/shard_map/ppermute | solution.py:736
  13.1 3.1 %collective-permute-start.4 = (f32[168,128]{1,0:T(8,128)S(1)}, f32[168,128]{1,0:T(8,128)S(1)}, u32[]{:S(2)}, u32[]{:S(2)}) collective-permute-start(f32[168,128]{1,0:T(8,128)S(1)} %collective-permute-done.1.refs_1_.refs_10_), channel_id=1, source_target_pairs={{0,8},{8,0},{16,24},{24,16},{1,9},{9,1},{17,25},{25,17},{2,10},{10... | collective-permute-start | bytes 258056 | tf_op jit(solution)/shard_map/ppermute | solution.py:736
  14.6 1.7 %collective-permute-start.3 = (f32[168,128]{1,0:T(8,128)S(1)}, f32[168,128]{1,0:T(8,128)S(1)}, u32[]{:S(2)}, u32[]{:S(2)}) collective-permute-start(f32[168,128]{1,0:T(8,128)S(1)} %collective-permute-done.refs_0_.refs_9_), channel_id=1, source_target_pairs={{0,8},{8,0},{16,24},{24,16},{1,9},{9,1},{17,25},{25,17},{2,10},{10... | collective-permute-start | bytes 258056 | tf_op jit(solution)/shard_map/ppermute | solution.py:736
  17.8 4.0 %collective-permute-start.8 = (f32[136,128]{1,0:T(8,128)S(1)}, f32[136,128]{1,0:T(8,128)S(1)}, u32[]{:S(2)}, u32[]{:S(2)}) collective-permute-start(f32[136,128]{1,0:T(8,128)S(1)} %get-tuple-element.54), channel_id=1, source_target_pairs={{0,24},{8,16},{16,8},{24,0},{1,25},{9,17},{17,9},{25,1},{2,26},{10... | collective-permute-start | bytes 208904 | tf_op jit(solution)/shard_map/ppermute | solution.py:836
  18.6 5.2 %collective-permute-start.7 = (f32[136,128]{1,0:T(8,128)S(1)}, f32[136,128]{1,0:T(8,128)S(1)}, u32[]{:S(2)}, u32[]{:S(2)}) collective-permute-start(f32[136,128]{1,0:T(8,128)S(1)} %get-tuple-element.54), channel_id=1, source_target_pairs={{0,16},{8,24},{16,0},{24,8},{1,17},{9,25},{17,1},{25,9},{2,18},{10... | collective-permute-start | bytes 208904 | tf_op jit(solution)/shard_map/ppermute | solution.py:836
  19.9 3.9 %collective-permute-start.6 = (f32[136,128]{1,0:T(8,128)S(1)}, f32[136,128]{1,0:T(8,128)S(1)}, u32[]{:S(2)}, u32[]{:S(2)}) collective-permute-start(f32[136,128]{1,0:T(8,128)S(1)} %get-tuple-element.54), channel_id=1, source_target_pairs={{0,8},{8,0},{16,24},{24,16},{1,9},{9,1},{17,25},{25,17},{2,10},{10... | collective-permute-start | bytes 208904 | tf_op jit(solution)/shard_map/ppermute | solution.py:836
  24.6 7.7 %collective-permute-start.9 = (f32[64,256]{1,0:T(8,128)S(1)}, f32[64,256]{1,0:T(8,128)S(1)}, u32[]{:S(2)}, u32[]{:S(2)}) collective-permute-start(f32[64,256]{1,0:T(8,128)S(1)} %get-tuple-element.74), channel_id=1, source_target_pairs={{0,4},{2,6},{4,0},{6,2},{1,5},{3,7},{5,1},{7,3},{8,12},{10,14},{12... | collective-permute-start | bytes 196616 | tf_op jit(solution)/shard_map/ppermute | solution.py:866
  27.4 6.2 %collective-permute-start.10 = (f32[64,256]{1,0:T(8,128)S(1)}, f32[64,256]{1,0:T(8,128)S(1)}, u32[]{:S(2)}, u32[]{:S(2)}) collective-permute-start(f32[64,256]{1,0:T(8,128)S(1)} %get-tuple-element.75), channel_id=1, source_target_pairs={{0,6},{2,4},{4,2},{6,0},{1,7},{3,5},{5,3},{7,1},{8,14},{10,12},{12... | collective-permute-start | bytes 196616 | tf_op jit(solution)/shard_map/ppermute | solution.py:866
  28.1 5.5 %collective-permute-start.11 = (f32[64,256]{1,0:T(8,128)S(1)}, f32[64,256]{1,0:T(8,128)S(1)}, u32[]{:S(2)}, u32[]{:S(2)}) collective-permute-start(f32[64,256]{1,0:T(8,128)S(1)} %get-tuple-element.76), channel_id=1, source_target_pairs={{0,2},{2,0},{4,6},{6,4},{1,3},{3,1},{5,7},{7,5},{8,10},{10,8},{12,... | collective-permute-start | bytes 196616 | tf_op jit(solution)/shard_map/ppermute | solution.py:866

commit v18 on v17

--- a/solution.py
+++ b/solution.py
@@ -832,11 +832,14 @@
             compiler_params=params,
             name="join",
         )(*given)
-    came = {
-        k: lax.ppermute(state, "seq", [(seq, seq ^ k * 2**direct) for seq in range(ns)])
-        for k in range(1, ns // 2**direct)
-    }
-    came = [came[k] for k in sorted(came)]
+
+    def across(value, k):
+        return lax.ppermute(value, "seq", [(seq, seq ^ k * 2**direct) for seq in range(ns)])
+
+    came = [across(state, 1)]
+    if bits > 1:
+        base, far = lax.optimization_barrier((base, across(state, 2)))
+        came += [far, across(far, 1)]
     known = [] if prefix is None else [prefix]
 
     parts = pl.pallas_call(

time: 34.4 us -> 34.5 us (level)
  waiting for transfers between devices: 12.7 us -> 14 us
  starting transfers between devices: 12.4 us -> 11.3 us
    ppermute x3, starting transfers between devices: 2.13 us -> 1.07 us  [across(): lax.ppermute(value, 'seq', [(seq, seq ^ k * 2 ** direct) for seq in range...]
    ppermute x3, waiting for transfers between devices: 2.82 us -> 3.68 us  [across(): lax.ppermute(value, 'seq', [(seq, seq ^ k * 2 ** direct) for seq in range...]
    ppermute x3, waiting for transfers between devices: 4.99 us -> 5.38 us  [per_device(): result = result + lax.ppermute(parts[k], 'head', pairs)]
  transfers between devices with their start and end apart: 12 -> 12, of which waited for: 7 -> 8; matrix products, arithmetic and copies ran while one was open for 0% -> 0% of each run, Pallas kernels for 14% -> 14%
where the time goes in v18:
time: 34.5 us; the launch traced here: 34.4 us
  waiting for transfers between devices  14 us (41%)
  starting transfers between devices  11.3 us (33%)
  Pallas kernels  8.39 us (24%)
  other arithmetic  0.65 us (2%)
    ppermute x3, starting transfers between devices, per_device(): messages[k] = lax.ppermute(sent, ('seq', 'head'), pairs)  5.74 us
    ppermute x3, waiting for transfers between devices, per_device(): result = result + lax.ppermute(parts[k], 'head', pairs)  5.38 us
    ppermute x3, waiting for transfers between devices, per_device(): messages[k] = lax.ppermute(sent, ('seq', 'head'), pairs)  4.9 us
    ppermute x3, starting transfers between devices, per_device(): result = result + lax.ppermute(parts[k], 'head', pairs)  3.99 us
    ppermute x3, waiting for transfers between devices, across(): lax.ppermute(value, 'seq', [(seq, seq ^ k * 2 ** direct) for seq in range...  3.68 us
    pallas_call x1, Pallas kernels, per_device(): pl.pallas_call(functools.partial(prepare_kernel, dims), out_shape=(shape(...  2.07 us
    pallas_call x1, Pallas kernels, per_device(): pl.pallas_call(functools.partial(mix_kernel, dims), out_shape=(*halves(T,...  1.59 us
    pallas_call x1, Pallas kernels, per_device(): pl.pallas_call(functools.partial(project_kernel, dims), out_shape=(shape(...  1.51 us
  transfers between devices with their start and end apart: 12, of which 8 were waited for; matrix products, arithmetic and copies ran while one was open for 0% of the time, Pallas kernels for 14%

profile of v18, /device:TPU:0, one launch (start us, length us, event | category | flops | bytes accessed | tf_op | source)
XLA Modules:
  0.0 34.4 jit_solution(11686998290518291000)
XLA Ops:
  0.0 1.4 %tables.1.refs_3_ = f32[168,128]{1,0:T(8,128)S(1)} custom-call(f32[512,128]{1,0:T(8,128)} %bitcast.18, s32[1,256]{1,0:T(1,128)} %bitcast.20, f32[16,256]{1,0:T(8,128)} %refs_4_.3, f32[1,256]{1,0:T(1,128)} %bitcast.21, f32[2,256]{1,0:T(2,128)} %bitcast.19, f32[1,2]{1,0:T(1,128)} %bitcast.23, f32[1,2]{1,0:T(1,128)} %bitcast.24, f32[1,2]{1,0:T(1,128)} %bitcast.25, ...), custom_call_target="tpu_custom_call" | custom-call | tf_op jit(solution)/shard_map/tables/pallas_call | solution.py:656
  1.4 5.0 %collective-permute-start.2 = (f32[168,128]{1,0:T(8,128)S(1)}, f32[168,128]{1,0:T(8,128)S(1)}, u32[]{:S(2)}, u32[]{:S(2)}) collective-permute-start(f32[168,128]{1,0:T(8,128)S(1)} %tables.1.refs_3_), channel_id=1, source_target_pairs={{0,20},{2,22},{4,16},{6,18},{8,28},{10,30},{12,24},{14,26},{16,4},... | collective-permute-start | bytes 258056 | tf_op jit(solution)/shard_map/ppermute | solution.py:733
  6.5 0.5 %collective-permute-start.1 = (f32[168,128]{1,0:T(8,128)S(1)}, f32[168,128]{1,0:T(8,128)S(1)}, u32[]{:S(2)}, u32[]{:S(2)}) collective-permute-start(f32[168,128]{1,0:T(8,128)S(1)} %tables.1.refs_3_), channel_id=1, source_target_pairs={{0,14},{2,12},{4,10},{6,8},{8,6},{10,4},{12,2},{14,0},{16,30},{18,... | collective-permute-start | bytes 258056 | tf_op jit(solution)/shard_map/ppermute | solution.py:733
  7.0 0.2 collective-permute-start
  7.2 0.0 copy-start
  7.2 2.1 %prepare.1 = (f32[16,128]{1,0:T(8,128)S(1)}, f32[8,128]{1,0:T(8,128)S(1)}, bf16[256,256]{1,0:T(8,128)(2,1)S(1)}, bf16[128,256]{1,0:T(8,128)(2,1)S(1)}, bf16[128,...) custom-call(f32[512,128]{1,0:T(8,128)} %bitcast.27, ...), custom_call_target="tpu_custom_call" | custom-call | flops 16106127360 | bytes 262144 | tf_op jit(solution)/shard_map/prepare/pallas_call | solution.py:699
  9.3 3.8 %collective-permute-done.2.refs_2_.refs_11_ = f32[168,128]{1,0:T(8,128)S(1)} collective-permute-done((f32[168,128]{1,0:T(8,128)S(1)}, f32[168,128]{1,0:T(8,128)S(1)}, u32[]{:S(2)}, u32[]{:S(2)}) %collective-permute-start.2) | collective-permute-done | bytes 86048 | tf_op jit(solution)/shard_map/ppermute | solution.py:733
  13.0 0.0 collective-permute-start.5
  13.0 0.1 collective-permute-done.1.refs_1_.refs_10_
  13.1 0.4 %collective-permute-start.4 = (f32[168,128]{1,0:T(8,128)S(1)}, f32[168,128]{1,0:T(8,128)S(1)}, u32[]{:S(2)}, u32[]{:S(2)}) collective-permute-start(f32[168,128]{1,0:T(8,128)S(1)} %collective-permute-done.1.refs_1_.refs_10_), channel_id=1, source_target_pairs={{0,8},{8,0},{16,24},{24,16},{1,9},{9,1},{17,25},{25,17},{2,10},{10... | collective-permute-start | bytes 258056 | tf_op jit(solution)/shard_map/ppermute | solution.py:736
  13.5 1.0 %collective-permute-done.refs_0_.refs_9_ = f32[168,128]{1,0:T(8,128)S(1)} collective-permute-done((f32[168,128]{1,0:T(8,128)S(1)}, f32[168,128]{1,0:T(8,128)S(1)}, u32[]{:S(2)}, u32[]{:S(2)}) %collective-permute-start) | collective-permute-done | bytes 86048 | tf_op jit(solution)/shard_map/ppermute | solution.py:733
  14.6 0.1 collective-permute-start.3
  14.7 0.0 copy-done
  14.7 1.6 %mix.1 = (bf16[256,512]{1,0:T(8,128)(2,1)S(1)}, bf16[256,512]{1,0:T(8,128)(2,1)S(1)}, f32[256,256]{1,0:T(8,128)S(1)}) custom-call(f32[168,128]{1,0:T(8,128)S(1)} %collective-permute-done.refs_0_.refs_9_, f32[168,128]{1,0:T(8,128)S(1)} %collective-permute-done.1.refs_1_.refs_10_, f32[168,128]{1,0:T(8,128)S(1)} %collective-permute-done.2.refs_2_.refs_11_, ...), custom_call_target="tpu_custom_call" | custom-call | flops 16106127360 | bytes 262144 | tf_op jit(solution)/shard_map/mix/pallas_call | solution.py:738
  16.3 0.0 collective-permute-done.5.refs_14_
  16.3 0.0 collective-permute-done.4.refs_13_
  16.3 0.0 collective-permute-done.3.refs_12_
  16.3 1.5 %project.1 = (f32[136,128]{1,0:T(8,128)S(1)}, bf16[256,256]{1,0:T(8,128)(2,1)S(1)}, bf16[256,256]{1,0:T(8,128)(2,1)S(1)}, f32[256,128]{1,0:T(8,128)S(1)}, f32[25...) custom-call(bf16[256,512]{1,0:T(8,128)(2,1)S(1)} %get-tuple-element.47.refs_0_, ...), custom_call_target="tpu_custom_call" | custom-call | tf_op jit(solution)/shard_map/project/pallas_call | solution.py:756
  17.8 1.1 %collective-permute-start.7 = (f32[136,128]{1,0:T(8,128)S(1)}, f32[136,128]{1,0:T(8,128)S(1)}, u32[]{:S(2)}, u32[]{:S(2)}) collective-permute-start(f32[136,128]{1,0:T(8,128)S(1)} %get-tuple-element.56), channel_id=1, source_target_pairs={{0,16},{8,24},{16,0},{24,8},{1,17},{9,25},{17,1},{25,9},{2,18},{10... | collective-permute-start | bytes 208904 | tf_op jit(solution)/shard_map/ppermute | solution.py:837
  18.9 0.0 collective-permute-start.6
  18.9 1.1 %block.1 = (f32[256,128]{1,0:T(8,128)S(1)}, bf16[256,128]{1,0:T(8,128)(2,1)S(1)}, bf16[256,128]{1,0:T(8,128)(2,1)S(1)}, f32[256,128]{1,0:T(8,128)S(1)}, f32[256,128]{1,0:T(8,128)S(1)}, /*index=5*/f32[64,256]{1,0:T(8,128)S(1)}) custom-call(bf16[256,256]{1,0:T(8,128)(2,1)S(1)} %get-tuple-element.57.refs_0_, bf16[256,256]{1,0:T(8,128)(2,1)S(1)} %get-tuple-element.58.refs_1_, ...), custom_call_target="tpu_custom_call" | custom-call | flops 16106127360 | bytes 262144 | tf_op jit(solution)/shard_map/block/pallas_call | solution.py:785
  20.0 2.4 %collective-permute-done.7.refs_1_ = f32[136,128]{1,0:T(8,128)S(1)} collective-permute-done((f32[136,128]{1,0:T(8,128)S(1)}, f32[136,128]{1,0:T(8,128)S(1)}, u32[]{:S(2)}, u32[]{:S(2)}) %collective-permute-start.7) | collective-permute-done | bytes 69664 | tf_op jit(solution)/shard_map/ppermute | solution.py:837
  22.4 0.0 collective-permute-start.8
  22.4 0.0 collective-permute-done.6.refs_0_
  22.4 1.3 %collective-permute-done.8.refs_2_ = f32[136,128]{1,0:T(8,128)S(1)} collective-permute-done((f32[136,128]{1,0:T(8,128)S(1)}, f32[136,128]{1,0:T(8,128)S(1)}, u32[]{:S(2)}, u32[]{:S(2)}) %collective-permute-start.8) | collective-permute-done | bytes 69664 | tf_op jit(solution)/shard_map/ppermute | solution.py:837
  23.7 0.7 %output.1 = (f32[64,256]{1,0:T(8,128)S(1)}, f32[64,256]{1,0:T(8,128)S(1)}, f32[64,256]{1,0:T(8,128)S(1)}, f32[64,256]{1,0:T(8,128)S(1)}) custom-call(f32[136,128]{1,0:T(8,128)S(1)} %collective-permute-done.6.refs_0_, f32[136,128]{1,0:T(8,128)S(1)} %collective-permute-done.7.refs_1_, f32[136,128]{1,0:T(8,128)S(1)} %collective-permute-done.8.refs_2_, ...), custom_call_target="tpu_custom_call" | custom-call | tf_op jit(solution)/shard_map/output/pallas_call | solution.py:845
  24.4 2.7 %collective-permute-start.9 = (f32[64,256]{1,0:T(8,128)S(1)}, f32[64,256]{1,0:T(8,128)S(1)}, u32[]{:S(2)}, u32[]{:S(2)}) collective-permute-start(f32[64,256]{1,0:T(8,128)S(1)} %get-tuple-element.78), channel_id=1, source_target_pairs={{0,4},{2,6},{4,0},{6,2},{1,5},{3,7},{5,1},{7,3},{8,12},{10,14},{12... | collective-permute-start | bytes 196616 | tf_op jit(solution)/shard_map/ppermute | solution.py:869
  27.0 0.8 %collective-permute-start.10 = (f32[64,256]{1,0:T(8,128)S(1)}, f32[64,256]{1,0:T(8,128)S(1)}, u32[]{:S(2)}, u32[]{:S(2)}) collective-permute-start(f32[64,256]{1,0:T(8,128)S(1)} %get-tuple-element.79), channel_id=1, source_target_pairs={{0,6},{2,4},{4,2},{6,0},{1,7},{3,5},{5,3},{7,1},{8,14},{10,12},{12... | collective-permute-start | bytes 196616 | tf_op jit(solution)/shard_map/ppermute | solution.py:869
  27.9 0.5 %collective-permute-start.11 = (f32[64,256]{1,0:T(8,128)S(1)}, f32[64,256]{1,0:T(8,128)S(1)}, u32[]{:S(2)}, u32[]{:S(2)}) collective-permute-start(f32[64,256]{1,0:T(8,128)S(1)} %get-tuple-element.80), channel_id=1, source_target_pairs={{0,2},{2,0},{4,6},{6,4},{1,3},{3,1},{5,7},{7,5},{8,10},{10,8},{12,... | collective-permute-start | bytes 196616 | tf_op jit(solution)/shard_map/ppermute | solution.py:869
  28.4 3.9 %collective-permute-done.9 = f32[64,256]{1,0:T(8,128)S(1)} collective-permute-done((f32[64,256]{1,0:T(8,128)S(1)}, f32[64,256]{1,0:T(8,128)S(1)}, u32[]{:S(2)}, u32[]{:S(2)}) %collective-permute-start.9) | collective-permute-done | bytes 65568 | tf_op jit(solution)/shard_map/ppermute | solution.py:869
  32.2 1.2 %collective-permute-done.10 = f32[64,256]{1,0:T(8,128)S(1)} collective-permute-done((f32[64,256]{1,0:T(8,128)S(1)}, f32[64,256]{1,0:T(8,128)S(1)}, u32[]{:S(2)}, u32[]{:S(2)}) %collective-permute-start.10) | collective-permute-done | bytes 65568 | tf_op jit(solution)/shard_map/ppermute | solution.py:869
  33.5 0.3 collective-permute-done.11
  33.7 0.6 %add_add_fusion = f32[64,256]{1,0:T(8,128)} fusion(f32[64,256]{1,0:T(8,128)S(1)} %collective-permute-done.11, f32[64,256]{1,0:T(8,128)S(1)} %collective-permute-done.10, f32[64,256]{1,0:T(8,128)S(1)} %get-tuple-element.77, f32[64,256]{1,0:T(8,128)S(1)} %collective-permute-done.9), kind=kLoop, calls=%fused_computation | loop fusion | flops 49152 | bytes 327680 | tf_op jit(solution)/shard_map/add | solution.py:869
Async XLA Ops:
  1.4 11.6 %collective-permute-start.2 = (f32[168,128]{1,0:T(8,128)S(1)}, f32[168,128]{1,0:T(8,128)S(1)}, u32[]{:S(2)}, u32[]{:S(2)}) collective-permute-start(f32[168,128]{1,0:T(8,128)S(1)} %tables.1.refs_3_), channel_id=1, source_target_pairs={{0,20},{2,22},{4,16},{6,18},{8,28},{10,30},{12,24},{14,26},{16,4},... | collective-permute-start | bytes 258056 | tf_op jit(solution)/shard_map/ppermute | solution.py:733
  6.5 6.7 %collective-permute-start.1 = (f32[168,128]{1,0:T(8,128)S(1)}, f32[168,128]{1,0:T(8,128)S(1)}, u32[]{:S(2)}, u32[]{:S(2)}) collective-permute-start(f32[168,128]{1,0:T(8,128)S(1)} %tables.1.refs_3_), channel_id=1, source_target_pairs={{0,14},{2,12},{4,10},{6,8},{8,6},{10,4},{12,2},{14,0},{16,30},{18,... | collective-permute-start | bytes 258056 | tf_op jit(solution)/shard_map/ppermute | solution.py:733
  7.0 7.6 %collective-permute-start = (f32[168,128]{1,0:T(8,128)S(1)}, f32[168,128]{1,0:T(8,128)S(1)}, u32[]{:S(2)}, u32[]{:S(2)}) collective-permute-start(f32[168,128]{1,0:T(8,128)S(1)} %tables.1.refs_3_), channel_id=1, source_target_pairs={{0,26},{2,24},{4,30},{6,28},{8,18},{10,16},{12,22},{14,20},{16,10}... | collective-permute-start | bytes 258056 | tf_op jit(solution)/shard_map/ppermute | solution.py:733
  7.2 7.5 %copy-start = (f32[16,256]{1,0:T(8,128)S(1)}, f32[16,256]{1,0:T(8,128)}, u32[]{:S(2)}) copy-start(f32[16,256]{1,0:T(8,128)} %refs_4_.3) | copy-start | bytes 49156
  13.0 3.2 %collective-permute-start.5 = (f32[168,128]{1,0:T(8,128)S(1)}, f32[168,128]{1,0:T(8,128)S(1)}, u32[]{:S(2)}, u32[]{:S(2)}) collective-permute-start(f32[168,128]{1,0:T(8,128)S(1)} %collective-permute-done.2.refs_2_.refs_11_), channel_id=1, source_target_pairs={{0,8},{8,0},{16,24},{24,16},{1,9},{9,1},{17,25},{25,17},{2,10},{10... | collective-permute-start | bytes 258056 | tf_op jit(solution)/shard_map/ppermute | solution.py:736
  13.1 3.1 %collective-permute-start.4 = (f32[168,128]{1,0:T(8,128)S(1)}, f32[168,128]{1,0:T(8,128)S(1)}, u32[]{:S(2)}, u32[]{:S(2)}) collective-permute-start(f32[168,128]{1,0:T(8,128)S(1)} %collective-permute-done.1.refs_1_.refs_10_), channel_id=1, source_target_pairs={{0,8},{8,0},{16,24},{24,16},{1,9},{9,1},{17,25},{25,17},{2,10},{10... | collective-permute-start | bytes 258056 | tf_op jit(solution)/shard_map/ppermute | solution.py:736
  14.6 1.7 %collective-permute-start.3 = (f32[168,128]{1,0:T(8,128)S(1)}, f32[168,128]{1,0:T(8,128)S(1)}, u32[]{:S(2)}, u32[]{:S(2)}) collective-permute-start(f32[168,128]{1,0:T(8,128)S(1)} %collective-permute-done.refs_0_.refs_9_), channel_id=1, source_target_pairs={{0,8},{8,0},{16,24},{24,16},{1,9},{9,1},{17,25},{25,17},{2,10},{10... | collective-permute-start | bytes 258056 | tf_op jit(solution)/shard_map/ppermute | solution.py:736
  17.8 4.6 %collective-permute-start.7 = (f32[136,128]{1,0:T(8,128)S(1)}, f32[136,128]{1,0:T(8,128)S(1)}, u32[]{:S(2)}, u32[]{:S(2)}) collective-permute-start(f32[136,128]{1,0:T(8,128)S(1)} %get-tuple-element.56), channel_id=1, source_target_pairs={{0,16},{8,24},{16,0},{24,8},{1,17},{9,25},{17,1},{25,9},{2,18},{10... | collective-permute-start | bytes 208904 | tf_op jit(solution)/shard_map/ppermute | solution.py:837
  18.9 3.5 %collective-permute-start.6 = (f32[136,128]{1,0:T(8,128)S(1)}, f32[136,128]{1,0:T(8,128)S(1)}, u32[]{:S(2)}, u32[]{:S(2)}) collective-permute-start(f32[136,128]{1,0:T(8,128)S(1)} %get-tuple-element.56), channel_id=1, source_target_pairs={{0,8},{8,0},{16,24},{24,16},{1,9},{9,1},{17,25},{25,17},{2,10},{10... | collective-permute-start | bytes 208904 | tf_op jit(solution)/shard_map/ppermute | solution.py:837
  22.4 1.3 %collective-permute-start.8 = (f32[136,128]{1,0:T(8,128)S(1)}, f32[136,128]{1,0:T(8,128)S(1)}, u32[]{:S(2)}, u32[]{:S(2)}) collective-permute-start(f32[136,128]{1,0:T(8,128)S(1)} %collective-permute-done.7.refs_1_), channel_id=1, source_target_pairs={{0,8},{8,0},{16,24},{24,16},{1,9},{9,1},{17,25},{25,17},{2,10},{10... | collective-permute-start | bytes 208904 | tf_op jit(solution)/shard_map/ppermute | solution.py:837
  24.4 7.9 %collective-permute-start.9 = (f32[64,256]{1,0:T(8,128)S(1)}, f32[64,256]{1,0:T(8,128)S(1)}, u32[]{:S(2)}, u32[]{:S(2)}) collective-permute-start(f32[64,256]{1,0:T(8,128)S(1)} %get-tuple-element.78), channel_id=1, source_target_pairs={{0,4},{2,6},{4,0},{6,2},{1,5},{3,7},{5,1},{7,3},{8,12},{10,14},{12... | collective-permute-start | bytes 196616 | tf_op jit(solution)/shard_map/ppermute | solution.py:869
  27.0 6.4 %collective-permute-start.10 = (f32[64,256]{1,0:T(8,128)S(1)}, f32[64,256]{1,0:T(8,128)S(1)}, u32[]{:S(2)}, u32[]{:S(2)}) collective-permute-start(f32[64,256]{1,0:T(8,128)S(1)} %get-tuple-element.79), channel_id=1, source_target_pairs={{0,6},{2,4},{4,2},{6,0},{1,7},{3,5},{5,3},{7,1},{8,14},{10,12},{12... | collective-permute-start | bytes 196616 | tf_op jit(solution)/shard_map/ppermute | solution.py:869
  27.9 5.9 %collective-permute-start.11 = (f32[64,256]{1,0:T(8,128)S(1)}, f32[64,256]{1,0:T(8,128)S(1)}, u32[]{:S(2)}, u32[]{:S(2)}) collective-permute-start(f32[64,256]{1,0:T(8,128)S(1)} %get-tuple-element.80), channel_id=1, source_target_pairs={{0,2},{2,0},{4,6},{6,4},{1,3},{3,1},{5,7},{7,5},{8,10},{10,8},{12,... | collective-permute-start | bytes 196616 | tf_op jit(solution)/shard_map/ppermute | solution.py:869

commit v19 on v12

--- a/solution.py
+++ b/solution.py
@@ -18,8 +18,11 @@
 
 
 def partners(ns, nh):
-    count = max(ns, nh)
-    return [((ns - k) if 0 < k < ns else 0, k if k < nh else 0) for k in range(count)]
+    return [(k if k < ns else 0, k if k < nh else 0) for k in range(max(ns, nh))]
+
+
+def first_turn(count):
+    return list(range(1, count))
 
 
 def in_turn(count):
@@ -273,7 +276,7 @@
         return taken
 
     count = max(ns, nh)
-    packets = dict(zip(in_turn(count)[::-1] + [0], take(count)))
+    packets = dict(zip(first_turn(count)[::-1] + [0], take(count)))
     emb, pairs, triangles, groups, blocks = take(5)
     out_high, out_low, out_embedded = take(3)
     tokens = take(1)[0]
@@ -409,7 +412,7 @@
         return taken
 
     high, low, embedded, small, own_high, own_low, state_high, state_low, upto = take(9)
-    order = in_turn(nh)[::-1]
+    order = first_turn(nh)[::-1]
     nears = dict(zip(order, take(nh - 1)))
     others = dict(zip(order, take(nh - 1)))
     out_state, out_high, out_low, out_scale = take(4)
@@ -698,17 +701,17 @@
 
     count = max(ns, nh)
     messages = {0: message}
-    for k in in_turn(count):
-        seq_bits, head_bits = partners(ns, nh)[k]
+    for k in first_turn(count):
+        seq_bits, shift = partners(ns, nh)[k]
         pairs = [
-            (seq * nh + head, (seq ^ seq_bits) * nh + (head ^ head_bits))
+            (seq * nh + head, (seq ^ seq_bits) * nh + (head + shift) % nh)
             for seq in range(ns)
             for head in range(nh)
         ]
         sent = message if k < nh else message[0 : top_rows(dims)]
         messages[k] = lax.ppermute(sent, ("seq", "head"), pairs)
     swap = [(seq, seq ^ 1) for seq in range(ns)]
-    order = in_turn(nh)[::-1]
+    order = first_turn(nh)[::-1]
     others = [lax.ppermute(messages[k], "seq", swap) for k in order]
 
     mixed_high, mixed_low, embedded = pl.pallas_call(
@@ -721,7 +724,7 @@
         cost_estimate=heavy,
         name="mix",
     )(
-        *[messages[k] for k in in_turn(count)[::-1] + [0]],
+        *[messages[k] for k in first_turn(count)[::-1] + [0]],
         embedding,
         pair_table,
         triangles,

time: 34 us -> 34.2 us (level)
  starting transfers between devices: 11.7 us -> 13 us
  waiting for transfers between devices: 13 us -> 12 us
    ppermute x3, starting transfers between devices: 5.74 us -> 7.39 us  [per_device(): messages[k] = lax.ppermute(sent, ('seq', 'head'), pairs)]
    ppermute x3, waiting for transfers between devices: 4.9 us -> 3.29 us  [per_device(): messages[k] = lax.ppermute(sent, ('seq', 'head'), pairs)]
    ppermute x2, starting transfers between devices: 1.48 us -> 0.45 us  [per_device(): lax.ppermute(state, 'seq', [(seq, seq ^ 2 ** bit) for seq in range(ns)])]
    ppermute x2, waiting for transfers between devices: 3.32 us -> 4.16 us  [per_device(): lax.ppermute(state, 'seq', [(seq, seq ^ 2 ** bit) for seq in range(ns)])]
    ppermute x3, starting transfers between devices: 4.02 us -> 4.54 us  [per_device(): result = result + lax.ppermute(parts[k], 'head', pairs)]
  transfers between devices with their start and end apart: 11 -> 11, of which waited for: 7 -> 6; matrix products, arithmetic and copies ran while one was open for 0% -> 0% of each run, Pallas kernels for 14% -> 14%
where the time goes in v19:
time: 34.2 us; the launch traced here: 34.1 us
  starting transfers between devices  13 us (38%)
  waiting for transfers between devices  12 us (35%)
  Pallas kernels  8.4 us (25%)
  other arithmetic  0.65 us (2%)
    ppermute x3, starting transfers between devices, per_device(): messages[k] = lax.ppermute(sent, ('seq', 'head'), pairs)  7.39 us
    ppermute x3, starting transfers between devices, per_device(): result = result + lax.ppermute(parts[k], 'head', pairs)  4.54 us
    ppermute x3, waiting for transfers between devices, per_device(): result = result + lax.ppermute(parts[k], 'head', pairs)  4.52 us
    ppermute x2, waiting for transfers between devices, per_device(): lax.ppermute(state, 'seq', [(seq, seq ^ 2 ** bit) for seq in range(ns)])  4.16 us
    ppermute x3, waiting for transfers between devices, per_device(): messages[k] = lax.ppermute(sent, ('seq', 'head'), pairs)  3.29 us
    pallas_call x1, Pallas kernels, per_device(): pl.pallas_call(functools.partial(prepare_kernel, dims), out_shape=(shape(...  2.08 us
    pallas_call x1, Pallas kernels, per_device(): pl.pallas_call(functools.partial(mix_kernel, dims), out_shape=(*halves(T,...  1.59 us
    pallas_call x1, Pallas kernels, per_device(): pl.pallas_call(functools.partial(project_kernel, dims), out_shape=(shape(...  1.51 us
  transfers between devices with their start and end apart: 11, of which 6 were waited for; matrix products, arithmetic and copies ran while one was open for 0% of the time, Pallas kernels for 14%

profile of v19, /device:TPU:0, one launch (start us, length us, event | category | flops | bytes accessed | tf_op | source)
XLA Modules:
  0.0 34.1 jit_solution(2045350976113469916)
XLA Ops:
  0.0 1.4 %tables.1.refs_3_ = f32[168,128]{1,0:T(8,128)S(1)} custom-call(f32[512,128]{1,0:T(8,128)} %bitcast.18, s32[1,256]{1,0:T(1,128)} %bitcast.20, f32[16,256]{1,0:T(8,128)} %refs_4_.3, f32[1,256]{1,0:T(1,128)} %bitcast.21, f32[2,256]{1,0:T(2,128)} %bitcast.19, f32[1,2]{1,0:T(1,128)} %bitcast.23, f32[1,2]{1,0:T(1,128)} %bitcast.24, f32[1,2]{1,0:T(1,128)} %bitcast.25, ...), custom_call_target="tpu_custom_call" | custom-call | tf_op jit(solution)/shard_map/tables/pallas_call | solution.py:635
  1.4 2.5 %collective-permute-start.2 = (f32[168,128]{1,0:T(8,128)S(1)}, f32[168,128]{1,0:T(8,128)S(1)}, u32[]{:S(2)}, u32[]{:S(2)}) collective-permute-start(f32[168,128]{1,0:T(8,128)S(1)} %tables.1.refs_3_), channel_id=1, source_target_pairs={{0,10},{2,12},{4,14},{6,8},{8,2},{10,4},{12,6},{14,0},{16,26},{18,... | collective-permute-start | bytes 258056 | tf_op jit(solution)/shard_map/ppermute | solution.py:712
  4.0 3.5 %collective-permute-start.1 = (f32[168,128]{1,0:T(8,128)S(1)}, f32[168,128]{1,0:T(8,128)S(1)}, u32[]{:S(2)}, u32[]{:S(2)}) collective-permute-start(f32[168,128]{1,0:T(8,128)S(1)} %tables.1.refs_3_), channel_id=1, source_target_pairs={{0,20},{2,22},{4,16},{6,18},{8,28},{10,30},{12,24},{14,26},{16,4},... | collective-permute-start | bytes 258056 | tf_op jit(solution)/shard_map/ppermute | solution.py:712
  7.5 1.4 %collective-permute-start = (f32[168,128]{1,0:T(8,128)S(1)}, f32[168,128]{1,0:T(8,128)S(1)}, u32[]{:S(2)}, u32[]{:S(2)}) collective-permute-start(f32[168,128]{1,0:T(8,128)S(1)} %tables.1.refs_3_), channel_id=1, source_target_pairs={{0,30},{2,24},{4,26},{6,28},{8,22},{10,16},{12,18},{14,20},{16,14}... | collective-permute-start | bytes 258056 | tf_op jit(solution)/shard_map/ppermute | solution.py:712
  8.8 0.0 copy-start
  8.8 2.1 %prepare.1 = (f32[16,128]{1,0:T(8,128)S(1)}, f32[8,128]{1,0:T(8,128)S(1)}, bf16[256,256]{1,0:T(8,128)(2,1)S(1)}, bf16[128,256]{1,0:T(8,128)(2,1)S(1)}, bf16[128,...) custom-call(f32[512,128]{1,0:T(8,128)} %bitcast.27, ...), custom_call_target="tpu_custom_call" | custom-call | flops 16106127360 | bytes 262144 | tf_op jit(solution)/shard_map/prepare/pallas_call | solution.py:678
  10.9 0.0 collective-permute-done.2.refs_2_.refs_11_
  10.9 0.1 collective-permute-start.5
  11.1 3.2 %collective-permute-done.1.refs_1_.refs_10_ = f32[168,128]{1,0:T(8,128)S(1)} collective-permute-done((f32[168,128]{1,0:T(8,128)S(1)}, f32[168,128]{1,0:T(8,128)S(1)}, u32[]{:S(2)}, u32[]{:S(2)}) %collective-permute-start.1) | collective-permute-done | bytes 86048 | tf_op jit(solution)/shard_map/ppermute | solution.py:712
  14.3 0.0 collective-permute-start.4
  14.3 0.1 collective-permute-done.refs_0_.refs_9_
  14.4 0.4 %collective-permute-start.3 = (f32[168,128]{1,0:T(8,128)S(1)}, f32[168,128]{1,0:T(8,128)S(1)}, u32[]{:S(2)}, u32[]{:S(2)}) collective-permute-start(f32[168,128]{1,0:T(8,128)S(1)} %collective-permute-done.refs_0_.refs_9_), channel_id=1, source_target_pairs={{0,8},{8,0},{16,24},{24,16},{1,9},{9,1},{17,25},{25,17},{2,10},{10... | collective-permute-start | bytes 258056 | tf_op jit(solution)/shard_map/ppermute | solution.py:715
  14.8 0.0 copy-done
  14.8 1.6 %mix.1 = (bf16[256,512]{1,0:T(8,128)(2,1)S(1)}, bf16[256,512]{1,0:T(8,128)(2,1)S(1)}, f32[256,256]{1,0:T(8,128)S(1)}) custom-call(f32[168,128]{1,0:T(8,128)S(1)} %collective-permute-done.refs_0_.refs_9_, f32[168,128]{1,0:T(8,128)S(1)} %collective-permute-done.1.refs_1_.refs_10_, f32[168,128]{1,0:T(8,128)S(1)} %collective-permute-done.2.refs_2_.refs_11_, ...), custom_call_target="tpu_custom_call" | custom-call | flops 16106127360 | bytes 262144 | tf_op jit(solution)/shard_map/mix/pallas_call | solution.py:717
  16.4 0.0 collective-permute-done.5.refs_14_
  16.4 0.0 collective-permute-done.4.refs_13_
  16.4 0.0 collective-permute-done.3.refs_12_
  16.4 1.5 %project.1 = (f32[136,128]{1,0:T(8,128)S(1)}, bf16[256,256]{1,0:T(8,128)(2,1)S(1)}, bf16[256,256]{1,0:T(8,128)(2,1)S(1)}, f32[256,128]{1,0:T(8,128)S(1)}, f32[25...) custom-call(bf16[256,512]{1,0:T(8,128)(2,1)S(1)} %get-tuple-element.47.refs_0_, ...), custom_call_target="tpu_custom_call" | custom-call | tf_op jit(solution)/shard_map/project/pallas_call | solution.py:735
  17.9 0.2 collective-permute-start.6
  18.1 1.2 %collective-permute-done.6.refs_1_ = f32[136,128]{1,0:T(8,128)S(1)} collective-permute-done((f32[136,128]{1,0:T(8,128)S(1)}, f32[136,128]{1,0:T(8,128)S(1)}, u32[]{:S(2)}, u32[]{:S(2)}) %collective-permute-start.6) | collective-permute-done | bytes 69664 | tf_op jit(solution)/shard_map/ppermute | solution.py:796
  19.3 0.3 collective-permute-start.7
  19.6 1.1 %block.1 = (f32[256,128]{1,0:T(8,128)S(1)}, bf16[256,128]{1,0:T(8,128)(2,1)S(1)}, bf16[256,128]{1,0:T(8,128)(2,1)S(1)}, f32[256,128]{1,0:T(8,128)S(1)}, f32[256,128]{1,0:T(8,128)S(1)}, /*index=5*/f32[64,256]{1,0:T(8,128)S(1)}) custom-call(bf16[256,256]{1,0:T(8,128)(2,1)S(1)} %get-tuple-element.59.refs_0_, bf16[256,256]{1,0:T(8,128)(2,1)S(1)} %get-tuple-element.60.refs_1_, ...), custom_call_target="tpu_custom_call" | custom-call | flops 16106127360 | bytes 262144 | tf_op jit(solution)/shard_map/block/pallas_call | solution.py:764
  20.7 3.0 %collective-permute-done.7.refs_1_ = f32[136,128]{1,0:T(8,128)S(1)} collective-permute-done((f32[136,128]{1,0:T(8,128)S(1)}, f32[136,128]{1,0:T(8,128)S(1)}, u32[]{:S(2)}, u32[]{:S(2)}) %collective-permute-start.7) | collective-permute-done | bytes 69664 | tf_op jit(solution)/shard_map/ppermute | solution.py:796
  23.7 0.7 %output.1 = (f32[64,256]{1,0:T(8,128)S(1)}, f32[64,256]{1,0:T(8,128)S(1)}, f32[64,256]{1,0:T(8,128)S(1)}, f32[64,256]{1,0:T(8,128)S(1)}) custom-call(f32[136,128]{1,0:T(8,128)S(1)} %get-tuple-element.57.refs_0_, f32[136,128]{1,0:T(8,128)S(1)} %collective-permute-done.7.refs_1_, bf16[256,128]{1,0:T(8,128)(2,1)S(1)} %get-tuple-element.69.refs_2_, ...), custom_call_target="tpu_custom_call" | custom-call | tf_op jit(solution)/shard_map/output/pallas_call | solution.py:818
  24.4 0.7 %collective-permute-start.8 = (f32[64,256]{1,0:T(8,128)S(1)}, f32[64,256]{1,0:T(8,128)S(1)}, u32[]{:S(2)}, u32[]{:S(2)}) collective-permute-start(f32[64,256]{1,0:T(8,128)S(1)} %get-tuple-element.78), channel_id=1, source_target_pairs={{0,4},{2,6},{4,0},{6,2},{1,5},{3,7},{5,1},{7,3},{8,12},{10,14},{12... | collective-permute-start | bytes 196616 | tf_op jit(solution)/shard_map/ppermute | solution.py:842
  25.1 3.9 %collective-permute-start.9 = (f32[64,256]{1,0:T(8,128)S(1)}, f32[64,256]{1,0:T(8,128)S(1)}, u32[]{:S(2)}, u32[]{:S(2)}) collective-permute-start(f32[64,256]{1,0:T(8,128)S(1)} %get-tuple-element.79), channel_id=1, source_target_pairs={{0,6},{2,4},{4,2},{6,0},{1,7},{3,5},{5,3},{7,1},{8,14},{10,12},{12... | collective-permute-start | bytes 196616 | tf_op jit(solution)/shard_map/ppermute | solution.py:842
  28.9 0.0 collective-permute-start.10
  28.9 4.0 %collective-permute-done.8 = f32[64,256]{1,0:T(8,128)S(1)} collective-permute-done((f32[64,256]{1,0:T(8,128)S(1)}, f32[64,256]{1,0:T(8,128)S(1)}, u32[]{:S(2)}, u32[]{:S(2)}) %collective-permute-start.8) | collective-permute-done | bytes 65568 | tf_op jit(solution)/shard_map/ppermute | solution.py:842
  32.9 0.0 collective-permute-done.9
  32.9 0.6 %collective-permute-done.10 = f32[64,256]{1,0:T(8,128)S(1)} collective-permute-done((f32[64,256]{1,0:T(8,128)S(1)}, f32[64,256]{1,0:T(8,128)S(1)}, u32[]{:S(2)}, u32[]{:S(2)}) %collective-permute-start.10) | collective-permute-done | bytes 65568 | tf_op jit(solution)/shard_map/ppermute | solution.py:842
  33.4 0.6 %add_add_fusion = f32[64,256]{1,0:T(8,128)} fusion(f32[64,256]{1,0:T(8,128)S(1)} %collective-permute-done.10, f32[64,256]{1,0:T(8,128)S(1)} %collective-permute-done.9, f32[64,256]{1,0:T(8,128)S(1)} %get-tuple-element.77, f32[64,256]{1,0:T(8,128)S(1)} %collective-permute-done.8), kind=kLoop, calls=%fused_computation | loop fusion | flops 49152 | bytes 327680 | tf_op jit(solution)/shard_map/add | solution.py:842
  (1 shorter events, 0.0 us)
Async XLA Ops:
  1.4 9.5 %collective-permute-start.2 = (f32[168,128]{1,0:T(8,128)S(1)}, f32[168,128]{1,0:T(8,128)S(1)}, u32[]{:S(2)}, u32[]{:S(2)}) collective-permute-start(f32[168,128]{1,0:T(8,128)S(1)} %tables.1.refs_3_), channel_id=1, source_target_pairs={{0,10},{2,12},{4,14},{6,8},{8,2},{10,4},{12,6},{14,0},{16,26},{18,... | collective-permute-start | bytes 258056 | tf_op jit(solution)/shard_map/ppermute | solution.py:712
  4.0 10.3 %collective-permute-start.1 = (f32[168,128]{1,0:T(8,128)S(1)}, f32[168,128]{1,0:T(8,128)S(1)}, u32[]{:S(2)}, u32[]{:S(2)}) collective-permute-start(f32[168,128]{1,0:T(8,128)S(1)} %tables.1.refs_3_), channel_id=1, source_target_pairs={{0,20},{2,22},{4,16},{6,18},{8,28},{10,30},{12,24},{14,26},{16,4},... | collective-permute-start | bytes 258056 | tf_op jit(solution)/shard_map/ppermute | solution.py:712
  7.5 6.9 %collective-permute-start = (f32[168,128]{1,0:T(8,128)S(1)}, f32[168,128]{1,0:T(8,128)S(1)}, u32[]{:S(2)}, u32[]{:S(2)}) collective-permute-start(f32[168,128]{1,0:T(8,128)S(1)} %tables.1.refs_3_), channel_id=1, source_target_pairs={{0,30},{2,24},{4,26},{6,28},{8,22},{10,16},{12,18},{14,20},{16,14}... | collective-permute-start | bytes 258056 | tf_op jit(solution)/shard_map/ppermute | solution.py:712
  8.8 6.0 %copy-start = (f32[16,256]{1,0:T(8,128)S(1)}, f32[16,256]{1,0:T(8,128)}, u32[]{:S(2)}) copy-start(f32[16,256]{1,0:T(8,128)} %refs_4_.3) | copy-start | bytes 49156
  10.9 5.5 %collective-permute-start.5 = (f32[168,128]{1,0:T(8,128)S(1)}, f32[168,128]{1,0:T(8,128)S(1)}, u32[]{:S(2)}, u32[]{:S(2)}) collective-permute-start(f32[168,128]{1,0:T(8,128)S(1)} %collective-permute-done.2.refs_2_.refs_11_), channel_id=1, source_target_pairs={{0,8},{8,0},{16,24},{24,16},{1,9},{9,1},{17,25},{25,17},{2,10},{10... | collective-permute-start | bytes 258056 | tf_op jit(solution)/shard_map/ppermute | solution.py:715
  14.3 2.1 %collective-permute-start.4 = (f32[168,128]{1,0:T(8,128)S(1)}, f32[168,128]{1,0:T(8,128)S(1)}, u32[]{:S(2)}, u32[]{:S(2)}) collective-permute-start(f32[168,128]{1,0:T(8,128)S(1)} %collective-permute-done.1.refs_1_.refs_10_), channel_id=1, source_target_pairs={{0,8},{8,0},{16,24},{24,16},{1,9},{9,1},{17,25},{25,17},{2,10},{10... | collective-permute-start | bytes 258056 | tf_op jit(solution)/shard_map/ppermute | solution.py:715
  14.4 2.0 %collective-permute-start.3 = (f32[168,128]{1,0:T(8,128)S(1)}, f32[168,128]{1,0:T(8,128)S(1)}, u32[]{:S(2)}, u32[]{:S(2)}) collective-permute-start(f32[168,128]{1,0:T(8,128)S(1)} %collective-permute-done.refs_0_.refs_9_), channel_id=1, source_target_pairs={{0,8},{8,0},{16,24},{24,16},{1,9},{9,1},{17,25},{25,17},{2,10},{10... | collective-permute-start | bytes 258056 | tf_op jit(solution)/shard_map/ppermute | solution.py:715
  17.9 1.3 %collective-permute-start.6 = (f32[136,128]{1,0:T(8,128)S(1)}, f32[136,128]{1,0:T(8,128)S(1)}, u32[]{:S(2)}, u32[]{:S(2)}) collective-permute-start(f32[136,128]{1,0:T(8,128)S(1)} %get-tuple-element.56.refs_0_), channel_id=1, source_target_pairs={{0,8},{8,0},{16,24},{24,16},{1,9},{9,1},{17,25},{25,17},{2,10},{10... | collective-permute-start | bytes 208904 | tf_op jit(solution)/shard_map/ppermute | solution.py:796
  19.3 4.4 %collective-permute-start.7 = (f32[136,128]{1,0:T(8,128)S(1)}, f32[136,128]{1,0:T(8,128)S(1)}, u32[]{:S(2)}, u32[]{:S(2)}) collective-permute-start(f32[136,128]{1,0:T(8,128)S(1)} %get-tuple-element.58), channel_id=1, source_target_pairs={{0,16},{8,24},{16,0},{24,8},{1,17},{9,25},{17,1},{25,9},{2,18},{10... | collective-permute-start | bytes 208904 | tf_op jit(solution)/shard_map/ppermute | solution.py:796
  24.4 8.5 %collective-permute-start.8 = (f32[64,256]{1,0:T(8,128)S(1)}, f32[64,256]{1,0:T(8,128)S(1)}, u32[]{:S(2)}, u32[]{:S(2)}) collective-permute-start(f32[64,256]{1,0:T(8,128)S(1)} %get-tuple-element.78), channel_id=1, source_target_pairs={{0,4},{2,6},{4,0},{6,2},{1,5},{3,7},{5,1},{7,3},{8,12},{10,14},{12... | collective-permute-start | bytes 196616 | tf_op jit(solution)/shard_map/ppermute | solution.py:842
  25.1 7.8 %collective-permute-start.9 = (f32[64,256]{1,0:T(8,128)S(1)}, f32[64,256]{1,0:T(8,128)S(1)}, u32[]{:S(2)}, u32[]{:S(2)}) collective-permute-start(f32[64,256]{1,0:T(8,128)S(1)} %get-tuple-element.79), channel_id=1, source_target_pairs={{0,6},{2,4},{4,2},{6,0},{1,7},{3,5},{5,3},{7,1},{8,14},{10,12},{12... | collective-permute-start | bytes 196616 | tf_op jit(solution)/shard_map/ppermute | solution.py:842
  28.9 4.5 %collective-permute-start.10 = (f32[64,256]{1,0:T(8,128)S(1)}, f32[64,256]{1,0:T(8,128)S(1)}, u32[]{:S(2)}, u32[]{:S(2)}) collective-permute-start(f32[64,256]{1,0:T(8,128)S(1)} %get-tuple-element.80), channel_id=1, source_target_pairs={{0,2},{2,0},{4,6},{6,4},{1,3},{3,1},{5,7},{7,5},{8,10},{10,8},{12,... | collective-permute-start | bytes 196616 | tf_op jit(solution)/shard_map/ppermute | solution.py:842

commit v20 on v12

--- a/solution.py
+++ b/solution.py
@@ -24,6 +24,13 @@
 
 def in_turn(count):
     return sorted(range(1, count), key=lambda k: (-k.bit_length(), k))
+
+
+def around(shift, count):
+    ring = [place ^ place >> 1 for place in range(count)]
+    if sorted(ring) != list(range(count)):
+        ring = list(range(count))
+    return [ring[(ring.index(plane) + shift) % count] for plane in range(count)]
 
 
 def iota(shape, axis):
@@ -556,7 +563,10 @@
     partial_ref[...] = dot_split(split2(value), (proj_high[...], proj_low[...]))
     mine = lax.axis_index("head")
     for k in range(nh):
-        place = pl.multiple_of(lax.bitwise_xor(mine, k) * share, 8)
+        to = 0
+        for plane, target in enumerate(around(k, nh)):
+            to = jnp.where(mine == plane, target, to)
+        place = pl.multiple_of(to * share, 8)
         part = partial_ref[pl.ds(place, share), :]
         outs[k][...] = part + own[...] if k == 0 else part
 
@@ -834,8 +844,8 @@
         groups,
     )
     result = parts[0]
-    for k in in_turn(nh):
-        pairs = [(source, source ^ k) for source in range(nh)]
+    for k in range(1, nh):
+        pairs = list(enumerate(around(k, nh)))
         result = result + lax.ppermute(parts[k], "head", pairs)
     return result
 

time: 34 us -> 33.8 us (level)
  waiting for transfers between devices: 13 us -> 11.4 us
  starting transfers between devices: 11.7 us -> 13.2 us
    ppermute x3, waiting for transfers between devices: 4.75 us -> 3.16 us  [per_device(): result = result + lax.ppermute(parts[k], 'head', pairs)]
    ppermute x3, starting transfers between devices: 4.02 us -> 5.46 us  [per_device(): result = result + lax.ppermute(parts[k], 'head', pairs)]
  transfers between devices with their start and end apart: 11 -> 11, of which waited for: 7 -> 6; matrix products, arithmetic and copies ran while one was open for 0% -> 0% of each run, Pallas kernels for 14% -> 14%
where the time goes in v20:
time: 33.8 us; the launch traced here: 33.7 us
  starting transfers between devices  13.2 us (39%)
  waiting for transfers between devices  11.4 us (34%)
  Pallas kernels  8.41 us (25%)
  other arithmetic  0.65 us (2%)
    ppermute x3, starting transfers between devices, per_device(): messages[k] = lax.ppermute(sent, ('seq', 'head'), pairs)  5.74 us
    ppermute x3, starting transfers between devices, per_device(): result = result + lax.ppermute(parts[k], 'head', pairs)  5.46 us
    ppermute x3, waiting for transfers between devices, per_device(): messages[k] = lax.ppermute(sent, ('seq', 'head'), pairs)  4.9 us
    ppermute x2, waiting for transfers between devices, per_device(): lax.ppermute(state, 'seq', [(seq, seq ^ 2 ** bit) for seq in range(ns)])  3.32 us
    ppermute x3, waiting for transfers between devices, per_device(): result = result + lax.ppermute(parts[k], 'head', pairs)  3.16 us
    pallas_call x1, Pallas kernels, per_device(): pl.pallas_call(functools.partial(prepare_kernel, dims), out_shape=(shape(...  2.07 us
    pallas_call x1, Pallas kernels, per_device(): pl.pallas_call(functools.partial(mix_kernel, dims), out_shape=(*halves(T,...  1.59 us
    pallas_call x1, Pallas kernels, per_device(): pl.pallas_call(functools.partial(project_kernel, dims), out_shape=(shape(...  1.51 us
  transfers between devices with their start and end apart: 11, of which 6 were waited for; matrix products, arithmetic and copies ran while one was open for 0% of the time, Pallas kernels for 14%

profile of v20, /device:TPU:0, one launch (start us, length us, event | category | flops | bytes accessed | tf_op | source)
XLA Modules:
  0.0 33.7 jit_solution(11252586498015750366)
XLA Ops:
  0.0 1.4 %tables.1.refs_3_ = f32[168,128]{1,0:T(8,128)S(1)} custom-call(f32[512,128]{1,0:T(8,128)} %bitcast.18, s32[1,256]{1,0:T(1,128)} %bitcast.20, f32[16,256]{1,0:T(8,128)} %refs_4_.3, f32[1,256]{1,0:T(1,128)} %bitcast.21, f32[2,256]{1,0:T(2,128)} %bitcast.19, f32[1,2]{1,0:T(1,128)} %bitcast.23, f32[1,2]{1,0:T(1,128)} %bitcast.24, f32[1,2]{1,0:T(1,128)} %bitcast.25, ...), custom_call_target="tpu_custom_call" | custom-call | tf_op jit(solution)/shard_map/tables/pallas_call | solution.py:642
  1.4 5.0 %collective-permute-start.2 = (f32[168,128]{1,0:T(8,128)S(1)}, f32[168,128]{1,0:T(8,128)S(1)}, u32[]{:S(2)}, u32[]{:S(2)}) collective-permute-start(f32[168,128]{1,0:T(8,128)S(1)} %tables.1.refs_3_), channel_id=1, source_target_pairs={{0,20},{2,22},{4,16},{6,18},{8,28},{10,30},{12,24},{14,26},{16,4},... | collective-permute-start | bytes 258056 | tf_op jit(solution)/shard_map/ppermute | solution.py:719
  6.5 0.5 %collective-permute-start.1 = (f32[168,128]{1,0:T(8,128)S(1)}, f32[168,128]{1,0:T(8,128)S(1)}, u32[]{:S(2)}, u32[]{:S(2)}) collective-permute-start(f32[168,128]{1,0:T(8,128)S(1)} %tables.1.refs_3_), channel_id=1, source_target_pairs={{0,14},{2,12},{4,10},{6,8},{8,6},{10,4},{12,2},{14,0},{16,30},{18,... | collective-permute-start | bytes 258056 | tf_op jit(solution)/shard_map/ppermute | solution.py:719
  7.0 0.2 collective-permute-start
  7.2 0.0 copy-start
  7.2 2.1 %prepare.1 = (f32[16,128]{1,0:T(8,128)S(1)}, f32[8,128]{1,0:T(8,128)S(1)}, bf16[256,256]{1,0:T(8,128)(2,1)S(1)}, bf16[128,256]{1,0:T(8,128)(2,1)S(1)}, bf16[128,...) custom-call(f32[512,128]{1,0:T(8,128)} %bitcast.27, ...), custom_call_target="tpu_custom_call" | custom-call | flops 16106127360 | bytes 262144 | tf_op jit(solution)/shard_map/prepare/pallas_call | solution.py:685
  9.3 3.8 %collective-permute-done.2.refs_2_.refs_11_ = f32[168,128]{1,0:T(8,128)S(1)} collective-permute-done((f32[168,128]{1,0:T(8,128)S(1)}, f32[168,128]{1,0:T(8,128)S(1)}, u32[]{:S(2)}, u32[]{:S(2)}) %collective-permute-start.2) | collective-permute-done | bytes 86048 | tf_op jit(solution)/shard_map/ppermute | solution.py:719
  13.0 0.0 collective-permute-start.5
  13.0 0.1 collective-permute-done.1.refs_1_.refs_10_
  13.1 0.4 %collective-permute-start.4 = (f32[168,128]{1,0:T(8,128)S(1)}, f32[168,128]{1,0:T(8,128)S(1)}, u32[]{:S(2)}, u32[]{:S(2)}) collective-permute-start(f32[168,128]{1,0:T(8,128)S(1)} %collective-permute-done.1.refs_1_.refs_10_), channel_id=1, source_target_pairs={{0,8},{8,0},{16,24},{24,16},{1,9},{9,1},{17,25},{25,17},{2,10},{10... | collective-permute-start | bytes 258056 | tf_op jit(solution)/shard_map/ppermute | solution.py:722
  13.5 1.0 %collective-permute-done.refs_0_.refs_9_ = f32[168,128]{1,0:T(8,128)S(1)} collective-permute-done((f32[168,128]{1,0:T(8,128)S(1)}, f32[168,128]{1,0:T(8,128)S(1)}, u32[]{:S(2)}, u32[]{:S(2)}) %collective-permute-start) | collective-permute-done | bytes 86048 | tf_op jit(solution)/shard_map/ppermute | solution.py:719
  14.6 0.1 collective-permute-start.3
  14.7 0.0 copy-done
  14.7 1.6 %mix.1 = (bf16[256,512]{1,0:T(8,128)(2,1)S(1)}, bf16[256,512]{1,0:T(8,128)(2,1)S(1)}, f32[256,256]{1,0:T(8,128)S(1)}) custom-call(f32[168,128]{1,0:T(8,128)S(1)} %collective-permute-done.refs_0_.refs_9_, f32[168,128]{1,0:T(8,128)S(1)} %collective-permute-done.1.refs_1_.refs_10_, f32[168,128]{1,0:T(8,128)S(1)} %collective-permute-done.2.refs_2_.refs_11_, ...), custom_call_target="tpu_custom_call" | custom-call | flops 16106127360 | bytes 262144 | tf_op jit(solution)/shard_map/mix/pallas_call | solution.py:724
  16.3 0.0 collective-permute-done.5.refs_14_
  16.3 0.0 collective-permute-done.4.refs_13_
  16.3 0.0 collective-permute-done.3.refs_12_
  16.3 1.5 %project.1 = (f32[136,128]{1,0:T(8,128)S(1)}, bf16[256,256]{1,0:T(8,128)(2,1)S(1)}, bf16[256,256]{1,0:T(8,128)(2,1)S(1)}, f32[256,128]{1,0:T(8,128)S(1)}, f32[25...) custom-call(bf16[256,512]{1,0:T(8,128)(2,1)S(1)} %get-tuple-element.47.refs_0_, ...), custom_call_target="tpu_custom_call" | custom-call | tf_op jit(solution)/shard_map/project/pallas_call | solution.py:742
  17.8 0.5 %collective-permute-start.6 = (f32[136,128]{1,0:T(8,128)S(1)}, f32[136,128]{1,0:T(8,128)S(1)}, u32[]{:S(2)}, u32[]{:S(2)}) collective-permute-start(f32[136,128]{1,0:T(8,128)S(1)} %get-tuple-element.56.refs_0_), channel_id=1, source_target_pairs={{0,8},{8,0},{16,24},{24,16},{1,9},{9,1},{17,25},{25,17},{2,10},{10... | collective-permute-start | bytes 208904 | tf_op jit(solution)/shard_map/ppermute | solution.py:803
  18.3 0.9 %collective-permute-done.6.refs_1_ = f32[136,128]{1,0:T(8,128)S(1)} collective-permute-done((f32[136,128]{1,0:T(8,128)S(1)}, f32[136,128]{1,0:T(8,128)S(1)}, u32[]{:S(2)}, u32[]{:S(2)}) %collective-permute-start.6) | collective-permute-done | bytes 69664 | tf_op jit(solution)/shard_map/ppermute | solution.py:803
  19.2 1.0 %collective-permute-start.7 = (f32[136,128]{1,0:T(8,128)S(1)}, f32[136,128]{1,0:T(8,128)S(1)}, u32[]{:S(2)}, u32[]{:S(2)}) collective-permute-start(f32[136,128]{1,0:T(8,128)S(1)} %get-tuple-element.58), channel_id=1, source_target_pairs={{0,16},{8,24},{16,0},{24,8},{1,17},{9,25},{17,1},{25,9},{2,18},{10... | collective-permute-start | bytes 208904 | tf_op jit(solution)/shard_map/ppermute | solution.py:803
  20.2 1.1 %block.1 = (f32[256,128]{1,0:T(8,128)S(1)}, bf16[256,128]{1,0:T(8,128)(2,1)S(1)}, bf16[256,128]{1,0:T(8,128)(2,1)S(1)}, f32[256,128]{1,0:T(8,128)S(1)}, f32[256,128]{1,0:T(8,128)S(1)}, /*index=5*/f32[64,256]{1,0:T(8,128)S(1)}) custom-call(bf16[256,256]{1,0:T(8,128)(2,1)S(1)} %get-tuple-element.59.refs_0_, bf16[256,256]{1,0:T(8,128)(2,1)S(1)} %get-tuple-element.60.refs_1_, ...), custom_call_target="tpu_custom_call" | custom-call | flops 16106127360 | bytes 262144 | tf_op jit(solution)/shard_map/block/pallas_call | solution.py:771
  21.3 2.4 %collective-permute-done.7.refs_1_ = f32[136,128]{1,0:T(8,128)S(1)} collective-permute-done((f32[136,128]{1,0:T(8,128)S(1)}, f32[136,128]{1,0:T(8,128)S(1)}, u32[]{:S(2)}, u32[]{:S(2)}) %collective-permute-start.7) | collective-permute-done | bytes 69664 | tf_op jit(solution)/shard_map/ppermute | solution.py:803
  23.7 0.7 %output.1 = (f32[64,256]{1,0:T(8,128)S(1)}, f32[64,256]{1,0:T(8,128)S(1)}, f32[64,256]{1,0:T(8,128)S(1)}, f32[64,256]{1,0:T(8,128)S(1)}) custom-call(f32[136,128]{1,0:T(8,128)S(1)} %get-tuple-element.57.refs_0_, f32[136,128]{1,0:T(8,128)S(1)} %collective-permute-done.7.refs_1_, bf16[256,128]{1,0:T(8,128)(2,1)S(1)} %get-tuple-element.69.refs_2_, ...), custom_call_target="tpu_custom_call" | custom-call | tf_op jit(solution)/shard_map/output/pallas_call | solution.py:825
  24.4 1.0 %collective-permute-start.8 = (f32[64,256]{1,0:T(8,128)S(1)}, f32[64,256]{1,0:T(8,128)S(1)}, u32[]{:S(2)}, u32[]{:S(2)}) collective-permute-start(f32[64,256]{1,0:T(8,128)S(1)} %get-tuple-element.78), channel_id=1, source_target_pairs={{0,2},{2,6},{4,0},{6,4},{1,3},{3,7},{5,1},{7,5},{8,10},{10,14},{12... | collective-permute-start | bytes 196616 | tf_op jit(solution)/shard_map/ppermute | solution.py:849
  25.4 3.2 %collective-permute-start.9 = (f32[64,256]{1,0:T(8,128)S(1)}, f32[64,256]{1,0:T(8,128)S(1)}, u32[]{:S(2)}, u32[]{:S(2)}) collective-permute-start(f32[64,256]{1,0:T(8,128)S(1)} %get-tuple-element.79), channel_id=1, source_target_pairs={{0,6},{2,4},{4,2},{6,0},{1,7},{3,5},{5,3},{7,1},{8,14},{10,12},{12... | collective-permute-start | bytes 196616 | tf_op jit(solution)/shard_map/ppermute | solution.py:849
  28.6 1.3 %collective-permute-start.10 = (f32[64,256]{1,0:T(8,128)S(1)}, f32[64,256]{1,0:T(8,128)S(1)}, u32[]{:S(2)}, u32[]{:S(2)}) collective-permute-start(f32[64,256]{1,0:T(8,128)S(1)} %get-tuple-element.80), channel_id=1, source_target_pairs={{0,4},{2,0},{4,6},{6,2},{1,5},{3,1},{5,7},{7,3},{8,12},{10,8},{12,... | collective-permute-start | bytes 196616 | tf_op jit(solution)/shard_map/ppermute | solution.py:849
  29.9 3.1 %collective-permute-done.8 = f32[64,256]{1,0:T(8,128)S(1)} collective-permute-done((f32[64,256]{1,0:T(8,128)S(1)}, f32[64,256]{1,0:T(8,128)S(1)}, u32[]{:S(2)}, u32[]{:S(2)}) %collective-permute-start.8) | collective-permute-done | bytes 65568 | tf_op jit(solution)/shard_map/ppermute | solution.py:849
  33.0 0.0 collective-permute-done.9
  33.0 0.0 collective-permute-done.10
  33.1 0.6 %add_add_fusion = f32[64,256]{1,0:T(8,128)} fusion(f32[64,256]{1,0:T(8,128)S(1)} %collective-permute-done.10, f32[64,256]{1,0:T(8,128)S(1)} %collective-permute-done.9, f32[64,256]{1,0:T(8,128)S(1)} %get-tuple-element.77, f32[64,256]{1,0:T(8,128)S(1)} %collective-permute-done.8), kind=kLoop, calls=%fused_computation | loop fusion | flops 49152 | bytes 327680 | tf_op jit(solution)/shard_map/add | solution.py:849
  (1 shorter events, 0.0 us)
Async XLA Ops:
  1.4 11.6 %collective-permute-start.2 = (f32[168,128]{1,0:T(8,128)S(1)}, f32[168,128]{1,0:T(8,128)S(1)}, u32[]{:S(2)}, u32[]{:S(2)}) collective-permute-start(f32[168,128]{1,0:T(8,128)S(1)} %tables.1.refs_3_), channel_id=1, source_target_pairs={{0,20},{2,22},{4,16},{6,18},{8,28},{10,30},{12,24},{14,26},{16,4},... | collective-permute-start | bytes 258056 | tf_op jit(solution)/shard_map/ppermute | solution.py:719
  6.5 6.7 %collective-permute-start.1 = (f32[168,128]{1,0:T(8,128)S(1)}, f32[168,128]{1,0:T(8,128)S(1)}, u32[]{:S(2)}, u32[]{:S(2)}) collective-permute-start(f32[168,128]{1,0:T(8,128)S(1)} %tables.1.refs_3_), channel_id=1, source_target_pairs={{0,14},{2,12},{4,10},{6,8},{8,6},{10,4},{12,2},{14,0},{16,30},{18,... | collective-permute-start | bytes 258056 | tf_op jit(solution)/shard_map/ppermute | solution.py:719
  7.0 7.6 %collective-permute-start = (f32[168,128]{1,0:T(8,128)S(1)}, f32[168,128]{1,0:T(8,128)S(1)}, u32[]{:S(2)}, u32[]{:S(2)}) collective-permute-start(f32[168,128]{1,0:T(8,128)S(1)} %tables.1.refs_3_), channel_id=1, source_target_pairs={{0,26},{2,24},{4,30},{6,28},{8,18},{10,16},{12,22},{14,20},{16,10}... | collective-permute-start | bytes 258056 | tf_op jit(solution)/shard_map/ppermute | solution.py:719
  7.2 7.5 %copy-start = (f32[16,256]{1,0:T(8,128)S(1)}, f32[16,256]{1,0:T(8,128)}, u32[]{:S(2)}) copy-start(f32[16,256]{1,0:T(8,128)} %refs_4_.3) | copy-start | bytes 49156
  13.0 3.2 %collective-permute-start.5 = (f32[168,128]{1,0:T(8,128)S(1)}, f32[168,128]{1,0:T(8,128)S(1)}, u32[]{:S(2)}, u32[]{:S(2)}) collective-permute-start(f32[168,128]{1,0:T(8,128)S(1)} %collective-permute-done.2.refs_2_.refs_11_), channel_id=1, source_target_pairs={{0,8},{8,0},{16,24},{24,16},{1,9},{9,1},{17,25},{25,17},{2,10},{10... | collective-permute-start | bytes 258056 | tf_op jit(solution)/shard_map/ppermute | solution.py:722
  13.1 3.1 %collective-permute-start.4 = (f32[168,128]{1,0:T(8,128)S(1)}, f32[168,128]{1,0:T(8,128)S(1)}, u32[]{:S(2)}, u32[]{:S(2)}) collective-permute-start(f32[168,128]{1,0:T(8,128)S(1)} %collective-permute-done.1.refs_1_.refs_10_), channel_id=1, source_target_pairs={{0,8},{8,0},{16,24},{24,16},{1,9},{9,1},{17,25},{25,17},{2,10},{10... | collective-permute-start | bytes 258056 | tf_op jit(solution)/shard_map/ppermute | solution.py:722
  14.6 1.7 %collective-permute-start.3 = (f32[168,128]{1,0:T(8,128)S(1)}, f32[168,128]{1,0:T(8,128)S(1)}, u32[]{:S(2)}, u32[]{:S(2)}) collective-permute-start(f32[168,128]{1,0:T(8,128)S(1)} %collective-permute-done.refs_0_.refs_9_), channel_id=1, source_target_pairs={{0,8},{8,0},{16,24},{24,16},{1,9},{9,1},{17,25},{25,17},{2,10},{10... | collective-permute-start | bytes 258056 | tf_op jit(solution)/shard_map/ppermute | solution.py:722
  17.8 1.4 %collective-permute-start.6 = (f32[136,128]{1,0:T(8,128)S(1)}, f32[136,128]{1,0:T(8,128)S(1)}, u32[]{:S(2)}, u32[]{:S(2)}) collective-permute-start(f32[136,128]{1,0:T(8,128)S(1)} %get-tuple-element.56.refs_0_), channel_id=1, source_target_pairs={{0,8},{8,0},{16,24},{24,16},{1,9},{9,1},{17,25},{25,17},{2,10},{10... | collective-permute-start | bytes 208904 | tf_op jit(solution)/shard_map/ppermute | solution.py:803
  19.2 4.5 %collective-permute-start.7 = (f32[136,128]{1,0:T(8,128)S(1)}, f32[136,128]{1,0:T(8,128)S(1)}, u32[]{:S(2)}, u32[]{:S(2)}) collective-permute-start(f32[136,128]{1,0:T(8,128)S(1)} %get-tuple-element.58), channel_id=1, source_target_pairs={{0,16},{8,24},{16,0},{24,8},{1,17},{9,25},{17,1},{25,9},{2,18},{10... | collective-permute-start | bytes 208904 | tf_op jit(solution)/shard_map/ppermute | solution.py:803
  24.4 8.6 %collective-permute-start.8 = (f32[64,256]{1,0:T(8,128)S(1)}, f32[64,256]{1,0:T(8,128)S(1)}, u32[]{:S(2)}, u32[]{:S(2)}) collective-permute-start(f32[64,256]{1,0:T(8,128)S(1)} %get-tuple-element.78), channel_id=1, source_target_pairs={{0,2},{2,6},{4,0},{6,4},{1,3},{3,7},{5,1},{7,5},{8,10},{10,14},{12... | collective-permute-start | bytes 196616 | tf_op jit(solution)/shard_map/ppermute | solution.py:849
  25.4 7.6 %collective-permute-start.9 = (f32[64,256]{1,0:T(8,128)S(1)}, f32[64,256]{1,0:T(8,128)S(1)}, u32[]{:S(2)}, u32[]{:S(2)}) collective-permute-start(f32[64,256]{1,0:T(8,128)S(1)} %get-tuple-element.79), channel_id=1, source_target_pairs={{0,6},{2,4},{4,2},{6,0},{1,7},{3,5},{5,3},{7,1},{8,14},{10,12},{12... | collective-permute-start | bytes 196616 | tf_op jit(solution)/shard_map/ppermute | solution.py:849
  28.6 4.5 %collective-permute-start.10 = (f32[64,256]{1,0:T(8,128)S(1)}, f32[64,256]{1,0:T(8,128)S(1)}, u32[]{:S(2)}, u32[]{:S(2)}) collective-permute-start(f32[64,256]{1,0:T(8,128)S(1)} %get-tuple-element.80), channel_id=1, source_target_pairs={{0,4},{2,0},{4,6},{6,2},{1,5},{3,1},{5,7},{7,3},{8,12},{10,8},{12,... | collective-permute-start | bytes 196616 | tf_op jit(solution)/shard_map/ppermute | solution.py:849

commit v21 on v19

--- a/solution.py
+++ b/solution.py
@@ -25,8 +25,11 @@
     return list(range(1, count))
 
 
-def in_turn(count):
-    return sorted(range(1, count), key=lambda k: (-k.bit_length(), k))
+def around(shift, count):
+    ring = [place ^ place >> 1 for place in range(count)]
+    if sorted(ring) != list(range(count)):
+        ring = list(range(count))
+    return [ring[(ring.index(plane) + shift) % count] for plane in range(count)]
 
 
 def iota(shape, axis):
@@ -559,7 +562,10 @@
     partial_ref[...] = dot_split(split2(value), (proj_high[...], proj_low[...]))
     mine = lax.axis_index("head")
     for k in range(nh):
-        place = pl.multiple_of(lax.bitwise_xor(mine, k) * share, 8)
+        to = 0
+        for plane, target in enumerate(around(k, nh)):
+            to = jnp.where(mine == plane, target, to)
+        place = pl.multiple_of(to * share, 8)
         part = partial_ref[pl.ds(place, share), :]
         outs[k][...] = part + own[...] if k == 0 else part
 
@@ -837,8 +843,8 @@
         groups,
     )
     result = parts[0]
-    for k in in_turn(nh):
-        pairs = [(source, source ^ k) for source in range(nh)]
+    for k in range(1, nh):
+        pairs = list(enumerate(around(k, nh)))
         result = result + lax.ppermute(parts[k], "head", pairs)
     return result
 

time: 34.2 us -> 33.7 us (0.985)
  waiting for transfers between devices: 12 us -> 10.5 us
  starting transfers between devices: 13 us -> 14 us
    ppermute x3, waiting for transfers between devices: 4.52 us -> 3.02 us  [per_device(): result = result + lax.ppermute(parts[k], 'head', pairs)]
    ppermute x3, starting transfers between devices: 4.54 us -> 5.53 us  [per_device(): result = result + lax.ppermute(parts[k], 'head', pairs)]
  transfers between devices with their start and end apart: 11 -> 11, of which waited for: 6 -> 7; matrix products, arithmetic and copies ran while one was open for 0% -> 0% of each run, Pallas kernels for 14% -> 14%
where the time goes in v21:
time: 33.7 us; the launch traced here: 33.6 us
  starting transfers between devices  14 us (42%)
  waiting for transfers between devices  10.5 us (31%)
  Pallas kernels  8.4 us (25%)
  other arithmetic  0.65 us (2%)
    ppermute x3, starting transfers between devices, per_device(): messages[k] = lax.ppermute(sent, ('seq', 'head'), pairs)  7.39 us
    ppermute x3, starting transfers between devices, per_device(): result = result + lax.ppermute(parts[k], 'head', pairs)  5.53 us
    ppermute x2, waiting for transfers between devices, per_device(): lax.ppermute(state, 'seq', [(seq, seq ^ 2 ** bit) for seq in range(ns)])  4.16 us
    ppermute x3, waiting for transfers between devices, per_device(): messages[k] = lax.ppermute(sent, ('seq', 'head'), pairs)  3.29 us
    ppermute x3, waiting for transfers between devices, per_device(): result = result + lax.ppermute(parts[k], 'head', pairs)  3.02 us
    pallas_call x1, Pallas kernels, per_device(): pl.pallas_call(functools.partial(prepare_kernel, dims), out_shape=(shape(...  2.08 us
    pallas_call x1, Pallas kernels, per_device(): pl.pallas_call(functools.partial(mix_kernel, dims), out_shape=(*halves(T,...  1.59 us
    pallas_call x1, Pallas kernels, per_device(): pl.pallas_call(functools.partial(project_kernel, dims), out_shape=(shape(...  1.51 us
  transfers between devices with their start and end apart: 11, of which 7 were waited for; matrix products, arithmetic and copies ran while one was open for 0% of the time, Pallas kernels for 14%

profile of v21, /device:TPU:0, one launch (start us, length us, event | category | flops | bytes accessed | tf_op | source)
XLA Modules:
  0.0 33.6 jit_solution(6925184257021374165)
XLA Ops:
  0.0 1.4 %tables.1.refs_3_ = f32[168,128]{1,0:T(8,128)S(1)} custom-call(f32[512,128]{1,0:T(8,128)} %bitcast.18, s32[1,256]{1,0:T(1,128)} %bitcast.20, f32[16,256]{1,0:T(8,128)} %refs_4_.3, f32[1,256]{1,0:T(1,128)} %bitcast.21, f32[2,256]{1,0:T(2,128)} %bitcast.19, f32[1,2]{1,0:T(1,128)} %bitcast.23, f32[1,2]{1,0:T(1,128)} %bitcast.24, f32[1,2]{1,0:T(1,128)} %bitcast.25, ...), custom_call_target="tpu_custom_call" | custom-call | tf_op jit(solution)/shard_map/tables/pallas_call | solution.py:641
  1.4 2.5 %collective-permute-start.2 = (f32[168,128]{1,0:T(8,128)S(1)}, f32[168,128]{1,0:T(8,128)S(1)}, u32[]{:S(2)}, u32[]{:S(2)}) collective-permute-start(f32[168,128]{1,0:T(8,128)S(1)} %tables.1.refs_3_), channel_id=1, source_target_pairs={{0,10},{2,12},{4,14},{6,8},{8,2},{10,4},{12,6},{14,0},{16,26},{18,... | collective-permute-start | bytes 258056 | tf_op jit(solution)/shard_map/ppermute | solution.py:718
  4.0 3.5 %collective-permute-start.1 = (f32[168,128]{1,0:T(8,128)S(1)}, f32[168,128]{1,0:T(8,128)S(1)}, u32[]{:S(2)}, u32[]{:S(2)}) collective-permute-start(f32[168,128]{1,0:T(8,128)S(1)} %tables.1.refs_3_), channel_id=1, source_target_pairs={{0,20},{2,22},{4,16},{6,18},{8,28},{10,30},{12,24},{14,26},{16,4},... | collective-permute-start | bytes 258056 | tf_op jit(solution)/shard_map/ppermute | solution.py:718
  7.5 1.4 %collective-permute-start = (f32[168,128]{1,0:T(8,128)S(1)}, f32[168,128]{1,0:T(8,128)S(1)}, u32[]{:S(2)}, u32[]{:S(2)}) collective-permute-start(f32[168,128]{1,0:T(8,128)S(1)} %tables.1.refs_3_), channel_id=1, source_target_pairs={{0,30},{2,24},{4,26},{6,28},{8,22},{10,16},{12,18},{14,20},{16,14}... | collective-permute-start | bytes 258056 | tf_op jit(solution)/shard_map/ppermute | solution.py:718
  8.8 0.0 copy-start
  8.8 2.1 %prepare.1 = (f32[16,128]{1,0:T(8,128)S(1)}, f32[8,128]{1,0:T(8,128)S(1)}, bf16[256,256]{1,0:T(8,128)(2,1)S(1)}, bf16[128,256]{1,0:T(8,128)(2,1)S(1)}, bf16[128,...) custom-call(f32[512,128]{1,0:T(8,128)} %bitcast.27, ...), custom_call_target="tpu_custom_call" | custom-call | flops 16106127360 | bytes 262144 | tf_op jit(solution)/shard_map/prepare/pallas_call | solution.py:684
  10.9 0.0 collective-permute-done.2.refs_2_.refs_11_
  10.9 0.1 collective-permute-start.5
  11.1 3.2 %collective-permute-done.1.refs_1_.refs_10_ = f32[168,128]{1,0:T(8,128)S(1)} collective-permute-done((f32[168,128]{1,0:T(8,128)S(1)}, f32[168,128]{1,0:T(8,128)S(1)}, u32[]{:S(2)}, u32[]{:S(2)}) %collective-permute-start.1) | collective-permute-done | bytes 86048 | tf_op jit(solution)/shard_map/ppermute | solution.py:718
  14.3 0.0 collective-permute-start.4
  14.3 0.1 collective-permute-done.refs_0_.refs_9_
  14.4 0.4 %collective-permute-start.3 = (f32[168,128]{1,0:T(8,128)S(1)}, f32[168,128]{1,0:T(8,128)S(1)}, u32[]{:S(2)}, u32[]{:S(2)}) collective-permute-start(f32[168,128]{1,0:T(8,128)S(1)} %collective-permute-done.refs_0_.refs_9_), channel_id=1, source_target_pairs={{0,8},{8,0},{16,24},{24,16},{1,9},{9,1},{17,25},{25,17},{2,10},{10... | collective-permute-start | bytes 258056 | tf_op jit(solution)/shard_map/ppermute | solution.py:721
  14.8 0.0 copy-done
  14.8 1.6 %mix.1 = (bf16[256,512]{1,0:T(8,128)(2,1)S(1)}, bf16[256,512]{1,0:T(8,128)(2,1)S(1)}, f32[256,256]{1,0:T(8,128)S(1)}) custom-call(f32[168,128]{1,0:T(8,128)S(1)} %collective-permute-done.refs_0_.refs_9_, f32[168,128]{1,0:T(8,128)S(1)} %collective-permute-done.1.refs_1_.refs_10_, f32[168,128]{1,0:T(8,128)S(1)} %collective-permute-done.2.refs_2_.refs_11_, ...), custom_call_target="tpu_custom_call" | custom-call | flops 16106127360 | bytes 262144 | tf_op jit(solution)/shard_map/mix/pallas_call | solution.py:723
  16.4 0.0 collective-permute-done.5.refs_14_
  16.4 0.0 collective-permute-done.4.refs_13_
  16.4 0.0 collective-permute-done.3.refs_12_
  16.4 1.5 %project.1 = (f32[136,128]{1,0:T(8,128)S(1)}, bf16[256,256]{1,0:T(8,128)(2,1)S(1)}, bf16[256,256]{1,0:T(8,128)(2,1)S(1)}, f32[256,128]{1,0:T(8,128)S(1)}, f32[25...) custom-call(bf16[256,512]{1,0:T(8,128)(2,1)S(1)} %get-tuple-element.47.refs_0_, ...), custom_call_target="tpu_custom_call" | custom-call | tf_op jit(solution)/shard_map/project/pallas_call | solution.py:741
  17.9 0.2 collective-permute-start.6
  18.1 1.2 %collective-permute-done.6.refs_1_ = f32[136,128]{1,0:T(8,128)S(1)} collective-permute-done((f32[136,128]{1,0:T(8,128)S(1)}, f32[136,128]{1,0:T(8,128)S(1)}, u32[]{:S(2)}, u32[]{:S(2)}) %collective-permute-start.6) | collective-permute-done | bytes 69664 | tf_op jit(solution)/shard_map/ppermute | solution.py:802
  19.3 0.3 collective-permute-start.7
  19.6 1.1 %block.1 = (f32[256,128]{1,0:T(8,128)S(1)}, bf16[256,128]{1,0:T(8,128)(2,1)S(1)}, bf16[256,128]{1,0:T(8,128)(2,1)S(1)}, f32[256,128]{1,0:T(8,128)S(1)}, f32[256,128]{1,0:T(8,128)S(1)}, /*index=5*/f32[64,256]{1,0:T(8,128)S(1)}) custom-call(bf16[256,256]{1,0:T(8,128)(2,1)S(1)} %get-tuple-element.59.refs_0_, bf16[256,256]{1,0:T(8,128)(2,1)S(1)} %get-tuple-element.60.refs_1_, ...), custom_call_target="tpu_custom_call" | custom-call | flops 16106127360 | bytes 262144 | tf_op jit(solution)/shard_map/block/pallas_call | solution.py:770
  20.7 3.0 %collective-permute-done.7.refs_1_ = f32[136,128]{1,0:T(8,128)S(1)} collective-permute-done((f32[136,128]{1,0:T(8,128)S(1)}, f32[136,128]{1,0:T(8,128)S(1)}, u32[]{:S(2)}, u32[]{:S(2)}) %collective-permute-start.7) | collective-permute-done | bytes 69664 | tf_op jit(solution)/shard_map/ppermute | solution.py:802
  23.7 0.7 %output.1 = (f32[64,256]{1,0:T(8,128)S(1)}, f32[64,256]{1,0:T(8,128)S(1)}, f32[64,256]{1,0:T(8,128)S(1)}, f32[64,256]{1,0:T(8,128)S(1)}) custom-call(f32[136,128]{1,0:T(8,128)S(1)} %get-tuple-element.57.refs_0_, f32[136,128]{1,0:T(8,128)S(1)} %collective-permute-done.7.refs_1_, bf16[256,128]{1,0:T(8,128)(2,1)S(1)} %get-tuple-element.69.refs_2_, ...), custom_call_target="tpu_custom_call" | custom-call | tf_op jit(solution)/shard_map/output/pallas_call | solution.py:824
  24.4 2.2 %collective-permute-start.8 = (f32[64,256]{1,0:T(8,128)S(1)}, f32[64,256]{1,0:T(8,128)S(1)}, u32[]{:S(2)}, u32[]{:S(2)}) collective-permute-start(f32[64,256]{1,0:T(8,128)S(1)} %get-tuple-element.78), channel_id=1, source_target_pairs={{0,2},{2,6},{4,0},{6,4},{1,3},{3,7},{5,1},{7,5},{8,10},{10,14},{12... | collective-permute-start | bytes 196616 | tf_op jit(solution)/shard_map/ppermute | solution.py:848
  26.5 1.4 %collective-permute-start.9 = (f32[64,256]{1,0:T(8,128)S(1)}, f32[64,256]{1,0:T(8,128)S(1)}, u32[]{:S(2)}, u32[]{:S(2)}) collective-permute-start(f32[64,256]{1,0:T(8,128)S(1)} %get-tuple-element.79), channel_id=1, source_target_pairs={{0,6},{2,4},{4,2},{6,0},{1,7},{3,5},{5,3},{7,1},{8,14},{10,12},{12... | collective-permute-start | bytes 196616 | tf_op jit(solution)/shard_map/ppermute | solution.py:848
  28.0 1.9 %collective-permute-start.10 = (f32[64,256]{1,0:T(8,128)S(1)}, f32[64,256]{1,0:T(8,128)S(1)}, u32[]{:S(2)}, u32[]{:S(2)}) collective-permute-start(f32[64,256]{1,0:T(8,128)S(1)} %get-tuple-element.80), channel_id=1, source_target_pairs={{0,4},{2,0},{4,6},{6,2},{1,5},{3,1},{5,7},{7,3},{8,12},{10,8},{12,... | collective-permute-start | bytes 196616 | tf_op jit(solution)/shard_map/ppermute | solution.py:848
  29.9 0.1 collective-permute-done.8
  30.0 2.7 %collective-permute-done.9 = f32[64,256]{1,0:T(8,128)S(1)} collective-permute-done((f32[64,256]{1,0:T(8,128)S(1)}, f32[64,256]{1,0:T(8,128)S(1)}, u32[]{:S(2)}, u32[]{:S(2)}) %collective-permute-start.9) | collective-permute-done | bytes 65568 | tf_op jit(solution)/shard_map/ppermute | solution.py:848
  32.7 0.2 collective-permute-done.10
  32.9 0.6 %add_add_fusion = f32[64,256]{1,0:T(8,128)} fusion(f32[64,256]{1,0:T(8,128)S(1)} %collective-permute-done.10, f32[64,256]{1,0:T(8,128)S(1)} %collective-permute-done.9, f32[64,256]{1,0:T(8,128)S(1)} %get-tuple-element.77, f32[64,256]{1,0:T(8,128)S(1)} %collective-permute-done.8), kind=kLoop, calls=%fused_computation | loop fusion | flops 49152 | bytes 327680 | tf_op jit(solution)/shard_map/add | solution.py:848
  (1 shorter events, 0.0 us)
Async XLA Ops:
  1.4 9.5 %collective-permute-start.2 = (f32[168,128]{1,0:T(8,128)S(1)}, f32[168,128]{1,0:T(8,128)S(1)}, u32[]{:S(2)}, u32[]{:S(2)}) collective-permute-start(f32[168,128]{1,0:T(8,128)S(1)} %tables.1.refs_3_), channel_id=1, source_target_pairs={{0,10},{2,12},{4,14},{6,8},{8,2},{10,4},{12,6},{14,0},{16,26},{18,... | collective-permute-start | bytes 258056 | tf_op jit(solution)/shard_map/ppermute | solution.py:718
  4.0 10.3 %collective-permute-start.1 = (f32[168,128]{1,0:T(8,128)S(1)}, f32[168,128]{1,0:T(8,128)S(1)}, u32[]{:S(2)}, u32[]{:S(2)}) collective-permute-start(f32[168,128]{1,0:T(8,128)S(1)} %tables.1.refs_3_), channel_id=1, source_target_pairs={{0,20},{2,22},{4,16},{6,18},{8,28},{10,30},{12,24},{14,26},{16,4},... | collective-permute-start | bytes 258056 | tf_op jit(solution)/shard_map/ppermute | solution.py:718
  7.5 6.9 %collective-permute-start = (f32[168,128]{1,0:T(8,128)S(1)}, f32[168,128]{1,0:T(8,128)S(1)}, u32[]{:S(2)}, u32[]{:S(2)}) collective-permute-start(f32[168,128]{1,0:T(8,128)S(1)} %tables.1.refs_3_), channel_id=1, source_target_pairs={{0,30},{2,24},{4,26},{6,28},{8,22},{10,16},{12,18},{14,20},{16,14}... | collective-permute-start | bytes 258056 | tf_op jit(solution)/shard_map/ppermute | solution.py:718
  8.8 6.0 %copy-start = (f32[16,256]{1,0:T(8,128)S(1)}, f32[16,256]{1,0:T(8,128)}, u32[]{:S(2)}) copy-start(f32[16,256]{1,0:T(8,128)} %refs_4_.3) | copy-start | bytes 49156
  10.9 5.5 %collective-permute-start.5 = (f32[168,128]{1,0:T(8,128)S(1)}, f32[168,128]{1,0:T(8,128)S(1)}, u32[]{:S(2)}, u32[]{:S(2)}) collective-permute-start(f32[168,128]{1,0:T(8,128)S(1)} %collective-permute-done.2.refs_2_.refs_11_), channel_id=1, source_target_pairs={{0,8},{8,0},{16,24},{24,16},{1,9},{9,1},{17,25},{25,17},{2,10},{10... | collective-permute-start | bytes 258056 | tf_op jit(solution)/shard_map/ppermute | solution.py:721
  14.3 2.1 %collective-permute-start.4 = (f32[168,128]{1,0:T(8,128)S(1)}, f32[168,128]{1,0:T(8,128)S(1)}, u32[]{:S(2)}, u32[]{:S(2)}) collective-permute-start(f32[168,128]{1,0:T(8,128)S(1)} %collective-permute-done.1.refs_1_.refs_10_), channel_id=1, source_target_pairs={{0,8},{8,0},{16,24},{24,16},{1,9},{9,1},{17,25},{25,17},{2,10},{10... | collective-permute-start | bytes 258056 | tf_op jit(solution)/shard_map/ppermute | solution.py:721
  14.4 2.0 %collective-permute-start.3 = (f32[168,128]{1,0:T(8,128)S(1)}, f32[168,128]{1,0:T(8,128)S(1)}, u32[]{:S(2)}, u32[]{:S(2)}) collective-permute-start(f32[168,128]{1,0:T(8,128)S(1)} %collective-permute-done.refs_0_.refs_9_), channel_id=1, source_target_pairs={{0,8},{8,0},{16,24},{24,16},{1,9},{9,1},{17,25},{25,17},{2,10},{10... | collective-permute-start | bytes 258056 | tf_op jit(solution)/shard_map/ppermute | solution.py:721
  17.9 1.3 %collective-permute-start.6 = (f32[136,128]{1,0:T(8,128)S(1)}, f32[136,128]{1,0:T(8,128)S(1)}, u32[]{:S(2)}, u32[]{:S(2)}) collective-permute-start(f32[136,128]{1,0:T(8,128)S(1)} %get-tuple-element.56.refs_0_), channel_id=1, source_target_pairs={{0,8},{8,0},{16,24},{24,16},{1,9},{9,1},{17,25},{25,17},{2,10},{10... | collective-permute-start | bytes 208904 | tf_op jit(solution)/shard_map/ppermute | solution.py:802
  19.3 4.4 %collective-permute-start.7 = (f32[136,128]{1,0:T(8,128)S(1)}, f32[136,128]{1,0:T(8,128)S(1)}, u32[]{:S(2)}, u32[]{:S(2)}) collective-permute-start(f32[136,128]{1,0:T(8,128)S(1)} %get-tuple-element.58), channel_id=1, source_target_pairs={{0,16},{8,24},{16,0},{24,8},{1,17},{9,25},{17,1},{25,9},{2,18},{10... | collective-permute-start | bytes 208904 | tf_op jit(solution)/shard_map/ppermute | solution.py:802
  24.4 5.6 %collective-permute-start.8 = (f32[64,256]{1,0:T(8,128)S(1)}, f32[64,256]{1,0:T(8,128)S(1)}, u32[]{:S(2)}, u32[]{:S(2)}) collective-permute-start(f32[64,256]{1,0:T(8,128)S(1)} %get-tuple-element.78), channel_id=1, source_target_pairs={{0,2},{2,6},{4,0},{6,4},{1,3},{3,7},{5,1},{7,5},{8,10},{10,14},{12... | collective-permute-start | bytes 196616 | tf_op jit(solution)/shard_map/ppermute | solution.py:848
  26.5 6.2 %collective-permute-start.9 = (f32[64,256]{1,0:T(8,128)S(1)}, f32[64,256]{1,0:T(8,128)S(1)}, u32[]{:S(2)}, u32[]{:S(2)}) collective-permute-start(f32[64,256]{1,0:T(8,128)S(1)} %get-tuple-element.79), channel_id=1, source_target_pairs={{0,6},{2,4},{4,2},{6,0},{1,7},{3,5},{5,3},{7,1},{8,14},{10,12},{12... | collective-permute-start | bytes 196616 | tf_op jit(solution)/shard_map/ppermute | solution.py:848
  28.0 5.0 %collective-permute-start.10 = (f32[64,256]{1,0:T(8,128)S(1)}, f32[64,256]{1,0:T(8,128)S(1)}, u32[]{:S(2)}, u32[]{:S(2)}) collective-permute-start(f32[64,256]{1,0:T(8,128)S(1)} %get-tuple-element.80), channel_id=1, source_target_pairs={{0,4},{2,0},{4,6},{6,2},{1,5},{3,1},{5,7},{7,3},{8,12},{10,8},{12,... | collective-permute-start | bytes 196616 | tf_op jit(solution)/shard_map/ppermute | solution.py:848

commit v22 on v21

--- a/solution.py
+++ b/solution.py
@@ -18,7 +18,10 @@
 
 
 def partners(ns, nh):
-    return [(k if k < ns else 0, k if k < nh else 0) for k in range(max(ns, nh))]
+    return [
+        ((k + 1) % (ns - 1) + 1 if 0 < k < ns else 0, k if k < nh else 0)
+        for k in range(max(ns, nh))
+    ]
 
 
 def first_turn(count):

time: 33.7 us -> 34 us (level)
  transfers between devices with their start and end apart: 11 -> 11, of which waited for: 7 -> 5; matrix products, arithmetic and copies ran while one was open for 0% -> 0% of each run, Pallas kernels for 14% -> 14%
where the time goes in v22:
time: 34 us; the launch traced here: 33.8 us
  starting transfers between devices  13.9 us (41%)
  waiting for transfers between devices  10.7 us (31%)
  Pallas kernels  8.41 us (25%)
  other arithmetic  0.65 us (2%)
    ppermute x3, starting transfers between devices, per_device(): messages[k] = lax.ppermute(sent, ('seq', 'head'), pairs)  7.63 us
    ppermute x3, starting transfers between devices, per_device(): result = result + lax.ppermute(parts[k], 'head', pairs)  5.34 us
    ppermute x2, waiting for transfers between devices, per_device(): lax.ppermute(state, 'seq', [(seq, seq ^ 2 ** bit) for seq in range(ns)])  4.24 us
    ppermute x3, waiting for transfers between devices, per_device(): result = result + lax.ppermute(parts[k], 'head', pairs)  3.27 us
    ppermute x3, waiting for transfers between devices, per_device(): messages[k] = lax.ppermute(sent, ('seq', 'head'), pairs)  3.19 us
    pallas_call x1, Pallas kernels, per_device(): pl.pallas_call(functools.partial(prepare_kernel, dims), out_shape=(shape(...  2.07 us
    pallas_call x1, Pallas kernels, per_device(): pl.pallas_call(functools.partial(mix_kernel, dims), out_shape=(*halves(T,...  1.59 us
    pallas_call x1, Pallas kernels, per_device(): pl.pallas_call(functools.partial(project_kernel, dims), out_shape=(shape(...  1.51 us
  transfers between devices with their start and end apart: 11, of which 5 were waited for; matrix products, arithmetic and copies ran while one was open for 0% of the time, Pallas kernels for 14%

profile of v22, /device:TPU:0, one launch (start us, length us, event | category | flops | bytes accessed | tf_op | source)
XLA Modules:
  0.0 33.8 jit_solution(1638833922792566607)
XLA Ops:
  0.0 1.4 %tables.1.refs_3_ = f32[168,128]{1,0:T(8,128)S(1)} custom-call(f32[512,128]{1,0:T(8,128)} %bitcast.18, s32[1,256]{1,0:T(1,128)} %bitcast.20, f32[16,256]{1,0:T(8,128)} %refs_4_.3, f32[1,256]{1,0:T(1,128)} %bitcast.21, f32[2,256]{1,0:T(2,128)} %bitcast.19, f32[1,2]{1,0:T(1,128)} %bitcast.23, f32[1,2]{1,0:T(1,128)} %bitcast.24, f32[1,2]{1,0:T(1,128)} %bitcast.25, ...), custom_call_target="tpu_custom_call" | custom-call | tf_op jit(solution)/shard_map/tables/pallas_call | solution.py:644
  1.4 3.4 %collective-permute-start.2 = (f32[168,128]{1,0:T(8,128)S(1)}, f32[168,128]{1,0:T(8,128)S(1)}, u32[]{:S(2)}, u32[]{:S(2)}) collective-permute-start(f32[168,128]{1,0:T(8,128)S(1)} %tables.1.refs_3_), channel_id=1, source_target_pairs={{0,26},{2,28},{4,30},{6,24},{8,18},{10,20},{12,22},{14,16},{16,10}... | collective-permute-start | bytes 258056 | tf_op jit(solution)/shard_map/ppermute | solution.py:721
  4.9 2.9 %collective-permute-start.1 = (f32[168,128]{1,0:T(8,128)S(1)}, f32[168,128]{1,0:T(8,128)S(1)}, u32[]{:S(2)}, u32[]{:S(2)}) collective-permute-start(f32[168,128]{1,0:T(8,128)S(1)} %tables.1.refs_3_), channel_id=1, source_target_pairs={{0,12},{2,14},{4,8},{6,10},{8,4},{10,6},{12,0},{14,2},{16,28},{18,... | collective-permute-start | bytes 258056 | tf_op jit(solution)/shard_map/ppermute | solution.py:721
  7.8 1.3 %collective-permute-start = (f32[168,128]{1,0:T(8,128)S(1)}, f32[168,128]{1,0:T(8,128)S(1)}, u32[]{:S(2)}, u32[]{:S(2)}) collective-permute-start(f32[168,128]{1,0:T(8,128)S(1)} %tables.1.refs_3_), channel_id=1, source_target_pairs={{0,22},{2,16},{4,18},{6,20},{8,30},{10,24},{12,26},{14,28},{16,6},... | collective-permute-start | bytes 258056 | tf_op jit(solution)/shard_map/ppermute | solution.py:721
  9.1 0.0 copy-start
  9.1 2.1 %prepare.1 = (f32[16,128]{1,0:T(8,128)S(1)}, f32[8,128]{1,0:T(8,128)S(1)}, bf16[256,256]{1,0:T(8,128)(2,1)S(1)}, bf16[128,256]{1,0:T(8,128)(2,1)S(1)}, bf16[128,...) custom-call(f32[512,128]{1,0:T(8,128)} %bitcast.27, ...), custom_call_target="tpu_custom_call" | custom-call | flops 16106127360 | bytes 262144 | tf_op jit(solution)/shard_map/prepare/pallas_call | solution.py:687
  11.2 0.0 collective-permute-done.2.refs_2_.refs_11_
  11.2 0.1 collective-permute-start.5
  11.2 2.9 %collective-permute-done.1.refs_1_.refs_10_ = f32[168,128]{1,0:T(8,128)S(1)} collective-permute-done((f32[168,128]{1,0:T(8,128)S(1)}, f32[168,128]{1,0:T(8,128)S(1)}, u32[]{:S(2)}, u32[]{:S(2)}) %collective-permute-start.1) | collective-permute-done | bytes 86048 | tf_op jit(solution)/shard_map/ppermute | solution.py:721
  14.1 0.2 collective-permute-start.4
  14.4 0.3 collective-permute-done.refs_0_.refs_9_
  14.7 0.0 collective-permute-start.3
  14.7 0.0 copy-done
  14.7 1.6 %mix.1 = (bf16[256,512]{1,0:T(8,128)(2,1)S(1)}, bf16[256,512]{1,0:T(8,128)(2,1)S(1)}, f32[256,256]{1,0:T(8,128)S(1)}) custom-call(f32[168,128]{1,0:T(8,128)S(1)} %collective-permute-done.refs_0_.refs_9_, f32[168,128]{1,0:T(8,128)S(1)} %collective-permute-done.1.refs_1_.refs_10_, f32[168,128]{1,0:T(8,128)S(1)} %collective-permute-done.2.refs_2_.refs_11_, ...), custom_call_target="tpu_custom_call" | custom-call | flops 16106127360 | bytes 262144 | tf_op jit(solution)/shard_map/mix/pallas_call | solution.py:726
  16.3 0.0 collective-permute-done.5.refs_14_
  16.3 0.0 collective-permute-done.4.refs_13_
  16.3 0.0 collective-permute-done.3.refs_12_
  16.3 1.5 %project.1 = (f32[136,128]{1,0:T(8,128)S(1)}, bf16[256,256]{1,0:T(8,128)(2,1)S(1)}, bf16[256,256]{1,0:T(8,128)(2,1)S(1)}, f32[256,128]{1,0:T(8,128)S(1)}, f32[25...) custom-call(bf16[256,512]{1,0:T(8,128)(2,1)S(1)} %get-tuple-element.47.refs_0_, ...), custom_call_target="tpu_custom_call" | custom-call | tf_op jit(solution)/shard_map/project/pallas_call | solution.py:744
  17.8 0.6 %collective-permute-start.6 = (f32[136,128]{1,0:T(8,128)S(1)}, f32[136,128]{1,0:T(8,128)S(1)}, u32[]{:S(2)}, u32[]{:S(2)}) collective-permute-start(f32[136,128]{1,0:T(8,128)S(1)} %get-tuple-element.56.refs_0_), channel_id=1, source_target_pairs={{0,8},{8,0},{16,24},{24,16},{1,9},{9,1},{17,25},{25,17},{2,10},{10... | collective-permute-start | bytes 208904 | tf_op jit(solution)/shard_map/ppermute | solution.py:805
  18.4 0.9 %collective-permute-done.6.refs_1_ = f32[136,128]{1,0:T(8,128)S(1)} collective-permute-done((f32[136,128]{1,0:T(8,128)S(1)}, f32[136,128]{1,0:T(8,128)S(1)}, u32[]{:S(2)}, u32[]{:S(2)}) %collective-permute-start.6) | collective-permute-done | bytes 69664 | tf_op jit(solution)/shard_map/ppermute | solution.py:805
  19.3 0.1 collective-permute-start.7
  19.4 1.1 %block.1 = (f32[256,128]{1,0:T(8,128)S(1)}, bf16[256,128]{1,0:T(8,128)(2,1)S(1)}, bf16[256,128]{1,0:T(8,128)(2,1)S(1)}, f32[256,128]{1,0:T(8,128)S(1)}, f32[256,128]{1,0:T(8,128)S(1)}, /*index=5*/f32[64,256]{1,0:T(8,128)S(1)}) custom-call(bf16[256,256]{1,0:T(8,128)(2,1)S(1)} %get-tuple-element.59.refs_0_, bf16[256,256]{1,0:T(8,128)(2,1)S(1)} %get-tuple-element.60.refs_1_, ...), custom_call_target="tpu_custom_call" | custom-call | flops 16106127360 | bytes 262144 | tf_op jit(solution)/shard_map/block/pallas_call | solution.py:773
  20.5 3.3 %collective-permute-done.7.refs_1_ = f32[136,128]{1,0:T(8,128)S(1)} collective-permute-done((f32[136,128]{1,0:T(8,128)S(1)}, f32[136,128]{1,0:T(8,128)S(1)}, u32[]{:S(2)}, u32[]{:S(2)}) %collective-permute-start.7) | collective-permute-done | bytes 69664 | tf_op jit(solution)/shard_map/ppermute | solution.py:805
  23.8 0.7 %output.1 = (f32[64,256]{1,0:T(8,128)S(1)}, f32[64,256]{1,0:T(8,128)S(1)}, f32[64,256]{1,0:T(8,128)S(1)}, f32[64,256]{1,0:T(8,128)S(1)}) custom-call(f32[136,128]{1,0:T(8,128)S(1)} %get-tuple-element.57.refs_0_, f32[136,128]{1,0:T(8,128)S(1)} %collective-permute-done.7.refs_1_, bf16[256,128]{1,0:T(8,128)(2,1)S(1)} %get-tuple-element.69.refs_2_, ...), custom_call_target="tpu_custom_call" | custom-call | tf_op jit(solution)/shard_map/output/pallas_call | solution.py:827
  24.5 1.7 %collective-permute-start.8 = (f32[64,256]{1,0:T(8,128)S(1)}, f32[64,256]{1,0:T(8,128)S(1)}, u32[]{:S(2)}, u32[]{:S(2)}) collective-permute-start(f32[64,256]{1,0:T(8,128)S(1)} %get-tuple-element.78), channel_id=1, source_target_pairs={{0,2},{2,6},{4,0},{6,4},{1,3},{3,7},{5,1},{7,5},{8,10},{10,14},{12... | collective-permute-start | bytes 196616 | tf_op jit(solution)/shard_map/ppermute | solution.py:851
  26.2 1.7 %collective-permute-start.9 = (f32[64,256]{1,0:T(8,128)S(1)}, f32[64,256]{1,0:T(8,128)S(1)}, u32[]{:S(2)}, u32[]{:S(2)}) collective-permute-start(f32[64,256]{1,0:T(8,128)S(1)} %get-tuple-element.79), channel_id=1, source_target_pairs={{0,6},{2,4},{4,2},{6,0},{1,7},{3,5},{5,3},{7,1},{8,14},{10,12},{12... | collective-permute-start | bytes 196616 | tf_op jit(solution)/shard_map/ppermute | solution.py:851
  27.9 1.9 %collective-permute-start.10 = (f32[64,256]{1,0:T(8,128)S(1)}, f32[64,256]{1,0:T(8,128)S(1)}, u32[]{:S(2)}, u32[]{:S(2)}) collective-permute-start(f32[64,256]{1,0:T(8,128)S(1)} %get-tuple-element.80), channel_id=1, source_target_pairs={{0,4},{2,0},{4,6},{6,2},{1,5},{3,1},{5,7},{7,3},{8,12},{10,8},{12,... | collective-permute-start | bytes 196616 | tf_op jit(solution)/shard_map/ppermute | solution.py:851
  29.9 3.3 %collective-permute-done.8 = f32[64,256]{1,0:T(8,128)S(1)} collective-permute-done((f32[64,256]{1,0:T(8,128)S(1)}, f32[64,256]{1,0:T(8,128)S(1)}, u32[]{:S(2)}, u32[]{:S(2)}) %collective-permute-start.8) | collective-permute-done | bytes 65568 | tf_op jit(solution)/shard_map/ppermute | solution.py:851
  33.2 0.0 collective-permute-done.9
  33.2 0.0 collective-permute-done.10
  33.2 0.6 %add_add_fusion = f32[64,256]{1,0:T(8,128)} fusion(f32[64,256]{1,0:T(8,128)S(1)} %collective-permute-done.10, f32[64,256]{1,0:T(8,128)S(1)} %collective-permute-done.9, f32[64,256]{1,0:T(8,128)S(1)} %get-tuple-element.77, f32[64,256]{1,0:T(8,128)S(1)} %collective-permute-done.8), kind=kLoop, calls=%fused_computation | loop fusion | flops 49152 | bytes 327680 | tf_op jit(solution)/shard_map/add | solution.py:851
  (1 shorter events, 0.0 us)
Async XLA Ops:
  1.4 9.7 %collective-permute-start.2 = (f32[168,128]{1,0:T(8,128)S(1)}, f32[168,128]{1,0:T(8,128)S(1)}, u32[]{:S(2)}, u32[]{:S(2)}) collective-permute-start(f32[168,128]{1,0:T(8,128)S(1)} %tables.1.refs_3_), channel_id=1, source_target_pairs={{0,26},{2,28},{4,30},{6,24},{8,18},{10,20},{12,22},{14,16},{16,10}... | collective-permute-start | bytes 258056 | tf_op jit(solution)/shard_map/ppermute | solution.py:721
  4.9 9.2 %collective-permute-start.1 = (f32[168,128]{1,0:T(8,128)S(1)}, f32[168,128]{1,0:T(8,128)S(1)}, u32[]{:S(2)}, u32[]{:S(2)}) collective-permute-start(f32[168,128]{1,0:T(8,128)S(1)} %tables.1.refs_3_), channel_id=1, source_target_pairs={{0,12},{2,14},{4,8},{6,10},{8,4},{10,6},{12,0},{14,2},{16,28},{18,... | collective-permute-start | bytes 258056 | tf_op jit(solution)/shard_map/ppermute | solution.py:721
  7.8 6.9 %collective-permute-start = (f32[168,128]{1,0:T(8,128)S(1)}, f32[168,128]{1,0:T(8,128)S(1)}, u32[]{:S(2)}, u32[]{:S(2)}) collective-permute-start(f32[168,128]{1,0:T(8,128)S(1)} %tables.1.refs_3_), channel_id=1, source_target_pairs={{0,22},{2,16},{4,18},{6,20},{8,30},{10,24},{12,26},{14,28},{16,6},... | collective-permute-start | bytes 258056 | tf_op jit(solution)/shard_map/ppermute | solution.py:721
  9.1 5.6 %copy-start = (f32[16,256]{1,0:T(8,128)S(1)}, f32[16,256]{1,0:T(8,128)}, u32[]{:S(2)}) copy-start(f32[16,256]{1,0:T(8,128)} %refs_4_.3) | copy-start | bytes 49156
  11.2 5.1 %collective-permute-start.5 = (f32[168,128]{1,0:T(8,128)S(1)}, f32[168,128]{1,0:T(8,128)S(1)}, u32[]{:S(2)}, u32[]{:S(2)}) collective-permute-start(f32[168,128]{1,0:T(8,128)S(1)} %collective-permute-done.2.refs_2_.refs_11_), channel_id=1, source_target_pairs={{0,8},{8,0},{16,24},{24,16},{1,9},{9,1},{17,25},{25,17},{2,10},{10... | collective-permute-start | bytes 258056 | tf_op jit(solution)/shard_map/ppermute | solution.py:724
  14.1 2.2 %collective-permute-start.4 = (f32[168,128]{1,0:T(8,128)S(1)}, f32[168,128]{1,0:T(8,128)S(1)}, u32[]{:S(2)}, u32[]{:S(2)}) collective-permute-start(f32[168,128]{1,0:T(8,128)S(1)} %collective-permute-done.1.refs_1_.refs_10_), channel_id=1, source_target_pairs={{0,8},{8,0},{16,24},{24,16},{1,9},{9,1},{17,25},{25,17},{2,10},{10... | collective-permute-start | bytes 258056 | tf_op jit(solution)/shard_map/ppermute | solution.py:724
  14.7 1.6 %collective-permute-start.3 = (f32[168,128]{1,0:T(8,128)S(1)}, f32[168,128]{1,0:T(8,128)S(1)}, u32[]{:S(2)}, u32[]{:S(2)}) collective-permute-start(f32[168,128]{1,0:T(8,128)S(1)} %collective-permute-done.refs_0_.refs_9_), channel_id=1, source_target_pairs={{0,8},{8,0},{16,24},{24,16},{1,9},{9,1},{17,25},{25,17},{2,10},{10... | collective-permute-start | bytes 258056 | tf_op jit(solution)/shard_map/ppermute | solution.py:724
  17.8 1.5 %collective-permute-start.6 = (f32[136,128]{1,0:T(8,128)S(1)}, f32[136,128]{1,0:T(8,128)S(1)}, u32[]{:S(2)}, u32[]{:S(2)}) collective-permute-start(f32[136,128]{1,0:T(8,128)S(1)} %get-tuple-element.56.refs_0_), channel_id=1, source_target_pairs={{0,8},{8,0},{16,24},{24,16},{1,9},{9,1},{17,25},{25,17},{2,10},{10... | collective-permute-start | bytes 208904 | tf_op jit(solution)/shard_map/ppermute | solution.py:805
  19.3 4.5 %collective-permute-start.7 = (f32[136,128]{1,0:T(8,128)S(1)}, f32[136,128]{1,0:T(8,128)S(1)}, u32[]{:S(2)}, u32[]{:S(2)}) collective-permute-start(f32[136,128]{1,0:T(8,128)S(1)} %get-tuple-element.58), channel_id=1, source_target_pairs={{0,16},{8,24},{16,0},{24,8},{1,17},{9,25},{17,1},{25,9},{2,18},{10... | collective-permute-start | bytes 208904 | tf_op jit(solution)/shard_map/ppermute | solution.py:805
  24.5 8.6 %collective-permute-start.8 = (f32[64,256]{1,0:T(8,128)S(1)}, f32[64,256]{1,0:T(8,128)S(1)}, u32[]{:S(2)}, u32[]{:S(2)}) collective-permute-start(f32[64,256]{1,0:T(8,128)S(1)} %get-tuple-element.78), channel_id=1, source_target_pairs={{0,2},{2,6},{4,0},{6,4},{1,3},{3,7},{5,1},{7,5},{8,10},{10,14},{12... | collective-permute-start | bytes 196616 | tf_op jit(solution)/shard_map/ppermute | solution.py:851
  26.2 6.9 %collective-permute-start.9 = (f32[64,256]{1,0:T(8,128)S(1)}, f32[64,256]{1,0:T(8,128)S(1)}, u32[]{:S(2)}, u32[]{:S(2)}) collective-permute-start(f32[64,256]{1,0:T(8,128)S(1)} %get-tuple-element.79), channel_id=1, source_target_pairs={{0,6},{2,4},{4,2},{6,0},{1,7},{3,5},{5,3},{7,1},{8,14},{10,12},{12... | collective-permute-start | bytes 196616 | tf_op jit(solution)/shard_map/ppermute | solution.py:851
  27.9 5.2 %collective-permute-start.10 = (f32[64,256]{1,0:T(8,128)S(1)}, f32[64,256]{1,0:T(8,128)S(1)}, u32[]{:S(2)}, u32[]{:S(2)}) collective-permute-start(f32[64,256]{1,0:T(8,128)S(1)} %get-tuple-element.80), channel_id=1, source_target_pairs={{0,4},{2,0},{4,6},{6,2},{1,5},{3,1},{5,7},{7,3},{8,12},{10,8},{12,... | collective-permute-start | bytes 196616 | tf_op jit(solution)/shard_map/ppermute | solution.py:851

commit v23 on v21

--- a/solution.py
+++ b/solution.py
@@ -481,13 +481,13 @@
 
     high, low, scale, write, inner, stepped, total, choose = take(8)
     rest_high, rest_low, small = take(3)
-    base, read_high, read_low, out_fade, out_gate, own, hidden_ref = take(7)
+    base, read_high, read_low, out_fade, own, hidden_ref = take(6)
     rows = dot_split((high[...], low[...]), (rest_high[...], rest_low[...]))
-    out_gate[...] = silu(rows[:, 0:ch] * scale[...])
+    gate = silu(rows[:, 0:ch] * scale[...])
     read = rows[:, ch:] * scale[...]
     read = split2(read)
     read_high[...], read_low[...] = read
-    out_fade[...] = jnp.exp(total[...])
+    out_fade[...] = jnp.exp(total[...]) * gate
     products = dot_split(read, split2(write[...]), NT)
     stepped_high, stepped_low = split2(stepped[...])
     select = (iota((8, ch), 1) == iota((8, ch), 0) * P).astype(f32).astype(bf16)
@@ -505,7 +505,7 @@
             split2(weights), (stepped_high[:, start:stop], stepped_low[:, start:stop])
         )
         parts.append(part + small[2:3, start:stop] * inner[:, start:stop])
-    base[...] = jnp.concatenate(parts, axis=1)
+    base[...] = jnp.concatenate(parts, axis=1) * gate
     share = T // nh
     hidden_ref[...] = high[...].astype(f32) + low[...].astype(f32)
     place = pl.multiple_of(lax.axis_index("head") * share, 8)
@@ -530,7 +530,8 @@
     out_total[0:ch, :] = jnp.where(
         later, factor * came_state + state, factor * state + came_state
     )
-    out_total[ch : ch + hl, :] = log + came_log
+    if out_total.shape[0] > ch:
+        out_total[ch : ch + hl, :] = log + came_log
     if prefix is None:
         out_prefix[0:ch, :] = jnp.where(later, came_state, 0.0)
         out_prefix[ch : ch + hl, :] = jnp.where(later, came_log, 0.0)
@@ -550,11 +551,11 @@
 def output_kernel(dims, bit, *refs):
     V, D, hl, ch, nh, ns, T, N = dims
     P = ch // hl
-    prefix, came, read_high, read_low, base, fade, gate, own, proj_high, proj_low = refs[:10]
-    groups, outs, partial_ref = refs[10], refs[11 : 11 + nh], refs[11 + nh]
+    prefix, came, read_high, read_low, base, fade, own, proj_high, proj_low, groups = refs[:10]
+    outs, partial_ref = refs[10 : 10 + nh], refs[10 + nh]
     entering = prefix_joined(dims, bit, prefix, came)
     carried = dot_split((read_high[...], read_low[...]), split2(entering), NT)
-    value = (base[...] + carried * fade[...]) * gate[...]
+    value = base[...] + carried * fade[...]
     square = dot(jnp.concatenate(split2(value * value), axis=0), groups[0:ch, 0:ch])
     square = square[T:] + square[0:T]
     value = value * lax.rsqrt(square * (1.0 / P) + epsilon)
@@ -767,17 +768,16 @@
         *others,
     )
 
-    base, read_high, read_low, fade, gate, own = pl.pallas_call(
+    base, read_high, read_low, fade, own = pl.pallas_call(
         functools.partial(block_kernel, dims),
         out_shape=(
             shape(T, ch),
             *halves(T, N),
             shape(T, ch),
-            shape(T, ch),
             shape(share, D),
         ),
         in_specs=[vmem] * 11,
-        out_specs=(vmem,) * 6,
+        out_specs=(vmem,) * 5,
         scratch_shapes=[pltpu.VMEM((T, D), f32)],
         compiler_params=params,
         cost_estimate=heavy,
@@ -812,7 +812,7 @@
 
         state, prefix = pl.pallas_call(
             functools.partial(join, bit, prefix is not None),
-            out_shape=(shape(ch + 8, N),) * 2,
+            out_shape=(shape(ch if bit == bits - 2 else ch + 8, N), shape(ch + 8, N)),
             in_specs=[vmem] * len(given),
             out_specs=(vmem,) * 2,
             compiler_params=params,
@@ -824,7 +824,7 @@
     parts = pl.pallas_call(
         functools.partial(output_kernel, dims, bits - 1),
         out_shape=(shape(share, D),) * nh,
-        in_specs=[vmem] * 11,
+        in_specs=[vmem] * 10,
         out_specs=(vmem,) * nh,
         scratch_shapes=[pltpu.VMEM((T, D), f32)],
         compiler_params=params,
@@ -836,7 +836,6 @@
         read_low,
         base,
         fade,
-        gate,
         own,
         proj_high,
         proj_low,

time: 33.7 us -> 33.7 us (level)
  no operation moved by 1% of the time
where the time goes in v23:
time: 33.7 us; the launch traced here: 33.5 us
  starting transfers between devices  13.9 us (41%)
  waiting for transfers between devices  10.4 us (31%)
  Pallas kernels  8.4 us (25%)
  other arithmetic  0.65 us (2%)
    ppermute x3, starting transfers between devices, per_device(): messages[k] = lax.ppermute(sent, ('seq', 'head'), pairs)  7.39 us
    ppermute x3, starting transfers between devices, per_device(): result = result + lax.ppermute(parts[k], 'head', pairs)  5.52 us
    ppermute x2, waiting for transfers between devices, per_device(): lax.ppermute(state, 'seq', [(seq, seq ^ 2 ** bit) for seq in range(ns)])  4.12 us
    ppermute x3, waiting for transfers between devices, per_device(): messages[k] = lax.ppermute(sent, ('seq', 'head'), pairs)  3.29 us
    ppermute x3, waiting for transfers between devices, per_device(): result = result + lax.ppermute(parts[k], 'head', pairs)  3.02 us
    pallas_call x1, Pallas kernels, per_device(): pl.pallas_call(functools.partial(prepare_kernel, dims), out_shape=(shape(...  2.08 us
    pallas_call x1, Pallas kernels, per_device(): pl.pallas_call(functools.partial(mix_kernel, dims), out_shape=(*halves(T,...  1.59 us
    pallas_call x1, Pallas kernels, per_device(): pl.pallas_call(functools.partial(project_kernel, dims), out_shape=(shape(...  1.5 us
  transfers between devices with their start and end apart: 11, of which 7 were waited for; matrix products, arithmetic and copies ran while one was open for 0% of the time, Pallas kernels for 14%

profile of v23, /device:TPU:0, one launch (start us, length us, event | category | flops | bytes accessed | tf_op | source)
XLA Modules:
  0.0 33.5 jit_solution(11880234112434737635)
XLA Ops:
  0.0 1.4 %tables.1.refs_3_ = f32[168,128]{1,0:T(8,128)S(1)} custom-call(f32[512,128]{1,0:T(8,128)} %bitcast.18, s32[1,256]{1,0:T(1,128)} %bitcast.20, f32[16,256]{1,0:T(8,128)} %refs_4_.3, f32[1,256]{1,0:T(1,128)} %bitcast.21, f32[2,256]{1,0:T(2,128)} %bitcast.19, f32[1,2]{1,0:T(1,128)} %bitcast.23, f32[1,2]{1,0:T(1,128)} %bitcast.24, f32[1,2]{1,0:T(1,128)} %bitcast.25, ...), custom_call_target="tpu_custom_call" | custom-call | tf_op jit(solution)/shard_map/tables/pallas_call | solution.py:642
  1.4 2.5 %collective-permute-start.2 = (f32[168,128]{1,0:T(8,128)S(1)}, f32[168,128]{1,0:T(8,128)S(1)}, u32[]{:S(2)}, u32[]{:S(2)}) collective-permute-start(f32[168,128]{1,0:T(8,128)S(1)} %tables.1.refs_3_), channel_id=1, source_target_pairs={{0,10},{2,12},{4,14},{6,8},{8,2},{10,4},{12,6},{14,0},{16,26},{18,... | collective-permute-start | bytes 258056 | tf_op jit(solution)/shard_map/ppermute | solution.py:719
  4.0 3.5 %collective-permute-start.1 = (f32[168,128]{1,0:T(8,128)S(1)}, f32[168,128]{1,0:T(8,128)S(1)}, u32[]{:S(2)}, u32[]{:S(2)}) collective-permute-start(f32[168,128]{1,0:T(8,128)S(1)} %tables.1.refs_3_), channel_id=1, source_target_pairs={{0,20},{2,22},{4,16},{6,18},{8,28},{10,30},{12,24},{14,26},{16,4},... | collective-permute-start | bytes 258056 | tf_op jit(solution)/shard_map/ppermute | solution.py:719
  7.5 1.4 %collective-permute-start = (f32[168,128]{1,0:T(8,128)S(1)}, f32[168,128]{1,0:T(8,128)S(1)}, u32[]{:S(2)}, u32[]{:S(2)}) collective-permute-start(f32[168,128]{1,0:T(8,128)S(1)} %tables.1.refs_3_), channel_id=1, source_target_pairs={{0,30},{2,24},{4,26},{6,28},{8,22},{10,16},{12,18},{14,20},{16,14}... | collective-permute-start | bytes 258056 | tf_op jit(solution)/shard_map/ppermute | solution.py:719
  8.8 0.0 copy-start
  8.8 2.1 %prepare.1 = (f32[16,128]{1,0:T(8,128)S(1)}, f32[8,128]{1,0:T(8,128)S(1)}, bf16[256,256]{1,0:T(8,128)(2,1)S(1)}, bf16[128,256]{1,0:T(8,128)(2,1)S(1)}, bf16[128,...) custom-call(f32[512,128]{1,0:T(8,128)} %bitcast.27, ...), custom_call_target="tpu_custom_call" | custom-call | flops 16106127360 | bytes 262144 | tf_op jit(solution)/shard_map/prepare/pallas_call | solution.py:685
  10.9 0.0 collective-permute-done.2.refs_2_.refs_11_
  10.9 0.1 collective-permute-start.5
  11.1 3.2 %collective-permute-done.1.refs_1_.refs_10_ = f32[168,128]{1,0:T(8,128)S(1)} collective-permute-done((f32[168,128]{1,0:T(8,128)S(1)}, f32[168,128]{1,0:T(8,128)S(1)}, u32[]{:S(2)}, u32[]{:S(2)}) %collective-permute-start.1) | collective-permute-done | bytes 86048 | tf_op jit(solution)/shard_map/ppermute | solution.py:719
  14.3 0.0 collective-permute-start.4
  14.3 0.1 collective-permute-done.refs_0_.refs_9_
  14.4 0.4 %collective-permute-start.3 = (f32[168,128]{1,0:T(8,128)S(1)}, f32[168,128]{1,0:T(8,128)S(1)}, u32[]{:S(2)}, u32[]{:S(2)}) collective-permute-start(f32[168,128]{1,0:T(8,128)S(1)} %collective-permute-done.refs_0_.refs_9_), channel_id=1, source_target_pairs={{0,8},{8,0},{16,24},{24,16},{1,9},{9,1},{17,25},{25,17},{2,10},{10... | collective-permute-start | bytes 258056 | tf_op jit(solution)/shard_map/ppermute | solution.py:722
  14.8 0.0 copy-done
  14.8 1.6 %mix.1 = (bf16[256,512]{1,0:T(8,128)(2,1)S(1)}, bf16[256,512]{1,0:T(8,128)(2,1)S(1)}, f32[256,256]{1,0:T(8,128)S(1)}) custom-call(f32[168,128]{1,0:T(8,128)S(1)} %collective-permute-done.refs_0_.refs_9_, f32[168,128]{1,0:T(8,128)S(1)} %collective-permute-done.1.refs_1_.refs_10_, f32[168,128]{1,0:T(8,128)S(1)} %collective-permute-done.2.refs_2_.refs_11_, ...), custom_call_target="tpu_custom_call" | custom-call | flops 16106127360 | bytes 262144 | tf_op jit(solution)/shard_map/mix/pallas_call | solution.py:724
  16.4 0.0 collective-permute-done.5.refs_14_
  16.4 0.0 collective-permute-done.4.refs_13_
  16.4 0.0 collective-permute-done.3.refs_12_
  16.4 1.5 %project.1 = (f32[136,128]{1,0:T(8,128)S(1)}, bf16[256,256]{1,0:T(8,128)(2,1)S(1)}, bf16[256,256]{1,0:T(8,128)(2,1)S(1)}, f32[256,128]{1,0:T(8,128)S(1)}, f32[25...) custom-call(bf16[256,512]{1,0:T(8,128)(2,1)S(1)} %get-tuple-element.46.refs_0_, ...), custom_call_target="tpu_custom_call" | custom-call | tf_op jit(solution)/shard_map/project/pallas_call | solution.py:742
  17.9 0.2 collective-permute-start.6
  18.1 1.2 %collective-permute-done.6.refs_1_ = f32[136,128]{1,0:T(8,128)S(1)} collective-permute-done((f32[136,128]{1,0:T(8,128)S(1)}, f32[136,128]{1,0:T(8,128)S(1)}, u32[]{:S(2)}, u32[]{:S(2)}) %collective-permute-start.6) | collective-permute-done | bytes 69664 | tf_op jit(solution)/shard_map/ppermute | solution.py:802
  19.3 0.3 collective-permute-start.7
  19.6 1.1 %block.1 = (f32[256,128]{1,0:T(8,128)S(1)}, bf16[256,128]{1,0:T(8,128)(2,1)S(1)}, bf16[256,128]{1,0:T(8,128)(2,1)S(1)}, f32[256,128]{1,0:T(8,128)S(1)}, f32[64,256]{1,0:T(8,128)S(1)}) custom-call(bf16[256,256]{1,0:T(8,128)(2,1)S(1)} %get-tuple-element.58.refs_0_, bf16[256,256]{1,0:T(8,128)(2,1)S(1)} %get-tuple-element.59.refs_1_, ...), custom_call_target="tpu_custom_call" | custom-call | flops 16106127360 | bytes 262144 | tf_op jit(solution)/shard_map/block/pallas_call | solution.py:771
  20.7 3.0 %collective-permute-done.7.refs_1_ = f32[128,128]{1,0:T(8,128)S(1)} collective-permute-done((f32[128,128]{1,0:T(8,128)S(1)}, f32[128,128]{1,0:T(8,128)S(1)}, u32[]{:S(2)}, u32[]{:S(2)}) %collective-permute-start.7) | collective-permute-done | bytes 65568 | tf_op jit(solution)/shard_map/ppermute | solution.py:802
  23.6 0.7 %output.1 = (f32[64,256]{1,0:T(8,128)S(1)}, f32[64,256]{1,0:T(8,128)S(1)}, f32[64,256]{1,0:T(8,128)S(1)}, f32[64,256]{1,0:T(8,128)S(1)}) custom-call(f32[136,128]{1,0:T(8,128)S(1)} %get-tuple-element.56.refs_0_, f32[128,128]{1,0:T(8,128)S(1)} %collective-permute-done.7.refs_1_, bf16[256,128]{1,0:T(8,128)(2,1)S(1)} %get-tuple-element.68.refs_2_, ...), custom_call_target="tpu_custom_call" | custom-call | tf_op jit(solution)/shard_map/output/pallas_call | solution.py:824
  24.3 2.1 %collective-permute-start.8 = (f32[64,256]{1,0:T(8,128)S(1)}, f32[64,256]{1,0:T(8,128)S(1)}, u32[]{:S(2)}, u32[]{:S(2)}) collective-permute-start(f32[64,256]{1,0:T(8,128)S(1)} %get-tuple-element.76), channel_id=1, source_target_pairs={{0,2},{2,6},{4,0},{6,4},{1,3},{3,7},{5,1},{7,5},{8,10},{10,14},{12... | collective-permute-start | bytes 196616 | tf_op jit(solution)/shard_map/ppermute | solution.py:847
  26.4 1.5 %collective-permute-start.9 = (f32[64,256]{1,0:T(8,128)S(1)}, f32[64,256]{1,0:T(8,128)S(1)}, u32[]{:S(2)}, u32[]{:S(2)}) collective-permute-start(f32[64,256]{1,0:T(8,128)S(1)} %get-tuple-element.77), channel_id=1, source_target_pairs={{0,6},{2,4},{4,2},{6,0},{1,7},{3,5},{5,3},{7,1},{8,14},{10,12},{12... | collective-permute-start | bytes 196616 | tf_op jit(solution)/shard_map/ppermute | solution.py:847
  27.9 1.9 %collective-permute-start.10 = (f32[64,256]{1,0:T(8,128)S(1)}, f32[64,256]{1,0:T(8,128)S(1)}, u32[]{:S(2)}, u32[]{:S(2)}) collective-permute-start(f32[64,256]{1,0:T(8,128)S(1)} %get-tuple-element.78), channel_id=1, source_target_pairs={{0,4},{2,0},{4,6},{6,2},{1,5},{3,1},{5,7},{7,3},{8,12},{10,8},{12,... | collective-permute-start | bytes 196616 | tf_op jit(solution)/shard_map/ppermute | solution.py:847
  29.9 0.1 collective-permute-done.8
  29.9 2.7 %collective-permute-done.9 = f32[64,256]{1,0:T(8,128)S(1)} collective-permute-done((f32[64,256]{1,0:T(8,128)S(1)}, f32[64,256]{1,0:T(8,128)S(1)}, u32[]{:S(2)}, u32[]{:S(2)}) %collective-permute-start.9) | collective-permute-done | bytes 65568 | tf_op jit(solution)/shard_map/ppermute | solution.py:847
  32.6 0.3 collective-permute-done.10
  32.9 0.6 %add_add_fusion = f32[64,256]{1,0:T(8,128)} fusion(f32[64,256]{1,0:T(8,128)S(1)} %collective-permute-done.10, f32[64,256]{1,0:T(8,128)S(1)} %collective-permute-done.9, f32[64,256]{1,0:T(8,128)S(1)} %get-tuple-element.75, f32[64,256]{1,0:T(8,128)S(1)} %collective-permute-done.8), kind=kLoop, calls=%fused_computation | loop fusion | flops 49152 | bytes 327680 | tf_op jit(solution)/shard_map/add | solution.py:847
  (1 shorter events, 0.0 us)
Async XLA Ops:
  1.4 9.5 %collective-permute-start.2 = (f32[168,128]{1,0:T(8,128)S(1)}, f32[168,128]{1,0:T(8,128)S(1)}, u32[]{:S(2)}, u32[]{:S(2)}) collective-permute-start(f32[168,128]{1,0:T(8,128)S(1)} %tables.1.refs_3_), channel_id=1, source_target_pairs={{0,10},{2,12},{4,14},{6,8},{8,2},{10,4},{12,6},{14,0},{16,26},{18,... | collective-permute-start | bytes 258056 | tf_op jit(solution)/shard_map/ppermute | solution.py:719
  4.0 10.3 %collective-permute-start.1 = (f32[168,128]{1,0:T(8,128)S(1)}, f32[168,128]{1,0:T(8,128)S(1)}, u32[]{:S(2)}, u32[]{:S(2)}) collective-permute-start(f32[168,128]{1,0:T(8,128)S(1)} %tables.1.refs_3_), channel_id=1, source_target_pairs={{0,20},{2,22},{4,16},{6,18},{8,28},{10,30},{12,24},{14,26},{16,4},... | collective-permute-start | bytes 258056 | tf_op jit(solution)/shard_map/ppermute | solution.py:719
  7.5 6.9 %collective-permute-start = (f32[168,128]{1,0:T(8,128)S(1)}, f32[168,128]{1,0:T(8,128)S(1)}, u32[]{:S(2)}, u32[]{:S(2)}) collective-permute-start(f32[168,128]{1,0:T(8,128)S(1)} %tables.1.refs_3_), channel_id=1, source_target_pairs={{0,30},{2,24},{4,26},{6,28},{8,22},{10,16},{12,18},{14,20},{16,14}... | collective-permute-start | bytes 258056 | tf_op jit(solution)/shard_map/ppermute | solution.py:719
  8.8 6.0 %copy-start = (f32[16,256]{1,0:T(8,128)S(1)}, f32[16,256]{1,0:T(8,128)}, u32[]{:S(2)}) copy-start(f32[16,256]{1,0:T(8,128)} %refs_4_.3) | copy-start | bytes 49156
  10.9 5.5 %collective-permute-start.5 = (f32[168,128]{1,0:T(8,128)S(1)}, f32[168,128]{1,0:T(8,128)S(1)}, u32[]{:S(2)}, u32[]{:S(2)}) collective-permute-start(f32[168,128]{1,0:T(8,128)S(1)} %collective-permute-done.2.refs_2_.refs_11_), channel_id=1, source_target_pairs={{0,8},{8,0},{16,24},{24,16},{1,9},{9,1},{17,25},{25,17},{2,10},{10... | collective-permute-start | bytes 258056 | tf_op jit(solution)/shard_map/ppermute | solution.py:722
  14.3 2.1 %collective-permute-start.4 = (f32[168,128]{1,0:T(8,128)S(1)}, f32[168,128]{1,0:T(8,128)S(1)}, u32[]{:S(2)}, u32[]{:S(2)}) collective-permute-start(f32[168,128]{1,0:T(8,128)S(1)} %collective-permute-done.1.refs_1_.refs_10_), channel_id=1, source_target_pairs={{0,8},{8,0},{16,24},{24,16},{1,9},{9,1},{17,25},{25,17},{2,10},{10... | collective-permute-start | bytes 258056 | tf_op jit(solution)/shard_map/ppermute | solution.py:722
  14.4 2.0 %collective-permute-start.3 = (f32[168,128]{1,0:T(8,128)S(1)}, f32[168,128]{1,0:T(8,128)S(1)}, u32[]{:S(2)}, u32[]{:S(2)}) collective-permute-start(f32[168,128]{1,0:T(8,128)S(1)} %collective-permute-done.refs_0_.refs_9_), channel_id=1, source_target_pairs={{0,8},{8,0},{16,24},{24,16},{1,9},{9,1},{17,25},{25,17},{2,10},{10... | collective-permute-start | bytes 258056 | tf_op jit(solution)/shard_map/ppermute | solution.py:722
  17.9 1.3 %collective-permute-start.6 = (f32[136,128]{1,0:T(8,128)S(1)}, f32[136,128]{1,0:T(8,128)S(1)}, u32[]{:S(2)}, u32[]{:S(2)}) collective-permute-start(f32[136,128]{1,0:T(8,128)S(1)} %get-tuple-element.55.refs_0_), channel_id=1, source_target_pairs={{0,8},{8,0},{16,24},{24,16},{1,9},{9,1},{17,25},{25,17},{2,10},{10... | collective-permute-start | bytes 208904 | tf_op jit(solution)/shard_map/ppermute | solution.py:802
  19.3 4.3 %collective-permute-start.7 = (f32[128,128]{1,0:T(8,128)S(1)}, f32[128,128]{1,0:T(8,128)S(1)}, u32[]{:S(2)}, u32[]{:S(2)}) collective-permute-start(f32[128,128]{1,0:T(8,128)S(1)} %get-tuple-element.57), channel_id=1, source_target_pairs={{0,16},{8,24},{16,0},{24,8},{1,17},{9,25},{17,1},{25,9},{2,18},{10... | collective-permute-start | bytes 196616 | tf_op jit(solution)/shard_map/ppermute | solution.py:802
  24.3 5.6 %collective-permute-start.8 = (f32[64,256]{1,0:T(8,128)S(1)}, f32[64,256]{1,0:T(8,128)S(1)}, u32[]{:S(2)}, u32[]{:S(2)}) collective-permute-start(f32[64,256]{1,0:T(8,128)S(1)} %get-tuple-element.76), channel_id=1, source_target_pairs={{0,2},{2,6},{4,0},{6,4},{1,3},{3,7},{5,1},{7,5},{8,10},{10,14},{12... | collective-permute-start | bytes 196616 | tf_op jit(solution)/shard_map/ppermute | solution.py:847
  26.4 6.2 %collective-permute-start.9 = (f32[64,256]{1,0:T(8,128)S(1)}, f32[64,256]{1,0:T(8,128)S(1)}, u32[]{:S(2)}, u32[]{:S(2)}) collective-permute-start(f32[64,256]{1,0:T(8,128)S(1)} %get-tuple-element.77), channel_id=1, source_target_pairs={{0,6},{2,4},{4,2},{6,0},{1,7},{3,5},{5,3},{7,1},{8,14},{10,12},{12... | collective-permute-start | bytes 196616 | tf_op jit(solution)/shard_map/ppermute | solution.py:847
  27.9 5.0 %collective-permute-start.10 = (f32[64,256]{1,0:T(8,128)S(1)}, f32[64,256]{1,0:T(8,128)S(1)}, u32[]{:S(2)}, u32[]{:S(2)}) collective-permute-start(f32[64,256]{1,0:T(8,128)S(1)} %get-tuple-element.78), channel_id=1, source_target_pairs={{0,4},{2,0},{4,6},{6,2},{1,5},{3,1},{5,7},{7,3},{8,12},{10,8},{12,... | collective-permute-start | bytes 196616 | tf_op jit(solution)/shard_map/ppermute | solution.py:847
